TPU v7x, 32 devices: a whole 2x2x4 slice. The times are simulated.
32 devices in a mesh: parts: 1, clus: 4 (over z), lvl: 4 (over y, x), rep: 2 (over core).
Axes of the slice: x: 2, y: 2, z: 4, core: 2. Of those that a mesh axis runs over, the one named last changes fastest.
Arguments:
- voxel_field: bfloat16 [256, 24, 512], P(('lvl', 'rep'), None, ('parts', 'clus')), may hold values from -6 to 6
- row_basis: bfloat16 [256, 64, 512], P(('lvl', 'rep'), None, ('parts', 'clus')), may hold values from -0.375 to 0.375
- near_block: bfloat16 [256, 256, 512], P(('lvl', 'rep'), None, ('parts', 'clus')), may hold values from -0.375 to 0.375
- up_transfer: bfloat16 [64, 64, 512], P(None, None, ('parts', 'clus')), may hold values from -0.25 to 0.25
- coupling: bfloat16 [64, 64, 8, 2, 512], P(None, None, ('lvl', 'rep'), None, ('parts', 'clus')), may hold values from -0.1875 to 0.1875
- parent_coupling: bfloat16 [64, 64, 8, 2, 64], P(None, None, ('lvl', 'rep'), None, ('parts', 'clus')), may hold values from -0.1875 to 0.1875
- down_transfer: bfloat16 [64, 64, 512], P(None, None, ('parts', 'clus')), may hold values from -0.75 to 0.75
- column_basis: bfloat16 [64, 256, 512], P(None, ('lvl', 'rep'), ('parts', 'clus')), may hold values from -0.75 to 0.75
- parent_perm: int32 [64], P('parts'), may hold values from 0 to 63, as said below
- partner_owner: int32 [8, 512, 2], P(('lvl', 'rep'), ('parts', 'clus')), may hold values from 0 to 3, all different within a row; in each aligned block of 128 rows (0 to 127, 128 to 255, ..., all dimensions but the last counted through in order) at most 128 rows name the same one
- partner_local: int32 [8, 512, 2], P(('lvl', 'rep'), ('parts', 'clus')), may hold values from 0 to 127
- parent_owner: int32 [8, 64, 2], P(('lvl', 'rep'), ('parts', 'clus')), may hold values from 0 to 3, all different within a row; in each aligned block of 16 rows (0 to 15, 16 to 31, ..., all dimensions but the last counted through in order) at most 16 rows name the same one
- parent_local: int32 [8, 64, 2], P(('lvl', 'rep'), ('parts', 'clus')), may hold values from 0 to 15
- block_count: int32 [512], P(('parts', 'clus')), may hold values from 4 to 16
Outputs:
- adjoint: bfloat16 [256, 24, 512], P(('lvl', 'rep'), None, ('parts', 'clus'))
Inputs may be any that keep to these rules, and one draw needn't show every extreme that they name: `parent_perm`: a permutation of the 64 parents; of the 16 parents of each aligned block, exactly 4 land in each aligned block of 16. `partner_owner`: the slots of one leaf in one slot group name distinct owners; in the rows of one device (one slot group, 128 leaves of one owner) no owner is named by more than 128 slots. `parent_owner`: the slots of one parent in one slot group name distinct owners; in the rows of one device (one slot group, 16 parents of one owner) no owner is named by more than 16 slots.
All inputs are finite; a program needn't handle non-finite values.
Results may differ from a plain program's by a relative error of at most 0.0059.
Values may be sent and summed in bfloat16 or wider, within the bound.
No kernel may reach another device: no remote copies, remote signals or barrier semaphores. Data moves between devices by JAX's collectives and lax.ppermute only.
A program may use at most 128 MiB of HBM per device.

v0:
```python
import jax
import jax.numpy as jnp
from jax import lax
from jax.sharding import PartitionSpec as P


def per_device(
    voxel_field,
    row_basis,
    near_block,
    up_transfer,
    coupling,
    parent_coupling,
    down_transfer,
    column_basis,
    parent_perm,
    partner_owner,
    partner_local,
    parent_owner,
    parent_local,
    block_count,
):
    slab_rows, vectors, leaves = voxel_field.shape
    rank_width = row_basis.shape[1]
    parents = parent_coupling.shape[4]
    children = leaves // parents
    slot_dev = partner_owner.shape[2]
    pslot_dev = parent_owner.shape[2]
    owner_self = lax.axis_index("clus")
    own_perm = lax.dynamic_slice_in_dim(parent_perm, owner_self * parents, parents)
    send_order = jnp.argsort(own_perm // parents, stable=True)
    field_blocks = voxel_field.reshape(slab_rows, vectors, parents, children)
    outgoing = jnp.take(field_blocks, send_order, axis=2).reshape(slab_rows, vectors, leaves)
    arrived = lax.all_to_all(outgoing, "clus", split_axis=2, concat_axis=2, tiled=True)
    flagged = jnp.where(parent_perm // parents == owner_self, 0, 1)
    sources = jnp.argsort(flagged, stable=True)[:parents]
    col_slots = jnp.take(parent_perm, sources) % parents
    placing = jnp.argsort(col_slots)
    regrouped = jnp.take(
        arrived.reshape(slab_rows, vectors, parents, children), placing, axis=2
    ).reshape(slab_rows, vectors, leaves)
    partial_value = jnp.einsum(
        "mvl,mkl->vkl", regrouped, row_basis, preferred_element_type=jnp.float32
    )
    coeffs = lax.psum(partial_value, ("lvl", "rep")).astype(jnp.bfloat16)
    parent_coeffs = jnp.einsum(
        "jkpc,vjpc->vkp",
        up_transfer.reshape(rank_width, rank_width, parents, children),
        coeffs.reshape(vectors, rank_width, parents, children),
        preferred_element_type=jnp.float32,
    ).astype(jnp.bfloat16)
    near = lax.psum_scatter(
        jnp.einsum("pml,pvl->mvl", near_block, regrouped, preferred_element_type=jnp.float32),
        ("lvl", "rep"),
        scatter_dimension=0,
        tiled=True,
    )
    leaf_owner = partner_owner[0].reshape(-1)
    leaf_local = partner_local[0].reshape(-1)
    up_owner = parent_owner[0].reshape(-1)
    up_local = parent_local[0].reshape(-1)
    whole_leaf, whole_up = (
        lax.all_gather(coeffs, "clus", axis=2, tiled=True),
        lax.all_gather(parent_coeffs, "clus", axis=2, tiled=True),
    )
    leaf_rows = jnp.take(whole_leaf, leaf_owner * leaves + leaf_local, axis=2)
    up_rows = jnp.take(whole_up, up_owner * parents + up_local, axis=2)
    group_index = lax.axis_index(("lvl", "rep"))
    slot_number = group_index * slot_dev + jnp.arange(slot_dev, dtype=jnp.int32)[None, :]
    live_mask = slot_number < block_count[:, None]
    leaf_rows = leaf_rows.reshape(vectors, rank_width, leaves, slot_dev)
    leaf_rows = jnp.where(live_mask[None, None], leaf_rows, jnp.zeros_like(leaf_rows))
    leaf_blocks = coupling.reshape(rank_width, rank_width, slot_dev, leaves)
    leaf_far = jnp.einsum(
        "jkil,vjli->vkl", leaf_blocks, leaf_rows, preferred_element_type=jnp.float32
    )
    up_rows = up_rows.reshape(vectors, rank_width, parents, pslot_dev)
    parent_blocks = parent_coupling.reshape(rank_width, rank_width, pslot_dev, parents)
    parent_part = jnp.einsum(
        "jkip,vjpi->vkp", parent_blocks, up_rows, preferred_element_type=jnp.float32
    )
    leaf_total, parent_total = lax.psum((leaf_far, parent_part), ("lvl", "rep"))
    parent_far = parent_total.astype(jnp.bfloat16)
    downward = jnp.einsum(
        "jkpc,vjp->vkpc",
        down_transfer.reshape(rank_width, rank_width, parents, children),
        parent_far,
        preferred_element_type=jnp.float32,
    )
    far_coeffs = (leaf_total + downward.reshape(vectors, rank_width, leaves)).astype(jnp.bfloat16)
    far_field = jnp.einsum(
        "kml,vkl->mvl", column_basis, far_coeffs, preferred_element_type=jnp.float32
    )
    return (near + far_field).astype(jnp.bfloat16)


def solution(mesh):
    return jax.shard_map(
        per_device,
        mesh=mesh,
        in_specs=(
            P(("lvl", "rep"), None, ("parts", "clus")),
            P(("lvl", "rep"), None, ("parts", "clus")),
            P(("lvl", "rep"), None, ("parts", "clus")),
            P(None, None, ("parts", "clus")),
            P(None, None, ("lvl", "rep"), None, ("parts", "clus")),
            P(None, None, ("lvl", "rep"), None, ("parts", "clus")),
            P(None, None, ("parts", "clus")),
            P(None, ("lvl", "rep"), ("parts", "clus")),
            P("parts"),
            P(("lvl", "rep"), ("parts", "clus"), None),
            P(("lvl", "rep"), ("parts", "clus"), None),
            P(("lvl", "rep"), ("parts", "clus"), None),
            P(("lvl", "rep"), ("parts", "clus"), None),
            P(("parts", "clus")),
        ),
        out_specs=P(("lvl", "rep"), None, ("parts", "clus")),
        check_vma=False,
    )
```

profile of v0, /device:TPU:0, one launch (start us, length us, event | category | flops | bytes accessed | tf_op | source)
XLA Modules:
  0.0 250.7 jit_solution(14813169856755665465)
XLA Ops:
  6.5 0.8 and_select_fusion.3
  7.3 1.2 sort.51
  8.6 1.3 copy.107
  9.9 0.8 gather_fusion.3
  11.6 1.4 reshape.228
  13.0 6.3 %all-to-all-start = ((bf16[4,2,12288]{2,1,0:T(2,128)(2,1)}), bf16[4,2,12288]{2,1,0:T(2,128)(2,1)S(1)}, u32[]{:S(2)}, u32[]{:S(2)}) async-start(bf16[4,2,12288]{2,1,0:T(2,128)(2,1)} %reshape.228), calls=%async_computation | async-start | bytes 393216 | tf_op jit(solution)/shard_map/all_to_all | solution.py:34
  19.4 2.1 sort.52
  22.2 1.3 sort.53
  23.5 2.5 %copy.117 = bf16[32,64,128]{1,0,2:T(8,128)(2,1)} copy(bf16[32,64,128]{2,1,0:T(8,128)(2,1)S(1)} %copy-done.6) | data formatting | bytes 1048576 | tf_op args[1]
  27.4 0.8 gather_fusion.4
  28.6 0.9 copy-done.2
  30.3 53.5 %all-reduce.4 = bf16[24,64,128]{1,0,2:T(8,128)(2,1)S(1)} all-reduce(f32[24,64,128]{1,0,2:T(8,128)S(1)} %convolution_bitcast_fusion.1), channel_id=1, replica_groups=mesh['parts'=1,'clus'=4,'lvl'=4,'rep'=2] {'lvl','rep'}, use_global_device_ids=true, to_apply=%region_4.6 | all-reduce | flops 196608 | bytes 1179648 | tf_op jit(solution)/shard_map/psum | solution.py:45
  83.8 1.3 copy.118
  85.6 7.8 %copy.121 = bf16[64,64,2,128]{1,0,2,3:T(8,128)(2,1)} copy(bf16[64,64,2,128]{3,2,1,0:T(2,128)(2,1)} %bitcast.93) | data formatting | bytes 4194304 | tf_op jit(solution)/shard_map/reshape | solution.py:73
  93.6 28.6 %all-gather.2.cloned.1.call-done = bf16[24,64,512]{2,1,0:T(8,128)(2,1)} async-done(((bf16[24,64,128]{2,1,0:T(8,128)(2,1)}), bf16[24,64,512]{2,1,0:T(8,128)(2,1)}) %all-gather.2.cloned.1.call-update) | async-done | bytes 1572880 | tf_op jit(solution)/shard_map/all_gather | solution.py:63
  122.2 5.0 %copy.120 = bf16[24,64,512]{1,0,2:T(8,128)(2,1)} copy(bf16[24,64,512]{2,1,0:T(8,128)(2,1)} %all-gather.2.cloned.1.call-done) | data formatting | bytes 3145728 | tf_op jit(solution)/shard_map/all_gather | solution.py:63
  127.1 2.9 %gather_fusion.1 = bf16[256,24,64]{2,1,0:T(8,128)(2,1)S(1)} fusion(bf16[24,64,512]{1,0,2:T(8,128)(2,1)} %copy.120, s32[1024]{0:T(1024)S(1)} %pad_clamp_fusion.1), kind=kCustom, calls=%fused_computation.3 | custom fusion | bytes 1573888 | tf_op jit(solution)/shard_map/jit(_take)/gather | solution.py:66
  130.0 4.8 %fusion.6 = f32[24,64,128]{1,0,2:T(8,128)} fusion(bf16[64,64,2,128]{1,0,2,3:T(8,128)(2,1)} %copy.121, bf16[24,64,128,2]{1,0,3,2:T(8,128)(2,1)S(1)} %bitcast.90, pred[128,2]{1,0:T(8,128)(4,1)S(1)} %copy.115, pred[128,2]{1,0:T(8,128)(4,1)S(1)} %broadcast_compare_fusion), kind=kOutput, calls=%fused_computation.13 | convolution fusion | flops 51118080 | bytes 3670528 | tf_op jit(solution)/shard_map/jkil,vjli->vkl/dot_general | solution.py:74
  135.1 3.4 %copy.113 = bf16[32,256,128]{1,0,2:T(8,128)(2,1)S(1)} copy(bf16[32,256,128]{2,1,0:T(8,128)(2,1)} %param.18) | data formatting | bytes 4194304 | tf_op args[2]
  138.5 3.8 %convolution_bitcast_fusion = f32[256,24,128]{0,1,2:T(8,128)} fusion(bf16[32,256,128]{1,0,2:T(8,128)(2,1)S(1)} %copy.113, bf16[32,24,128]{0,2,1:T(8,128)(2,1)} %copy-done.2), kind=kOutput, calls=%fused_computation.5 | convolution fusion | flops 50331648 | bytes 5439488 | tf_op jit(solution)/shard_map/pml,pvl->mvl/dot_general | solution.py:53
  142.2 3.6 %copy.114 = f32[256,24,128]{2,1,0:T(8,128)} copy(f32[256,24,128]{0,1,2:T(8,128)} %convolution_bitcast_fusion) | data formatting | bytes 6291456 | tf_op jit(solution)/shard_map/pml,pvl->mvl/transpose | solution.py:53
  145.8 1.2 copy-done.5
  147.1 3.7 %copy.135 = bf16[64,64,128]{1,0,2:T(8,128)(2,1)} copy(bf16[64,64,128]{2,1,0:T(8,128)(2,1)S(1)} %copy-done.5) | data formatting | bytes 2097152 | tf_op jit(solution)/shard_map/reshape | solution.py:48
  151.1 3.9 %copy.136 = bf16[64,64,128]{1,0,2:T(8,128)(2,1)S(1)} copy(bf16[64,64,128]{2,1,0:T(8,128)(2,1)} %param.22) | data formatting | bytes 2097152 | tf_op jit(solution)/shard_map/reshape | solution.py:86
  155.0 3.8 %copy.129 = bf16[64,32,128]{0,1,2:T(8,128)(2,1)} copy(bf16[64,32,128]{2,1,0:T(8,128)(2,1)} %param.23) | data formatting | bytes 1048576 | tf_op args[7]
  158.8 2.1 fusion.10
  160.9 15.0 %all_gather.7 = bf16[24,64,64]{1,0,2:T(8,128)(2,1)S(1)} all-gather(bf16[24,64,16]{1,0,2:T(8,128)(2,1)S(1)} %fusion.10), channel_id=1, replica_groups=mesh['parts'=1,'clus'=4,'lvl'=4,'rep'=2] {'clus'}, dimensions={2}, use_global_device_ids=true | all-gather | bytes 245760 | tf_op jit(solution)/shard_map/all_gather | solution.py:64
  177.0 25.3 %psum.23 = bf16[24,64,16]{1,0,2:T(8,128)(2,1)S(1)} all-reduce(f32[24,64,16]{1,0,2:T(8,128)S(1)} %convolution_bitcast_fusion.2), channel_id=1, replica_groups=mesh['parts'=1,'clus'=4,'lvl'=4,'rep'=2] {'lvl','rep'}, use_global_device_ids=true, to_apply=%region_6.8 | all-reduce | flops 24576 | bytes 147456 | tf_op jit(solution)/shard_map/psum | solution.py:82
  202.3 1.5 fusion.19
  203.8 2.4 fusion
  207.5 35.0 %reduce-scatter.2.cloned.1.call-done = f32[32,24,128]{2,1,0:T(8,128)} async-done(((f32[256,24,128]{2,1,0:T(8,128)}), f32[32,24,128]{2,1,0:T(8,128)}) %reduce-scatter.2.cloned.1.call-update) | async-done | bytes 393232 | tf_op jit(solution)/shard_map/reduce_scatter | solution.py:52
  242.4 1.7 fusion.16
  (68 shorter events, 7.4 us)
Async XLA Ops:
  6.5 170.0 %copy-start = (bf16[64,64,1,2,16]{1,4,3,2,0:T(8,128)(2,1)S(1)}, bf16[64,64,1,2,16]{1,4,3,2,0:T(8,128)(2,1)}, u32[]{:S(2)}) copy-start(bf16[64,64,1,2,16]{1,4,3,2,0:T(8,128)(2,1)} %param.21) | copy-start | bytes 786436
  10.8 8.6 %copy-start.1 = (s32[64]{0:T(128)S(1)}, s32[64]{0:T(128)}, u32[]{:S(2)}) copy-start(s32[64]{0:T(128)} %param.24) | copy-start | bytes 772
  11.1 12.5 %copy-start.6 = (bf16[32,64,128]{2,1,0:T(8,128)(2,1)S(1)}, bf16[32,64,128]{2,1,0:T(8,128)(2,1)}, u32[]{:S(2)}) copy-start(bf16[32,64,128]{2,1,0:T(8,128)(2,1)} %param.17) | copy-start | bytes 1572868
  13.0 13.8 %all-to-all-start = ((bf16[4,2,12288]{2,1,0:T(2,128)(2,1)}), bf16[4,2,12288]{2,1,0:T(2,128)(2,1)S(1)}, u32[]{:S(2)}, u32[]{:S(2)}) async-start(bf16[4,2,12288]{2,1,0:T(2,128)(2,1)} %reshape.228), calls=%async_computation | async-start | bytes 393216 | tf_op jit(solution)/shard_map/all_to_all | solution.py:34
  19.4 102.8 %all-gather.2.cloned.1.call-start = ((), (), s32[]{:S(2)}) async-start(), calls=%async_computation.3 | async-start | bytes 1966080 | tf_op jit(solution)/shard_map/all_gather | solution.py:63
  28.3 1.2 copy-start.4
  28.6 0.9 copy-start.2
  30.3 54.9 %copy-start.7 = (s32[1,128,2]{1,2,0:T(2,128)S(1)}, s32[1,128,2]{1,2,0:T(2,128)}, u32[]{:S(2)}) copy-start(s32[1,128,2]{1,2,0:T(2,128)} %param.26) | copy-start | bytes 3076
  30.3 54.9 %copy-start.8 = (s32[1,128,2]{1,2,0:T(2,128)S(1)}, s32[1,128,2]{1,2,0:T(2,128)}, u32[]{:S(2)}) copy-start(s32[1,128,2]{1,2,0:T(2,128)} %param.25) | copy-start | bytes 3076
  85.1 118.7 %all-reduce.3.cloned.1.call-start = ((), (), s32[]{:S(2)}) async-start(), calls=%async_computation.4 | async-start | bytes 3145728 | tf_op jit(solution)/shard_map/psum | solution.py:82
  85.6 7.9 %copy-start.11 = (s32[128]{0:T(128)S(1)}, s32[128]{0:T(128)}, u32[]{:S(2)}) copy-start(s32[128]{0:T(128)} %param.29) | copy-start | bytes 1540
  134.8 107.6 %reduce-scatter.2.cloned.1.call-start = ((), (), s32[]{:S(2)}) async-start(), calls=%async_computation.2 | async-start | bytes 3538944 | tf_op jit(solution)/shard_map/reduce_scatter | solution.py:52
  145.8 1.2 copy-start.5
  147.1 3.7 %copy-start.9 = (s32[1,16,2]{1,2,0:T(2,128)S(1)}, s32[1,16,2]{1,2,0:T(2,128)}, u32[]{:S(2)}) copy-start(s32[1,16,2]{1,2,0:T(2,128)} %param.28) | copy-start | bytes 388
  147.1 3.7 %copy-start.10 = (s32[1,16,2]{1,2,0:T(2,128)S(1)}, s32[1,16,2]{1,2,0:T(2,128)}, u32[]{:S(2)}) copy-start(s32[1,16,2]{1,2,0:T(2,128)} %param.27) | copy-start | bytes 388
  203.8 2.5 copy-start.3
Sparse Core Ops, SparseCore 0:
  85.3 36.8 all-gather.1
  135.0 57.7 all-reduce.2
  196.5 45.8 reduce-scatter.1
where the time goes:
time: 252 us; the launch traced here: 251 us
  blocking collectives  93.8 us (37%)
  waiting for transfers between devices  64.4 us (26%)
  local copies, waits for them, and re-layouts  48.1 us (19%)
  matrix products  14 us (6%)
  between operations  13.4 us (5%)
  other arithmetic  10.3 us (4%)
  starting transfers between devices  6.58 us (3%)
    psum x1, blocking collectives, per_device(): coeffs = lax.psum(partial_value, ('lvl', 'rep')).astype(jnp.bfloat16)  53.5 us
    reduce_scatter x1, waiting for transfers between devices, per_device(): lax.psum_scatter(jnp.einsum('pml,pvl->mvl', near_block, regrouped, prefer...  35 us
    all_gather x1, waiting for transfers between devices, per_device(): lax.all_gather(coeffs, 'clus', axis=2, tiled=True)  28.6 us
    psum x1, blocking collectives, per_device(): leaf_total, parent_total = lax.psum((leaf_far, parent_part), ('lvl', 'rep'))  25.3 us
    unnamed x30, local copies, waits for them, and re-layouts  15.2 us
    all_gather x1, blocking collectives, per_device(): lax.all_gather(parent_coeffs, 'clus', axis=2, tiled=True)  15 us
    reshape x1, local copies, waits for them, and re-layouts, per_device(): leaf_blocks = coupling.reshape(rank_width, rank_width, slot_dev, leaves)  7.84 us
    all_to_all x1, starting transfers between devices, per_device(): lax.all_to_all(outgoing, 'clus', split_axis=2, concat_axis=2, tiled=True)  6.32 us
  transfers between devices with their start and end apart: 4, of which 3 were waited for; matrix products, arithmetic and copies ran while one was open for 18% of the time, Pallas kernels for 0%

commit v1 on v0

v1 whole, which is shorter than its diff:
```python
import functools

import jax
import jax.numpy as jnp
from jax import lax
from jax.experimental import pallas as pl
from jax.experimental.pallas import tpu as pltpu
from jax.sharding import PartitionSpec as P

F32 = jnp.float32
BF16 = jnp.bfloat16
VMEM_LIMIT = 40 * 1024 * 1024


def vmem():
    return pl.BlockSpec(memory_space=pltpu.VMEM)


def smem():
    return pl.BlockSpec(memory_space=pltpu.SMEM)


def params(**more):
    return pltpu.CompilerParams(vmem_limit_bytes=VMEM_LIMIT, **more)


def cost(flops, nbytes):
    return pl.CostEstimate(flops=flops, bytes_accessed=nbytes, transcendentals=0)


def iota(shape, dim):
    return lax.broadcasted_iota(jnp.int32, shape, dim)


def row_of(ref, row):
    return ref[pl.ds(row, 1), :]


def mac_rows(total_steps, weight_at, row_at, accs, unroll):
    def body(step, carry):
        weight = weight_at(step)
        return tuple(acc + weight * row_at(step, n) for n, acc in enumerate(carry))

    return lax.fori_loop(0, total_steps, body, tuple(accs), unroll=unroll)


def pack_kernel(owners, vh, perm_ref, ids_ref, own_ref, peer_ref, out_ref, rows_scr, count_scr):
    slab, vectors, leaves = own_ref.shape
    parents = perm_ref.shape[0] // owners
    children = leaves // parents
    reps = vectors // vh
    width = leaves // owners
    me, parity = ids_ref[0], ids_ref[2]
    for owner in range(owners):
        count_scr[owner] = 0
    row = iota((leaves, leaves), 0)
    lane = iota((leaves, leaves), 1)
    parent_of_row = row // children
    target = row % children
    for parent in range(parents):
        place = perm_ref[me * parents + parent]
        owner = place // parents
        rank = count_scr[owner]
        count_scr[owner] = rank + 1
        code = (owner ^ me) * leaves + rank * children
        target = target + jnp.where(parent_of_row == parent, code, 0)
    part = (slab // owners) * vh
    rows_scr[0] = own_ref[...].reshape(slab * vectors, leaves).astype(F32)
    rows_scr[1] = peer_ref[...].reshape(slab * vectors, leaves).astype(F32)
    pieces = []
    for q in range(owners):
        start = q * (slab // owners) * vectors + parity
        pieces.append(
            jnp.concatenate(
                [rows_scr[s, pl.ds(start, part, stride=reps), :] for s in range(2)], axis=0
            ).astype(BF16)
        )
    for s in range(owners):
        total = jnp.zeros((2 * part, leaves), F32)
        for q in range(owners):
            onehot = jnp.where(target + (q * width - s * leaves) == lane, 1.0, 0.0).astype(BF16)
            total = total + jnp.dot(pieces[q], onehot, preferred_element_type=F32)
        out_ref[s] = total.astype(BF16)


def place_kernel(owners, children, perm_ref, ids_ref, out_ref, code_scr, count_scr):
    leaves = out_ref.shape[1]
    everyone = perm_ref.shape[0]
    parents = everyone // owners
    me = ids_ref[0]
    for owner in range(owners):
        count_scr[owner] = 0

    def body(parent, carry):
        place = perm_ref[parent]
        source = parent // parents
        mine = (place // parents) == me
        rank = count_scr[source]
        slot = jnp.where(mine, place % parents, parents)
        code_scr[slot] = (source ^ me) * leaves + rank * children
        count_scr[source] = rank + jnp.where(mine, 1, 0)
        return carry

    lax.fori_loop(0, everyone, body, 0, unroll=8)
    lane = iota(out_ref.shape, 1)
    code = lane % children
    for parent in range(parents):
        code = code + jnp.where(lane // children == parent, code_scr[parent], 0)
    out_ref[...] = code


def coeff_kernel(owners, lvls, vh, vs, ids_ref, code_ref, *refs):
    chunks = refs[:owners]
    own_ref, peer_ref = refs[owners : owners + 2]
    field_ref, keep_ref = refs[owners + 2 : owners + 4]
    sends = refs[owners + 4 :]
    slab, rank_width, leaves = own_ref.shape
    width = leaves // owners
    part = (slab // owners) * vh
    lvl = ids_ref[1]
    code = jnp.broadcast_to(code_ref[0:1, :], (leaves, leaves))
    row = iota((leaves, leaves), 0)
    for q in range(owners):
        total = jnp.zeros((2 * part, leaves), F32)
        for s in range(owners):
            onehot = jnp.where(code + (q * width - s * leaves) == row, 1.0, 0.0).astype(BF16)
            total = total + jnp.dot(chunks[s][...], onehot, preferred_element_type=F32)
        for half in range(2):
            field_ref[half, q * part : (q + 1) * part, :] = total[half * part : (half + 1) * part]
    for t in list(range(1, lvls)) + [0]:
        first = (lvl ^ t) * vs
        accs = [jnp.zeros((rank_width, leaves), F32) for _ in range(vs)]
        for half, ref in enumerate((own_ref, peer_ref)):
            accs = mac_rows(
                slab,
                lambda m, ref=ref: ref[m].astype(F32),
                lambda m, n, half=half: field_ref[
                    half, pl.ds(m * vh + jnp.minimum(first + n, vh - 1), 1), :
                ],
                accs,
                4,
            )
        for n in range(vs):
            block = slice(n * rank_width, (n + 1) * rank_width)
            if t == 0:
                keep_ref[block, :] = accs[n]
            else:
                sends[t - 1][block, :] = accs[n].astype(BF16)


def packed_rows(vs, rank_width, children):
    rows = vs * rank_width + vs * (rank_width // children)
    return -(-rows // 32) * 32


def up_kernel(vs, children, keep_ref, *refs):
    recvs, up_ref, out_ref, coeff_scr = refs[:-3], refs[-3], refs[-2], refs[-1]
    rank_width, _, leaves = up_ref.shape
    high_count = rank_width // children
    total = keep_ref[...]
    for ref in recvs:
        total = total + ref[...].astype(F32)
    coeffs = total.astype(BF16)
    out_ref[0 : vs * rank_width, :] = coeffs
    coeff_scr[...] = coeffs.astype(F32)
    accs = mac_rows(
        rank_width,
        lambda j: up_ref[j].astype(F32),
        lambda j, n: row_of(coeff_scr, n * rank_width + j),
        [jnp.zeros((rank_width, leaves), F32) for _ in range(vs)],
        8,
    )
    each = jnp.concatenate(accs, axis=0)
    high = each.astype(BF16)
    rest = each - high.astype(F32)
    low = rest.astype(BF16)
    last = (rest - low.astype(F32)).astype(BF16)
    same = (iota((leaves, leaves), 0) // children) == (iota((leaves, leaves), 1) // children)
    group = jnp.where(same, 1.0, 0.0).astype(BF16)
    summed = (
        jnp.dot(high, group, preferred_element_type=F32)
        + jnp.dot(low, group, preferred_element_type=F32)
        + jnp.dot(last, group, preferred_element_type=F32)
    )
    summed = summed.reshape(vs * high_count, children, leaves)
    diagonal = iota(summed.shape, 1) == iota(summed.shape, 2) % children
    parents = jnp.where(diagonal, summed, 0.0).sum(axis=1)
    extra = out_ref.shape[0] - vs * rank_width
    padded = jnp.concatenate(
        [parents, jnp.zeros((extra - vs * high_count, leaves), F32)], axis=0
    )
    out_ref[vs * rank_width :, :] = padded.astype(BF16)


def table_kernel(children, leaf_ref, parent_ref, leaf_out, parent_out, spread_out):
    slots, leaves = leaf_ref.shape
    sources = leaf_out.shape[0]
    for codes, out in ((leaf_ref, leaf_out), (parent_ref, parent_out)):
        for i in range(codes.shape[0]):
            code = jnp.broadcast_to(codes[i : i + 1, :], (sources, leaves))
            hit = code == iota((sources, leaves), 0)
            out[:, i * leaves : (i + 1) * leaves] = jnp.where(hit, 1.0, 0.0).astype(BF16)
    row = iota((leaves, leaves), 0)
    base = (iota((leaves, leaves), 1) // children) * children
    for low in range(children):
        spread_out[:, low * leaves : (low + 1) * leaves] = jnp.where(
            row == base + low, 1.0, 0.0
        ).astype(BF16)


def far_kernel(
    owners, vs, children, leaf_table, parent_table, spread_ref, block_ref, couple_ref, pcouple_ref,
    out_ref, rows_scr, prows_scr, acc_scr, pacc_scr,
):
    step, steps = pl.program_id(0), pl.num_programs(0)
    _, rank_width, _, leaves = couple_ref.shape
    slots = leaf_table.shape[1] // leaves
    pslots = parent_table.shape[1] // leaves
    high_count = rank_width // children
    per_block = block_ref.shape[0] // owners
    mine = vs * rank_width
    tail = per_block - mine

    @pl.when(step == 0)
    def _():
        rows = jnp.zeros((mine, slots * leaves), F32)
        prows = jnp.zeros((tail, pslots * leaves), F32)
        for o in range(owners):
            part = slice(o * leaves, (o + 1) * leaves)
            start = o * per_block
            rows = rows + jnp.dot(
                block_ref[start : start + mine, :], leaf_table[part, :],
                preferred_element_type=F32,
            )
            prows = prows + jnp.dot(
                block_ref[start + mine : start + per_block, :], parent_table[part, :],
                preferred_element_type=F32,
            )
        for i in range(slots):
            rows_scr[i] = rows[:, i * leaves : (i + 1) * leaves]
        for i in range(pslots):
            wide = jnp.dot(
                prows[:, i * leaves : (i + 1) * leaves].astype(BF16), spread_ref[...],
                preferred_element_type=F32,
            )
            for low in range(children):
                prows_scr[i, low] = wide[:, low * leaves : (low + 1) * leaves]
        acc_scr[...] = jnp.zeros_like(acc_scr)
        pacc_scr[...] = jnp.zeros_like(pacc_scr)

    accs = mac_rows(
        rank_width,
        lambda j: couple_ref[0, j].astype(F32),
        lambda j, n: rows_scr[step, pl.ds(n * rank_width + j, 1), :],
        [acc_scr[n * rank_width : (n + 1) * rank_width, :] for n in range(vs)],
        8,
    )
    for n in range(vs):
        acc_scr[n * rank_width : (n + 1) * rank_width, :] = accs[n]

    def body(high, carry):
        for low in range(children):
            weight = pcouple_ref[0, high * children + low]
            carry = tuple(
                acc + weight * prows_scr[step, low, pl.ds(n * high_count + high, 1), :]
                for n, acc in enumerate(carry)
            )
        return carry

    paccs = lax.fori_loop(
        0, high_count, body,
        tuple(pacc_scr[n * high_count : (n + 1) * high_count, :] for n in range(vs)),
    )
    for n in range(vs):
        pacc_scr[n * high_count : (n + 1) * high_count, :] = paccs[n]

    @pl.when(step == steps - 1)
    def _():
        out_ref[0:mine, :] = acc_scr[...].astype(out_ref.dtype)
        out_ref[mine:, :] = pacc_scr[...].astype(out_ref.dtype)


def down_kernel(vs, children, spread_ref, keep_ref, *refs):
    recvs, down_ref, out_ref, rows_scr = refs[:-3], refs[-3], refs[-2], refs[-1]
    rank_width, _, leaves = down_ref.shape
    high_count = rank_width // children
    total = keep_ref[...]
    for ref in recvs:
        total = total + ref[...].astype(F32)
    mine = vs * rank_width
    wide = jnp.dot(total[mine:, :].astype(BF16), spread_ref[...], preferred_element_type=F32)
    for low in range(children):
        rows_scr[low] = wide[:, low * leaves : (low + 1) * leaves]

    def body(high, carry):
        for low in range(children):
            weight = down_ref[high * children + low].astype(F32)
            carry = tuple(
                acc + weight * rows_scr[low, pl.ds(n * high_count + high, 1), :]
                for n, acc in enumerate(carry)
            )
        return carry

    accs = lax.fori_loop(
        0, high_count, body,
        tuple(total[n * rank_width : (n + 1) * rank_width, :] for n in range(vs)),
    )
    for n in range(vs):
        out_ref[n * rank_width : (n + 1) * rank_width, :] = accs[n].astype(BF16)


def near_kernel(vh, place_ref, field_ref, own_ref, peer_ref, out_ref):
    slab, rows, leaves = own_ref.shape
    halves = 2
    voxels = rows // halves
    group = 6
    for half in range(halves):
        span = slice(half * voxels, (half + 1) * voxels)
        for first in range(0, vh, group):
            accs = [jnp.zeros((voxels, leaves), F32) for _ in range(group)]
            for slice_of, ref in enumerate((own_ref, peer_ref)):
                accs = mac_rows(
                    slab,
                    lambda p, ref=ref: ref[p, span, :].astype(F32),
                    lambda p, n, s=slice_of, first=first: field_ref[
                        s, pl.ds(p * vh + first + n, 1), :
                    ],
                    accs,
                    4,
                )
            for n in range(group):
                start = half * vh * voxels + (first + n) * voxels
                out_ref[start : start + voxels, :] = accs[n].astype(out_ref.dtype)


def near_sum_kernel(ids_ref, keep_ref, *refs):
    recvs, mine_ref, send_ref = refs[:-2], refs[-2], refs[-1]
    count = mine_ref.shape[0]
    parity = ids_ref[2]

    def summed(start):
        start = pl.multiple_of(start, count)
        total = keep_ref[pl.ds(start, count), :]
        for ref in recvs:
            total = total + ref[pl.ds(start, count), :].astype(F32)
        return total

    mine_ref[...] = summed(parity * count)
    send_ref[...] = summed((1 - parity) * count).astype(BF16)


def out_kernel(lvls, vh, vs, ids_ref, column_ref, near_mine, near_peer, *refs):
    blocks, out_ref, rows_scr, out_scr = refs[: 2 * lvls], refs[-3], refs[-2], refs[-1]
    rank_width, voxels, leaves = column_ref.shape
    vectors = out_ref.shape[1]
    lvl, parity = ids_ref[1], ids_ref[2]
    for b, ref in enumerate(blocks):
        rows_scr[b] = ref[...].astype(F32)
    for t in range(lvls):
        first = (lvl ^ t) * vs
        accs = mac_rows(
            rank_width,
            lambda k: column_ref[k].astype(F32),
            lambda k, n: rows_scr[
                (n // vs) * lvls + t, pl.ds((n % vs) * rank_width + k, 1), :
            ],
            [jnp.zeros((voxels, leaves), F32) for _ in range(2 * vs)],
            4,
        )
        for n in range(2 * vs):
            rep = n // vs
            place = first + n % vs
            near_ref = (near_mine, near_peer)[rep]

            def store(n=n, rep=rep, place=place, near_ref=near_ref):
                start = pl.multiple_of(place * voxels, voxels)
                near = near_ref[pl.ds(start, voxels), :].astype(F32)
                vector = place * 2 + (parity if rep == 0 else 1 - parity)
                out_scr[pl.ds(vector, voxels, stride=vectors), :] = accs[n] + near

            if lvls * vs == vh:
                store()
            else:
                pl.when(place < vh)(store)
    out_ref[...] = out_scr[...].reshape(voxels, vectors, leaves).astype(BF16)


def per_device(sizes, *args):
    (
        voxel_field, row_basis, near_block, up_transfer, coupling, parent_coupling,
        down_transfer, column_basis, parent_perm, partner_owner, partner_local,
        parent_owner, parent_local, block_count,
    ) = args
    owners, lvls, reps = sizes
    slab, vectors, leaves = voxel_field.shape
    rank_width = row_basis.shape[1]
    parents = parent_coupling.shape[4]
    children = leaves // parents
    slot_dev = partner_owner.shape[2]
    pslot_dev = parent_owner.shape[2]
    vh = vectors // reps
    vs = -(-vh // lvls)
    high_count = rank_width // children
    sds = jax.ShapeDtypeStruct

    me = lax.axis_index("clus")
    lvl = lax.axis_index("lvl")
    parity = lax.axis_index("rep")
    ids = jnp.stack([me, lvl, parity]).astype(jnp.int32)

    def swap(value, axis, count, step):
        return lax.ppermute(value, axis, [(i, i ^ step) for i in range(count)])

    def other(value):
        return swap(value, "rep", reps, 1)

    with jax.named_scope("swap_cores"):
        field_peer = other(voxel_field)
        row_peer = other(row_basis)

    chunk_rows = 2 * (slab // owners) * vh
    with jax.named_scope("pack_field"):
        packed = pl.pallas_call(
            functools.partial(pack_kernel, owners, vh),
            out_shape=[sds((owners, chunk_rows, leaves), BF16)],
            in_specs=[smem(), smem(), vmem(), vmem()],
            out_specs=[vmem()],
            scratch_shapes=[
                pltpu.VMEM((2, slab * vectors, leaves), F32),
                pltpu.SMEM((owners,), jnp.int32),
            ],
            compiler_params=params(),
            cost_estimate=cost(2 * 768 * 128 * 512, 800000),
        )(parent_perm, ids, voxel_field, field_peer)[0]
    with jax.named_scope("regroup_sends"):
        chunks = [packed[0]] + [swap(packed[s], "clus", owners, s) for s in range(1, owners)]
    with jax.named_scope("place_codes"):
        codes = pl.pallas_call(
            functools.partial(place_kernel, owners, children),
            out_shape=sds((8, leaves), jnp.int32),
            in_specs=[smem(), smem()],
            out_specs=vmem(),
            scratch_shapes=[
                pltpu.SMEM((parents + 1,), jnp.int32),
                pltpu.SMEM((owners,), jnp.int32),
            ],
            compiler_params=params(),
        )(parent_perm, ids)

    with jax.named_scope("partner_codes"):
        group = lvl * reps + parity
        slot_number = group * slot_dev + jnp.arange(slot_dev, dtype=jnp.int32)[:, None]
        live = slot_number < block_count[None, :]
        leaf_code = (partner_owner[0] ^ me).T * leaves + partner_local[0].T
        leaf_code = jnp.where(live, leaf_code, -1)
        up_code = (parent_owner[0] ^ me).T * leaves + parent_local[0].T * children
        up_code = (up_code[:, :, None] + jnp.arange(children, dtype=jnp.int32)).reshape(
            pslot_dev, leaves
        )
        both = jnp.concatenate([leaf_code, up_code], axis=0)
        both_peer = other(both)
        leaf_code = jnp.concatenate([both[:slot_dev], both_peer[:slot_dev]], axis=0)
        up_code = jnp.concatenate([both[slot_dev:], both_peer[slot_dev:]], axis=0)
    slots, pslots = 2 * slot_dev, 2 * pslot_dev
    with jax.named_scope("partner_tables"):
        leaf_table, parent_table, spread = pl.pallas_call(
            functools.partial(table_kernel, children),
            out_shape=[
                sds((owners * leaves, slots * leaves), BF16),
                sds((owners * leaves, pslots * leaves), BF16),
                sds((leaves, children * leaves), BF16),
            ],
            in_specs=[vmem(), vmem()],
            out_specs=[vmem(), vmem(), vmem()],
            compiler_params=params(),
        )(leaf_code, up_code)

    with jax.named_scope("coupling_layout"):
        couple = jnp.moveaxis(coupling[:, :, 0], 2, 0)
        couple_all = jnp.concatenate([couple, other(couple)], axis=0)
        pcouple = parent_coupling[:, :, 0].reshape(
            rank_width, high_count, children, pslot_dev, parents
        )
        pcouple = jnp.transpose(pcouple, (3, 0, 1, 4, 2)).reshape(
            pslot_dev, rank_width, high_count, leaves
        )
        pcouple_all = jnp.concatenate([pcouple, other(pcouple)], axis=0).astype(F32)
        near_other = other(near_block)

    with jax.named_scope("leaf_coeffs"):
        outs = pl.pallas_call(
            functools.partial(coeff_kernel, owners, lvls, vh, vs),
            out_shape=[
                sds((2, slab * vh, leaves), F32),
                sds((vs * rank_width, leaves), F32),
            ]
            + [sds((vs * rank_width, leaves), BF16)] * (lvls - 1),
            in_specs=[smem(), vmem()] + [vmem()] * (owners + 2),
            out_specs=[vmem()] * (lvls + 1),
            compiler_params=params(),
            cost_estimate=cost(4 * 25 * 10**6, 3000000),
        )(ids, codes, *chunks, row_basis, row_peer)
    field, keep, sends = outs[0], outs[1], outs[2:]
    with jax.named_scope("coeff_sends"):
        recvs = [swap(sends[t - 1], "lvl", lvls, t) for t in range(1, lvls)]
    block_rows = packed_rows(vs, rank_width, children)
    with jax.named_scope("parent_coeffs"):
        block = pl.pallas_call(
            functools.partial(up_kernel, vs, children),
            out_shape=sds((block_rows, leaves), BF16),
            in_specs=[vmem()] * (lvls + 1),
            out_specs=vmem(),
            scratch_shapes=[pltpu.VMEM((vs * rank_width, leaves), F32)],
            compiler_params=params(),
            cost_estimate=cost(10**7, 1500000),
        )(keep, *recvs, up_transfer)

    def near_part(t):
        with jax.named_scope("self_blocks"):
            return pl.pallas_call(
                functools.partial(near_kernel, vh),
                out_shape=sds((2 * vh * slab, leaves), F32 if t == 0 else BF16),
                grid_spec=pltpu.PrefetchScalarGridSpec(
                    num_scalar_prefetch=1,
                    grid=(1,),
                    in_specs=[
                        pl.BlockSpec((2, slab * vh, leaves), lambda i, place: (0, 0, 0)),
                        pl.BlockSpec((slab, 2 * slab, leaves), lambda i, place: (0, place[0], 0)),
                        pl.BlockSpec((slab, 2 * slab, leaves), lambda i, place: (0, place[0], 0)),
                    ],
                    out_specs=pl.BlockSpec((2 * vh * slab, leaves), lambda i, place: (0, 0)),
                ),
                compiler_params=params(),
                cost_estimate=cost(4 * 25 * 10**6, 2000000),
            )((lvl ^ t).reshape(1).astype(jnp.int32), field, near_block, near_other)

    near_parts = [near_part(t) for t in range(lvls)]

    with jax.named_scope("owner_sends"):
        blocks = [block] + [swap(block, "clus", owners, s) for s in range(1, owners)]
        mine = jnp.concatenate(blocks, axis=0)
    with jax.named_scope("level_sends"):
        alls = [mine] + [swap(mine, "lvl", lvls, t) for t in range(1, lvls)]

    with jax.named_scope("self_sends"):
        near_recvs = [swap(near_parts[t], "lvl", lvls, t) for t in range(1, lvls)]
        near_mine, near_send = pl.pallas_call(
            near_sum_kernel,
            out_shape=[sds((vh * slab, leaves), F32), sds((vh * slab, leaves), BF16)],
            in_specs=[smem()] + [vmem()] * lvls,
            out_specs=[vmem()] * 2,
            compiler_params=params(),
            cost_estimate=cost(10**6, 2500000),
        )(ids, near_parts[0], *near_recvs)
        near_peer = other(near_send)

    def far_part(t):
        with jax.named_scope("coupling_products"):
            return pl.pallas_call(
                functools.partial(far_kernel, owners, vs, children),
                out_shape=sds((block_rows, leaves), F32 if t == 0 else BF16),
                grid=(slots,),
                in_specs=[
                    pl.BlockSpec(leaf_table.shape, lambda i: (0, 0)),
                    pl.BlockSpec(parent_table.shape, lambda i: (0, 0)),
                    pl.BlockSpec(spread.shape, lambda i: (0, 0)),
                    pl.BlockSpec(mine.shape, lambda i: (0, 0)),
                    pl.BlockSpec((1, rank_width, rank_width, leaves), lambda i: (i, 0, 0, 0)),
                    pl.BlockSpec((1, rank_width, high_count, leaves), lambda i: (i, 0, 0, 0)),
                ],
                out_specs=pl.BlockSpec((block_rows, leaves), lambda i: (0, 0)),
                scratch_shapes=[
                    pltpu.VMEM((slots, vs * rank_width, leaves), F32),
                    pltpu.VMEM((pslots, children, block_rows - vs * rank_width, leaves), F32),
                    pltpu.VMEM((vs * rank_width, leaves), F32),
                    pltpu.VMEM((block_rows - vs * rank_width, leaves), F32),
                ],
                compiler_params=params(),
                cost_estimate=cost(4 * 25 * 10**6, 5000000),
            )(leaf_table, parent_table, spread, alls[t], couple_all, pcouple_all)

    far_parts = [far_part(t) for t in range(lvls)]
    with jax.named_scope("far_sends"):
        far_recvs = [swap(far_parts[t], "lvl", lvls, t) for t in range(1, lvls)]
    with jax.named_scope("down_products"):
        far = pl.pallas_call(
            functools.partial(down_kernel, vs, children),
            out_shape=sds((vs * rank_width, leaves), BF16),
            in_specs=[vmem()] * (lvls + 2),
            out_specs=vmem(),
            scratch_shapes=[
                pltpu.VMEM((children, block_rows - vs * rank_width, leaves), F32)
            ],
            compiler_params=params(),
            cost_estimate=cost(10**7, 1500000),
        )(spread, far_parts[0], *far_recvs, down_transfer)
    with jax.named_scope("far_coeff_sends"):
        far_blocks = [far] + [swap(far, "lvl", lvls, t) for t in range(1, lvls)]
        far_others = [other(value) for value in far_blocks]
    with jax.named_scope("column_products"):
        return pl.pallas_call(
            functools.partial(out_kernel, lvls, vh, vs),
            out_shape=sds((slab, vectors, leaves), BF16),
            in_specs=[smem()] + [vmem()] * (3 + 2 * lvls),
            out_specs=vmem(),
            scratch_shapes=[
                pltpu.VMEM((2 * lvls, vs * rank_width, leaves), F32),
                pltpu.VMEM((slab * vectors, leaves), F32),
            ],
            compiler_params=params(),
            cost_estimate=cost(4 * 25 * 10**6, 3000000),
        )(ids, column_basis, near_mine, near_peer, *far_blocks, *far_others)


def solution(mesh):
    sizes = (mesh.shape["clus"], mesh.shape["lvl"], mesh.shape["rep"])
    return jax.shard_map(
        functools.partial(per_device, sizes),
        mesh=mesh,
        in_specs=(
            P(("lvl", "rep"), None, ("parts", "clus")),
            P(("lvl", "rep"), None, ("parts", "clus")),
            P(("lvl", "rep"), None, ("parts", "clus")),
            P(None, None, ("parts", "clus")),
            P(None, None, ("lvl", "rep"), None, ("parts", "clus")),
            P(None, None, ("lvl", "rep"), None, ("parts", "clus")),
            P(None, None, ("parts", "clus")),
            P(None, ("lvl", "rep"), ("parts", "clus")),
            P("parts"),
            P(("lvl", "rep"), ("parts", "clus"), None),
            P(("lvl", "rep"), ("parts", "clus"), None),
            P(("lvl", "rep"), ("parts", "clus"), None),
            P(("lvl", "rep"), ("parts", "clus"), None),
            P(("parts", "clus")),
        ),
        out_specs=P(("lvl", "rep"), None, ("parts", "clus")),
        check_vma=False,
    )
```

time: 252 us -> 104 us (0.41)
  blocking collectives: 93.8 us -> 0 us
  waiting for transfers between devices: 64.4 us -> 16.7 us
  Pallas kernels: 0 us -> 39.5 us
  local copies, waits for them, and re-layouts: 48.1 us -> 11.5 us
  starting transfers between devices: 6.58 us -> 32 us
  matrix products: 14 us -> 0 us
  between operations: 13.4 us -> 0.33 us
  other arithmetic: 10.3 us -> 3.8 us
    psum x2 -> x0, blocking collectives: 78.8 us -> none  [the longest x1 53.5 us: per_device(): coeffs = lax.psum(partial_value, ('lvl', 'rep')).astype(jnp.bfloat16)]
    pallas_call x0 -> x16, Pallas kernels: none -> 39.5 us  [the longest x4 13.3 us: near_part(): pl.pallas_call(functools.partial(near_kernel, vh), out_shape=sds((2 * vh...]
    reduce_scatter x1 -> x0, waiting for transfers between devices: 35 us -> none  [per_device(): lax.psum_scatter(jnp.einsum('pml,pvl->mvl', near_block, regrouped, prefer...]
    ppermute x0 -> x32, starting transfers between devices: none -> 32 us  [swap(): return lax.ppermute(value, axis, [(i, i ^ step) for i in range(count)])]
    all_gather x1 -> x0, waiting for transfers between devices: 28.6 us -> none  [per_device(): lax.all_gather(coeffs, 'clus', axis=2, tiled=True)]
    ppermute x0 -> x32, waiting for transfers between devices: none -> 16.7 us  [swap(): return lax.ppermute(value, axis, [(i, i ^ step) for i in range(count)])]
    all_gather x1 -> x0, blocking collectives: 15 us -> none  [per_device(): lax.all_gather(parent_coeffs, 'clus', axis=2, tiled=True)]
    dot_general x7 -> x0, matrix products: 14 us -> none  [the longest x1 4.77 us: per_device(): jnp.einsum('jkil,vjli->vkl', leaf_blocks, leaf_rows, preferred_element_ty...]
  transfers between devices with their start and end apart: 4 -> 32, of which waited for: 3 -> 9; matrix products, arithmetic and copies ran while one was open for 18% -> 13% of each run, Pallas kernels for 0% -> 34%
where the time goes in v1:
time: 104 us
  Pallas kernels  39.5 us (38%)
  starting transfers between devices  32 us (31%)
  waiting for transfers between devices  16.7 us (16%)
  local copies, waits for them, and re-layouts  11.5 us (11%)
  other arithmetic  3.8 us (4%)
    ppermute x32, starting transfers between devices, swap(): return lax.ppermute(value, axis, [(i, i ^ step) for i in range(count)])  32 us
    ppermute x32, waiting for transfers between devices, swap(): return lax.ppermute(value, axis, [(i, i ^ step) for i in range(count)])  16.7 us
    pallas_call x4, Pallas kernels, near_part(): pl.pallas_call(functools.partial(near_kernel, vh), out_shape=sds((2 * vh...  13.3 us
    pallas_call x4, Pallas kernels, far_part(): pl.pallas_call(functools.partial(far_kernel, owners, vs, children), out_s...  13 us
    unnamed x34, local copies, waits for them, and re-layouts  7.41 us
    pallas_call x1, Pallas kernels, per_device(): pl.pallas_call(functools.partial(coeff_kernel, owners, lvls, vh, vs), out...  3.87 us
    pallas_call x1, Pallas kernels, per_device(): pl.pallas_call(functools.partial(out_kernel, lvls, vh, vs), out_shape=sds...  3.66 us
    concatenate x1, other arithmetic, per_device(): couple_all = jnp.concatenate([couple, other(couple)], axis=0)  2.58 us
  transfers between devices with their start and end apart: 32, of which 9 were waited for; matrix products, arithmetic and copies ran while one was open for 13% of the time, Pallas kernels for 34%

profile of v1, /device:TPU:0, one launch (start us, length us, event | category | flops | bytes accessed | tf_op | source)
XLA Modules:
  0.0 103.8 jit_solution(11587536351708664785)
XLA Ops:
  0.6 3.5 %copy.24 = bf16[64,64,1,2,128]{4,1,0,3,2:T(8,128)(2,1)} copy(bf16[64,64,1,2,128]{4,3,2,1,0:T(2,128)(2,1)} %param.18) | data formatting | bytes 4194304 | tf_op args[4]
  4.9 3.5 %collective-permute-done.peer_ref = bf16[32,24,128]{2,1,0:T(8,128)(2,1)S(1)} collective-permute-done((bf16[32,24,128]{2,1,0:T(8,128)(2,1)S(1)}, bf16[32,24,128]{2,1,0:T(8,128)(2,1)S(1)}, u32[]{:S(2)}, u32[]{:S(2)}) %collective-permute-start) | collective-permute-done | bytes 196640 | tf_op jit(solution)/shard_map/swap_cores/ppermute | solution.py:412
  9.4 2.9 %collective-permute-start.1 = (bf16[192,128]{1,0:T(8,128)(2,1)S(1)}, bf16[192,128]{1,0:T(8,128)(2,1)S(1)}, u32[]{:S(2)}, u32[]{:S(2)}) collective-permute-start(bf16[192,128]{1,0:T(8,128)(2,1)S(1)} %get-tuple-element.27), channel_id=1, source_target_pairs={{0,8},{8,0},{16,24},{24,16},{1,9},{9,1},{17,25},{25,17},{2,10},{10... | collective-permute-start | bytes 147464 | tf_op jit(solution)/shard_map/regroup_sends/ppermute | solution.py:412
  12.6 2.7 %collective-permute-start.2 = (bf16[192,128]{1,0:T(8,128)(2,1)S(1)}, bf16[192,128]{1,0:T(8,128)(2,1)S(1)}, u32[]{:S(2)}, u32[]{:S(2)}) collective-permute-start(bf16[192,128]{1,0:T(8,128)(2,1)S(1)} %get-tuple-element.26), channel_id=1, source_target_pairs={{0,16},{8,24},{16,0},{24,8},{1,17},{9,25},{17,1},{25,9},{2,18},{10... | collective-permute-start | bytes 147464 | tf_op jit(solution)/shard_map/regroup_sends/ppermute | solution.py:412
  15.3 3.2 %collective-permute-start.3 = (bf16[192,128]{1,0:T(8,128)(2,1)S(1)}, bf16[192,128]{1,0:T(8,128)(2,1)S(1)}, u32[]{:S(2)}, u32[]{:S(2)}) collective-permute-start(bf16[192,128]{1,0:T(8,128)(2,1)S(1)} %get-tuple-element.25), channel_id=1, source_target_pairs={{0,24},{8,16},{16,8},{24,0},{1,25},{9,17},{17,9},{25,1},{2,26},{10... | collective-permute-start | bytes 147464 | tf_op jit(solution)/shard_map/regroup_sends/ppermute | solution.py:412
  18.5 1.5 %place_codes.1.code_ref = s32[8,128]{1,0:T(8,128)S(1)} custom-call(s32[64]{0:T(128)S(1)} %copy-done.10, s32[3]{0:T(128)S(1)} %pad_add_fusion.3.ids_ref), custom_call_target="tpu_custom_call" | custom-call | tf_op jit(solution)/shard_map/place_codes/pallas_call | solution.py:438
  21.2 3.9 %leaf_coeffs.1 = (f32[2,384,128]{2,1,0:T(8,128)S(1)}, f32[192,128]{1,0:T(8,128)S(1)}, bf16[192,128]{1,0:T(8,128)(2,1)S(1)}, bf16[192,128]{1,0:T(8,128)(2,1)}, bf16[192,128]{1,0:T(8,128)(2,1)}) custom-call(s32[3]{0:T(128)S(1)} %pad_add_fusion.3.ids_ref, s32[8,128]{1,0:T(8,128)S(1)} %place_codes.1.code_ref, bf16[192,128]{1,0:T(8,128)(2,1)S(1)} %get-tuple-element.28.refs_0_, ...), custom_call_target="tpu_custom_call" | custom-call | flops 100000000 | bytes 3000000 | tf_op jit(solution)/shard_map/leaf_coeffs/pallas_call | solution.py:491
  25.0 1.5 %collective-permute-start.11 = (bf16[192,128]{1,0:T(8,128)(2,1)S(1)}, bf16[192,128]{1,0:T(8,128)(2,1)S(1)}, u32[]{:S(2)}, u32[]{:S(2)}) collective-permute-start(bf16[192,128]{1,0:T(8,128)(2,1)S(1)} %get-tuple-element.22), channel_id=1, source_target_pairs={{0,2},{2,0},{4,6},{6,4},{1,3},{3,1},{5,7},{7,5},{8,10},{10,8},{12,... | collective-permute-start | bytes 147464 | tf_op jit(solution)/shard_map/coeff_sends/ppermute | solution.py:412
  26.5 1.5 %collective-permute-start.12 = (bf16[192,128]{1,0:T(8,128)(2,1)}, bf16[192,128]{1,0:T(8,128)(2,1)}, u32[]{:S(2)}, u32[]{:S(2)}) collective-permute-start(bf16[192,128]{1,0:T(8,128)(2,1)} %get-tuple-element.23), channel_id=1, source_target_pairs={{0,4},{2,6},{4,0},{6,2},{1,5},{3,7},{5,1},{7,3},{8,12},{10,14},{12... | collective-permute-start | bytes 147464 | tf_op jit(solution)/shard_map/coeff_sends/ppermute | solution.py:412
  29.6 2.1 %copy.18 = bf16[64,64,1,2,16]{0,4,3,1,2:T(8,128)(2,1)S(1)} copy(bf16[64,64,1,2,16]{1,4,3,2,0:T(8,128)(2,1)} %param.19) | data formatting | bytes 524288 | tf_op args[5]
  32.7 2.1 %copy.21 = bf16[2,64,8,128]{3,2,1,0:T(8,128)(2,1)} copy(bf16[2,64,8,128]{1,3,2,0:T(8,128)(2,1)} %bitcast.33) | data formatting | bytes 524288 | tf_op jit(solution)/shard_map/coupling_layout/reshape | solution.py:484
  37.0 1.6 %parent_coeffs.1 = bf16[224,128]{1,0:T(8,128)(2,1)S(1)} custom-call(f32[192,128]{1,0:T(8,128)S(1)} %copy-done.7, bf16[192,128]{1,0:T(8,128)(2,1)S(1)} %copy-done.9, bf16[192,128]{1,0:T(8,128)(2,1)} %collective-permute-done.12.refs_1_, bf16[192,128]{1,0:T(8,128)(2,1)} %collective-permute-done.13.refs_2_, bf16[64,64,128]{2,1,0:T(8,128)(2,1)S(1)} %copy-done.1), custom_call_target="tpu_custom_call" | custom-call | flops 10000000 | bytes 1500000 | tf_op jit(solution)/shard_map/parent_coeffs/pallas_call | solution.py:508
  38.6 2.8 %collective-permute-start.16 = (bf16[224,128]{1,0:T(8,128)(2,1)S(1)}, bf16[224,128]{1,0:T(8,128)(2,1)S(1)}, u32[]{:S(2)}, u32[]{:S(2)}) collective-permute-start(bf16[224,128]{1,0:T(8,128)(2,1)S(1)} %parent_coeffs.1), channel_id=1, source_target_pairs={{0,24},{8,16},{16,8},{24,0},{1,25},{9,17},{17,9},{25,1},{2,26},{10... | collective-permute-start | bytes 172040 | tf_op jit(solution)/shard_map/owner_sends/ppermute | solution.py:412
  42.2 2.9 %collective-permute-done.16 = bf16[224,128]{1,0:T(8,128)(2,1)S(1)} collective-permute-done((bf16[224,128]{1,0:T(8,128)(2,1)S(1)}, bf16[224,128]{1,0:T(8,128)(2,1)S(1)}, u32[]{:S(2)}, u32[]{:S(2)}) %collective-permute-start.16) | collective-permute-done | bytes 57376 | tf_op jit(solution)/shard_map/owner_sends/ppermute | solution.py:412
  45.1 2.3 %collective-permute-done.15 = bf16[224,128]{1,0:T(8,128)(2,1)S(1)} collective-permute-done((bf16[224,128]{1,0:T(8,128)(2,1)S(1)}, bf16[224,128]{1,0:T(8,128)(2,1)S(1)}, u32[]{:S(2)}, u32[]{:S(2)}) %collective-permute-start.15) | collective-permute-done | bytes 57376 | tf_op jit(solution)/shard_map/owner_sends/ppermute | solution.py:412
  47.3 1.9 %collective-permute-done.14 = bf16[224,128]{1,0:T(8,128)(2,1)S(1)} collective-permute-done((bf16[224,128]{1,0:T(8,128)(2,1)S(1)}, bf16[224,128]{1,0:T(8,128)(2,1)S(1)}, u32[]{:S(2)}, u32[]{:S(2)}) %collective-permute-start.14) | collective-permute-done | bytes 57376 | tf_op jit(solution)/shard_map/owner_sends/ppermute | solution.py:412
  51.8 1.6 %collective-permute-start.21 = (bf16[896,128]{1,0:T(8,128)(2,1)S(1)}, bf16[896,128]{1,0:T(8,128)(2,1)S(1)}, u32[]{:S(2)}, u32[]{:S(2)}) collective-permute-start(bf16[896,128]{1,0:T(8,128)(2,1)S(1)} %pad_maximum_fusion.1.block_ref), channel_id=1, source_target_pairs={{0,4},{2,6},{4,0},{6,2},{1,5},{3,7},{5,1},{7,3},{8,12},{10,14},{12... | collective-permute-start | bytes 688136 | tf_op jit(solution)/shard_map/level_sends/ppermute | solution.py:412
  54.3 3.3 %self_blocks.5 = bf16[768,128]{1,0:T(8,128)(2,1)S(1)} custom-call(s32[1]{0:T(128)} %bitcast.7.place_ref, f32[2,384,128]{2,1,0:T(8,128)S(1)} %get-tuple-element.15.field_ref, bf16[32,256,128]{2,1,0:T(8,128)(2,1)S(1)} %copy-done, bf16[32,256,128]{2,1,0:T(8,128)(2,1)} %collective-permute-done.5.peer_ref), custom_call_target="tpu_custom_call" | custom-call | flops 100000000 | bytes 2000000 | tf_op jit(solution)/shard_map/self_blocks/pallas_call | solution.py:520
  58.7 3.3 %self_blocks.6 = bf16[768,128]{1,0:T(8,128)(2,1)S(1)} custom-call(s32[1]{0:T(128)} %bitcast.8.place_ref, f32[2,384,128]{2,1,0:T(8,128)S(1)} %get-tuple-element.15.field_ref, bf16[32,256,128]{2,1,0:T(8,128)(2,1)S(1)} %copy-done, bf16[32,256,128]{2,1,0:T(8,128)(2,1)} %collective-permute-done.5.peer_ref), custom_call_target="tpu_custom_call" | custom-call | flops 100000000 | bytes 2000000 | tf_op jit(solution)/shard_map/self_blocks/pallas_call | solution.py:520
  62.0 3.3 %self_blocks.7 = bf16[768,128]{1,0:T(8,128)(2,1)S(1)} custom-call(s32[1]{0:T(128)} %bitcast.9.place_ref, f32[2,384,128]{2,1,0:T(8,128)S(1)} %get-tuple-element.15.field_ref, bf16[32,256,128]{2,1,0:T(8,128)(2,1)S(1)} %copy-done, bf16[32,256,128]{2,1,0:T(8,128)(2,1)} %collective-permute-done.5.peer_ref), custom_call_target="tpu_custom_call" | custom-call | flops 100000000 | bytes 2000000 | tf_op jit(solution)/shard_map/self_blocks/pallas_call | solution.py:520
  65.3 1.6 %collective-permute-start.7 = (bf16[768,128]{1,0:T(8,128)(2,1)S(1)}, bf16[768,128]{1,0:T(8,128)(2,1)S(1)}, u32[]{:S(2)}, u32[]{:S(2)}) collective-permute-start(bf16[768,128]{1,0:T(8,128)(2,1)S(1)} %self_blocks.6), channel_id=1, source_target_pairs={{0,4},{2,6},{4,0},{6,2},{1,5},{3,7},{5,1},{7,3},{8,12},{10,14},{12... | collective-permute-start | bytes 589832 | tf_op jit(solution)/shard_map/self_sends/ppermute | solution.py:412
  67.8 2.6 %pad_maximum_fusion.couple_ref = bf16[4,64,64,128]{3,2,1,0:T(8,128)(2,1)S(1)} fusion(bf16[2,64,64,128]{3,2,1,0:T(8,128)(2,1)} %collective-permute-done.17, bf16[2,64,64,128]{3,2,1,0:T(8,128)(2,1)} %bitcast.31), kind=kLoop, calls=%fused_computation | loop fusion | flops 2097152 | bytes 8388608 | tf_op jit(solution)/shard_map/coupling_layout/concatenate | solution.py:480
  70.4 3.3 %coupling_products.5 = bf16[224,128]{1,0:T(8,128)(2,1)S(1)} custom-call(bf16[512,512]{1,0:T(8,128)(2,1)S(1)} %get-tuple-element.19.leaf_table, bf16[512,512]{1,0:T(8,128)(2,1)S(1)} %get-tuple-element.20.parent_table, bf16[128,1024]{1,0:T(8,128)(2,1)S(1)} %get-tuple-element.18.spread_ref, bf16[896,128]{1,0:T(8,128)(2,1)S(1)} %collective-permute-done.19.block_ref, ...), custom_call_target="tpu_custom_call" | custom-call | flops 100000000 | bytes 5000000 | tf_op jit(solution)/shard_map/coupling_products/pallas_call | solution.py:559
  74.8 3.2 %coupling_products.6 = bf16[224,128]{1,0:T(8,128)(2,1)S(1)} custom-call(bf16[512,512]{1,0:T(8,128)(2,1)S(1)} %get-tuple-element.19.leaf_table, bf16[512,512]{1,0:T(8,128)(2,1)S(1)} %get-tuple-element.20.parent_table, bf16[128,1024]{1,0:T(8,128)(2,1)S(1)} %get-tuple-element.18.spread_ref, bf16[896,128]{1,0:T(8,128)(2,1)S(1)} %collective-permute-done.21.block_ref, ...), custom_call_target="tpu_custom_call" | custom-call | flops 100000000 | bytes 5000000 | tf_op jit(solution)/shard_map/coupling_products/pallas_call | solution.py:559
  78.1 1.6 %collective-permute-start.22 = (bf16[224,128]{1,0:T(8,128)(2,1)S(1)}, bf16[224,128]{1,0:T(8,128)(2,1)S(1)}, u32[]{:S(2)}, u32[]{:S(2)}) collective-permute-start(bf16[224,128]{1,0:T(8,128)(2,1)S(1)} %coupling_products.6), channel_id=1, source_target_pairs={{0,4},{2,6},{4,0},{6,2},{1,5},{3,7},{5,1},{7,3},{8,12},{10,14},{12... | collective-permute-start | bytes 172040 | tf_op jit(solution)/shard_map/far_sends/ppermute | solution.py:412
  79.7 3.2 %coupling_products.7 = bf16[224,128]{1,0:T(8,128)(2,1)S(1)} custom-call(bf16[512,512]{1,0:T(8,128)(2,1)S(1)} %get-tuple-element.19.leaf_table, bf16[512,512]{1,0:T(8,128)(2,1)S(1)} %get-tuple-element.20.parent_table, bf16[128,1024]{1,0:T(8,128)(2,1)S(1)} %get-tuple-element.18.spread_ref, bf16[896,128]{1,0:T(8,128)(2,1)S(1)} %collective-permute-done.23.block_ref, ...), custom_call_target="tpu_custom_call" | custom-call | flops 100000000 | bytes 5000000 | tf_op jit(solution)/shard_map/coupling_products/pallas_call | solution.py:559
  83.9 3.2 %coupling_products.4.keep_ref = f32[224,128]{1,0:T(8,128)S(1)} custom-call(bf16[512,512]{1,0:T(8,128)(2,1)S(1)} %get-tuple-element.19.leaf_table, bf16[512,512]{1,0:T(8,128)(2,1)S(1)} %get-tuple-element.20.parent_table, bf16[128,1024]{1,0:T(8,128)(2,1)S(1)} %get-tuple-element.18.spread_ref, bf16[896,128]{1,0:T(8,128)(2,1)S(1)} %pad_maximum_fusion.1.block_ref, ...), custom_call_target="tpu_custom_call" | custom-call | flops 100000000 | bytes 5000000 | tf_op jit(solution)/shard_map/coupling_products/pallas_call | solution.py:559
  87.1 3.3 %self_blocks.4.keep_ref = f32[768,128]{1,0:T(8,128)S(1)} custom-call(s32[1]{0:T(128)} %bitcast.1.place_ref, f32[2,384,128]{2,1,0:T(8,128)S(1)} %get-tuple-element.15.field_ref, bf16[32,256,128]{2,1,0:T(8,128)(2,1)S(1)} %copy-done, bf16[32,256,128]{2,1,0:T(8,128)(2,1)} %collective-permute-done.5.peer_ref), custom_call_target="tpu_custom_call" | custom-call | flops 100000000 | bytes 2000000 | tf_op jit(solution)/shard_map/self_blocks/pallas_call | solution.py:520
  92.4 1.5 %collective-permute-start.26 = (bf16[192,128]{1,0:T(8,128)(2,1)S(1)}, bf16[192,128]{1,0:T(8,128)(2,1)S(1)}, u32[]{:S(2)}, u32[]{:S(2)}) collective-permute-start(bf16[192,128]{1,0:T(8,128)(2,1)S(1)} %down_products.1.refs_0_), channel_id=1, source_target_pairs={{0,4},{2,6},{4,0},{6,2},{1,5},{3,7},{5,1},{7,3},{8,12},{10,14},{12... | collective-permute-start | bytes 147464 | tf_op jit(solution)/shard_map/far_coeff_sends/ppermute | solution.py:412
  96.5 2.3 %collective-permute-done.27.refs_3_ = bf16[192,128]{1,0:T(8,128)(2,1)S(1)} collective-permute-done((bf16[192,128]{1,0:T(8,128)(2,1)S(1)}, bf16[192,128]{1,0:T(8,128)(2,1)S(1)}, u32[]{:S(2)}, u32[]{:S(2)}) %collective-permute-start.27) | collective-permute-done | bytes 49184 | tf_op jit(solution)/shard_map/far_coeff_sends/ppermute | solution.py:412
  98.9 1.2 %collective-permute-done.31.refs_7_ = bf16[192,128]{1,0:T(8,128)(2,1)S(1)} collective-permute-done((bf16[192,128]{1,0:T(8,128)(2,1)S(1)}, bf16[192,128]{1,0:T(8,128)(2,1)S(1)}, u32[]{:S(2)}, u32[]{:S(2)}) %collective-permute-start.31) | collective-permute-done | bytes 49184 | tf_op jit(solution)/shard_map/far_coeff_sends/ppermute | solution.py:412
  100.1 3.7 %column_products.1 = bf16[32,24,128]{2,1,0:T(8,128)(2,1)} custom-call(s32[3]{0:T(128)S(1)} %pad_add_fusion.3.ids_ref, bf16[64,32,128]{2,1,0:T(8,128)(2,1)S(1)} %copy-done.3, f32[384,128]{1,0:T(8,128)S(1)} %get-tuple-element.16.near_mine, bf16[384,128]{1,0:T(8,128)(2,1)S(1)} %collective-permute-done.9.near_peer, bf16[192,128]{1,0:T(8,128)(2,1)S(1)} %down_products.1.refs_0_, ...), custom_call_target="tpu_custom_call" | custom-call | flops 100000000 | bytes 3000000 | tf_op jit(solution)/shard_map/column_products/pallas_call | solution.py:601
  (100 shorter events, 21.4 us)
Async XLA Ops:
  0.0 54.2 %collective-permute-start.5 = (bf16[32,256,128]{2,1,0:T(8,128)(2,1)}, bf16[32,256,128]{2,1,0:T(8,128)(2,1)}, u32[]{:S(2)}, u32[]{:S(2)}) collective-permute-start(bf16[32,256,128]{2,1,0:T(8,128)(2,1)} %own_ref.9), channel_id=1, source_target_pairs={{0,1},{1,0},{2,3},{3,2},{4,5},{5,4},{6,7},{7,6},{8,9},{9,8},{10,11... | collective-permute-start | bytes 6291464 | tf_op jit(solution)/shard_map/coupling_layout/ppermute | solution.py:412
  4.1 62.8 %collective-permute-start.17 = (bf16[2,64,64,128]{3,2,1,0:T(8,128)(2,1)}, bf16[2,64,64,128]{3,2,1,0:T(8,128)(2,1)}, u32[]{:S(2)}, u32[]{:S(2)}) collective-permute-start(bf16[2,64,64,128]{3,2,1,0:T(8,128)(2,1)} %bitcast.31), channel_id=1, source_target_pairs={{0,1},{1,0},{2,3},{3,2},{4,5},{5,4},{6,7},{7,6},{8,9},{9,8},{10,11... | collective-permute-start | bytes 6291464 | tf_op jit(solution)/shard_map/coupling_layout/ppermute | solution.py:412
  4.3 4.1 %collective-permute-start = (bf16[32,24,128]{2,1,0:T(8,128)(2,1)S(1)}, bf16[32,24,128]{2,1,0:T(8,128)(2,1)S(1)}, u32[]{:S(2)}, u32[]{:S(2)}) collective-permute-start(bf16[32,24,128]{2,1,0:T(8,128)(2,1)S(1)} %copy-done.5), channel_id=1, source_target_pairs={{0,1},{1,0},{2,3},{3,2},{4,5},{5,4},{6,7},{7,6},{8,9},{9,8},{10,11... | collective-permute-start | bytes 589832 | tf_op jit(solution)/shard_map/swap_cores/ppermute | solution.py:412
  4.6 16.6 %collective-permute-start.4 = (bf16[32,64,128]{2,1,0:T(8,128)(2,1)S(1)}, bf16[32,64,128]{2,1,0:T(8,128)(2,1)S(1)}, u32[]{:S(2)}, u32[]{:S(2)}) collective-permute-start(bf16[32,64,128]{2,1,0:T(8,128)(2,1)S(1)} %copy-done.4), channel_id=1, source_target_pairs={{0,1},{1,0},{2,3},{3,2},{4,5},{5,4},{6,7},{7,6},{8,9},{9,8},{10,11... | collective-permute-start | bytes 1572872 | tf_op jit(solution)/shard_map/swap_cores/ppermute | solution.py:412
  9.4 5.8 %collective-permute-start.1 = (bf16[192,128]{1,0:T(8,128)(2,1)S(1)}, bf16[192,128]{1,0:T(8,128)(2,1)S(1)}, u32[]{:S(2)}, u32[]{:S(2)}) collective-permute-start(bf16[192,128]{1,0:T(8,128)(2,1)S(1)} %get-tuple-element.27), channel_id=1, source_target_pairs={{0,8},{8,0},{16,24},{24,16},{1,9},{9,1},{17,25},{25,17},{2,10},{10... | collective-permute-start | bytes 147464 | tf_op jit(solution)/shard_map/regroup_sends/ppermute | solution.py:412
  12.6 7.4 %collective-permute-start.2 = (bf16[192,128]{1,0:T(8,128)(2,1)S(1)}, bf16[192,128]{1,0:T(8,128)(2,1)S(1)}, u32[]{:S(2)}, u32[]{:S(2)}) collective-permute-start(bf16[192,128]{1,0:T(8,128)(2,1)S(1)} %get-tuple-element.26), channel_id=1, source_target_pairs={{0,16},{8,24},{16,0},{24,8},{1,17},{9,25},{17,1},{25,9},{2,18},{10... | collective-permute-start | bytes 147464 | tf_op jit(solution)/shard_map/regroup_sends/ppermute | solution.py:412
  15.3 5.9 %collective-permute-start.3 = (bf16[192,128]{1,0:T(8,128)(2,1)S(1)}, bf16[192,128]{1,0:T(8,128)(2,1)S(1)}, u32[]{:S(2)}, u32[]{:S(2)}) collective-permute-start(bf16[192,128]{1,0:T(8,128)(2,1)S(1)} %get-tuple-element.25), channel_id=1, source_target_pairs={{0,24},{8,16},{16,8},{24,0},{1,25},{9,17},{17,9},{25,1},{2,26},{10... | collective-permute-start | bytes 147464 | tf_op jit(solution)/shard_map/regroup_sends/ppermute | solution.py:412
  25.0 4.5 %collective-permute-start.11 = (bf16[192,128]{1,0:T(8,128)(2,1)S(1)}, bf16[192,128]{1,0:T(8,128)(2,1)S(1)}, u32[]{:S(2)}, u32[]{:S(2)}) collective-permute-start(bf16[192,128]{1,0:T(8,128)(2,1)S(1)} %get-tuple-element.22), channel_id=1, source_target_pairs={{0,2},{2,0},{4,6},{6,4},{1,3},{3,1},{5,7},{7,5},{8,10},{10,8},{12,... | collective-permute-start | bytes 147464 | tf_op jit(solution)/shard_map/coeff_sends/ppermute | solution.py:412
  26.5 8.3 %collective-permute-start.12 = (bf16[192,128]{1,0:T(8,128)(2,1)}, bf16[192,128]{1,0:T(8,128)(2,1)}, u32[]{:S(2)}, u32[]{:S(2)}) collective-permute-start(bf16[192,128]{1,0:T(8,128)(2,1)} %get-tuple-element.23), channel_id=1, source_target_pairs={{0,4},{2,6},{4,0},{6,2},{1,5},{3,7},{5,1},{7,3},{8,12},{10,14},{12... | collective-permute-start | bytes 147464 | tf_op jit(solution)/shard_map/coeff_sends/ppermute | solution.py:412
  28.0 7.3 %collective-permute-start.13 = (bf16[192,128]{1,0:T(8,128)(2,1)}, bf16[192,128]{1,0:T(8,128)(2,1)}, u32[]{:S(2)}, u32[]{:S(2)}) collective-permute-start(bf16[192,128]{1,0:T(8,128)(2,1)} %get-tuple-element.24), channel_id=1, source_target_pairs={{0,6},{2,4},{4,2},{6,0},{1,7},{3,5},{5,3},{7,1},{8,14},{10,12},{12... | collective-permute-start | bytes 147464 | tf_op jit(solution)/shard_map/coeff_sends/ppermute | solution.py:412
  29.6 11.9 %collective-permute-start.10 = (s32[4,128]{1,0:T(4,128)S(1)}, s32[4,128]{1,0:T(4,128)}, u32[]{:S(2)}, u32[]{:S(2)}) collective-permute-start(s32[4,128]{1,0:T(4,128)S(1)} %pad_add_fusion), channel_id=1, source_target_pairs={{0,1},{1,0},{2,3},{3,2},{4,5},{5,4},{6,7},{7,6},{8,9},{9,8},{10,11... | collective-permute-start | bytes 6152 | tf_op jit(solution)/shard_map/partner_codes/ppermute | solution.py:412
  34.8 15.9 %collective-permute-start.18 = (bf16[2,64,8,128]{3,2,1,0:T(8,128)(2,1)}, bf16[2,64,8,128]{3,2,1,0:T(8,128)(2,1)S(1)}, u32[]{:S(2)}, u32[]{:S(2)}) collective-permute-start(bf16[2,64,8,128]{3,2,1,0:T(8,128)(2,1)} %copy.21), channel_id=1, source_target_pairs={{0,1},{1,0},{2,3},{3,2},{4,5},{5,4},{6,7},{7,6},{8,9},{9,8},{10,11... | collective-permute-start | bytes 786440 | tf_op jit(solution)/shard_map/coupling_layout/ppermute | solution.py:412
  38.6 6.5 %collective-permute-start.16 = (bf16[224,128]{1,0:T(8,128)(2,1)S(1)}, bf16[224,128]{1,0:T(8,128)(2,1)S(1)}, u32[]{:S(2)}, u32[]{:S(2)}) collective-permute-start(bf16[224,128]{1,0:T(8,128)(2,1)S(1)} %parent_coeffs.1), channel_id=1, source_target_pairs={{0,24},{8,16},{16,8},{24,0},{1,25},{9,17},{17,9},{25,1},{2,26},{10... | collective-permute-start | bytes 172040 | tf_op jit(solution)/shard_map/owner_sends/ppermute | solution.py:412
  42.2 5.1 %collective-permute-start.15 = (bf16[224,128]{1,0:T(8,128)(2,1)S(1)}, bf16[224,128]{1,0:T(8,128)(2,1)S(1)}, u32[]{:S(2)}, u32[]{:S(2)}) collective-permute-start(bf16[224,128]{1,0:T(8,128)(2,1)S(1)} %parent_coeffs.1), channel_id=1, source_target_pairs={{0,16},{8,24},{16,0},{24,8},{1,17},{9,25},{17,1},{25,9},{2,18},{10... | collective-permute-start | bytes 172040 | tf_op jit(solution)/shard_map/owner_sends/ppermute | solution.py:412
  45.1 4.2 %collective-permute-start.14 = (bf16[224,128]{1,0:T(8,128)(2,1)S(1)}, bf16[224,128]{1,0:T(8,128)(2,1)S(1)}, u32[]{:S(2)}, u32[]{:S(2)}) collective-permute-start(bf16[224,128]{1,0:T(8,128)(2,1)S(1)} %parent_coeffs.1), channel_id=1, source_target_pairs={{0,8},{8,0},{16,24},{24,16},{1,9},{9,1},{17,25},{25,17},{2,10},{10... | collective-permute-start | bytes 172040 | tf_op jit(solution)/shard_map/owner_sends/ppermute | solution.py:412
  49.3 16.0 %collective-permute-start.19 = (bf16[896,128]{1,0:T(8,128)(2,1)S(1)}, bf16[896,128]{1,0:T(8,128)(2,1)S(1)}, u32[]{:S(2)}, u32[]{:S(2)}) collective-permute-start(bf16[896,128]{1,0:T(8,128)(2,1)S(1)} %pad_maximum_fusion.1.block_ref), channel_id=1, source_target_pairs={{0,2},{2,0},{4,6},{6,4},{1,3},{3,1},{5,7},{7,5},{8,10},{10,8},{12,... | collective-permute-start | bytes 688136 | tf_op jit(solution)/shard_map/level_sends/ppermute | solution.py:412
  51.8 21.9 %collective-permute-start.21 = (bf16[896,128]{1,0:T(8,128)(2,1)S(1)}, bf16[896,128]{1,0:T(8,128)(2,1)S(1)}, u32[]{:S(2)}, u32[]{:S(2)}) collective-permute-start(bf16[896,128]{1,0:T(8,128)(2,1)S(1)} %pad_maximum_fusion.1.block_ref), channel_id=1, source_target_pairs={{0,4},{2,6},{4,0},{6,2},{1,5},{3,7},{5,1},{7,3},{8,12},{10,14},{12... | collective-permute-start | bytes 688136 | tf_op jit(solution)/shard_map/level_sends/ppermute | solution.py:412
  53.3 24.7 %collective-permute-start.23 = (bf16[896,128]{1,0:T(8,128)(2,1)S(1)}, bf16[896,128]{1,0:T(8,128)(2,1)S(1)}, u32[]{:S(2)}, u32[]{:S(2)}) collective-permute-start(bf16[896,128]{1,0:T(8,128)(2,1)S(1)} %pad_maximum_fusion.1.block_ref), channel_id=1, source_target_pairs={{0,6},{2,4},{4,2},{6,0},{1,7},{3,5},{5,3},{7,1},{8,14},{10,12},{12... | collective-permute-start | bytes 688136 | tf_op jit(solution)/shard_map/level_sends/ppermute | solution.py:412
  57.6 36.3 %collective-permute-start.6 = (bf16[768,128]{1,0:T(8,128)(2,1)S(1)}, bf16[768,128]{1,0:T(8,128)(2,1)S(1)}, u32[]{:S(2)}, u32[]{:S(2)}) collective-permute-start(bf16[768,128]{1,0:T(8,128)(2,1)S(1)} %self_blocks.5), channel_id=1, source_target_pairs={{0,2},{2,0},{4,6},{6,4},{1,3},{3,1},{5,7},{7,5},{8,10},{10,8},{12,... | collective-permute-start | bytes 589832 | tf_op jit(solution)/shard_map/self_sends/ppermute | solution.py:412
  65.3 29.5 %collective-permute-start.7 = (bf16[768,128]{1,0:T(8,128)(2,1)S(1)}, bf16[768,128]{1,0:T(8,128)(2,1)S(1)}, u32[]{:S(2)}, u32[]{:S(2)}) collective-permute-start(bf16[768,128]{1,0:T(8,128)(2,1)S(1)} %self_blocks.6), channel_id=1, source_target_pairs={{0,4},{2,6},{4,0},{6,2},{1,5},{3,7},{5,1},{7,3},{8,12},{10,14},{12... | collective-permute-start | bytes 589832 | tf_op jit(solution)/shard_map/self_sends/ppermute | solution.py:412
  66.9 27.9 %collective-permute-start.8 = (bf16[768,128]{1,0:T(8,128)(2,1)S(1)}, bf16[768,128]{1,0:T(8,128)(2,1)S(1)}, u32[]{:S(2)}, u32[]{:S(2)}) collective-permute-start(bf16[768,128]{1,0:T(8,128)(2,1)S(1)} %self_blocks.7), channel_id=1, source_target_pairs={{0,6},{2,4},{4,2},{6,0},{1,7},{3,5},{5,3},{7,1},{8,14},{10,12},{12... | collective-permute-start | bytes 589832 | tf_op jit(solution)/shard_map/self_sends/ppermute | solution.py:412
  73.7 9.2 %collective-permute-start.20 = (bf16[224,128]{1,0:T(8,128)(2,1)S(1)}, bf16[224,128]{1,0:T(8,128)(2,1)S(1)}, u32[]{:S(2)}, u32[]{:S(2)}) collective-permute-start(bf16[224,128]{1,0:T(8,128)(2,1)S(1)} %coupling_products.5), channel_id=1, source_target_pairs={{0,2},{2,0},{4,6},{6,4},{1,3},{3,1},{5,7},{7,5},{8,10},{10,8},{12,... | collective-permute-start | bytes 172040 | tf_op jit(solution)/shard_map/far_sends/ppermute | solution.py:412
  78.1 12.4 %collective-permute-start.22 = (bf16[224,128]{1,0:T(8,128)(2,1)S(1)}, bf16[224,128]{1,0:T(8,128)(2,1)S(1)}, u32[]{:S(2)}, u32[]{:S(2)}) collective-permute-start(bf16[224,128]{1,0:T(8,128)(2,1)S(1)} %coupling_products.6), channel_id=1, source_target_pairs={{0,4},{2,6},{4,0},{6,2},{1,5},{3,7},{5,1},{7,3},{8,12},{10,14},{12... | collective-permute-start | bytes 172040 | tf_op jit(solution)/shard_map/far_sends/ppermute | solution.py:412
  82.9 7.6 %collective-permute-start.24 = (bf16[224,128]{1,0:T(8,128)(2,1)S(1)}, bf16[224,128]{1,0:T(8,128)(2,1)S(1)}, u32[]{:S(2)}, u32[]{:S(2)}) collective-permute-start(bf16[224,128]{1,0:T(8,128)(2,1)S(1)} %coupling_products.7), channel_id=1, source_target_pairs={{0,6},{2,4},{4,2},{6,0},{1,7},{3,5},{5,3},{7,1},{8,14},{10,12},{12... | collective-permute-start | bytes 172040 | tf_op jit(solution)/shard_map/far_sends/ppermute | solution.py:412
  91.3 4.8 %collective-permute-start.25 = (bf16[192,128]{1,0:T(8,128)(2,1)S(1)}, bf16[192,128]{1,0:T(8,128)(2,1)S(1)}, u32[]{:S(2)}, u32[]{:S(2)}) collective-permute-start(bf16[192,128]{1,0:T(8,128)(2,1)S(1)} %down_products.1.refs_0_), channel_id=1, source_target_pairs={{0,2},{2,0},{4,6},{6,4},{1,3},{3,1},{5,7},{7,5},{8,10},{10,8},{12,... | collective-permute-start | bytes 147464 | tf_op jit(solution)/shard_map/far_coeff_sends/ppermute | solution.py:412
  92.4 4.1 %collective-permute-start.26 = (bf16[192,128]{1,0:T(8,128)(2,1)S(1)}, bf16[192,128]{1,0:T(8,128)(2,1)S(1)}, u32[]{:S(2)}, u32[]{:S(2)}) collective-permute-start(bf16[192,128]{1,0:T(8,128)(2,1)S(1)} %down_products.1.refs_0_), channel_id=1, source_target_pairs={{0,4},{2,6},{4,0},{6,2},{1,5},{3,7},{5,1},{7,3},{8,12},{10,14},{12... | collective-permute-start | bytes 147464 | tf_op jit(solution)/shard_map/far_coeff_sends/ppermute | solution.py:412
  93.9 5.0 %collective-permute-start.27 = (bf16[192,128]{1,0:T(8,128)(2,1)S(1)}, bf16[192,128]{1,0:T(8,128)(2,1)S(1)}, u32[]{:S(2)}, u32[]{:S(2)}) collective-permute-start(bf16[192,128]{1,0:T(8,128)(2,1)S(1)} %down_products.1.refs_0_), channel_id=1, source_target_pairs={{0,6},{2,4},{4,2},{6,0},{1,7},{3,5},{5,3},{7,1},{8,14},{10,12},{12... | collective-permute-start | bytes 147464 | tf_op jit(solution)/shard_map/far_coeff_sends/ppermute | solution.py:412
  95.5 4.7 %collective-permute-start.9 = (bf16[384,128]{1,0:T(8,128)(2,1)S(1)}, bf16[384,128]{1,0:T(8,128)(2,1)S(1)}, u32[]{:S(2)}, u32[]{:S(2)}) collective-permute-start(bf16[384,128]{1,0:T(8,128)(2,1)S(1)} %get-tuple-element.17), channel_id=1, source_target_pairs={{0,1},{1,0},{2,3},{3,2},{4,5},{5,4},{6,7},{7,6},{8,9},{9,8},{10,11... | collective-permute-start | bytes 294920 | tf_op jit(solution)/shard_map/self_sends/ppermute | solution.py:412
  95.5 3.4 %collective-permute-start.28 = (bf16[192,128]{1,0:T(8,128)(2,1)S(1)}, bf16[192,128]{1,0:T(8,128)(2,1)S(1)}, u32[]{:S(2)}, u32[]{:S(2)}) collective-permute-start(bf16[192,128]{1,0:T(8,128)(2,1)S(1)} %down_products.1.refs_0_), channel_id=1, source_target_pairs={{0,1},{1,0},{2,3},{3,2},{4,5},{5,4},{6,7},{7,6},{8,9},{9,8},{10,11... | collective-permute-start | bytes 147464 | tf_op jit(solution)/shard_map/far_coeff_sends/ppermute | solution.py:412
  96.0 2.9 %collective-permute-start.29 = (bf16[192,128]{1,0:T(8,128)(2,1)S(1)}, bf16[192,128]{1,0:T(8,128)(2,1)S(1)}, u32[]{:S(2)}, u32[]{:S(2)}) collective-permute-start(bf16[192,128]{1,0:T(8,128)(2,1)S(1)} %collective-permute-done.25.refs_1_), channel_id=1, source_target_pairs={{0,1},{1,0},{2,3},{3,2},{4,5},{5,4},{6,7},{7,6},{8,9},{9,8},{10,11... | collective-permute-start | bytes 147464 | tf_op jit(solution)/shard_map/far_coeff_sends/ppermute | solution.py:412
  96.5 2.4 %collective-permute-start.30 = (bf16[192,128]{1,0:T(8,128)(2,1)S(1)}, bf16[192,128]{1,0:T(8,128)(2,1)S(1)}, u32[]{:S(2)}, u32[]{:S(2)}) collective-permute-start(bf16[192,128]{1,0:T(8,128)(2,1)S(1)} %collective-permute-done.26.refs_2_), channel_id=1, source_target_pairs={{0,1},{1,0},{2,3},{3,2},{4,5},{5,4},{6,7},{7,6},{8,9},{9,8},{10,11... | collective-permute-start | bytes 147464 | tf_op jit(solution)/shard_map/far_coeff_sends/ppermute | solution.py:412
  98.9 1.2 %collective-permute-start.31 = (bf16[192,128]{1,0:T(8,128)(2,1)S(1)}, bf16[192,128]{1,0:T(8,128)(2,1)S(1)}, u32[]{:S(2)}, u32[]{:S(2)}) collective-permute-start(bf16[192,128]{1,0:T(8,128)(2,1)S(1)} %collective-permute-done.27.refs_3_), channel_id=1, source_target_pairs={{0,1},{1,0},{2,3},{3,2},{4,5},{5,4},{6,7},{7,6},{8,9},{9,8},{10,11... | collective-permute-start | bytes 147464 | tf_op jit(solution)/shard_map/far_coeff_sends/ppermute | solution.py:412
  (16 other events, 152.3 us)

commit v2 on v0

v2 whole, which is shorter than its diff:
```python
import functools

import jax
import jax.numpy as jnp
from jax import lax
from jax.experimental import pallas as pl
from jax.experimental.pallas import tpu as pltpu
from jax.sharding import PartitionSpec as P

F32 = jnp.float32
BF16 = jnp.bfloat16
VMEM_LIMIT = 12 * 1024 * 1024


def vmem():
    return pl.BlockSpec(memory_space=pltpu.VMEM)


def smem():
    return pl.BlockSpec(memory_space=pltpu.SMEM)


def params(**more):
    return pltpu.CompilerParams(vmem_limit_bytes=VMEM_LIMIT, **more)


def cost(flops, nbytes):
    return pl.CostEstimate(flops=flops, bytes_accessed=nbytes, transcendentals=0)


def iota(shape, dim):
    return lax.broadcasted_iota(jnp.int32, shape, dim)


def row_of(ref, row):
    return ref[pl.ds(row, 1), :]


def mac_rows(total_steps, weight_at, row_at, accs, unroll):
    def body(step, carry):
        weight = weight_at(step)
        return tuple(acc + weight * row_at(step, n) for n, acc in enumerate(carry))

    return lax.fori_loop(0, total_steps, body, tuple(accs), unroll=unroll)


def pack_kernel(owners, vh, parents, ids_ref, own_ref, out_ref, rows_scr):
    slab, vectors, leaves = own_ref.shape
    children = leaves // parents
    reps = vectors // vh
    width = leaves // owners
    me, parity = ids_ref[0], ids_ref[2]
    row = iota((leaves, leaves), 0)
    lane = iota((leaves, leaves), 1)
    parent_of_row = row // children
    target = row % children
    bits = 32 // owners
    counts = jnp.int32(0)
    for parent in range(parents):
        owner = ids_ref[3 + me * parents + parent] // parents
        shift = owner * bits
        rank = lax.shift_right_logical(counts, shift) & ((1 << bits) - 1)
        counts = counts + lax.shift_left(jnp.int32(1), shift)
        code = (owner ^ me) * leaves + rank * children
        target = target + jnp.where(parent_of_row == parent, code, 0)
    part = (slab // owners) * vh
    rows_scr[...] = own_ref[...].reshape(slab * vectors, leaves).astype(F32)
    pieces = []
    for q in range(owners):
        start = q * (slab // owners) * vectors
        pieces.append(
            jnp.concatenate(
                [
                    rows_scr[pl.ds(start + first, part, stride=reps), :]
                    for first in (parity, 1 - parity)
                ],
                axis=0,
            ).astype(BF16)
        )
    for s in range(owners):
        total = jnp.zeros((2 * part, leaves), F32)
        for q in range(owners):
            onehot = jnp.where(target + (q * width - s * leaves) == lane, 1.0, 0.0).astype(BF16)
            total = total + jnp.dot(pieces[q], onehot, preferred_element_type=F32)
        out_ref[s] = total.astype(BF16)


def place_kernel(owners, parents, ids_ref, out_ref, code_scr):
    leaves = out_ref.shape[1]
    children = leaves // parents
    me = ids_ref[0]
    for source in range(owners):
        rank = jnp.int32(0)
        base = (source ^ me) * leaves
        for parent in range(parents):
            place = ids_ref[3 + source * parents + parent]
            mine = (place // parents) == me
            slot = jnp.where(mine, place % parents, parents)
            code_scr[slot] = base + rank * children
            rank = rank + jnp.where(mine, 1, 0)
    lane = iota(out_ref.shape, 1)
    code = lane % children
    for parent in range(parents):
        code = code + jnp.where(lane // children == parent, code_scr[parent], 0)
    out_ref[...] = code


def regroup_kernel(owners, code_ref, *refs):
    chunks, mine_ref, other_ref = refs[:owners], refs[owners], refs[owners + 1]
    leaves = mine_ref.shape[1]
    width = leaves // owners
    part = mine_ref.shape[0] // owners
    code = jnp.broadcast_to(code_ref[0:1, :], (leaves, leaves))
    row = iota((leaves, leaves), 0)
    for q in range(owners):
        total = jnp.zeros((2 * part, leaves), F32)
        for s in range(owners):
            onehot = jnp.where(code + (q * width - s * leaves) == row, 1.0, 0.0).astype(BF16)
            total = total + jnp.dot(chunks[s][...], onehot, preferred_element_type=F32)
        mine_ref[q * part : (q + 1) * part, :] = total[:part]
        other_ref[q * part : (q + 1) * part, :] = total[part:].astype(BF16)


def coeff_products(lvl, lvls, vh, vs, basis_ref, field_ref, start_of, finish):
    slab, rank_width, leaves = basis_ref.shape
    for t in range(lvls):
        first = (lvl ^ t) * vs
        accs = mac_rows(
            slab,
            lambda m: basis_ref[m].astype(F32),
            lambda m, n: row_of(field_ref, m * vh + jnp.minimum(first + n, vh - 1)),
            [start_of(t, n) for n in range(vs)],
            8,
        )
        for n in range(vs):
            finish(t, n, accs[n])


def coeff_own_kernel(lvls, vh, vs, ids_ref, basis_ref, field_ref, out_ref):
    rank_width, leaves = basis_ref.shape[1:]

    def finish(t, n, acc):
        start = (t * vs + n) * rank_width
        out_ref[start : start + rank_width, :] = acc

    coeff_products(
        ids_ref[1], lvls, vh, vs, basis_ref, field_ref,
        lambda t, n: jnp.zeros((rank_width, leaves), F32), finish,
    )


def coeff_peer_kernel(
    lvls, vh, vs, ids_ref, basis_ref, field_ref, own_ref, wide_ref, keep_ref, *sends
):
    rank_width = basis_ref.shape[1]
    wide_ref[...] = field_ref[...].astype(F32)

    def start_of(t, n):
        start = (t * vs + n) * rank_width
        return own_ref[start : start + rank_width, :]

    def finish(t, n, acc):
        block = slice(n * rank_width, (n + 1) * rank_width)
        if t == 0:
            keep_ref[block, :] = acc
        else:
            sends[t - 1][block, :] = acc.astype(BF16)

    coeff_products(ids_ref[1], lvls, vh, vs, basis_ref, wide_ref, start_of, finish)


def packs(vs, rank_width, leaves):
    per = max(1, leaves // rank_width)
    return [list(range(first, min(first + per, vs))) for first in range(0, vs, per)]


def up_kernel(vs, parents, keep_ref, *refs):
    recvs, up_ref, out_ref, coeff_scr = refs[:-3], refs[-3], refs[-2], refs[-1]
    rank_width, _, leaves = up_ref.shape
    total = keep_ref[...]
    for ref in recvs:
        total = total + ref[...].astype(F32)
    coeffs = total.astype(BF16)
    out_ref[0 : vs * rank_width, :] = coeffs
    coeff_scr[...] = coeffs.astype(F32)
    accs = mac_rows(
        rank_width,
        lambda j: up_ref[j].astype(F32),
        lambda j, n: row_of(coeff_scr, n * rank_width + j),
        [jnp.zeros((rank_width, leaves), F32) for _ in range(vs)],
        8,
    )
    mine = (iota((parents, leaves), 1) // (leaves // parents)) == iota((parents, leaves), 0)
    group = jnp.where(mine, 1.0, 0.0).astype(BF16)
    for b, members in enumerate(packs(vs, rank_width, leaves)):
        sums = []
        for n in members:
            rest, result = accs[n], jnp.zeros((parents, rank_width), F32)
            for _ in range(3):
                piece = rest.astype(BF16)
                result = result + lax.dot_general(
                    group, piece, (((1,), (1,)), ((), ())), preferred_element_type=F32
                )
                rest = rest - piece.astype(F32)
            sums.append(result)
        missing = leaves - len(sums) * rank_width
        if missing:
            sums.append(jnp.zeros((parents, missing), F32))
        start = vs * rank_width + b * parents
        out_ref[start : start + parents, :] = jnp.concatenate(sums, axis=1).astype(BF16)


def table_kernel(
    owners, parents, slots, own_codes, peer_codes, own_ref, peer_ref,
    leaf_out, parent_out, couple_out, rows_scr,
):
    leaves = own_codes.shape[1]
    sources = leaf_out.shape[0]
    count = parent_out.shape[0] // 2
    for half, codes in enumerate((own_codes, peer_codes)):
        for i in range(slots):
            hit = jnp.broadcast_to(codes[i : i + 1, :], (sources, leaves)) == iota(
                (sources, leaves), 0
            )
            start = (half * slots + i) * leaves
            leaf_out[:, start : start + leaves] = jnp.where(hit, 1.0, 0.0).astype(BF16)
        uppers = owners * parents
        same = iota((uppers, uppers), 0) == iota((uppers, uppers), 1)
        same = jnp.where(same, 1.0, 0.0).astype(BF16)
        pslots = count // parents
        for i in range(pslots):
            code = jnp.broadcast_to(codes[slots + i : slots + i + 1, :], (uppers, leaves))
            hit = jnp.where(code == iota(code.shape, 0), 1.0, 0.0).astype(BF16)
            turned = lax.dot_general(
                hit, same, (((0,), (0,)), ((), ())), preferred_element_type=F32
            )
            start = half * count + i * parents
            parent_out[start : start + parents, :] = turned[:parents].astype(BF16)
    rank_width, pslots = own_ref.shape[0], own_ref.shape[1] // parents
    for half, ref in enumerate((own_ref, peer_ref)):
        rows_scr[...] = ref[...].reshape(rank_width * pslots * parents, rank_width).astype(F32)
        for i in range(pslots):
            place = (half * pslots + i) * rank_width
            for parent in range(parents):
                block = rows_scr[pl.ds(i * parents + parent, rank_width, stride=pslots * parents), :]
                couple_out[parent, place : place + rank_width, :] = block.astype(BF16)


def far_kernel(owners, vs, pslots, leaf_table, parent_table, pcouple_ref, block_ref, *refs):
    extras = refs[:-8]
    own_ref, peer_any, out_ref, rows_scr, prows_scr, pout_scr, couple_scr, sems = refs[-8:]
    slots, rank_width, _, leaves = own_ref.shape
    parents = pcouple_ref.shape[0]
    copies = []
    for i in range(slots):
        copies.append(pltpu.make_async_copy(peer_any.at[i], couple_scr.at[i], sems.at[i]))
        copies[-1].start()
    per_block = block_ref.shape[0] // owners
    mine = vs * rank_width
    rows = jnp.zeros((mine, 2 * slots * leaves), F32)
    for o in range(0, owners, 2):
        pair = [block_ref[p * per_block : p * per_block + mine, :] for p in (o, o + 1)]
        rows = rows + jnp.dot(
            jnp.concatenate(pair, axis=1),
            leaf_table[o * leaves : (o + 2) * leaves, :],
            preferred_element_type=F32,
        )
    for i in range(2 * slots):
        rows_scr[i] = rows[:, i * leaves : (i + 1) * leaves]

    for b, members in enumerate(packs(vs, rank_width, leaves)):
        source = jnp.concatenate(
            [
                block_ref[pl.ds(o * per_block + mine + b * parents, parents), :]
                for o in range(owners)
            ],
            axis=0,
        )
        picked = jnp.dot(parent_table[...], source, preferred_element_type=F32)
        for i in range(2 * pslots):
            for k, n in enumerate(members):
                prows_scr[:, n, i * rank_width : (i + 1) * rank_width] = picked[
                    i * parents : (i + 1) * parents, k * rank_width : (k + 1) * rank_width
                ]
    for parent in range(parents):
        pout_scr[parent] = jnp.dot(
            prows_scr[parent].astype(BF16), pcouple_ref[parent], preferred_element_type=F32
        )
    for b, members in enumerate(packs(vs, rank_width, leaves)):
        parts = [pout_scr[:, n, :] for n in members]
        missing = leaves - len(parts) * rank_width
        if missing:
            parts.append(jnp.zeros((parents, missing), F32))
        out_ref[mine + b * parents : mine + (b + 1) * parents, :] = jnp.concatenate(
            parts, axis=1
        ).astype(out_ref.dtype)
    start = mine + len(packs(vs, rank_width, leaves)) * parents
    for ref in extras:
        out_ref[start : start + ref.shape[0], :] = ref[...]
        start += ref.shape[0]

    accs = [jnp.zeros((rank_width, leaves), F32) for _ in range(vs)]
    for s in range(2 * slots):
        if s >= slots:
            copies[s - slots].wait()
        ref, i = (own_ref, s) if s < slots else (couple_scr, s - slots)
        accs = mac_rows(
            rank_width,
            lambda j, ref=ref, i=i: ref[i, j].astype(F32),
            lambda j, n, s=s: rows_scr[s, pl.ds(n * rank_width + j, 1), :],
            accs,
            8,
        )
    for n in range(vs):
        out_ref[n * rank_width : (n + 1) * rank_width, :] = accs[n].astype(out_ref.dtype)


def down_kernel(vs, parents, keep_ref, *refs):
    recvs, down_ref, out_ref, rows_scr = refs[:-3], refs[-3], refs[-2], refs[-1]
    rank_width, _, leaves = down_ref.shape
    total = keep_ref[...]
    for ref in recvs:
        total = total + ref[0 : total.shape[0], :].astype(F32)
    mine = vs * rank_width
    below = (iota((parents, leaves), 1) // (leaves // parents)) == iota((parents, leaves), 0)
    spread = jnp.where(below, 1.0, 0.0).astype(BF16)
    for b, members in enumerate(packs(vs, rank_width, leaves)):
        part = total[mine + b * parents : mine + (b + 1) * parents, :].astype(BF16)
        wide = lax.dot_general(
            part, spread, (((0,), (0,)), ((), ())), preferred_element_type=F32
        )
        count = len(members) * rank_width
        start = members[0] * rank_width
        rows_scr[start : start + count, :] = wide[:count]
    accs = mac_rows(
        rank_width,
        lambda j: down_ref[j].astype(F32),
        lambda j, n: row_of(rows_scr, n * rank_width + j),
        [total[n * rank_width : (n + 1) * rank_width, :] for n in range(vs)],
        8,
    )
    for n in range(vs):
        out_ref[n * rank_width : (n + 1) * rank_width, :] = accs[n].astype(BF16)


def near_kernel(
    vh, step, ids_ref, own_field, peer_field, own_ref, peer_any, out_ref, peer_scr, acc_scr, sem
):
    slab, _, leaves = own_ref.shape
    group = 6
    target = pl.multiple_of((ids_ref[1] ^ step) * (2 * slab), 2 * slab)
    copy = pltpu.make_async_copy(peer_any.at[:, pl.ds(target, 2 * slab), :], peer_scr, sem)
    copy.start()

    def products(field_ref, ref, base, first, half, accs):
        span = pl.ds(pl.multiple_of(base + half * slab, slab), slab)
        return mac_rows(
            slab,
            lambda p: ref[p, span, :].astype(F32),
            lambda p, n: row_of(field_ref, p * vh + first + n),
            accs,
            8,
        )

    places = [(half, first) for half in range(2) for first in range(0, vh, group)]
    for half, first in places:
        accs = [jnp.zeros((slab, leaves), F32) for _ in range(group)]
        accs = products(own_field, own_ref, target, first, half, accs)
        for n in range(group):
            start = (half * vh + first + n) * slab
            acc_scr[start : start + slab, :] = accs[n]
    copy.wait()
    for half, first in places:
        starts = [(half * vh + first + n) * slab for n in range(group)]
        accs = [acc_scr[start : start + slab, :] for start in starts]
        accs = products(peer_field, peer_scr, 0, first, half, accs)
        for n, start in enumerate(starts):
            out_ref[start : start + slab, :] = accs[n].astype(out_ref.dtype)


def near_sum_kernel(skip, ids_ref, keep_ref, *refs):
    recvs, mine_ref, send_ref = refs[:-2], refs[-2], refs[-1]
    count = mine_ref.shape[0]
    parity = ids_ref[2]

    def summed(start):
        start = pl.multiple_of(start, 16)
        total = keep_ref[pl.ds(start, count), :]
        for ref in recvs:
            total = total + ref[pl.ds(skip + start, count), :].astype(F32)
        return total

    mine_ref[...] = summed(parity * count)
    send_ref[...] = summed((1 - parity) * count).astype(BF16)


def column_kernel(vs, column_ref, mine_ref, other_ref, out_ref, rows_scr):
    rank_width, voxels, leaves = column_ref.shape
    rows_scr[0] = mine_ref[...].astype(F32)
    rows_scr[1] = other_ref[...].astype(F32)
    accs = mac_rows(
        rank_width,
        lambda k: column_ref[k].astype(F32),
        lambda k, n: rows_scr[n // vs, pl.ds((n % vs) * rank_width + k, 1), :],
        [jnp.zeros((voxels, leaves), F32) for _ in range(2 * vs)],
        8,
    )
    for n in range(2 * vs):
        out_ref[n * voxels : (n + 1) * voxels, :] = accs[n]


def out_kernel(lvls, vh, vs, early, ids_ref, column_ref, near_mine, near_peer, *refs):
    done, blocks = refs[:early], refs[early : -3]
    out_ref, rows_scr, out_scr = refs[-3:]
    rank_width, voxels, leaves = column_ref.shape
    vectors = out_ref.shape[1]
    lvl, parity = ids_ref[1], ids_ref[2]
    late = lvls - early
    for b, ref in enumerate(blocks):
        rows_scr[b] = ref[...].astype(F32)

    def store(place, rep, value):
        def write():
            vector = place * 2 + (parity if rep == 0 else 1 - parity)
            out_scr[pl.ds(vector, voxels, stride=vectors), :] = value

        if lvls * vs == vh:
            write()
        else:
            pl.when(place < vh)(write)

    for t in range(lvls):
        first = (lvl ^ t) * vs
        if t < early:
            accs = [done[t][n * voxels : (n + 1) * voxels, :] for n in range(2 * vs)]
        else:
            accs = mac_rows(
                rank_width,
                lambda k: column_ref[k].astype(F32),
                lambda k, n: rows_scr[
                    (n // vs) * late + t - early, pl.ds((n % vs) * rank_width + k, 1), :
                ],
                [jnp.zeros((voxels, leaves), F32) for _ in range(2 * vs)],
                8,
            )
        for n in range(2 * vs):
            place = first + n % vs
            near_ref = (near_mine, near_peer)[n // vs]
            inside = jnp.minimum(place, vh - 1)
            near = near_ref[pl.ds(pl.multiple_of(inside * voxels, voxels), voxels), :]
            store(place, n // vs, accs[n] + near.astype(F32))
    out_ref[...] = out_scr[...].reshape(voxels, vectors, leaves).astype(BF16)


def after(value, *others):
    return lax.optimization_barrier((value,) + others)[0]


def per_device(sizes, *args):
    (
        voxel_field, row_basis, near_block, up_transfer, coupling, parent_coupling,
        down_transfer, column_basis, parent_perm, partner_owner, partner_local,
        parent_owner, parent_local, block_count,
    ) = args
    owners, lvls, reps = sizes
    slab, vectors, leaves = voxel_field.shape
    rank_width = row_basis.shape[1]
    parents = parent_coupling.shape[4]
    children = leaves // parents
    slots = partner_owner.shape[2]
    pslots = parent_owner.shape[2]
    vh = vectors // reps
    vs = -(-vh // lvls)
    sds = jax.ShapeDtypeStruct

    me = lax.axis_index("clus")
    lvl = lax.axis_index("lvl")
    parity = lax.axis_index("rep")
    ids = jnp.concatenate([jnp.stack([me, lvl, parity]).astype(jnp.int32), parent_perm])

    def call(name, kernel, ins, outs, scratch=(), us=1.0, scalars=0, whole=()):
        specs = [
            smem() if i < scalars else pl.BlockSpec(memory_space=pltpu.HBM) if i in whole else vmem()
            for i in range(len(ins))
        ]
        with jax.named_scope(name):
            return pl.pallas_call(
                kernel,
                out_shape=outs,
                in_specs=specs,
                out_specs=jax.tree.map(lambda _: vmem(), outs),
                scratch_shapes=list(scratch),
                compiler_params=params(),
                cost_estimate=cost(0, int(us * 3.3e6)),
            )(*ins)

    def swap(value, axis, count, step):
        return lax.ppermute(value, axis, [(i, i ^ step) for i in range(count)])

    def other(value):
        return swap(value, "rep", reps, 1)

    with jax.named_scope("swap_row_basis"):
        row_peer = other(row_basis)
    with jax.named_scope("swap_parent_coupling"):
        pcouple = jnp.transpose(parent_coupling, (0, 2, 3, 4, 1)).reshape(
            rank_width, pslots * parents, rank_width
        )
        pcouple_peer = other(pcouple)
    with jax.named_scope("swap_self_blocks"):
        near_peer_block = other(near_block)

    chunk_rows = 2 * (slab // owners) * vh
    packed = call(
        "pack_field",
        functools.partial(pack_kernel, owners, vh, parents),
        (ids, voxel_field),
        sds((owners, chunk_rows, leaves), BF16),
        [pltpu.VMEM((slab * vectors, leaves), F32)],
        1.0, scalars=1,
    )
    with jax.named_scope("regroup_sends"):
        chunks = [packed[0]] + [swap(packed[s], "clus", owners, s) for s in range(1, owners)]
    codes = call(
        "place_codes",
        functools.partial(place_kernel, owners, parents),
        (after(ids, chunks[1]),),
        sds((8, leaves), jnp.int32),
        [pltpu.SMEM((parents + 1,), jnp.int32)],
        0.3, scalars=1,
    )
    with jax.named_scope("coupling_layout"):
        couple = jnp.moveaxis(after(coupling, chunks[1])[:, :, 0], 2, 0)

    codes = after(codes, couple, row_peer)

    field, field_send = call(
        "regroup_field",
        functools.partial(regroup_kernel, owners),
        (codes, *chunks),
        [sds((slab * vh, leaves), F32), sds((slab * vh, leaves), BF16)],
        (), 0.4,
    )
    with jax.named_scope("swap_field"):
        field_recv = other(field_send)
    coeff_own = call(
        "coeffs_own_slab",
        functools.partial(coeff_own_kernel, lvls, vh, vs),
        (ids, row_basis, field),
        sds((lvls * vs * rank_width, leaves), F32),
        (), 1.6, scalars=1,
    )
    outs = call(
        "coeffs_other_slab",
        functools.partial(coeff_peer_kernel, lvls, vh, vs),
        (ids, row_peer, field_recv, coeff_own),
        [sds((slab * vh, leaves), F32), sds((vs * rank_width, leaves), F32)]
        + [sds((vs * rank_width, leaves), BF16)] * (lvls - 1),
        (), 1.6, scalars=1,
    )
    field_peer, keep, sends = outs[0], outs[1], outs[2:]
    with jax.named_scope("coeff_sends"):
        recvs = [swap(sends[t - 1], "lvl", lvls, t) for t in range(1, lvls)]

    with jax.named_scope("partner_codes"):
        held = lax.optimization_barrier(
            (partner_owner, partner_local, parent_owner, parent_local, block_count, keep)
        )
        group = lvl * reps + parity
        slot_number = group * slots + jnp.arange(slots, dtype=jnp.int32)[:, None]
        leaf_code = (held[0][0] ^ me).T * leaves + held[1][0].T
        leaf_code = jnp.where(slot_number < held[4][None, :], leaf_code, -1)
        up_code = (held[2][0] ^ me).T * parents + held[3][0].T
        up_code = jnp.pad(up_code, ((0, 0), (0, leaves - parents)), constant_values=-1)
        partners = jnp.concatenate([leaf_code, up_code], axis=0)
        partners_peer = other(partners)
    with jax.named_scope("swap_coupling"):
        couple_peer = other(after(couple, keep))

    def near_part(t, place):
        return call(
            "self_blocks",
            functools.partial(near_kernel, vh, t),
            (ids, place, field_peer, near_block, near_peer_block),
            sds((2 * vh * slab, leaves), F32 if t == 0 else BF16),
            [
                pltpu.VMEM((slab, 2 * slab, leaves), BF16),
                pltpu.VMEM((2 * vh * slab, leaves), F32),
                pltpu.SemaphoreType.DMA,
            ],
            2.4, scalars=1, whole=(4,),
        )

    near_parts = [None] * lvls
    near_parts[1] = near_part(1, after(field, field_peer))
    up_after = after(up_transfer, near_parts[1], partners)

    block_rows = vs * rank_width + len(packs(vs, rank_width, leaves)) * parents
    block = call(
        "parent_coeffs",
        functools.partial(up_kernel, vs, parents),
        (keep, *recvs, up_after),
        sds((block_rows, leaves), BF16),
        [pltpu.VMEM((vs * rank_width, leaves), F32)],
        0.8,
    )
    with jax.named_scope("owner_sends"):
        blocks = [block] + [swap(block, "clus", owners, s) for s in range(1, owners)]
    later = after(field, block)
    for t in range(2, lvls):
        near_parts[t] = near_part(t, later)
    with jax.named_scope("all_owners"):
        blocks = list(lax.optimization_barrier(tuple(blocks) + tuple(near_parts[2:])))[:owners]
        mine = jnp.concatenate(blocks, axis=0)
    with jax.named_scope("level_sends"):
        alls = [mine] + [swap(mine, "lvl", lvls, t) for t in range(1, lvls)]

    near_parts[0] = near_part(0, after(field, mine))
    leaf_table, parent_table, pcouple_all = call(
        "partner_tables",
        functools.partial(table_kernel, owners, parents, slots),
        (after(partners, mine), partners_peer, pcouple, pcouple_peer),
        [
            sds((owners * leaves, 2 * slots * leaves), BF16),
            sds((2 * pslots * parents, owners * parents), BF16),
            sds((parents, 2 * pslots * rank_width, rank_width), BF16),
        ],
        [pltpu.VMEM((rank_width * pslots * parents, rank_width), F32)],
        1.5,
    )
    def far_part(t, block):
        extras = () if t == 0 else (near_parts[t],)
        rows = block_rows if t == 0 else block_rows + 2 * vh * slab
        return call(
            "coupling_products",
            functools.partial(far_kernel, owners, vs, pslots),
            (leaf_table, parent_table, pcouple_all, block, *extras, couple, couple_peer),
            sds((rows, leaves), F32 if t == 0 else BF16),
            [
                pltpu.VMEM((2 * slots, vs * rank_width, leaves), F32),
                pltpu.VMEM((parents, 8, 2 * pslots * rank_width), F32),
                pltpu.VMEM((parents, 8, rank_width), F32),
                pltpu.VMEM((slots, rank_width, rank_width, leaves), BF16),
                pltpu.SemaphoreType.DMA((slots,)),
            ],
            3.2, whole=(5 + len(extras),),
        )

    alls[1] = after(alls[1], near_parts[0])
    far_parts = [far_part(t, alls[t]) for t in range(lvls)]
    with jax.named_scope("far_sends"):
        far_recvs = [swap(far_parts[t], "lvl", lvls, t) for t in range(1, lvls)]
    far = call(
        "down_products",
        functools.partial(down_kernel, vs, parents),
        (far_parts[0], *far_recvs, down_transfer),
        sds((vs * rank_width, leaves), BF16),
        [pltpu.VMEM((vs * rank_width, leaves), F32)],
        0.8,
    )
    with jax.named_scope("far_coeff_sends"):
        far_blocks = [far] + [swap(far, "lvl", lvls, t) for t in range(1, lvls)]
        far_others = [other(value) for value in far_blocks]
    early = lvls - 1
    done = [
        call(
            "column_products_early",
            functools.partial(column_kernel, vs),
            (column_basis, far_blocks[t], far_others[t]),
            sds((2 * vs * slab, leaves), F32),
            [pltpu.VMEM((2, vs * rank_width, leaves), F32)],
            0.5,
        )
        for t in range(early)
    ]
    near_mine, near_send = call(
        "self_sums",
        functools.partial(near_sum_kernel, block_rows),
        (ids, after(near_parts[0], done[0]), *far_recvs),
        [sds((vh * slab, leaves), F32), sds((vh * slab, leaves), BF16)],
        (), 0.65, scalars=1,
    )
    with jax.named_scope("swap_self_sums"):
        near_peer = other(near_send)
    return call(
        "column_products",
        functools.partial(out_kernel, lvls, vh, vs, early),
        (
            ids, column_basis, near_mine, near_peer, *done,
            *far_blocks[early:], *far_others[early:],
        ),
        sds((slab, vectors, leaves), BF16),
        [
            pltpu.VMEM((2 * (lvls - early), vs * rank_width, leaves), F32),
            pltpu.VMEM((slab * vectors, leaves), F32),
        ],
        1.85, scalars=1,
    )


def solution(mesh):
    sizes = (mesh.shape["clus"], mesh.shape["lvl"], mesh.shape["rep"])
    return jax.shard_map(
        functools.partial(per_device, sizes),
        mesh=mesh,
        in_specs=(
            P(("lvl", "rep"), None, ("parts", "clus")),
            P(("lvl", "rep"), None, ("parts", "clus")),
            P(("lvl", "rep"), None, ("parts", "clus")),
            P(None, None, ("parts", "clus")),
            P(None, None, ("lvl", "rep"), None, ("parts", "clus")),
            P(None, None, ("lvl", "rep"), None, ("parts", "clus")),
            P(None, None, ("parts", "clus")),
            P(None, ("lvl", "rep"), ("parts", "clus")),
            P("parts"),
            P(("lvl", "rep"), ("parts", "clus"), None),
            P(("lvl", "rep"), ("parts", "clus"), None),
            P(("lvl", "rep"), ("parts", "clus"), None),
            P(("lvl", "rep"), ("parts", "clus"), None),
            P(("parts", "clus")),
        ),
        out_specs=P(("lvl", "rep"), None, ("parts", "clus")),
        check_vma=False,
    )
```

time: 252 us -> 78.8 us (0.31)
  blocking collectives: 93.8 us -> 0 us
  waiting for transfers between devices: 64.4 us -> 11.6 us
  local copies, waits for them, and re-layouts: 48.1 us -> 4.82 us
  Pallas kernels: 0 us -> 35 us
  starting transfers between devices: 6.58 us -> 25.8 us
  matrix products: 14 us -> 0 us
  between operations: 13.4 us -> 0.46 us
  other arithmetic: 10.3 us -> 0.82 us
    psum x2 -> x0, blocking collectives: 78.8 us -> none  [the longest x1 53.5 us: per_device(): coeffs = lax.psum(partial_value, ('lvl', 'rep')).astype(jnp.bfloat16)]
    pallas_call x0 -> x21, Pallas kernels: none -> 35 us  [call(): pl.pallas_call(kernel, out_shape=outs, in_specs=specs, out_specs=jax.tree...]
    reduce_scatter x1 -> x0, waiting for transfers between devices: 35 us -> none  [per_device(): lax.psum_scatter(jnp.einsum('pml,pvl->mvl', near_block, regrouped, prefer...]
    all_gather x1 -> x0, waiting for transfers between devices: 28.6 us -> none  [per_device(): lax.all_gather(coeffs, 'clus', axis=2, tiled=True)]
    ppermute x0 -> x29, starting transfers between devices: none -> 25.8 us  [swap(): return lax.ppermute(value, axis, [(i, i ^ step) for i in range(count)])]
    reshape x4 -> x0, local copies, waits for them, and re-layouts: 16 us -> none  [the longest x1 7.84 us: per_device(): leaf_blocks = coupling.reshape(rank_width, rank_width, slot_dev, leaves)]
    all_gather x1 -> x0, blocking collectives: 15 us -> none  [per_device(): lax.all_gather(parent_coeffs, 'clus', axis=2, tiled=True)]
    dot_general x7 -> x0, matrix products: 14 us -> none  [the longest x1 4.77 us: per_device(): jnp.einsum('jkil,vjli->vkl', leaf_blocks, leaf_rows, preferred_element_ty...]
  transfers between devices with their start and end apart: 4 -> 29, of which waited for: 3 -> 7; matrix products, arithmetic and copies ran while one was open for 18% -> 4% of each run, Pallas kernels for 0% -> 41%
where the time goes in v2:
time: 78.8 us; the launch traced here: 78.4 us
  Pallas kernels  35 us (44%)
  starting transfers between devices  25.8 us (33%)
  waiting for transfers between devices  11.6 us (15%)
  local copies, waits for them, and re-layouts  4.82 us (6%)
  other arithmetic  0.82 us (1%)
    pallas_call x21, Pallas kernels, call(): pl.pallas_call(kernel, out_shape=outs, in_specs=specs, out_specs=jax.tree...  35 us
    ppermute x29, starting transfers between devices, swap(): return lax.ppermute(value, axis, [(i, i ^ step) for i in range(count)])  25.8 us
    ppermute x29, waiting for transfers between devices, swap(): return lax.ppermute(value, axis, [(i, i ^ step) for i in range(count)])  11.6 us
    unnamed x29, local copies, waits for them, and re-layouts  2.6 us
    optimization_barrier x1, local copies, waits for them, and re-layouts, after(): return lax.optimization_barrier((value,) + others)[0]  2.19 us
  transfers between devices with their start and end apart: 29, of which 7 were waited for; matrix products, arithmetic and copies ran while one was open for 4% of the time, Pallas kernels for 41%

profile of v2, /device:TPU:0, one launch (start us, length us, event | category | flops | bytes accessed | tf_op | source)
XLA Modules:
  0.0 78.4 jit_solution(3093670970432992271)
XLA Ops:
  2.2 1.0 %pack_field.1 = bf16[4,192,128]{2,1,0:T(8,128)(2,1)S(1)} custom-call(s32[67]{0:T(128)S(1)} %pad_add_fusion.ids_ref, bf16[32,24,128]{2,1,0:T(8,128)(2,1)S(1)} %copy-done.7), custom_call_target="tpu_custom_call" | custom-call | bytes 3300000 | tf_op jit(solution)/shard_map/pack_field/pallas_call | solution.py:487
  3.2 3.1 %collective-permute-start = (bf16[192,128]{1,0:T(8,128)(2,1)S(1)}, bf16[192,128]{1,0:T(8,128)(2,1)S(1)}, u32[]{:S(2)}, u32[]{:S(2)}) collective-permute-start(bf16[192,128]{1,0:T(8,128)(2,1)S(1)} %get-tuple-element.72), channel_id=1, source_target_pairs={{0,8},{8,0},{16,24},{24,16},{1,9},{9,1},{17,25},{25,17},{2,10},{10... | collective-permute-start | bytes 147464 | tf_op jit(solution)/shard_map/regroup_sends/ppermute | solution.py:498
  6.3 2.6 %collective-permute-start.2 = (bf16[192,128]{1,0:T(8,128)(2,1)S(1)}, bf16[192,128]{1,0:T(8,128)(2,1)S(1)}, u32[]{:S(2)}, u32[]{:S(2)}) collective-permute-start(bf16[192,128]{1,0:T(8,128)(2,1)S(1)} %get-tuple-element.70), channel_id=1, source_target_pairs={{0,16},{8,24},{16,0},{24,8},{1,17},{9,25},{17,1},{25,9},{2,18},{10... | collective-permute-start | bytes 147464 | tf_op jit(solution)/shard_map/regroup_sends/ppermute | solution.py:498
  8.9 1.1 %place_codes.1.code_ref = s32[8,128]{1,0:T(8,128)S(1)} custom-call(s32[67]{0:T(128)S(1)} %pad_add_fusion.ids_ref), custom_call_target="tpu_custom_call" | custom-call | bytes 990000 | tf_op jit(solution)/shard_map/place_codes/pallas_call | solution.py:487
  10.0 2.2 %copy.17 = bf16[64,64,1,2,128]{4,1,0,3,2:T(8,128)(2,1)S(1)} copy(bf16[64,64,1,2,128]{4,3,2,1,0:T(2,128)(2,1)} %param.18) | data formatting | bytes 4194304 | tf_op jit(solution)/shard_map/coupling_layout/optimization_barrier | solution.py:456
  12.3 2.5 %collective-permute-done.3.refs_3_ = bf16[192,128]{1,0:T(8,128)(2,1)S(1)} collective-permute-done((bf16[192,128]{1,0:T(8,128)(2,1)S(1)}, bf16[192,128]{1,0:T(8,128)(2,1)S(1)}, u32[]{:S(2)}, u32[]{:S(2)}) %collective-permute-start.3) | collective-permute-done | bytes 49184 | tf_op jit(solution)/shard_map/regroup_sends/ppermute | solution.py:498
  15.3 1.6 %coeffs_own_slab.1.own_ref = f32[768,128]{1,0:T(8,128)S(1)} custom-call(s32[67]{0:T(128)S(1)} %pad_add_fusion.ids_ref, bf16[32,64,128]{2,1,0:T(8,128)(2,1)S(1)} %copy-done.5, f32[384,128]{1,0:T(8,128)S(1)} %get-tuple-element.59.field_ref.own_field), custom_call_target="tpu_custom_call" | custom-call | bytes 5280000 | tf_op jit(solution)/shard_map/coeffs_own_slab/pallas_call | solution.py:487
  16.9 1.7 %coeffs_other_slab.1 = (f32[384,128]{1,0:T(8,128)S(1)}, f32[192,128]{1,0:T(8,128)S(1)}, bf16[192,128]{1,0:T(8,128)(2,1)S(1)}, bf16[192,128]{1,0:T(8,128)(2,1)S(1)}, bf16[192,128]{1,0:T(8,128)(2,1)S(1)}) custom-call(s32[67]{0:T(128)S(1)} %pad_add_fusion.ids_ref, bf16[32,64,128]{2,1,0:T(8,128)(2,1)S(1)} %collective-permute-done.1.basis_ref, ...), custom_call_target="tpu_custom_call" | custom-call | bytes 5280000 | tf_op jit(solution)/shard_map/coeffs_other_slab/pallas_call | solution.py:487
  19.1 1.5 %collective-permute-start.5 = (bf16[192,128]{1,0:T(8,128)(2,1)S(1)}, bf16[192,128]{1,0:T(8,128)(2,1)S(1)}, u32[]{:S(2)}, u32[]{:S(2)}) collective-permute-start(bf16[192,128]{1,0:T(8,128)(2,1)S(1)} %get-tuple-element.43), channel_id=1, source_target_pairs={{0,2},{2,0},{4,6},{6,4},{1,3},{3,1},{5,7},{7,5},{8,10},{10,8},{12,... | collective-permute-start | bytes 147464 | tf_op jit(solution)/shard_map/coeff_sends/ppermute | solution.py:498
  20.6 1.5 %collective-permute-start.6 = (bf16[192,128]{1,0:T(8,128)(2,1)S(1)}, bf16[192,128]{1,0:T(8,128)(2,1)S(1)}, u32[]{:S(2)}, u32[]{:S(2)}) collective-permute-start(bf16[192,128]{1,0:T(8,128)(2,1)S(1)} %get-tuple-element.44), channel_id=1, source_target_pairs={{0,4},{2,6},{4,0},{6,2},{1,5},{3,7},{5,1},{7,3},{8,12},{10,14},{12... | collective-permute-start | bytes 147464 | tf_op jit(solution)/shard_map/coeff_sends/ppermute | solution.py:498
  22.7 1.6 %copy-done = bf16[32,256,128]{2,1,0:T(8,128)(2,1)S(1)} copy-done((bf16[32,256,128]{2,1,0:T(8,128)(2,1)S(1)}, bf16[32,256,128]{2,1,0:T(8,128)(2,1)}, u32[]{:S(2)}) %copy-start) | copy-done | bytes 2097176
  24.3 2.9 %self_blocks.4.refs_0_ = bf16[768,128]{1,0:T(8,128)(2,1)S(1)} custom-call(s32[67]{0:T(128)S(1)} %pad_add_fusion.ids_ref, f32[384,128]{1,0:T(8,128)S(1)} %get-tuple-element.59.field_ref.own_field, f32[384,128]{1,0:T(8,128)S(1)} %get-tuple-element.46.peer_field, bf16[32,256,128]{2,1,0:T(8,128)(2,1)S(1)} %copy-done, ...), custom_call_target="tpu_custom_call" | custom-call | bytes 7920000 | tf_op jit(solution)/shard_map/self_blocks/pallas_call | solution.py:487
  28.1 2.1 %collective-permute-start.10 = (bf16[224,128]{1,0:T(8,128)(2,1)S(1)}, bf16[224,128]{1,0:T(8,128)(2,1)S(1)}, u32[]{:S(2)}, u32[]{:S(2)}) collective-permute-start(bf16[224,128]{1,0:T(8,128)(2,1)S(1)} %parent_coeffs.1), channel_id=1, source_target_pairs={{0,16},{8,24},{16,0},{24,8},{1,17},{9,25},{17,1},{25,9},{2,18},{10... | collective-permute-start | bytes 172040 | tf_op jit(solution)/shard_map/owner_sends/ppermute | solution.py:498
  30.2 2.3 %collective-permute-start.11 = (bf16[224,128]{1,0:T(8,128)(2,1)S(1)}, bf16[224,128]{1,0:T(8,128)(2,1)S(1)}, u32[]{:S(2)}, u32[]{:S(2)}) collective-permute-start(bf16[224,128]{1,0:T(8,128)(2,1)S(1)} %parent_coeffs.1), channel_id=1, source_target_pairs={{0,24},{8,16},{16,8},{24,0},{1,25},{9,17},{17,9},{25,1},{2,26},{10... | collective-permute-start | bytes 172040 | tf_op jit(solution)/shard_map/owner_sends/ppermute | solution.py:498
  32.5 2.6 %self_blocks.5.refs_0_ = bf16[768,128]{1,0:T(8,128)(2,1)S(1)} custom-call(s32[67]{0:T(128)S(1)} %pad_add_fusion.ids_ref, f32[384,128]{1,0:T(8,128)S(1)} %get-tuple-element.59.field_ref.own_field, f32[384,128]{1,0:T(8,128)S(1)} %get-tuple-element.46.peer_field, bf16[32,256,128]{2,1,0:T(8,128)(2,1)S(1)} %copy-done.1, ...), custom_call_target="tpu_custom_call" | custom-call | bytes 7920000 | tf_op jit(solution)/shard_map/self_blocks/pallas_call | solution.py:487
  35.1 2.6 %self_blocks.6.refs_0_ = bf16[768,128]{1,0:T(8,128)(2,1)S(1)} custom-call(s32[67]{0:T(128)S(1)} %pad_add_fusion.ids_ref, f32[384,128]{1,0:T(8,128)S(1)} %get-tuple-element.59.field_ref.own_field, f32[384,128]{1,0:T(8,128)S(1)} %get-tuple-element.46.peer_field, bf16[32,256,128]{2,1,0:T(8,128)(2,1)S(1)} %copy-done.1, ...), custom_call_target="tpu_custom_call" | custom-call | bytes 7920000 | tf_op jit(solution)/shard_map/self_blocks/pallas_call | solution.py:487
  37.8 1.6 %collective-permute-start.15 = (bf16[896,128]{1,0:T(8,128)(2,1)S(1)}, bf16[896,128]{1,0:T(8,128)(2,1)S(1)}, u32[]{:S(2)}, u32[]{:S(2)}) collective-permute-start(bf16[896,128]{1,0:T(8,128)(2,1)S(1)} %constant_dynamic-update-slice_fusion.block_ref), channel_id=1, source_target_pairs={{0,2},{2,0},{4,6},{6,4},{1,3},{3,1},{5,7},{7,5},{8,10},{10,8},{12,... | collective-permute-start | bytes 688136 | tf_op jit(solution)/shard_map/level_sends/ppermute | solution.py:498
  39.4 1.5 %collective-permute-start.17 = (bf16[896,128]{1,0:T(8,128)(2,1)S(1)}, bf16[896,128]{1,0:T(8,128)(2,1)S(1)}, u32[]{:S(2)}, u32[]{:S(2)}) collective-permute-start(bf16[896,128]{1,0:T(8,128)(2,1)S(1)} %constant_dynamic-update-slice_fusion.block_ref), channel_id=1, source_target_pairs={{0,4},{2,6},{4,0},{6,2},{1,5},{3,7},{5,1},{7,3},{8,12},{10,14},{12... | collective-permute-start | bytes 688136 | tf_op jit(solution)/shard_map/level_sends/ppermute | solution.py:498
  41.4 2.6 %self_blocks.7.keep_ref = f32[768,128]{1,0:T(8,128)S(1)} custom-call(s32[67]{0:T(128)S(1)} %pad_add_fusion.ids_ref, f32[384,128]{1,0:T(8,128)S(1)} %get-tuple-element.59.field_ref.own_field, f32[384,128]{1,0:T(8,128)S(1)} %get-tuple-element.46.peer_field, bf16[32,256,128]{2,1,0:T(8,128)(2,1)S(1)} %copy-done.1, ...), custom_call_target="tpu_custom_call" | custom-call | bytes 7920000 | tf_op jit(solution)/shard_map/self_blocks/pallas_call | solution.py:487
  44.0 1.7 %partner_tables.1 = (bf16[512,512]{1,0:T(8,128)(2,1)S(1)}, bf16[64,64]{1,0:T(8,128)(2,1)S(1)}, bf16[16,256,64]{2,1,0:T(8,128)(2,1)S(1)}) custom-call(s32[4,128]{1,0:T(4,128)S(1)} %select_add_fusion.own_codes, s32[4,128]{1,0:T(4,128)S(1)} %collective-permute-done.12.peer_codes, bf16[64,32,64]{2,1,0:T(8,128)(2,1)S(1)} %bitcast.33, ...), custom_call_target="tpu_custom_call" | custom-call | bytes 4950000 | tf_op jit(solution)/shard_map/partner_tables/pallas_call | solution.py:487
  46.3 2.8 %coupling_products.5 = bf16[992,128]{1,0:T(8,128)(2,1)S(1)} custom-call(bf16[512,512]{1,0:T(8,128)(2,1)S(1)} %get-tuple-element.61.leaf_table, bf16[64,64]{1,0:T(8,128)(2,1)S(1)} %get-tuple-element.62.parent_table, bf16[16,256,64]{2,1,0:T(8,128)(2,1)S(1)} %get-tuple-element.63.pcouple_ref, bf16[896,128]{1,0:T(8,128)(2,1)S(1)} %collective-permute-done.15.block_ref, ...), custom_call_target="tpu_custom_call" | custom-call | bytes 10560000 | tf_op jit(solution)/shard_map/coupling_products/pallas_call | solution.py:487
  49.1 1.6 %collective-permute-start.16 = (bf16[992,128]{1,0:T(8,128)(2,1)S(1)}, bf16[992,128]{1,0:T(8,128)(2,1)S(1)}, u32[]{:S(2)}, u32[]{:S(2)}) collective-permute-start(bf16[992,128]{1,0:T(8,128)(2,1)S(1)} %coupling_products.5), channel_id=1, source_target_pairs={{0,2},{2,0},{4,6},{6,4},{1,3},{3,1},{5,7},{7,5},{8,10},{10,8},{12,... | collective-permute-start | bytes 761864 | tf_op jit(solution)/shard_map/far_sends/ppermute | solution.py:498
  50.7 1.3 %collective-permute-done.17.block_ref = bf16[896,128]{1,0:T(8,128)(2,1)S(1)} collective-permute-done((bf16[896,128]{1,0:T(8,128)(2,1)S(1)}, bf16[896,128]{1,0:T(8,128)(2,1)S(1)}, u32[]{:S(2)}, u32[]{:S(2)}) %collective-permute-start.17) | collective-permute-done | bytes 229408 | tf_op jit(solution)/shard_map/level_sends/ppermute | solution.py:498
  52.0 2.8 %coupling_products.6 = bf16[992,128]{1,0:T(8,128)(2,1)S(1)} custom-call(bf16[512,512]{1,0:T(8,128)(2,1)S(1)} %get-tuple-element.61.leaf_table, bf16[64,64]{1,0:T(8,128)(2,1)S(1)} %get-tuple-element.62.parent_table, bf16[16,256,64]{2,1,0:T(8,128)(2,1)S(1)} %get-tuple-element.63.pcouple_ref, bf16[896,128]{1,0:T(8,128)(2,1)S(1)} %collective-permute-done.17.block_ref, ...), custom_call_target="tpu_custom_call" | custom-call | bytes 10560000 | tf_op jit(solution)/shard_map/coupling_products/pallas_call | solution.py:487
  54.9 1.6 %collective-permute-start.18 = (bf16[992,128]{1,0:T(8,128)(2,1)S(1)}, bf16[992,128]{1,0:T(8,128)(2,1)S(1)}, u32[]{:S(2)}, u32[]{:S(2)}) collective-permute-start(bf16[992,128]{1,0:T(8,128)(2,1)S(1)} %coupling_products.6), channel_id=1, source_target_pairs={{0,4},{2,6},{4,0},{6,2},{1,5},{3,7},{5,1},{7,3},{8,12},{10,14},{12... | collective-permute-start | bytes 761864 | tf_op jit(solution)/shard_map/far_sends/ppermute | solution.py:498
  56.5 2.8 %coupling_products.7 = bf16[992,128]{1,0:T(8,128)(2,1)S(1)} custom-call(bf16[512,512]{1,0:T(8,128)(2,1)S(1)} %get-tuple-element.61.leaf_table, bf16[64,64]{1,0:T(8,128)(2,1)S(1)} %get-tuple-element.62.parent_table, bf16[16,256,64]{2,1,0:T(8,128)(2,1)S(1)} %get-tuple-element.63.pcouple_ref, bf16[896,128]{1,0:T(8,128)(2,1)S(1)} %collective-permute-done.19.block_ref, ...), custom_call_target="tpu_custom_call" | custom-call | bytes 10560000 | tf_op jit(solution)/shard_map/coupling_products/pallas_call | solution.py:487
  59.4 2.8 %coupling_products.4.keep_ref = f32[224,128]{1,0:T(8,128)S(1)} custom-call(bf16[512,512]{1,0:T(8,128)(2,1)S(1)} %get-tuple-element.61.leaf_table, bf16[64,64]{1,0:T(8,128)(2,1)S(1)} %get-tuple-element.62.parent_table, bf16[16,256,64]{2,1,0:T(8,128)(2,1)S(1)} %get-tuple-element.63.pcouple_ref, ...), custom_call_target="tpu_custom_call" | custom-call | bytes 10560000 | tf_op jit(solution)/shard_map/coupling_products/pallas_call | solution.py:487
  62.2 5.4 %collective-permute-done.18.refs_1_ = bf16[992,128]{1,0:T(8,128)(2,1)S(1)} collective-permute-done((bf16[992,128]{1,0:T(8,128)(2,1)S(1)}, bf16[992,128]{1,0:T(8,128)(2,1)S(1)}, u32[]{:S(2)}, u32[]{:S(2)}) %collective-permute-start.18) | collective-permute-done | bytes 253984 | tf_op jit(solution)/shard_map/far_sends/ppermute | solution.py:498
  68.5 1.8 %collective-permute-start.25 = (bf16[192,128]{1,0:T(8,128)(2,1)S(1)}, bf16[192,128]{1,0:T(8,128)(2,1)S(1)}, u32[]{:S(2)}, u32[]{:S(2)}) collective-permute-start(bf16[192,128]{1,0:T(8,128)(2,1)S(1)} %down_products.1.mine_ref), channel_id=1, source_target_pairs={{0,4},{2,6},{4,0},{6,2},{1,5},{3,7},{5,1},{7,3},{8,12},{10,14},{12... | collective-permute-start | bytes 147464 | tf_op jit(solution)/shard_map/far_coeff_sends/ppermute | solution.py:498
  70.3 1.7 %collective-permute-start.27 = (bf16[192,128]{1,0:T(8,128)(2,1)S(1)}, bf16[192,128]{1,0:T(8,128)(2,1)S(1)}, u32[]{:S(2)}, u32[]{:S(2)}) collective-permute-start(bf16[192,128]{1,0:T(8,128)(2,1)S(1)} %down_products.1.mine_ref), channel_id=1, source_target_pairs={{0,6},{2,4},{4,2},{6,0},{1,7},{3,5},{5,3},{7,1},{8,14},{10,12},{12... | collective-permute-start | bytes 147464 | tf_op jit(solution)/shard_map/far_coeff_sends/ppermute | solution.py:498
  73.8 1.5 %collective-permute-done.27.refs_3_ = bf16[192,128]{1,0:T(8,128)(2,1)S(1)} collective-permute-done((bf16[192,128]{1,0:T(8,128)(2,1)S(1)}, bf16[192,128]{1,0:T(8,128)(2,1)S(1)}, u32[]{:S(2)}, u32[]{:S(2)}) %collective-permute-start.27) | collective-permute-done | bytes 49184 | tf_op jit(solution)/shard_map/far_coeff_sends/ppermute | solution.py:498
  76.6 1.8 %column_products.1 = bf16[32,24,128]{2,1,0:T(8,128)(2,1)} custom-call(s32[67]{0:T(128)S(1)} %pad_add_fusion.ids_ref, bf16[64,32,128]{2,1,0:T(8,128)(2,1)S(1)} %copy-done.2, f32[384,128]{1,0:T(8,128)S(1)} %get-tuple-element.67.near_mine, bf16[384,128]{1,0:T(8,128)(2,1)S(1)} %collective-permute-done.22.near_peer, f32[192,128]{1,0:T(8,128)S(1)} %column_products_early.3.refs_0_, ...), custom_call_target="tpu_custom_call" | custom-call | bytes 6105000 | tf_op jit(solution)/shard_map/column_products/pallas_call | solution.py:487
  (84 shorter events, 9.8 us)
Async XLA Ops:
  0.0 22.7 %collective-permute-start.8 = (bf16[32,256,128]{2,1,0:T(8,128)(2,1)}, bf16[32,256,128]{2,1,0:T(8,128)(2,1)}, u32[]{:S(2)}, u32[]{:S(2)}) collective-permute-start(bf16[32,256,128]{2,1,0:T(8,128)(2,1)} %own_ref.9), channel_id=1, source_target_pairs={{0,1},{1,0},{2,3},{3,2},{4,5},{5,4},{6,7},{7,6},{8,9},{9,8},{10,11... | collective-permute-start | bytes 6291464 | tf_op jit(solution)/shard_map/swap_self_blocks/ppermute | solution.py:498
  0.5 11.8 %collective-permute-start.1 = (bf16[32,64,128]{2,1,0:T(8,128)(2,1)}, bf16[32,64,128]{2,1,0:T(8,128)(2,1)S(1)}, u32[]{:S(2)}, u32[]{:S(2)}) collective-permute-start(bf16[32,64,128]{2,1,0:T(8,128)(2,1)} %basis_ref.1), channel_id=1, source_target_pairs={{0,1},{1,0},{2,3},{3,2},{4,5},{5,4},{6,7},{7,6},{8,9},{9,8},{10,11... | collective-permute-start | bytes 1572872 | tf_op jit(solution)/shard_map/swap_row_basis/ppermute | solution.py:498
  3.2 5.7 %collective-permute-start = (bf16[192,128]{1,0:T(8,128)(2,1)S(1)}, bf16[192,128]{1,0:T(8,128)(2,1)S(1)}, u32[]{:S(2)}, u32[]{:S(2)}) collective-permute-start(bf16[192,128]{1,0:T(8,128)(2,1)S(1)} %get-tuple-element.72), channel_id=1, source_target_pairs={{0,8},{8,0},{16,24},{24,16},{1,9},{9,1},{17,25},{25,17},{2,10},{10... | collective-permute-start | bytes 147464 | tf_op jit(solution)/shard_map/regroup_sends/ppermute | solution.py:498
  6.3 6.0 %collective-permute-start.2 = (bf16[192,128]{1,0:T(8,128)(2,1)S(1)}, bf16[192,128]{1,0:T(8,128)(2,1)S(1)}, u32[]{:S(2)}, u32[]{:S(2)}) collective-permute-start(bf16[192,128]{1,0:T(8,128)(2,1)S(1)} %get-tuple-element.70), channel_id=1, source_target_pairs={{0,16},{8,24},{16,0},{24,8},{1,17},{9,25},{17,1},{25,9},{2,18},{10... | collective-permute-start | bytes 147464 | tf_op jit(solution)/shard_map/regroup_sends/ppermute | solution.py:498
  8.9 5.9 %collective-permute-start.3 = (bf16[192,128]{1,0:T(8,128)(2,1)S(1)}, bf16[192,128]{1,0:T(8,128)(2,1)S(1)}, u32[]{:S(2)}, u32[]{:S(2)}) collective-permute-start(bf16[192,128]{1,0:T(8,128)(2,1)S(1)} %get-tuple-element.69), channel_id=1, source_target_pairs={{0,24},{8,16},{16,8},{24,0},{1,25},{9,17},{17,9},{25,1},{2,26},{10... | collective-permute-start | bytes 147464 | tf_op jit(solution)/shard_map/regroup_sends/ppermute | solution.py:498
  12.2 10.4 %copy-start.8 = (s32[1,16,2]{1,2,0:T(2,128)S(1)}, s32[1,16,2]{1,2,0:T(2,128)}, u32[]{:S(2)}) copy-start(s32[1,16,2]{1,2,0:T(2,128)} %param.26) | copy-start | bytes 388
  12.2 10.4 %copy-start.9 = (s32[1,16,2]{1,2,0:T(2,128)S(1)}, s32[1,16,2]{1,2,0:T(2,128)}, u32[]{:S(2)}) copy-start(s32[1,16,2]{1,2,0:T(2,128)} %param.25) | copy-start | bytes 388
  12.2 10.4 %copy-start.10 = (s32[1,128,2]{1,2,0:T(2,128)S(1)}, s32[1,128,2]{1,2,0:T(2,128)}, u32[]{:S(2)}) copy-start(s32[1,128,2]{1,2,0:T(2,128)} %param.24) | copy-start | bytes 3076
  15.2 1.7 %collective-permute-start.4 = (bf16[384,128]{1,0:T(8,128)(2,1)S(1)}, bf16[384,128]{1,0:T(8,128)(2,1)S(1)}, u32[]{:S(2)}, u32[]{:S(2)}) collective-permute-start(bf16[384,128]{1,0:T(8,128)(2,1)S(1)} %get-tuple-element.41), channel_id=1, source_target_pairs={{0,1},{1,0},{2,3},{3,2},{4,5},{5,4},{6,7},{7,6},{8,9},{9,8},{10,11... | collective-permute-start | bytes 294920 | tf_op jit(solution)/shard_map/swap_field/ppermute | solution.py:498
  18.6 27.8 %collective-permute-start.14 = (bf16[2,64,64,128]{3,2,1,0:T(8,128)(2,1)S(1)}, bf16[2,64,64,128]{3,2,1,0:T(8,128)(2,1)}, u32[]{:S(2)}, u32[]{:S(2)}) collective-permute-start(bf16[2,64,64,128]{3,2,1,0:T(8,128)(2,1)S(1)} %bitcast.27), channel_id=1, source_target_pairs={{0,1},{1,0},{2,3},{3,2},{4,5},{5,4},{6,7},{7,6},{8,9},{9,8},{10,11... | collective-permute-start | bytes 6291464 | tf_op jit(solution)/shard_map/swap_coupling/ppermute | solution.py:498
  19.1 8.1 %collective-permute-start.5 = (bf16[192,128]{1,0:T(8,128)(2,1)S(1)}, bf16[192,128]{1,0:T(8,128)(2,1)S(1)}, u32[]{:S(2)}, u32[]{:S(2)}) collective-permute-start(bf16[192,128]{1,0:T(8,128)(2,1)S(1)} %get-tuple-element.43), channel_id=1, source_target_pairs={{0,2},{2,0},{4,6},{6,4},{1,3},{3,1},{5,7},{7,5},{8,10},{10,8},{12,... | collective-permute-start | bytes 147464 | tf_op jit(solution)/shard_map/coeff_sends/ppermute | solution.py:498
  20.6 6.6 %collective-permute-start.6 = (bf16[192,128]{1,0:T(8,128)(2,1)S(1)}, bf16[192,128]{1,0:T(8,128)(2,1)S(1)}, u32[]{:S(2)}, u32[]{:S(2)}) collective-permute-start(bf16[192,128]{1,0:T(8,128)(2,1)S(1)} %get-tuple-element.44), channel_id=1, source_target_pairs={{0,4},{2,6},{4,0},{6,2},{1,5},{3,7},{5,1},{7,3},{8,12},{10,14},{12... | collective-permute-start | bytes 147464 | tf_op jit(solution)/shard_map/coeff_sends/ppermute | solution.py:498
  22.1 5.1 %collective-permute-start.7 = (bf16[192,128]{1,0:T(8,128)(2,1)S(1)}, bf16[192,128]{1,0:T(8,128)(2,1)S(1)}, u32[]{:S(2)}, u32[]{:S(2)}) collective-permute-start(bf16[192,128]{1,0:T(8,128)(2,1)S(1)} %get-tuple-element.45), channel_id=1, source_target_pairs={{0,6},{2,4},{4,2},{6,0},{1,7},{3,5},{5,3},{7,1},{8,14},{10,12},{12... | collective-permute-start | bytes 147464 | tf_op jit(solution)/shard_map/coeff_sends/ppermute | solution.py:498
  28.1 9.7 %collective-permute-start.9 = (bf16[224,128]{1,0:T(8,128)(2,1)S(1)}, bf16[224,128]{1,0:T(8,128)(2,1)S(1)}, u32[]{:S(2)}, u32[]{:S(2)}) collective-permute-start(bf16[224,128]{1,0:T(8,128)(2,1)S(1)} %parent_coeffs.1), channel_id=1, source_target_pairs={{0,8},{8,0},{16,24},{24,16},{1,9},{9,1},{17,25},{25,17},{2,10},{10... | collective-permute-start | bytes 172040 | tf_op jit(solution)/shard_map/owner_sends/ppermute | solution.py:498
  28.1 9.7 %collective-permute-start.10 = (bf16[224,128]{1,0:T(8,128)(2,1)S(1)}, bf16[224,128]{1,0:T(8,128)(2,1)S(1)}, u32[]{:S(2)}, u32[]{:S(2)}) collective-permute-start(bf16[224,128]{1,0:T(8,128)(2,1)S(1)} %parent_coeffs.1), channel_id=1, source_target_pairs={{0,16},{8,24},{16,0},{24,8},{1,17},{9,25},{17,1},{25,9},{2,18},{10... | collective-permute-start | bytes 172040 | tf_op jit(solution)/shard_map/owner_sends/ppermute | solution.py:498
  30.2 7.6 %collective-permute-start.11 = (bf16[224,128]{1,0:T(8,128)(2,1)S(1)}, bf16[224,128]{1,0:T(8,128)(2,1)S(1)}, u32[]{:S(2)}, u32[]{:S(2)}) collective-permute-start(bf16[224,128]{1,0:T(8,128)(2,1)S(1)} %parent_coeffs.1), channel_id=1, source_target_pairs={{0,24},{8,16},{16,8},{24,0},{1,25},{9,17},{17,9},{25,1},{2,26},{10... | collective-permute-start | bytes 172040 | tf_op jit(solution)/shard_map/owner_sends/ppermute | solution.py:498
  32.5 8.9 %collective-permute-start.13 = (bf16[64,32,64]{2,1,0:T(8,128)(2,1)S(1)}, bf16[64,32,64]{2,1,0:T(8,128)(2,1)S(1)}, u32[]{:S(2)}, u32[]{:S(2)}) collective-permute-start(bf16[64,32,64]{2,1,0:T(8,128)(2,1)S(1)} %bitcast.32), channel_id=1, source_target_pairs={{0,1},{1,0},{2,3},{3,2},{4,5},{5,4},{6,7},{7,6},{8,9},{9,8},{10,11... | collective-permute-start | bytes 786440 | tf_op jit(solution)/shard_map/swap_parent_coupling/ppermute | solution.py:498
  37.8 8.5 %collective-permute-start.15 = (bf16[896,128]{1,0:T(8,128)(2,1)S(1)}, bf16[896,128]{1,0:T(8,128)(2,1)S(1)}, u32[]{:S(2)}, u32[]{:S(2)}) collective-permute-start(bf16[896,128]{1,0:T(8,128)(2,1)S(1)} %constant_dynamic-update-slice_fusion.block_ref), channel_id=1, source_target_pairs={{0,2},{2,0},{4,6},{6,4},{1,3},{3,1},{5,7},{7,5},{8,10},{10,8},{12,... | collective-permute-start | bytes 688136 | tf_op jit(solution)/shard_map/level_sends/ppermute | solution.py:498
  39.4 12.6 %collective-permute-start.17 = (bf16[896,128]{1,0:T(8,128)(2,1)S(1)}, bf16[896,128]{1,0:T(8,128)(2,1)S(1)}, u32[]{:S(2)}, u32[]{:S(2)}) collective-permute-start(bf16[896,128]{1,0:T(8,128)(2,1)S(1)} %constant_dynamic-update-slice_fusion.block_ref), channel_id=1, source_target_pairs={{0,4},{2,6},{4,0},{6,2},{1,5},{3,7},{5,1},{7,3},{8,12},{10,14},{12... | collective-permute-start | bytes 688136 | tf_op jit(solution)/shard_map/level_sends/ppermute | solution.py:498
  40.9 15.5 %collective-permute-start.19 = (bf16[896,128]{1,0:T(8,128)(2,1)S(1)}, bf16[896,128]{1,0:T(8,128)(2,1)S(1)}, u32[]{:S(2)}, u32[]{:S(2)}) collective-permute-start(bf16[896,128]{1,0:T(8,128)(2,1)S(1)} %constant_dynamic-update-slice_fusion.block_ref), channel_id=1, source_target_pairs={{0,6},{2,4},{4,2},{6,0},{1,7},{3,5},{5,3},{7,1},{8,14},{10,12},{12... | collective-permute-start | bytes 688136 | tf_op jit(solution)/shard_map/level_sends/ppermute | solution.py:498
  41.4 2.6 %collective-permute-start.12 = (s32[4,128]{1,0:T(4,128)S(1)}, s32[4,128]{1,0:T(4,128)S(1)}, u32[]{:S(2)}, u32[]{:S(2)}) collective-permute-start(s32[4,128]{1,0:T(4,128)S(1)} %select_add_fusion.own_codes), channel_id=1, source_target_pairs={{0,1},{1,0},{2,3},{3,2},{4,5},{5,4},{6,7},{7,6},{8,9},{9,8},{10,11... | collective-permute-start | bytes 6152 | tf_op jit(solution)/shard_map/partner_codes/ppermute | solution.py:498
  49.1 13.1 %collective-permute-start.16 = (bf16[992,128]{1,0:T(8,128)(2,1)S(1)}, bf16[992,128]{1,0:T(8,128)(2,1)S(1)}, u32[]{:S(2)}, u32[]{:S(2)}) collective-permute-start(bf16[992,128]{1,0:T(8,128)(2,1)S(1)} %coupling_products.5), channel_id=1, source_target_pairs={{0,2},{2,0},{4,6},{6,4},{1,3},{3,1},{5,7},{7,5},{8,10},{10,8},{12,... | collective-permute-start | bytes 761864 | tf_op jit(solution)/shard_map/far_sends/ppermute | solution.py:498
  54.9 12.7 %collective-permute-start.18 = (bf16[992,128]{1,0:T(8,128)(2,1)S(1)}, bf16[992,128]{1,0:T(8,128)(2,1)S(1)}, u32[]{:S(2)}, u32[]{:S(2)}) collective-permute-start(bf16[992,128]{1,0:T(8,128)(2,1)S(1)} %coupling_products.6), channel_id=1, source_target_pairs={{0,4},{2,6},{4,0},{6,2},{1,5},{3,7},{5,1},{7,3},{8,12},{10,14},{12... | collective-permute-start | bytes 761864 | tf_op jit(solution)/shard_map/far_sends/ppermute | solution.py:498
  59.3 8.3 %collective-permute-start.20 = (bf16[992,128]{1,0:T(8,128)(2,1)S(1)}, bf16[992,128]{1,0:T(8,128)(2,1)S(1)}, u32[]{:S(2)}, u32[]{:S(2)}) collective-permute-start(bf16[992,128]{1,0:T(8,128)(2,1)S(1)} %coupling_products.7), channel_id=1, source_target_pairs={{0,6},{2,4},{4,2},{6,0},{1,7},{3,5},{5,3},{7,1},{8,14},{10,12},{12... | collective-permute-start | bytes 761864 | tf_op jit(solution)/shard_map/far_sends/ppermute | solution.py:498
  68.4 3.6 %collective-permute-start.21 = (bf16[192,128]{1,0:T(8,128)(2,1)S(1)}, bf16[192,128]{1,0:T(8,128)(2,1)S(1)}, u32[]{:S(2)}, u32[]{:S(2)}) collective-permute-start(bf16[192,128]{1,0:T(8,128)(2,1)S(1)} %down_products.1.mine_ref), channel_id=1, source_target_pairs={{0,1},{1,0},{2,3},{3,2},{4,5},{5,4},{6,7},{7,6},{8,9},{9,8},{10,11... | collective-permute-start | bytes 147464 | tf_op jit(solution)/shard_map/far_coeff_sends/ppermute | solution.py:498
  68.5 4.8 %collective-permute-start.23 = (bf16[192,128]{1,0:T(8,128)(2,1)S(1)}, bf16[192,128]{1,0:T(8,128)(2,1)S(1)}, u32[]{:S(2)}, u32[]{:S(2)}) collective-permute-start(bf16[192,128]{1,0:T(8,128)(2,1)S(1)} %down_products.1.mine_ref), channel_id=1, source_target_pairs={{0,2},{2,0},{4,6},{6,4},{1,3},{3,1},{5,7},{7,5},{8,10},{10,8},{12,... | collective-permute-start | bytes 147464 | tf_op jit(solution)/shard_map/far_coeff_sends/ppermute | solution.py:498
  68.5 5.2 %collective-permute-start.25 = (bf16[192,128]{1,0:T(8,128)(2,1)S(1)}, bf16[192,128]{1,0:T(8,128)(2,1)S(1)}, u32[]{:S(2)}, u32[]{:S(2)}) collective-permute-start(bf16[192,128]{1,0:T(8,128)(2,1)S(1)} %down_products.1.mine_ref), channel_id=1, source_target_pairs={{0,4},{2,6},{4,0},{6,2},{1,5},{3,7},{5,1},{7,3},{8,12},{10,14},{12... | collective-permute-start | bytes 147464 | tf_op jit(solution)/shard_map/far_coeff_sends/ppermute | solution.py:498
  70.3 5.0 %collective-permute-start.27 = (bf16[192,128]{1,0:T(8,128)(2,1)S(1)}, bf16[192,128]{1,0:T(8,128)(2,1)S(1)}, u32[]{:S(2)}, u32[]{:S(2)}) collective-permute-start(bf16[192,128]{1,0:T(8,128)(2,1)S(1)} %down_products.1.mine_ref), channel_id=1, source_target_pairs={{0,6},{2,4},{4,2},{6,0},{1,7},{3,5},{5,3},{7,1},{8,14},{10,12},{12... | collective-permute-start | bytes 147464 | tf_op jit(solution)/shard_map/far_coeff_sends/ppermute | solution.py:498
  73.2 3.4 %collective-permute-start.22 = (bf16[384,128]{1,0:T(8,128)(2,1)S(1)}, bf16[384,128]{1,0:T(8,128)(2,1)S(1)}, u32[]{:S(2)}, u32[]{:S(2)}) collective-permute-start(bf16[384,128]{1,0:T(8,128)(2,1)S(1)} %get-tuple-element.68), channel_id=1, source_target_pairs={{0,1},{1,0},{2,3},{3,2},{4,5},{5,4},{6,7},{7,6},{8,9},{9,8},{10,11... | collective-permute-start | bytes 294920 | tf_op jit(solution)/shard_map/swap_self_sums/ppermute | solution.py:498
  73.3 2.1 %collective-permute-start.24 = (bf16[192,128]{1,0:T(8,128)(2,1)S(1)}, bf16[192,128]{1,0:T(8,128)(2,1)S(1)}, u32[]{:S(2)}, u32[]{:S(2)}) collective-permute-start(bf16[192,128]{1,0:T(8,128)(2,1)S(1)} %collective-permute-done.23.mine_ref), channel_id=1, source_target_pairs={{0,1},{1,0},{2,3},{3,2},{4,5},{5,4},{6,7},{7,6},{8,9},{9,8},{10,11... | collective-permute-start | bytes 147464 | tf_op jit(solution)/shard_map/far_coeff_sends/ppermute | solution.py:498
  73.8 2.1 %collective-permute-start.26 = (bf16[192,128]{1,0:T(8,128)(2,1)S(1)}, bf16[192,128]{1,0:T(8,128)(2,1)S(1)}, u32[]{:S(2)}, u32[]{:S(2)}) collective-permute-start(bf16[192,128]{1,0:T(8,128)(2,1)S(1)} %collective-permute-done.25.mine_ref), channel_id=1, source_target_pairs={{0,1},{1,0},{2,3},{3,2},{4,5},{5,4},{6,7},{7,6},{8,9},{9,8},{10,11... | collective-permute-start | bytes 147464 | tf_op jit(solution)/shard_map/far_coeff_sends/ppermute | solution.py:498
  75.3 1.2 %collective-permute-start.28 = (bf16[192,128]{1,0:T(8,128)(2,1)S(1)}, bf16[192,128]{1,0:T(8,128)(2,1)S(1)}, u32[]{:S(2)}, u32[]{:S(2)}) collective-permute-start(bf16[192,128]{1,0:T(8,128)(2,1)S(1)} %collective-permute-done.27.refs_3_), channel_id=1, source_target_pairs={{0,1},{1,0},{2,3},{3,2},{4,5},{5,4},{6,7},{7,6},{8,9},{9,8},{10,11... | collective-permute-start | bytes 147464 | tf_op jit(solution)/shard_map/far_coeff_sends/ppermute | solution.py:498
  (10 other events, 66.0 us)

commit v3 on v2

--- a/solution.py
+++ b/solution.py
@@ -378,14 +378,14 @@
             out_ref[start : start + slab, :] = accs[n].astype(out_ref.dtype)
 
 
-def near_sum_kernel(skip, ids_ref, keep_ref, *refs):
+def near_sum_kernel(skip, ids_ref, keep_ref, last_ref, *refs):
     recvs, mine_ref, send_ref = refs[:-2], refs[-2], refs[-1]
     count = mine_ref.shape[0]
     parity = ids_ref[2]
 
     def summed(start):
         start = pl.multiple_of(start, 16)
-        total = keep_ref[pl.ds(start, count), :]
+        total = keep_ref[pl.ds(start, count), :] + last_ref[pl.ds(start, count), :].astype(F32)
         for ref in recvs:
             total = total + ref[pl.ds(skip + start, count), :].astype(F32)
         return total
@@ -497,16 +497,23 @@
     def swap(value, axis, count, step):
         return lax.ppermute(value, axis, [(i, i ^ step) for i in range(count)])
 
+    def swaps(values, axis, count, backward=True):
+        order = range(count - 1, 0, -1) if backward else range(1, count)
+        got = {n: swap(values[n], axis, count, n) for n in order}
+        return [got[n] for n in range(1, count)]
+
     def other(value):
         return swap(value, "rep", reps, 1)
 
     with jax.named_scope("swap_row_basis"):
         row_peer = other(row_basis)
+
     with jax.named_scope("swap_parent_coupling"):
         pcouple = jnp.transpose(parent_coupling, (0, 2, 3, 4, 1)).reshape(
             rank_width, pslots * parents, rank_width
         )
         pcouple_peer = other(pcouple)
+
     with jax.named_scope("swap_self_blocks"):
         near_peer_block = other(near_block)
 
@@ -520,7 +527,7 @@
         1.0, scalars=1,
     )
     with jax.named_scope("regroup_sends"):
-        chunks = [packed[0]] + [swap(packed[s], "clus", owners, s) for s in range(1, owners)]
+        chunks = [packed[0]] + swaps([packed[s] for s in range(owners)], "clus", owners, False)
     codes = call(
         "place_codes",
         functools.partial(place_kernel, owners, parents),
@@ -532,7 +539,19 @@
     with jax.named_scope("coupling_layout"):
         couple = jnp.moveaxis(after(coupling, chunks[1])[:, :, 0], 2, 0)
 
-    codes = after(codes, couple, row_peer)
+    with jax.named_scope("partner_codes"):
+        held = lax.optimization_barrier(
+            (partner_owner, partner_local, parent_owner, parent_local, block_count, chunks[1])
+        )
+        group = lvl * reps + parity
+        slot_number = group * slots + jnp.arange(slots, dtype=jnp.int32)[:, None]
+        leaf_code = (held[0][0] ^ me).T * leaves + held[1][0].T
+        leaf_code = jnp.where(slot_number < held[4][None, :], leaf_code, -1)
+        up_code = (held[2][0] ^ me).T * parents + held[3][0].T
+        up_code = jnp.pad(up_code, ((0, 0), (0, leaves - parents)), constant_values=-1)
+        partners = jnp.concatenate([leaf_code, up_code], axis=0)
+        partners_peer = other(partners)
+    codes = after(codes, couple, row_peer, partners_peer)
 
     field, field_send = call(
         "regroup_field",
@@ -560,20 +579,8 @@
     )
     field_peer, keep, sends = outs[0], outs[1], outs[2:]
     with jax.named_scope("coeff_sends"):
-        recvs = [swap(sends[t - 1], "lvl", lvls, t) for t in range(1, lvls)]
-
-    with jax.named_scope("partner_codes"):
-        held = lax.optimization_barrier(
-            (partner_owner, partner_local, parent_owner, parent_local, block_count, keep)
-        )
-        group = lvl * reps + parity
-        slot_number = group * slots + jnp.arange(slots, dtype=jnp.int32)[:, None]
-        leaf_code = (held[0][0] ^ me).T * leaves + held[1][0].T
-        leaf_code = jnp.where(slot_number < held[4][None, :], leaf_code, -1)
-        up_code = (held[2][0] ^ me).T * parents + held[3][0].T
-        up_code = jnp.pad(up_code, ((0, 0), (0, leaves - parents)), constant_values=-1)
-        partners = jnp.concatenate([leaf_code, up_code], axis=0)
-        partners_peer = other(partners)
+        recvs = swaps([None, *sends], "lvl", lvls, True)
+
     with jax.named_scope("swap_coupling"):
         couple_peer = other(after(couple, keep))
 
@@ -592,20 +599,20 @@
         )
 
     near_parts = [None] * lvls
-    near_parts[1] = near_part(1, after(field, field_peer))
-    up_after = after(up_transfer, near_parts[1], partners)
+    near_parts[1] = near_part(1, after(field, keep))
+    up_after = after(up_transfer, near_parts[1])
 
     block_rows = vs * rank_width + len(packs(vs, rank_width, leaves)) * parents
     block = call(
         "parent_coeffs",
         functools.partial(up_kernel, vs, parents),
-        (keep, *recvs, up_after),
+        (keep, *recvs[::-1], up_after),
         sds((block_rows, leaves), BF16),
         [pltpu.VMEM((vs * rank_width, leaves), F32)],
         0.8,
     )
     with jax.named_scope("owner_sends"):
-        blocks = [block] + [swap(block, "clus", owners, s) for s in range(1, owners)]
+        blocks = [block] + swaps([block] * owners, "clus", owners, False)
     later = after(field, block)
     for t in range(2, lvls):
         near_parts[t] = near_part(t, later)
@@ -613,9 +620,10 @@
         blocks = list(lax.optimization_barrier(tuple(blocks) + tuple(near_parts[2:])))[:owners]
         mine = jnp.concatenate(blocks, axis=0)
     with jax.named_scope("level_sends"):
-        alls = [mine] + [swap(mine, "lvl", lvls, t) for t in range(1, lvls)]
-
-    near_parts[0] = near_part(0, after(field, mine))
+        alls = [mine] + swaps([mine] * lvls, "lvl", lvls, False)
+
+    later = after(field, mine)
+    near_parts[0] = near_part(0, later)
     leaf_table, parent_table, pcouple_all = call(
         "partner_tables",
         functools.partial(table_kernel, owners, parents, slots),
@@ -629,8 +637,8 @@
         1.5,
     )
     def far_part(t, block):
-        extras = () if t == 0 else (near_parts[t],)
-        rows = block_rows if t == 0 else block_rows + 2 * vh * slab
+        extras = (near_parts[t],) if 0 < t < lvls - 1 else ()
+        rows = block_rows + (2 * vh * slab if extras else 0)
         return call(
             "coupling_products",
             functools.partial(far_kernel, owners, vs, pslots),
@@ -649,7 +657,10 @@
     alls[1] = after(alls[1], near_parts[0])
     far_parts = [far_part(t, alls[t]) for t in range(lvls)]
     with jax.named_scope("far_sends"):
-        far_recvs = [swap(far_parts[t], "lvl", lvls, t) for t in range(1, lvls)]
+        far_recvs = swaps(far_parts, "lvl", lvls, False)
+    with jax.named_scope("self_sends"):
+        last = lvls - 1
+        near_recv = swap(after(near_parts[last], far_recvs[-1], far_parts[0]), "lvl", lvls, last)
     far = call(
         "down_products",
         functools.partial(down_kernel, vs, parents),
@@ -659,7 +670,7 @@
         0.8,
     )
     with jax.named_scope("far_coeff_sends"):
-        far_blocks = [far] + [swap(far, "lvl", lvls, t) for t in range(1, lvls)]
+        far_blocks = [far] + swaps([far] * lvls, "lvl", lvls, True)
         far_others = [other(value) for value in far_blocks]
     early = lvls - 1
     done = [
@@ -676,7 +687,7 @@
     near_mine, near_send = call(
         "self_sums",
         functools.partial(near_sum_kernel, block_rows),
-        (ids, after(near_parts[0], done[0]), *far_recvs),
+        (ids, after(near_parts[0], done[0]), near_recv, *far_recvs[:-1]),
         [sds((vh * slab, leaves), F32), sds((vh * slab, leaves), BF16)],
         (), 0.65, scalars=1,
     )

time: 78.8 us -> 75 us (0.952)
  waiting for transfers between devices: 11.6 us -> 5.1 us
  starting transfers between devices: 25.8 us -> 28.6 us
  local copies, waits for them, and re-layouts: 4.82 us -> 3.19 us
  other arithmetic: 0.82 us -> 2.21 us
    ppermute x29 -> x30, waiting for transfers between devices: 11.6 us -> 5.1 us  [swap(): return lax.ppermute(value, axis, [(i, i ^ step) for i in range(count)])]
    ppermute x29 -> x30, starting transfers between devices: 25.8 us -> 28.6 us  [swap(): return lax.ppermute(value, axis, [(i, i ^ step) for i in range(count)])]
    unnamed x29 -> x17, local copies, waits for them, and re-layouts: 2.6 us -> 0.99 us
  transfers between devices with their start and end apart: 29 -> 30, of which waited for: 7 -> 10; matrix products, arithmetic and copies ran while one was open for 4% -> 5% of each run, Pallas kernels for 41% -> 43%
where the time goes in v3:
time: 75 us; the launch traced here: 74.7 us
  Pallas kernels  35.3 us (47%)
  starting transfers between devices  28.6 us (38%)
  waiting for transfers between devices  5.1 us (7%)
  local copies, waits for them, and re-layouts  3.19 us (4%)
  other arithmetic  2.21 us (3%)
    pallas_call x21, Pallas kernels, call(): pl.pallas_call(kernel, out_shape=outs, in_specs=specs, out_specs=jax.tree...  35.3 us
    ppermute x30, starting transfers between devices, swap(): return lax.ppermute(value, axis, [(i, i ^ step) for i in range(count)])  28.6 us
    ppermute x30, waiting for transfers between devices, swap(): return lax.ppermute(value, axis, [(i, i ^ step) for i in range(count)])  5.1 us
    optimization_barrier x1, local copies, waits for them, and re-layouts, after(): return lax.optimization_barrier((value,) + others)[0]  2.17 us
  transfers between devices with their start and end apart: 30, of which 10 were waited for; matrix products, arithmetic and copies ran while one was open for 5% of the time, Pallas kernels for 43%

profile of v3, /device:TPU:0, one launch (start us, length us, event | category | flops | bytes accessed | tf_op | source)
XLA Modules:
  0.0 74.7 jit_solution(8320314999135060227)
XLA Ops:
  0.7 0.9 %copy-done.6 = bf16[32,24,128]{2,1,0:T(8,128)(2,1)S(1)} copy-done((bf16[32,24,128]{2,1,0:T(8,128)(2,1)S(1)}, bf16[32,24,128]{2,1,0:T(8,128)(2,1)}, u32[]{:S(2)}) %copy-start.6) | copy-done | bytes 196632
  1.7 1.0 %pack_field.1 = bf16[4,192,128]{2,1,0:T(8,128)(2,1)S(1)} custom-call(s32[67]{0:T(128)S(1)} %pad_add_fusion.ids_ref, bf16[32,24,128]{2,1,0:T(8,128)(2,1)S(1)} %copy-done.6), custom_call_target="tpu_custom_call" | custom-call | bytes 3300000 | tf_op jit(solution)/shard_map/pack_field/pallas_call | solution.py:487
  2.7 3.1 %collective-permute-start = (bf16[192,128]{1,0:T(8,128)(2,1)S(1)}, bf16[192,128]{1,0:T(8,128)(2,1)S(1)}, u32[]{:S(2)}, u32[]{:S(2)}) collective-permute-start(bf16[192,128]{1,0:T(8,128)(2,1)S(1)} %get-tuple-element.74), channel_id=1, source_target_pairs={{0,8},{8,0},{16,24},{24,16},{1,9},{9,1},{17,25},{25,17},{2,10},{10... | collective-permute-start | bytes 147464 | tf_op jit(solution)/shard_map/regroup_sends/ppermute | solution.py:498
  5.8 2.6 %collective-permute-start.3 = (bf16[192,128]{1,0:T(8,128)(2,1)S(1)}, bf16[192,128]{1,0:T(8,128)(2,1)S(1)}, u32[]{:S(2)}, u32[]{:S(2)}) collective-permute-start(bf16[192,128]{1,0:T(8,128)(2,1)S(1)} %get-tuple-element.72), channel_id=1, source_target_pairs={{0,16},{8,24},{16,0},{24,8},{1,17},{9,25},{17,1},{25,9},{2,18},{10... | collective-permute-start | bytes 147464 | tf_op jit(solution)/shard_map/regroup_sends/ppermute | solution.py:498
  9.3 0.8 %compare_select_fusion = s32[2,128]{1,0:T(2,128)S(1)} fusion(s32[1,128,2]{1,2,0:T(2,128)} %param.24, s32[1,128,2]{1,2,0:T(2,128)} %param.23, s32[]{:T(128)} %axis_index.33, s32[128]{0:T(128)} %param.27, s32[2]{0:T(128)S(1)} %iota_add_fusion), kind=kLoop, calls=%fused_computation.11 | loop fusion | flops 1280 | bytes 3596 | tf_op jit(solution)/shard_map/partner_codes/jit(_where)/select_n | solution.py:549
  10.5 1.1 %place_codes.1.code_ref = s32[8,128]{1,0:T(8,128)S(1)} custom-call(s32[67]{0:T(128)S(1)} %pad_add_fusion.ids_ref), custom_call_target="tpu_custom_call" | custom-call | bytes 990000 | tf_op jit(solution)/shard_map/place_codes/pallas_call | solution.py:487
  11.5 2.2 %copy.17 = bf16[64,64,1,2,128]{4,1,0,3,2:T(8,128)(2,1)S(1)} copy(bf16[64,64,1,2,128]{4,3,2,1,0:T(2,128)(2,1)} %param.18) | data formatting | bytes 4194304 | tf_op jit(solution)/shard_map/coupling_layout/optimization_barrier | solution.py:456
  14.7 1.6 %coeffs_own_slab.1.own_ref = f32[768,128]{1,0:T(8,128)S(1)} custom-call(s32[67]{0:T(128)S(1)} %pad_add_fusion.ids_ref, bf16[32,64,128]{2,1,0:T(8,128)(2,1)S(1)} %copy-done.4, f32[384,128]{1,0:T(8,128)S(1)} %get-tuple-element.60.field_ref.own_field), custom_call_target="tpu_custom_call" | custom-call | bytes 5280000 | tf_op jit(solution)/shard_map/coeffs_own_slab/pallas_call | solution.py:487
  16.4 1.7 %coeffs_other_slab.1 = (f32[384,128]{1,0:T(8,128)S(1)}, f32[192,128]{1,0:T(8,128)S(1)}, bf16[192,128]{1,0:T(8,128)(2,1)S(1)}, bf16[192,128]{1,0:T(8,128)(2,1)S(1)}, bf16[192,128]{1,0:T(8,128)(2,1)S(1)}) custom-call(s32[67]{0:T(128)S(1)} %pad_add_fusion.ids_ref, bf16[32,64,128]{2,1,0:T(8,128)(2,1)S(1)} %collective-permute-done.1.basis_ref, ...), custom_call_target="tpu_custom_call" | custom-call | bytes 5280000 | tf_op jit(solution)/shard_map/coeffs_other_slab/pallas_call | solution.py:487
  18.6 2.5 %collective-permute-start.6 = (bf16[192,128]{1,0:T(8,128)(2,1)S(1)}, bf16[192,128]{1,0:T(8,128)(2,1)S(1)}, u32[]{:S(2)}, u32[]{:S(2)}) collective-permute-start(bf16[192,128]{1,0:T(8,128)(2,1)S(1)} %get-tuple-element.49), channel_id=1, source_target_pairs={{0,6},{2,4},{4,2},{6,0},{1,7},{3,5},{5,3},{7,1},{8,14},{10,12},{12... | collective-permute-start | bytes 147464 | tf_op jit(solution)/shard_map/coeff_sends/ppermute | solution.py:498
  22.1 2.6 %self_blocks.4.refs_0_ = bf16[768,128]{1,0:T(8,128)(2,1)S(1)} custom-call(s32[67]{0:T(128)S(1)} %pad_add_fusion.ids_ref, f32[384,128]{1,0:T(8,128)S(1)} %get-tuple-element.60.field_ref.own_field, f32[384,128]{1,0:T(8,128)S(1)} %get-tuple-element.53.peer_field, bf16[32,256,128]{2,1,0:T(8,128)(2,1)S(1)} %copy-done, ...), custom_call_target="tpu_custom_call" | custom-call | bytes 7920000 | tf_op jit(solution)/shard_map/self_blocks/pallas_call | solution.py:487
  25.6 0.8 %parent_coeffs.1 = bf16[224,128]{1,0:T(8,128)(2,1)S(1)} custom-call(f32[192,128]{1,0:T(8,128)S(1)} %get-tuple-element.48.keep_ref, bf16[192,128]{1,0:T(8,128)(2,1)S(1)} %collective-permute-done.6.refs_0_, bf16[192,128]{1,0:T(8,128)(2,1)S(1)} %collective-permute-done.7.refs_1_, bf16[192,128]{1,0:T(8,128)(2,1)S(1)} %collective-permute-done.8.refs_2_, ...), custom_call_target="tpu_custom_call" | custom-call | bytes 2640000 | tf_op jit(solution)/shard_map/parent_coeffs/pallas_call | solution.py:487
  27.0 3.3 %collective-permute-start.11 = (bf16[224,128]{1,0:T(8,128)(2,1)S(1)}, bf16[224,128]{1,0:T(8,128)(2,1)S(1)}, u32[]{:S(2)}, u32[]{:S(2)}) collective-permute-start(bf16[224,128]{1,0:T(8,128)(2,1)S(1)} %parent_coeffs.1), channel_id=1, source_target_pairs={{0,16},{8,24},{16,0},{24,8},{1,17},{9,25},{17,1},{25,9},{2,18},{10... | collective-permute-start | bytes 172040 | tf_op jit(solution)/shard_map/owner_sends/ppermute | solution.py:498
  30.9 2.6 %self_blocks.5.refs_0_ = bf16[768,128]{1,0:T(8,128)(2,1)S(1)} custom-call(s32[67]{0:T(128)S(1)} %pad_add_fusion.ids_ref, f32[384,128]{1,0:T(8,128)S(1)} %get-tuple-element.60.field_ref.own_field, f32[384,128]{1,0:T(8,128)S(1)} %get-tuple-element.53.peer_field, bf16[32,256,128]{2,1,0:T(8,128)(2,1)S(1)} %copy-done, ...), custom_call_target="tpu_custom_call" | custom-call | bytes 7920000 | tf_op jit(solution)/shard_map/self_blocks/pallas_call | solution.py:487
  33.5 2.6 %self_blocks.6 = bf16[768,128]{1,0:T(8,128)(2,1)S(1)} custom-call(s32[67]{0:T(128)S(1)} %pad_add_fusion.ids_ref, f32[384,128]{1,0:T(8,128)S(1)} %get-tuple-element.60.field_ref.own_field, f32[384,128]{1,0:T(8,128)S(1)} %get-tuple-element.53.peer_field, bf16[32,256,128]{2,1,0:T(8,128)(2,1)S(1)} %copy-done, ...), custom_call_target="tpu_custom_call" | custom-call | bytes 7920000 | tf_op jit(solution)/shard_map/self_blocks/pallas_call | solution.py:487
  37.1 1.5 %collective-permute-start.17 = (bf16[896,128]{1,0:T(8,128)(2,1)S(1)}, bf16[896,128]{1,0:T(8,128)(2,1)S(1)}, u32[]{:S(2)}, u32[]{:S(2)}) collective-permute-start(bf16[896,128]{1,0:T(8,128)(2,1)S(1)} %constant_dynamic-update-slice_fusion.block_ref), channel_id=1, source_target_pairs={{0,4},{2,6},{4,0},{6,2},{1,5},{3,7},{5,1},{7,3},{8,12},{10,14},{12... | collective-permute-start | bytes 688136 | tf_op jit(solution)/shard_map/level_sends/ppermute | solution.py:498
  38.6 1.3 %collective-permute-start.19 = (bf16[896,128]{1,0:T(8,128)(2,1)S(1)}, bf16[896,128]{1,0:T(8,128)(2,1)S(1)}, u32[]{:S(2)}, u32[]{:S(2)}) collective-permute-start(bf16[896,128]{1,0:T(8,128)(2,1)S(1)} %constant_dynamic-update-slice_fusion.block_ref), channel_id=1, source_target_pairs={{0,6},{2,4},{4,2},{6,0},{1,7},{3,5},{5,3},{7,1},{8,14},{10,12},{12... | collective-permute-start | bytes 688136 | tf_op jit(solution)/shard_map/level_sends/ppermute | solution.py:498
  40.0 2.6 %self_blocks.7.keep_ref = f32[768,128]{1,0:T(8,128)S(1)} custom-call(s32[67]{0:T(128)S(1)} %pad_add_fusion.ids_ref, f32[384,128]{1,0:T(8,128)S(1)} %get-tuple-element.60.field_ref.own_field, f32[384,128]{1,0:T(8,128)S(1)} %get-tuple-element.53.peer_field, bf16[32,256,128]{2,1,0:T(8,128)(2,1)S(1)} %copy-done, ...), custom_call_target="tpu_custom_call" | custom-call | bytes 7920000 | tf_op jit(solution)/shard_map/self_blocks/pallas_call | solution.py:487
  42.6 1.7 %partner_tables.1 = (bf16[512,512]{1,0:T(8,128)(2,1)S(1)}, bf16[64,64]{1,0:T(8,128)(2,1)S(1)}, bf16[16,256,64]{2,1,0:T(8,128)(2,1)S(1)}) custom-call(s32[4,128]{1,0:T(4,128)S(1)} %select_add_fusion.own_codes, s32[4,128]{1,0:T(4,128)S(1)} %collective-permute-done.2.peer_codes, bf16[64,32,64]{2,1,0:T(8,128)(2,1)S(1)} %bitcast.33, ...), custom_call_target="tpu_custom_call" | custom-call | bytes 4950000 | tf_op jit(solution)/shard_map/partner_tables/pallas_call | solution.py:487
  44.9 3.0 %coupling_products.5 = bf16[992,128]{1,0:T(8,128)(2,1)S(1)} custom-call(bf16[512,512]{1,0:T(8,128)(2,1)S(1)} %get-tuple-element.62.leaf_table, bf16[64,64]{1,0:T(8,128)(2,1)S(1)} %get-tuple-element.63.parent_table, bf16[16,256,64]{2,1,0:T(8,128)(2,1)S(1)} %get-tuple-element.64.pcouple_ref, bf16[896,128]{1,0:T(8,128)(2,1)S(1)} %collective-permute-done.15.block_ref, ...), custom_call_target="tpu_custom_call" | custom-call | bytes 10560000 | tf_op jit(solution)/shard_map/coupling_products/pallas_call | solution.py:487
  48.7 3.0 %coupling_products.6 = bf16[992,128]{1,0:T(8,128)(2,1)S(1)} custom-call(bf16[512,512]{1,0:T(8,128)(2,1)S(1)} %get-tuple-element.62.leaf_table, bf16[64,64]{1,0:T(8,128)(2,1)S(1)} %get-tuple-element.63.parent_table, bf16[16,256,64]{2,1,0:T(8,128)(2,1)S(1)} %get-tuple-element.64.pcouple_ref, bf16[896,128]{1,0:T(8,128)(2,1)S(1)} %collective-permute-done.17.block_ref, ...), custom_call_target="tpu_custom_call" | custom-call | bytes 10560000 | tf_op jit(solution)/shard_map/coupling_products/pallas_call | solution.py:487
  51.6 2.5 %collective-permute-start.18 = (bf16[992,128]{1,0:T(8,128)(2,1)S(1)}, bf16[992,128]{1,0:T(8,128)(2,1)S(1)}, u32[]{:S(2)}, u32[]{:S(2)}) collective-permute-start(bf16[992,128]{1,0:T(8,128)(2,1)S(1)} %coupling_products.6), channel_id=1, source_target_pairs={{0,4},{2,6},{4,0},{6,2},{1,5},{3,7},{5,1},{7,3},{8,12},{10,14},{12... | collective-permute-start | bytes 761864 | tf_op jit(solution)/shard_map/far_sends/ppermute | solution.py:498
  54.1 3.0 %coupling_products.7 = bf16[224,128]{1,0:T(8,128)(2,1)S(1)} custom-call(bf16[512,512]{1,0:T(8,128)(2,1)S(1)} %get-tuple-element.62.leaf_table, bf16[64,64]{1,0:T(8,128)(2,1)S(1)} %get-tuple-element.63.parent_table, bf16[16,256,64]{2,1,0:T(8,128)(2,1)S(1)} %get-tuple-element.64.pcouple_ref, bf16[896,128]{1,0:T(8,128)(2,1)S(1)} %collective-permute-done.19.block_ref, ...), custom_call_target="tpu_custom_call" | custom-call | bytes 10560000 | tf_op jit(solution)/shard_map/coupling_products/pallas_call | solution.py:487
  57.1 1.4 %collective-permute-start.20 = (bf16[224,128]{1,0:T(8,128)(2,1)S(1)}, bf16[224,128]{1,0:T(8,128)(2,1)S(1)}, u32[]{:S(2)}, u32[]{:S(2)}) collective-permute-start(bf16[224,128]{1,0:T(8,128)(2,1)S(1)} %coupling_products.7), channel_id=1, source_target_pairs={{0,6},{2,4},{4,2},{6,0},{1,7},{3,5},{5,3},{7,1},{8,14},{10,12},{12... | collective-permute-start | bytes 172040 | tf_op jit(solution)/shard_map/far_sends/ppermute | solution.py:498
  58.5 3.0 %coupling_products.4.keep_ref = f32[224,128]{1,0:T(8,128)S(1)} custom-call(bf16[512,512]{1,0:T(8,128)(2,1)S(1)} %get-tuple-element.62.leaf_table, bf16[64,64]{1,0:T(8,128)(2,1)S(1)} %get-tuple-element.63.parent_table, bf16[16,256,64]{2,1,0:T(8,128)(2,1)S(1)} %get-tuple-element.64.pcouple_ref, ...), custom_call_target="tpu_custom_call" | custom-call | bytes 10560000 | tf_op jit(solution)/shard_map/coupling_products/pallas_call | solution.py:487
  62.3 1.3 %collective-permute-start.22 = (bf16[768,128]{1,0:T(8,128)(2,1)S(1)}, bf16[768,128]{1,0:T(8,128)(2,1)S(1)}, u32[]{:S(2)}, u32[]{:S(2)}) collective-permute-start(bf16[768,128]{1,0:T(8,128)(2,1)S(1)} %self_blocks.6), channel_id=1, source_target_pairs={{0,6},{2,4},{4,2},{6,0},{1,7},{3,5},{5,3},{7,1},{8,14},{10,12},{12... | collective-permute-start | bytes 589832 | tf_op jit(solution)/shard_map/self_sends/ppermute | solution.py:498
  63.6 0.8 %down_products.1.mine_ref = bf16[192,128]{1,0:T(8,128)(2,1)S(1)} custom-call(f32[224,128]{1,0:T(8,128)S(1)} %coupling_products.4.keep_ref, bf16[992,128]{1,0:T(8,128)(2,1)S(1)} %collective-permute-done.16.refs_0_, bf16[992,128]{1,0:T(8,128)(2,1)S(1)} %collective-permute-done.18.refs_1_, bf16[224,128]{1,0:T(8,128)(2,1)S(1)} %collective-permute-done.20.refs_2_, ...), custom_call_target="tpu_custom_call" | custom-call | bytes 2640000 | tf_op jit(solution)/shard_map/down_products/pallas_call | solution.py:487
  64.5 1.0 %collective-permute-start.24 = (bf16[192,128]{1,0:T(8,128)(2,1)S(1)}, bf16[192,128]{1,0:T(8,128)(2,1)S(1)}, u32[]{:S(2)}, u32[]{:S(2)}) collective-permute-start(bf16[192,128]{1,0:T(8,128)(2,1)S(1)} %down_products.1.mine_ref), channel_id=1, source_target_pairs={{0,2},{2,0},{4,6},{6,4},{1,3},{3,1},{5,7},{7,5},{8,10},{10,8},{12,... | collective-permute-start | bytes 147464 | tf_op jit(solution)/shard_map/far_coeff_sends/ppermute | solution.py:498
  65.5 1.2 %collective-permute-start.26 = (bf16[192,128]{1,0:T(8,128)(2,1)S(1)}, bf16[192,128]{1,0:T(8,128)(2,1)S(1)}, u32[]{:S(2)}, u32[]{:S(2)}) collective-permute-start(bf16[192,128]{1,0:T(8,128)(2,1)S(1)} %down_products.1.mine_ref), channel_id=1, source_target_pairs={{0,4},{2,6},{4,0},{6,2},{1,5},{3,7},{5,1},{7,3},{8,12},{10,14},{12... | collective-permute-start | bytes 147464 | tf_op jit(solution)/shard_map/far_coeff_sends/ppermute | solution.py:498
  66.7 1.3 %collective-permute-start.28 = (bf16[192,128]{1,0:T(8,128)(2,1)S(1)}, bf16[192,128]{1,0:T(8,128)(2,1)S(1)}, u32[]{:S(2)}, u32[]{:S(2)}) collective-permute-start(bf16[192,128]{1,0:T(8,128)(2,1)S(1)} %down_products.1.mine_ref), channel_id=1, source_target_pairs={{0,6},{2,4},{4,2},{6,0},{1,7},{3,5},{5,3},{7,1},{8,14},{10,12},{12... | collective-permute-start | bytes 147464 | tf_op jit(solution)/shard_map/far_coeff_sends/ppermute | solution.py:498
  70.4 1.3 %collective-permute-done.28.refs_3_ = bf16[192,128]{1,0:T(8,128)(2,1)S(1)} collective-permute-done((bf16[192,128]{1,0:T(8,128)(2,1)S(1)}, bf16[192,128]{1,0:T(8,128)(2,1)S(1)}, u32[]{:S(2)}, u32[]{:S(2)}) %collective-permute-start.28) | collective-permute-done | bytes 49184 | tf_op jit(solution)/shard_map/far_coeff_sends/ppermute | solution.py:498
  72.9 1.8 %column_products.1 = bf16[32,24,128]{2,1,0:T(8,128)(2,1)} custom-call(s32[67]{0:T(128)S(1)} %pad_add_fusion.ids_ref, bf16[64,32,128]{2,1,0:T(8,128)(2,1)S(1)} %copy-done.1, f32[384,128]{1,0:T(8,128)S(1)} %get-tuple-element.69.near_mine, bf16[384,128]{1,0:T(8,128)(2,1)S(1)} %collective-permute-done.23.near_peer, f32[192,128]{1,0:T(8,128)S(1)} %column_products_early.3.refs_0_, ...), custom_call_target="tpu_custom_call" | custom-call | bytes 6105000 | tf_op jit(solution)/shard_map/column_products/pallas_call | solution.py:487
  (74 shorter events, 13.3 us)
Async XLA Ops:
  2.7 5.9 %collective-permute-start = (bf16[192,128]{1,0:T(8,128)(2,1)S(1)}, bf16[192,128]{1,0:T(8,128)(2,1)S(1)}, u32[]{:S(2)}, u32[]{:S(2)}) collective-permute-start(bf16[192,128]{1,0:T(8,128)(2,1)S(1)} %get-tuple-element.74), channel_id=1, source_target_pairs={{0,8},{8,0},{16,24},{24,16},{1,9},{9,1},{17,25},{25,17},{2,10},{10... | collective-permute-start | bytes 147464 | tf_op jit(solution)/shard_map/regroup_sends/ppermute | solution.py:498
  5.8 7.9 %collective-permute-start.1 = (bf16[32,64,128]{2,1,0:T(8,128)(2,1)}, bf16[32,64,128]{2,1,0:T(8,128)(2,1)S(1)}, u32[]{:S(2)}, u32[]{:S(2)}) collective-permute-start(bf16[32,64,128]{2,1,0:T(8,128)(2,1)} %basis_ref.1), channel_id=1, source_target_pairs={{0,1},{1,0},{2,3},{3,2},{4,5},{5,4},{6,7},{7,6},{8,9},{9,8},{10,11... | collective-permute-start | bytes 1572872 | tf_op jit(solution)/shard_map/swap_row_basis/ppermute | solution.py:498
  5.8 7.9 %collective-permute-start.3 = (bf16[192,128]{1,0:T(8,128)(2,1)S(1)}, bf16[192,128]{1,0:T(8,128)(2,1)S(1)}, u32[]{:S(2)}, u32[]{:S(2)}) collective-permute-start(bf16[192,128]{1,0:T(8,128)(2,1)S(1)} %get-tuple-element.72), channel_id=1, source_target_pairs={{0,16},{8,24},{16,0},{24,8},{1,17},{9,25},{17,1},{25,9},{2,18},{10... | collective-permute-start | bytes 147464 | tf_op jit(solution)/shard_map/regroup_sends/ppermute | solution.py:498
  8.4 5.9 %collective-permute-start.4 = (bf16[192,128]{1,0:T(8,128)(2,1)S(1)}, bf16[192,128]{1,0:T(8,128)(2,1)S(1)}, u32[]{:S(2)}, u32[]{:S(2)}) collective-permute-start(bf16[192,128]{1,0:T(8,128)(2,1)S(1)} %get-tuple-element.71), channel_id=1, source_target_pairs={{0,24},{8,16},{16,8},{24,0},{1,25},{9,17},{17,9},{25,1},{2,26},{10... | collective-permute-start | bytes 147464 | tf_op jit(solution)/shard_map/regroup_sends/ppermute | solution.py:498
  8.4 13.7 %collective-permute-start.9 = (bf16[32,256,128]{2,1,0:T(8,128)(2,1)}, bf16[32,256,128]{2,1,0:T(8,128)(2,1)S(1)}, u32[]{:S(2)}, u32[]{:S(2)}) collective-permute-start(bf16[32,256,128]{2,1,0:T(8,128)(2,1)} %own_ref.9), channel_id=1, source_target_pairs={{0,1},{1,0},{2,3},{3,2},{4,5},{5,4},{6,7},{7,6},{8,9},{9,8},{10,11... | collective-permute-start | bytes 6291464 | tf_op jit(solution)/shard_map/swap_self_blocks/ppermute | solution.py:498
  10.1 3.6 %collective-permute-start.2 = (s32[4,128]{1,0:T(4,128)S(1)}, s32[4,128]{1,0:T(4,128)S(1)}, u32[]{:S(2)}, u32[]{:S(2)}) collective-permute-start(s32[4,128]{1,0:T(4,128)S(1)} %select_add_fusion.own_codes), channel_id=1, source_target_pairs={{0,1},{1,0},{2,3},{3,2},{4,5},{5,4},{6,7},{7,6},{8,9},{9,8},{10,11... | collective-permute-start | bytes 6152 | tf_op jit(solution)/shard_map/partner_codes/ppermute | solution.py:498
  13.7 8.4 %copy-start = (bf16[32,256,128]{2,1,0:T(8,128)(2,1)S(1)}, bf16[32,256,128]{2,1,0:T(8,128)(2,1)}, u32[]{:S(2)}) copy-start(bf16[32,256,128]{2,1,0:T(8,128)(2,1)} %own_ref.9) | copy-start | bytes 6291460
  14.7 1.7 %collective-permute-start.5 = (bf16[384,128]{1,0:T(8,128)(2,1)S(1)}, bf16[384,128]{1,0:T(8,128)(2,1)S(1)}, u32[]{:S(2)}, u32[]{:S(2)}) collective-permute-start(bf16[384,128]{1,0:T(8,128)(2,1)S(1)} %get-tuple-element.47), channel_id=1, source_target_pairs={{0,1},{1,0},{2,3},{3,2},{4,5},{5,4},{6,7},{7,6},{8,9},{9,8},{10,11... | collective-permute-start | bytes 294920 | tf_op jit(solution)/shard_map/swap_field/ppermute | solution.py:498
  18.0 26.8 %collective-permute-start.14 = (bf16[2,64,64,128]{3,2,1,0:T(8,128)(2,1)S(1)}, bf16[2,64,64,128]{3,2,1,0:T(8,128)(2,1)S(1)}, u32[]{:S(2)}, u32[]{:S(2)}) collective-permute-start(bf16[2,64,64,128]{3,2,1,0:T(8,128)(2,1)S(1)} %bitcast.27), channel_id=1, source_target_pairs={{0,1},{1,0},{2,3},{3,2},{4,5},{5,4},{6,7},{7,6},{8,9},{9,8},{10,11... | collective-permute-start | bytes 6291464 | tf_op jit(solution)/shard_map/swap_coupling/ppermute | solution.py:498
  18.6 6.1 %collective-permute-start.6 = (bf16[192,128]{1,0:T(8,128)(2,1)S(1)}, bf16[192,128]{1,0:T(8,128)(2,1)S(1)}, u32[]{:S(2)}, u32[]{:S(2)}) collective-permute-start(bf16[192,128]{1,0:T(8,128)(2,1)S(1)} %get-tuple-element.49), channel_id=1, source_target_pairs={{0,6},{2,4},{4,2},{6,0},{1,7},{3,5},{5,3},{7,1},{8,14},{10,12},{12... | collective-permute-start | bytes 147464 | tf_op jit(solution)/shard_map/coeff_sends/ppermute | solution.py:498
  21.0 4.1 %collective-permute-start.7 = (bf16[192,128]{1,0:T(8,128)(2,1)S(1)}, bf16[192,128]{1,0:T(8,128)(2,1)S(1)}, u32[]{:S(2)}, u32[]{:S(2)}) collective-permute-start(bf16[192,128]{1,0:T(8,128)(2,1)S(1)} %get-tuple-element.50), channel_id=1, source_target_pairs={{0,4},{2,6},{4,0},{6,2},{1,5},{3,7},{5,1},{7,3},{8,12},{10,14},{12... | collective-permute-start | bytes 147464 | tf_op jit(solution)/shard_map/coeff_sends/ppermute | solution.py:498
  21.6 4.1 %collective-permute-start.8 = (bf16[192,128]{1,0:T(8,128)(2,1)S(1)}, bf16[192,128]{1,0:T(8,128)(2,1)S(1)}, u32[]{:S(2)}, u32[]{:S(2)}) collective-permute-start(bf16[192,128]{1,0:T(8,128)(2,1)S(1)} %get-tuple-element.51), channel_id=1, source_target_pairs={{0,2},{2,0},{4,6},{6,4},{1,3},{3,1},{5,7},{7,5},{8,10},{10,8},{12,... | collective-permute-start | bytes 147464 | tf_op jit(solution)/shard_map/coeff_sends/ppermute | solution.py:498
  22.1 8.8 %copy-start.5 = (bf16[64,64,1,2,16]{1,4,3,2,0:T(8,128)(2,1)S(1)}, bf16[64,64,1,2,16]{1,4,3,2,0:T(8,128)(2,1)}, u32[]{:S(2)}) copy-start(bf16[64,64,1,2,16]{1,4,3,2,0:T(8,128)(2,1)} %param.19) | copy-start | bytes 786436
  26.4 9.7 %collective-permute-start.10 = (bf16[224,128]{1,0:T(8,128)(2,1)S(1)}, bf16[224,128]{1,0:T(8,128)(2,1)S(1)}, u32[]{:S(2)}, u32[]{:S(2)}) collective-permute-start(bf16[224,128]{1,0:T(8,128)(2,1)S(1)} %parent_coeffs.1), channel_id=1, source_target_pairs={{0,8},{8,0},{16,24},{24,16},{1,9},{9,1},{17,25},{25,17},{2,10},{10... | collective-permute-start | bytes 172040 | tf_op jit(solution)/shard_map/owner_sends/ppermute | solution.py:498
  27.0 9.1 %collective-permute-start.11 = (bf16[224,128]{1,0:T(8,128)(2,1)S(1)}, bf16[224,128]{1,0:T(8,128)(2,1)S(1)}, u32[]{:S(2)}, u32[]{:S(2)}) collective-permute-start(bf16[224,128]{1,0:T(8,128)(2,1)S(1)} %parent_coeffs.1), channel_id=1, source_target_pairs={{0,16},{8,24},{16,0},{24,8},{1,17},{9,25},{17,1},{25,9},{2,18},{10... | collective-permute-start | bytes 172040 | tf_op jit(solution)/shard_map/owner_sends/ppermute | solution.py:498
  30.4 6.0 %collective-permute-start.12 = (bf16[224,128]{1,0:T(8,128)(2,1)S(1)}, bf16[224,128]{1,0:T(8,128)(2,1)S(1)}, u32[]{:S(2)}, u32[]{:S(2)}) collective-permute-start(bf16[224,128]{1,0:T(8,128)(2,1)S(1)} %parent_coeffs.1), channel_id=1, source_target_pairs={{0,24},{8,16},{16,8},{24,0},{1,25},{9,17},{17,9},{25,1},{2,26},{10... | collective-permute-start | bytes 172040 | tf_op jit(solution)/shard_map/owner_sends/ppermute | solution.py:498
  30.9 11.7 %collective-permute-start.13 = (bf16[64,32,64]{2,1,0:T(8,128)(2,1)S(1)}, bf16[64,32,64]{2,1,0:T(8,128)(2,1)S(1)}, u32[]{:S(2)}, u32[]{:S(2)}) collective-permute-start(bf16[64,32,64]{2,1,0:T(8,128)(2,1)S(1)} %bitcast.32), channel_id=1, source_target_pairs={{0,1},{1,0},{2,3},{3,2},{4,5},{5,4},{6,7},{7,6},{8,9},{9,8},{10,11... | collective-permute-start | bytes 786440 | tf_op jit(solution)/shard_map/swap_parent_coupling/ppermute | solution.py:498
  36.4 8.5 %collective-permute-start.15 = (bf16[896,128]{1,0:T(8,128)(2,1)S(1)}, bf16[896,128]{1,0:T(8,128)(2,1)S(1)}, u32[]{:S(2)}, u32[]{:S(2)}) collective-permute-start(bf16[896,128]{1,0:T(8,128)(2,1)S(1)} %constant_dynamic-update-slice_fusion.block_ref), channel_id=1, source_target_pairs={{0,2},{2,0},{4,6},{6,4},{1,3},{3,1},{5,7},{7,5},{8,10},{10,8},{12,... | collective-permute-start | bytes 688136 | tf_op jit(solution)/shard_map/level_sends/ppermute | solution.py:498
  37.1 11.6 %collective-permute-start.17 = (bf16[896,128]{1,0:T(8,128)(2,1)S(1)}, bf16[896,128]{1,0:T(8,128)(2,1)S(1)}, u32[]{:S(2)}, u32[]{:S(2)}) collective-permute-start(bf16[896,128]{1,0:T(8,128)(2,1)S(1)} %constant_dynamic-update-slice_fusion.block_ref), channel_id=1, source_target_pairs={{0,4},{2,6},{4,0},{6,2},{1,5},{3,7},{5,1},{7,3},{8,12},{10,14},{12... | collective-permute-start | bytes 688136 | tf_op jit(solution)/shard_map/level_sends/ppermute | solution.py:498
  38.6 15.5 %collective-permute-start.19 = (bf16[896,128]{1,0:T(8,128)(2,1)S(1)}, bf16[896,128]{1,0:T(8,128)(2,1)S(1)}, u32[]{:S(2)}, u32[]{:S(2)}) collective-permute-start(bf16[896,128]{1,0:T(8,128)(2,1)S(1)} %constant_dynamic-update-slice_fusion.block_ref), channel_id=1, source_target_pairs={{0,6},{2,4},{4,2},{6,0},{1,7},{3,5},{5,3},{7,1},{8,14},{10,12},{12... | collective-permute-start | bytes 688136 | tf_op jit(solution)/shard_map/level_sends/ppermute | solution.py:498
  47.9 15.8 %collective-permute-start.16 = (bf16[992,128]{1,0:T(8,128)(2,1)S(1)}, bf16[992,128]{1,0:T(8,128)(2,1)S(1)}, u32[]{:S(2)}, u32[]{:S(2)}) collective-permute-start(bf16[992,128]{1,0:T(8,128)(2,1)S(1)} %coupling_products.5), channel_id=1, source_target_pairs={{0,2},{2,0},{4,6},{6,4},{1,3},{3,1},{5,7},{7,5},{8,10},{10,8},{12,... | collective-permute-start | bytes 761864 | tf_op jit(solution)/shard_map/far_sends/ppermute | solution.py:498
  51.6 12.0 %collective-permute-start.18 = (bf16[992,128]{1,0:T(8,128)(2,1)S(1)}, bf16[992,128]{1,0:T(8,128)(2,1)S(1)}, u32[]{:S(2)}, u32[]{:S(2)}) collective-permute-start(bf16[992,128]{1,0:T(8,128)(2,1)S(1)} %coupling_products.6), channel_id=1, source_target_pairs={{0,4},{2,6},{4,0},{6,2},{1,5},{3,7},{5,1},{7,3},{8,12},{10,14},{12... | collective-permute-start | bytes 761864 | tf_op jit(solution)/shard_map/far_sends/ppermute | solution.py:498
  57.1 5.1 %collective-permute-start.20 = (bf16[224,128]{1,0:T(8,128)(2,1)S(1)}, bf16[224,128]{1,0:T(8,128)(2,1)S(1)}, u32[]{:S(2)}, u32[]{:S(2)}) collective-permute-start(bf16[224,128]{1,0:T(8,128)(2,1)S(1)} %coupling_products.7), channel_id=1, source_target_pairs={{0,6},{2,4},{4,2},{6,0},{1,7},{3,5},{5,3},{7,1},{8,14},{10,12},{12... | collective-permute-start | bytes 172040 | tf_op jit(solution)/shard_map/far_sends/ppermute | solution.py:498
  62.3 6.8 %collective-permute-start.22 = (bf16[768,128]{1,0:T(8,128)(2,1)S(1)}, bf16[768,128]{1,0:T(8,128)(2,1)S(1)}, u32[]{:S(2)}, u32[]{:S(2)}) collective-permute-start(bf16[768,128]{1,0:T(8,128)(2,1)S(1)} %self_blocks.6), channel_id=1, source_target_pairs={{0,6},{2,4},{4,2},{6,0},{1,7},{3,5},{5,3},{7,1},{8,14},{10,12},{12... | collective-permute-start | bytes 589832 | tf_op jit(solution)/shard_map/self_sends/ppermute | solution.py:498
  64.4 3.6 %collective-permute-start.21 = (bf16[192,128]{1,0:T(8,128)(2,1)S(1)}, bf16[192,128]{1,0:T(8,128)(2,1)S(1)}, u32[]{:S(2)}, u32[]{:S(2)}) collective-permute-start(bf16[192,128]{1,0:T(8,128)(2,1)S(1)} %down_products.1.mine_ref), channel_id=1, source_target_pairs={{0,1},{1,0},{2,3},{3,2},{4,5},{5,4},{6,7},{7,6},{8,9},{9,8},{10,11... | collective-permute-start | bytes 147464 | tf_op jit(solution)/shard_map/far_coeff_sends/ppermute | solution.py:498
  64.5 5.3 %collective-permute-start.24 = (bf16[192,128]{1,0:T(8,128)(2,1)S(1)}, bf16[192,128]{1,0:T(8,128)(2,1)S(1)}, u32[]{:S(2)}, u32[]{:S(2)}) collective-permute-start(bf16[192,128]{1,0:T(8,128)(2,1)S(1)} %down_products.1.mine_ref), channel_id=1, source_target_pairs={{0,2},{2,0},{4,6},{6,4},{1,3},{3,1},{5,7},{7,5},{8,10},{10,8},{12,... | collective-permute-start | bytes 147464 | tf_op jit(solution)/shard_map/far_coeff_sends/ppermute | solution.py:498
  65.5 4.8 %collective-permute-start.26 = (bf16[192,128]{1,0:T(8,128)(2,1)S(1)}, bf16[192,128]{1,0:T(8,128)(2,1)S(1)}, u32[]{:S(2)}, u32[]{:S(2)}) collective-permute-start(bf16[192,128]{1,0:T(8,128)(2,1)S(1)} %down_products.1.mine_ref), channel_id=1, source_target_pairs={{0,4},{2,6},{4,0},{6,2},{1,5},{3,7},{5,1},{7,3},{8,12},{10,14},{12... | collective-permute-start | bytes 147464 | tf_op jit(solution)/shard_map/far_coeff_sends/ppermute | solution.py:498
  66.7 5.0 %collective-permute-start.28 = (bf16[192,128]{1,0:T(8,128)(2,1)S(1)}, bf16[192,128]{1,0:T(8,128)(2,1)S(1)}, u32[]{:S(2)}, u32[]{:S(2)}) collective-permute-start(bf16[192,128]{1,0:T(8,128)(2,1)S(1)} %down_products.1.mine_ref), channel_id=1, source_target_pairs={{0,6},{2,4},{4,2},{6,0},{1,7},{3,5},{5,3},{7,1},{8,14},{10,12},{12... | collective-permute-start | bytes 147464 | tf_op jit(solution)/shard_map/far_coeff_sends/ppermute | solution.py:498
  69.7 3.2 %collective-permute-start.23 = (bf16[384,128]{1,0:T(8,128)(2,1)S(1)}, bf16[384,128]{1,0:T(8,128)(2,1)S(1)}, u32[]{:S(2)}, u32[]{:S(2)}) collective-permute-start(bf16[384,128]{1,0:T(8,128)(2,1)S(1)} %get-tuple-element.70), channel_id=1, source_target_pairs={{0,1},{1,0},{2,3},{3,2},{4,5},{5,4},{6,7},{7,6},{8,9},{9,8},{10,11... | collective-permute-start | bytes 294920 | tf_op jit(solution)/shard_map/swap_self_sums/ppermute | solution.py:498
  69.8 1.9 %collective-permute-start.25 = (bf16[192,128]{1,0:T(8,128)(2,1)S(1)}, bf16[192,128]{1,0:T(8,128)(2,1)S(1)}, u32[]{:S(2)}, u32[]{:S(2)}) collective-permute-start(bf16[192,128]{1,0:T(8,128)(2,1)S(1)} %collective-permute-done.24.mine_ref), channel_id=1, source_target_pairs={{0,1},{1,0},{2,3},{3,2},{4,5},{5,4},{6,7},{7,6},{8,9},{9,8},{10,11... | collective-permute-start | bytes 147464 | tf_op jit(solution)/shard_map/far_coeff_sends/ppermute | solution.py:498
  70.3 1.9 %collective-permute-start.27 = (bf16[192,128]{1,0:T(8,128)(2,1)S(1)}, bf16[192,128]{1,0:T(8,128)(2,1)S(1)}, u32[]{:S(2)}, u32[]{:S(2)}) collective-permute-start(bf16[192,128]{1,0:T(8,128)(2,1)S(1)} %collective-permute-done.26.mine_ref), channel_id=1, source_target_pairs={{0,1},{1,0},{2,3},{3,2},{4,5},{5,4},{6,7},{7,6},{8,9},{9,8},{10,11... | collective-permute-start | bytes 147464 | tf_op jit(solution)/shard_map/far_coeff_sends/ppermute | solution.py:498
  71.7 1.2 %collective-permute-start.29 = (bf16[192,128]{1,0:T(8,128)(2,1)S(1)}, bf16[192,128]{1,0:T(8,128)(2,1)S(1)}, u32[]{:S(2)}, u32[]{:S(2)}) collective-permute-start(bf16[192,128]{1,0:T(8,128)(2,1)S(1)} %collective-permute-done.28.refs_3_), channel_id=1, source_target_pairs={{0,1},{1,0},{2,3},{3,2},{4,5},{5,4},{6,7},{7,6},{8,9},{9,8},{10,11... | collective-permute-start | bytes 147464 | tf_op jit(solution)/shard_map/far_coeff_sends/ppermute | solution.py:498
  (5 other events, 20.7 us)

commit v4 on v3

--- a/solution.py
+++ b/solution.py
@@ -44,8 +44,19 @@
     return lax.fori_loop(0, total_steps, body, tuple(accs), unroll=unroll)
 
 
-def pack_kernel(owners, vh, parents, ids_ref, own_ref, out_ref, rows_scr):
+def pack_kernel(
+    owners, vh, parents, ids_ref, perm_any, own_any, out_ref, rows_scr, perm_ref, own_ref, sems
+):
     slab, vectors, leaves = own_ref.shape
+    perm_copy = pltpu.make_async_copy(perm_any, perm_ref, sems.at[0])
+    perm_copy.start()
+    copies = []
+    for c in range(4):
+        part = slice(c * slab // 4, (c + 1) * slab // 4)
+        copies.append(
+            pltpu.make_async_copy(own_any.at[part], own_ref.at[part], sems.at[1 + c])
+        )
+        copies[-1].start()
     children = leaves // parents
     reps = vectors // vh
     width = leaves // owners
@@ -56,14 +67,17 @@
     target = row % children
     bits = 32 // owners
     counts = jnp.int32(0)
+    perm_copy.wait()
     for parent in range(parents):
-        owner = ids_ref[3 + me * parents + parent] // parents
+        owner = perm_ref[me * parents + parent] // parents
         shift = owner * bits
         rank = lax.shift_right_logical(counts, shift) & ((1 << bits) - 1)
         counts = counts + lax.shift_left(jnp.int32(1), shift)
         code = (owner ^ me) * leaves + rank * children
         target = target + jnp.where(parent_of_row == parent, code, 0)
     part = (slab // owners) * vh
+    for copy in copies:
+        copy.wait()
     rows_scr[...] = own_ref[...].reshape(slab * vectors, leaves).astype(F32)
     pieces = []
     for q in range(owners):
@@ -85,7 +99,10 @@
         out_ref[s] = total.astype(BF16)
 
 
-def place_kernel(owners, parents, ids_ref, out_ref, code_scr):
+def place_kernel(owners, parents, ids_ref, perm_any, out_ref, code_scr, perm_ref, sem):
+    copy = pltpu.make_async_copy(perm_any, perm_ref, sem)
+    copy.start()
+    copy.wait()
     leaves = out_ref.shape[1]
     children = leaves // parents
     me = ids_ref[0]
@@ -93,7 +110,7 @@
         rank = jnp.int32(0)
         base = (source ^ me) * leaves
         for parent in range(parents):
-            place = ids_ref[3 + source * parents + parent]
+            place = perm_ref[source * parents + parent]
             mine = (place // parents) == me
             slot = jnp.where(mine, place % parents, parents)
             code_scr[slot] = base + rank * children
@@ -123,29 +140,33 @@
 
 def coeff_products(lvl, lvls, vh, vs, basis_ref, field_ref, start_of, finish):
     slab, rank_width, leaves = basis_ref.shape
-    for t in range(lvls):
-        first = (lvl ^ t) * vs
-        accs = mac_rows(
-            slab,
-            lambda m: basis_ref[m].astype(F32),
-            lambda m, n: row_of(field_ref, m * vh + jnp.minimum(first + n, vh - 1)),
-            [start_of(t, n) for n in range(vs)],
-            8,
-        )
-        for n in range(vs):
-            finish(t, n, accs[n])
+    half = rank_width // 2
+    for first_t in range(0, lvls, 2):
+        members = [(t, n) for t in (first_t, first_t + 1) for n in range(vs)]
+        places = [jnp.minimum((lvl ^ t) * vs + n, vh - 1) for t, n in members]
+        for low in range(0, rank_width, half):
+            part = slice(low, low + half)
+            accs = mac_rows(
+                slab,
+                lambda m: basis_ref[m, part, :].astype(F32),
+                lambda m, n: row_of(field_ref, m * vh + places[n]),
+                [start_of(t, n, low, half) for t, n in members],
+                8,
+            )
+            for (t, n), acc in zip(members, accs):
+                finish(t, n, low, half, acc)
 
 
 def coeff_own_kernel(lvls, vh, vs, ids_ref, basis_ref, field_ref, out_ref):
     rank_width, leaves = basis_ref.shape[1:]
 
-    def finish(t, n, acc):
-        start = (t * vs + n) * rank_width
-        out_ref[start : start + rank_width, :] = acc
+    def finish(t, n, low, half, acc):
+        start = (t * vs + n) * rank_width + low
+        out_ref[start : start + half, :] = acc
 
     coeff_products(
         ids_ref[1], lvls, vh, vs, basis_ref, field_ref,
-        lambda t, n: jnp.zeros((rank_width, leaves), F32), finish,
+        lambda t, n, low, half: jnp.zeros((half, leaves), F32), finish,
     )
 
 
@@ -155,16 +176,16 @@
     rank_width = basis_ref.shape[1]
     wide_ref[...] = field_ref[...].astype(F32)
 
-    def start_of(t, n):
-        start = (t * vs + n) * rank_width
-        return own_ref[start : start + rank_width, :]
-
-    def finish(t, n, acc):
-        block = slice(n * rank_width, (n + 1) * rank_width)
+    def start_of(t, n, low, half):
+        start = (t * vs + n) * rank_width + low
+        return own_ref[start : start + half, :]
+
+    def finish(t, n, low, half, acc):
+        start = n * rank_width + low
         if t == 0:
-            keep_ref[block, :] = acc
+            keep_ref[start : start + half, :] = acc
         else:
-            sends[t - 1][block, :] = acc.astype(BF16)
+            sends[t - 1][start : start + half, :] = acc.astype(BF16)
 
     coeff_products(ids_ref[1], lvls, vh, vs, basis_ref, wide_ref, start_of, finish)
 
@@ -282,10 +303,36 @@
                 prows_scr[:, n, i * rank_width : (i + 1) * rank_width] = picked[
                     i * parents : (i + 1) * parents, k * rank_width : (k + 1) * rank_width
                 ]
-    for parent in range(parents):
-        pout_scr[parent] = jnp.dot(
-            prows_scr[parent].astype(BF16), pcouple_ref[parent], preferred_element_type=F32
-        )
+    start = mine + len(packs(vs, rank_width, leaves)) * parents
+    for ref in extras:
+        out_ref[start : start + ref.shape[0], :] = ref[...]
+        start += ref.shape[0]
+
+    accs = tuple(jnp.zeros((rank_width, leaves), F32) for _ in range(vs))
+    turns = parents // (2 * slots)
+    width = rank_width // turns
+    for s in range(2 * slots):
+        if s >= slots:
+            copies[s - slots].wait()
+        ref, i = (own_ref, s) if s < slots else (couple_scr, s - slots)
+
+        def body(turn, carry, s=s, ref=ref, i=i):
+            parent = s * turns + turn
+            pout_scr[parent] = jnp.dot(
+                prows_scr[parent].astype(BF16), pcouple_ref[parent], preferred_element_type=F32
+            )
+            for k in range(width):
+                j = turn * width + k
+                weight = ref[i, j].astype(F32)
+                carry = tuple(
+                    acc + weight * rows_scr[s, pl.ds(n * rank_width + j, 1), :]
+                    for n, acc in enumerate(carry)
+                )
+            return carry
+
+        accs = lax.fori_loop(0, turns, body, accs)
+    for n in range(vs):
+        out_ref[n * rank_width : (n + 1) * rank_width, :] = accs[n].astype(out_ref.dtype)
     for b, members in enumerate(packs(vs, rank_width, leaves)):
         parts = [pout_scr[:, n, :] for n in members]
         missing = leaves - len(parts) * rank_width
@@ -294,25 +341,6 @@
         out_ref[mine + b * parents : mine + (b + 1) * parents, :] = jnp.concatenate(
             parts, axis=1
         ).astype(out_ref.dtype)
-    start = mine + len(packs(vs, rank_width, leaves)) * parents
-    for ref in extras:
-        out_ref[start : start + ref.shape[0], :] = ref[...]
-        start += ref.shape[0]
-
-    accs = [jnp.zeros((rank_width, leaves), F32) for _ in range(vs)]
-    for s in range(2 * slots):
-        if s >= slots:
-            copies[s - slots].wait()
-        ref, i = (own_ref, s) if s < slots else (couple_scr, s - slots)
-        accs = mac_rows(
-            rank_width,
-            lambda j, ref=ref, i=i: ref[i, j].astype(F32),
-            lambda j, n, s=s: rows_scr[s, pl.ds(n * rank_width + j, 1), :],
-            accs,
-            8,
-        )
-    for n in range(vs):
-        out_ref[n * rank_width : (n + 1) * rank_width, :] = accs[n].astype(out_ref.dtype)
 
 
 def down_kernel(vs, parents, keep_ref, *refs):
@@ -344,13 +372,20 @@
 
 
 def near_kernel(
-    vh, step, ids_ref, own_field, peer_field, own_ref, peer_any, out_ref, peer_scr, acc_scr, sem
+    vh, step, ids_ref, own_field, peer_field, own_ref, peer_any, out_ref, peer_scr, acc_scr, sems
 ):
     slab, _, leaves = own_ref.shape
     group = 6
     target = pl.multiple_of((ids_ref[1] ^ step) * (2 * slab), 2 * slab)
-    copy = pltpu.make_async_copy(peer_any.at[:, pl.ds(target, 2 * slab), :], peer_scr, sem)
-    copy.start()
+    copies = []
+    for c in range(4):
+        part = slice(c * slab // 4, (c + 1) * slab // 4)
+        copies.append(
+            pltpu.make_async_copy(
+                peer_any.at[part, pl.ds(target, 2 * slab), :], peer_scr.at[part], sems.at[c]
+            )
+        )
+        copies[-1].start()
 
     def products(field_ref, ref, base, first, half, accs):
         span = pl.ds(pl.multiple_of(base + half * slab, slab), slab)
@@ -359,7 +394,7 @@
             lambda p: ref[p, span, :].astype(F32),
             lambda p, n: row_of(field_ref, p * vh + first + n),
             accs,
-            8,
+            16,
         )
 
     places = [(half, first) for half in range(2) for first in range(0, vh, group)]
@@ -369,7 +404,8 @@
         for n in range(group):
             start = (half * vh + first + n) * slab
             acc_scr[start : start + slab, :] = accs[n]
-    copy.wait()
+    for copy in copies:
+        copy.wait()
     for half, first in places:
         starts = [(half * vh + first + n) * slab for n in range(group)]
         accs = [acc_scr[start : start + slab, :] for start in starts]
@@ -476,7 +512,7 @@
     me = lax.axis_index("clus")
     lvl = lax.axis_index("lvl")
     parity = lax.axis_index("rep")
-    ids = jnp.concatenate([jnp.stack([me, lvl, parity]).astype(jnp.int32), parent_perm])
+    ids = jnp.stack([me, lvl, parity]).astype(jnp.int32)
 
     def call(name, kernel, ins, outs, scratch=(), us=1.0, scalars=0, whole=()):
         specs = [
@@ -521,20 +557,33 @@
     packed = call(
         "pack_field",
         functools.partial(pack_kernel, owners, vh, parents),
-        (ids, voxel_field),
+        (
+            ids,
+            pltpu.with_memory_space_constraint(parent_perm, pltpu.HBM),
+            pltpu.with_memory_space_constraint(voxel_field, pltpu.HBM),
+        ),
         sds((owners, chunk_rows, leaves), BF16),
-        [pltpu.VMEM((slab * vectors, leaves), F32)],
-        1.0, scalars=1,
+        [
+            pltpu.VMEM((slab * vectors, leaves), F32),
+            pltpu.SMEM(parent_perm.shape, jnp.int32),
+            pltpu.VMEM(voxel_field.shape, BF16),
+            pltpu.SemaphoreType.DMA((5,)),
+        ],
+        1.0, scalars=1, whole=(1, 2),
     )
     with jax.named_scope("regroup_sends"):
         chunks = [packed[0]] + swaps([packed[s] for s in range(owners)], "clus", owners, False)
     codes = call(
         "place_codes",
         functools.partial(place_kernel, owners, parents),
-        (after(ids, chunks[1]),),
+        (after(ids, chunks[1]), pltpu.with_memory_space_constraint(parent_perm, pltpu.HBM)),
         sds((8, leaves), jnp.int32),
-        [pltpu.SMEM((parents + 1,), jnp.int32)],
-        0.3, scalars=1,
+        [
+            pltpu.SMEM((parents + 1,), jnp.int32),
+            pltpu.SMEM(parent_perm.shape, jnp.int32),
+            pltpu.SemaphoreType.DMA,
+        ],
+        0.3, scalars=1, whole=(1,),
     )
     with jax.named_scope("coupling_layout"):
         couple = jnp.moveaxis(after(coupling, chunks[1])[:, :, 0], 2, 0)
@@ -544,12 +593,13 @@
             (partner_owner, partner_local, parent_owner, parent_local, block_count, chunks[1])
         )
         group = lvl * reps + parity
-        slot_number = group * slots + jnp.arange(slots, dtype=jnp.int32)[:, None]
-        leaf_code = (held[0][0] ^ me).T * leaves + held[1][0].T
-        leaf_code = jnp.where(slot_number < held[4][None, :], leaf_code, -1)
-        up_code = (held[2][0] ^ me).T * parents + held[3][0].T
-        up_code = jnp.pad(up_code, ((0, 0), (0, leaves - parents)), constant_values=-1)
-        partners = jnp.concatenate([leaf_code, up_code], axis=0)
+        row = jnp.arange(slots + pslots, dtype=jnp.int32)[:, None]
+        wide = ((0, 0), (0, leaves - parents))
+        owner = jnp.concatenate([held[0][0].T, jnp.pad(held[2][0].T, wide)], axis=0) ^ me
+        local = jnp.concatenate([held[1][0].T, jnp.pad(held[3][0].T, wide)], axis=0)
+        live = (row >= slots) | (group * slots + row < held[4][None, :])
+        partners = owner * jnp.where(row < slots, leaves, parents) + local
+        partners = jnp.where(live, partners, -1)
         partners_peer = other(partners)
     codes = after(codes, couple, row_peer, partners_peer)
 
@@ -593,7 +643,7 @@
             [
                 pltpu.VMEM((slab, 2 * slab, leaves), BF16),
                 pltpu.VMEM((2 * vh * slab, leaves), F32),
-                pltpu.SemaphoreType.DMA,
+                pltpu.SemaphoreType.DMA((4,)),
             ],
             2.4, scalars=1, whole=(4,),
         )

time: 75 us -> 74.1 us (0.988)
  other arithmetic: 2.21 us -> 0.89 us
  local copies, waits for them, and re-layouts: 3.19 us -> 2.26 us
    unnamed x17 -> x15, local copies, waits for them, and re-layouts: 0.99 us -> 0.06 us
  transfers between devices with their start and end apart: 30 -> 30, of which waited for: 10 -> 9; matrix products, arithmetic and copies ran while one was open for 5% -> 4% of each run, Pallas kernels for 43% -> 46%
where the time goes in v4:
time: 74.1 us; the launch traced here: 73.9 us
  Pallas kernels  35.9 us (48%)
  starting transfers between devices  28.7 us (39%)
  waiting for transfers between devices  5.74 us (8%)
  local copies, waits for them, and re-layouts  2.26 us (3%)
  other arithmetic  0.89 us (1%)
    pallas_call x21, Pallas kernels, call(): pl.pallas_call(kernel, out_shape=outs, in_specs=specs, out_specs=jax.tree...  35.9 us
    ppermute x30, starting transfers between devices, swap(): return lax.ppermute(value, axis, [(i, i ^ step) for i in range(count)])  28.7 us
    ppermute x30, waiting for transfers between devices, swap(): return lax.ppermute(value, axis, [(i, i ^ step) for i in range(count)])  5.74 us
    optimization_barrier x1, local copies, waits for them, and re-layouts, after(): return lax.optimization_barrier((value,) + others)[0]  2.17 us
  transfers between devices with their start and end apart: 30, of which 9 were waited for; matrix products, arithmetic and copies ran while one was open for 4% of the time, Pallas kernels for 46%

profile of v4, /device:TPU:0, one launch (start us, length us, event | category | flops | bytes accessed | tf_op | source)
XLA Modules:
  0.0 73.9 jit_solution(11885674882054766118)
XLA Ops:
  0.6 1.8 %pack_field.1 = bf16[4,192,128]{2,1,0:T(8,128)(2,1)S(1)} custom-call(s32[3]{0:T(128)S(1)} %pad_add_fusion.2.ids_ref, s32[64]{0:T(128)} %perm_any.3, bf16[32,24,128]{2,1,0:T(8,128)(2,1)} %own_any.1), custom_call_target="tpu_custom_call" | custom-call | bytes 3300000 | tf_op jit(solution)/shard_map/pack_field/pallas_call | solution.py:523
  2.5 3.1 %collective-permute-start = (bf16[192,128]{1,0:T(8,128)(2,1)S(1)}, bf16[192,128]{1,0:T(8,128)(2,1)S(1)}, u32[]{:S(2)}, u32[]{:S(2)}) collective-permute-start(bf16[192,128]{1,0:T(8,128)(2,1)S(1)} %get-tuple-element.74), channel_id=1, source_target_pairs={{0,8},{8,0},{16,24},{24,16},{1,9},{9,1},{17,25},{25,17},{2,10},{10... | collective-permute-start | bytes 147464 | tf_op jit(solution)/shard_map/regroup_sends/ppermute | solution.py:534
  5.6 2.6 %collective-permute-start.3 = (bf16[192,128]{1,0:T(8,128)(2,1)S(1)}, bf16[192,128]{1,0:T(8,128)(2,1)S(1)}, u32[]{:S(2)}, u32[]{:S(2)}) collective-permute-start(bf16[192,128]{1,0:T(8,128)(2,1)S(1)} %get-tuple-element.72), channel_id=1, source_target_pairs={{0,16},{8,24},{16,0},{24,8},{1,17},{9,25},{17,1},{25,9},{2,18},{10... | collective-permute-start | bytes 147464 | tf_op jit(solution)/shard_map/regroup_sends/ppermute | solution.py:534
  8.2 0.8 %fusion.1.own_codes = s32[4,128]{1,0:T(4,128)S(1)} fusion(s32[2,16]{1,0:T(2,128)} %bitcast.38, s32[2,16]{1,0:T(2,128)} %bitcast.39, s32[2,128]{1,0:T(2,128)} %bitcast.40, s32[2,128]{1,0:T(2,128)} %bitcast.41, s32[4]{0:T(128)S(1)} %get-tuple-element.75, s32[]{:T(128)} %axis_index.33, s32[128]{0:T(128)} %param.27, s32[4]{0:T(128)S(1)} %get-tuple-element.76, ...), kind=kLoop, calls=%fused_computation.11 | loop fusion | flops 4096 | bytes 4904 | tf_op jit(solution)/shard_map/partner_codes/jit(_where)/select_n | solution.py:602
  9.0 1.7 %place_codes.1.code_ref = s32[8,128]{1,0:T(8,128)S(1)} custom-call(s32[3]{0:T(128)S(1)} %pad_add_fusion.2.ids_ref, s32[64]{0:T(128)} %perm_any.3), custom_call_target="tpu_custom_call" | custom-call | bytes 990000 | tf_op jit(solution)/shard_map/place_codes/pallas_call | solution.py:523
  10.8 2.2 %copy.17 = bf16[64,64,1,2,128]{4,1,0,3,2:T(8,128)(2,1)S(1)} copy(bf16[64,64,1,2,128]{4,3,2,1,0:T(2,128)(2,1)} %param.18) | data formatting | bytes 4194304 | tf_op jit(solution)/shard_map/coupling_layout/optimization_barrier | solution.py:492
  13.0 1.1 %collective-permute-done.4.refs_3_ = bf16[192,128]{1,0:T(8,128)(2,1)S(1)} collective-permute-done((bf16[192,128]{1,0:T(8,128)(2,1)S(1)}, bf16[192,128]{1,0:T(8,128)(2,1)S(1)}, u32[]{:S(2)}, u32[]{:S(2)}) %collective-permute-start.4) | collective-permute-done | bytes 49184 | tf_op jit(solution)/shard_map/regroup_sends/ppermute | solution.py:534
  14.5 1.5 %coeffs_own_slab.1.own_ref = f32[768,128]{1,0:T(8,128)S(1)} custom-call(s32[3]{0:T(128)S(1)} %pad_add_fusion.2.ids_ref, bf16[32,64,128]{2,1,0:T(8,128)(2,1)S(1)} %copy-done.4, f32[384,128]{1,0:T(8,128)S(1)} %get-tuple-element.60.field_ref.own_field), custom_call_target="tpu_custom_call" | custom-call | bytes 5280000 | tf_op jit(solution)/shard_map/coeffs_own_slab/pallas_call | solution.py:523
  16.0 1.6 %coeffs_other_slab.1 = (f32[384,128]{1,0:T(8,128)S(1)}, f32[192,128]{1,0:T(8,128)S(1)}, bf16[192,128]{1,0:T(8,128)(2,1)S(1)}, bf16[192,128]{1,0:T(8,128)(2,1)S(1)}, bf16[192,128]{1,0:T(8,128)(2,1)S(1)}) custom-call(s32[3]{0:T(128)S(1)} %pad_add_fusion.2.ids_ref, bf16[32,64,128]{2,1,0:T(8,128)(2,1)S(1)} %collective-permute-done.1.basis_ref, ...), custom_call_target="tpu_custom_call" | custom-call | bytes 5280000 | tf_op jit(solution)/shard_map/coeffs_other_slab/pallas_call | solution.py:523
  18.2 2.4 %collective-permute-start.6 = (bf16[192,128]{1,0:T(8,128)(2,1)S(1)}, bf16[192,128]{1,0:T(8,128)(2,1)S(1)}, u32[]{:S(2)}, u32[]{:S(2)}) collective-permute-start(bf16[192,128]{1,0:T(8,128)(2,1)S(1)} %get-tuple-element.49), channel_id=1, source_target_pairs={{0,6},{2,4},{4,2},{6,0},{1,7},{3,5},{5,3},{7,1},{8,14},{10,12},{12... | collective-permute-start | bytes 147464 | tf_op jit(solution)/shard_map/coeff_sends/ppermute | solution.py:534
  21.7 2.6 %self_blocks.4.refs_0_ = bf16[768,128]{1,0:T(8,128)(2,1)S(1)} custom-call(s32[3]{0:T(128)S(1)} %pad_add_fusion.2.ids_ref, f32[384,128]{1,0:T(8,128)S(1)} %get-tuple-element.60.field_ref.own_field, f32[384,128]{1,0:T(8,128)S(1)} %get-tuple-element.53.peer_field, bf16[32,256,128]{2,1,0:T(8,128)(2,1)S(1)} %copy-done, ...), custom_call_target="tpu_custom_call" | custom-call | bytes 7920000 | tf_op jit(solution)/shard_map/self_blocks/pallas_call | solution.py:523
  25.2 0.8 %parent_coeffs.1 = bf16[224,128]{1,0:T(8,128)(2,1)S(1)} custom-call(f32[192,128]{1,0:T(8,128)S(1)} %get-tuple-element.48.keep_ref, bf16[192,128]{1,0:T(8,128)(2,1)S(1)} %collective-permute-done.6.refs_0_, bf16[192,128]{1,0:T(8,128)(2,1)S(1)} %collective-permute-done.7.refs_1_, bf16[192,128]{1,0:T(8,128)(2,1)S(1)} %collective-permute-done.8.refs_2_, ...), custom_call_target="tpu_custom_call" | custom-call | bytes 2640000 | tf_op jit(solution)/shard_map/parent_coeffs/pallas_call | solution.py:523
  26.5 3.1 %collective-permute-start.11 = (bf16[224,128]{1,0:T(8,128)(2,1)S(1)}, bf16[224,128]{1,0:T(8,128)(2,1)S(1)}, u32[]{:S(2)}, u32[]{:S(2)}) collective-permute-start(bf16[224,128]{1,0:T(8,128)(2,1)S(1)} %parent_coeffs.1), channel_id=1, source_target_pairs={{0,16},{8,24},{16,0},{24,8},{1,17},{9,25},{17,1},{25,9},{2,18},{10... | collective-permute-start | bytes 172040 | tf_op jit(solution)/shard_map/owner_sends/ppermute | solution.py:534
  30.4 2.6 %self_blocks.5.refs_0_ = bf16[768,128]{1,0:T(8,128)(2,1)S(1)} custom-call(s32[3]{0:T(128)S(1)} %pad_add_fusion.2.ids_ref, f32[384,128]{1,0:T(8,128)S(1)} %get-tuple-element.60.field_ref.own_field, f32[384,128]{1,0:T(8,128)S(1)} %get-tuple-element.53.peer_field, bf16[32,256,128]{2,1,0:T(8,128)(2,1)S(1)} %copy-done, ...), custom_call_target="tpu_custom_call" | custom-call | bytes 7920000 | tf_op jit(solution)/shard_map/self_blocks/pallas_call | solution.py:523
  33.0 2.6 %self_blocks.6 = bf16[768,128]{1,0:T(8,128)(2,1)S(1)} custom-call(s32[3]{0:T(128)S(1)} %pad_add_fusion.2.ids_ref, f32[384,128]{1,0:T(8,128)S(1)} %get-tuple-element.60.field_ref.own_field, f32[384,128]{1,0:T(8,128)S(1)} %get-tuple-element.53.peer_field, bf16[32,256,128]{2,1,0:T(8,128)(2,1)S(1)} %copy-done, ...), custom_call_target="tpu_custom_call" | custom-call | bytes 7920000 | tf_op jit(solution)/shard_map/self_blocks/pallas_call | solution.py:523
  36.4 1.5 %collective-permute-start.17 = (bf16[896,128]{1,0:T(8,128)(2,1)S(1)}, bf16[896,128]{1,0:T(8,128)(2,1)S(1)}, u32[]{:S(2)}, u32[]{:S(2)}) collective-permute-start(bf16[896,128]{1,0:T(8,128)(2,1)S(1)} %constant_dynamic-update-slice_fusion.block_ref), channel_id=1, source_target_pairs={{0,4},{2,6},{4,0},{6,2},{1,5},{3,7},{5,1},{7,3},{8,12},{10,14},{12... | collective-permute-start | bytes 688136 | tf_op jit(solution)/shard_map/level_sends/ppermute | solution.py:534
  37.9 1.4 %collective-permute-start.19 = (bf16[896,128]{1,0:T(8,128)(2,1)S(1)}, bf16[896,128]{1,0:T(8,128)(2,1)S(1)}, u32[]{:S(2)}, u32[]{:S(2)}) collective-permute-start(bf16[896,128]{1,0:T(8,128)(2,1)S(1)} %constant_dynamic-update-slice_fusion.block_ref), channel_id=1, source_target_pairs={{0,6},{2,4},{4,2},{6,0},{1,7},{3,5},{5,3},{7,1},{8,14},{10,12},{12... | collective-permute-start | bytes 688136 | tf_op jit(solution)/shard_map/level_sends/ppermute | solution.py:534
  39.3 2.6 %self_blocks.7.keep_ref = f32[768,128]{1,0:T(8,128)S(1)} custom-call(s32[3]{0:T(128)S(1)} %pad_add_fusion.2.ids_ref, f32[384,128]{1,0:T(8,128)S(1)} %get-tuple-element.60.field_ref.own_field, f32[384,128]{1,0:T(8,128)S(1)} %get-tuple-element.53.peer_field, bf16[32,256,128]{2,1,0:T(8,128)(2,1)S(1)} %copy-done, ...), custom_call_target="tpu_custom_call" | custom-call | bytes 7920000 | tf_op jit(solution)/shard_map/self_blocks/pallas_call | solution.py:523
  41.8 1.7 %partner_tables.1 = (bf16[512,512]{1,0:T(8,128)(2,1)S(1)}, bf16[64,64]{1,0:T(8,128)(2,1)S(1)}, bf16[16,256,64]{2,1,0:T(8,128)(2,1)S(1)}) custom-call(s32[4,128]{1,0:T(4,128)S(1)} %fusion.1.own_codes, s32[4,128]{1,0:T(4,128)S(1)} %collective-permute-done.2.peer_codes, bf16[64,32,64]{2,1,0:T(8,128)(2,1)S(1)} %bitcast.37, ...), custom_call_target="tpu_custom_call" | custom-call | bytes 4950000 | tf_op jit(solution)/shard_map/partner_tables/pallas_call | solution.py:523
  44.2 2.8 %coupling_products.5 = bf16[992,128]{1,0:T(8,128)(2,1)S(1)} custom-call(bf16[512,512]{1,0:T(8,128)(2,1)S(1)} %get-tuple-element.62.leaf_table, bf16[64,64]{1,0:T(8,128)(2,1)S(1)} %get-tuple-element.63.parent_table, bf16[16,256,64]{2,1,0:T(8,128)(2,1)S(1)} %get-tuple-element.64.pcouple_ref, bf16[896,128]{1,0:T(8,128)(2,1)S(1)} %collective-permute-done.15.block_ref, ...), custom_call_target="tpu_custom_call" | custom-call | bytes 10560000 | tf_op jit(solution)/shard_map/coupling_products/pallas_call | solution.py:523
  48.1 2.8 %coupling_products.6 = bf16[992,128]{1,0:T(8,128)(2,1)S(1)} custom-call(bf16[512,512]{1,0:T(8,128)(2,1)S(1)} %get-tuple-element.62.leaf_table, bf16[64,64]{1,0:T(8,128)(2,1)S(1)} %get-tuple-element.63.parent_table, bf16[16,256,64]{2,1,0:T(8,128)(2,1)S(1)} %get-tuple-element.64.pcouple_ref, bf16[896,128]{1,0:T(8,128)(2,1)S(1)} %collective-permute-done.17.block_ref, ...), custom_call_target="tpu_custom_call" | custom-call | bytes 10560000 | tf_op jit(solution)/shard_map/coupling_products/pallas_call | solution.py:523
  50.9 2.5 %collective-permute-start.18 = (bf16[992,128]{1,0:T(8,128)(2,1)S(1)}, bf16[992,128]{1,0:T(8,128)(2,1)S(1)}, u32[]{:S(2)}, u32[]{:S(2)}) collective-permute-start(bf16[992,128]{1,0:T(8,128)(2,1)S(1)} %coupling_products.6), channel_id=1, source_target_pairs={{0,4},{2,6},{4,0},{6,2},{1,5},{3,7},{5,1},{7,3},{8,12},{10,14},{12... | collective-permute-start | bytes 761864 | tf_op jit(solution)/shard_map/far_sends/ppermute | solution.py:534
  53.4 2.8 %coupling_products.7 = bf16[224,128]{1,0:T(8,128)(2,1)S(1)} custom-call(bf16[512,512]{1,0:T(8,128)(2,1)S(1)} %get-tuple-element.62.leaf_table, bf16[64,64]{1,0:T(8,128)(2,1)S(1)} %get-tuple-element.63.parent_table, bf16[16,256,64]{2,1,0:T(8,128)(2,1)S(1)} %get-tuple-element.64.pcouple_ref, bf16[896,128]{1,0:T(8,128)(2,1)S(1)} %collective-permute-done.19.block_ref, ...), custom_call_target="tpu_custom_call" | custom-call | bytes 10560000 | tf_op jit(solution)/shard_map/coupling_products/pallas_call | solution.py:523
  56.3 1.5 %collective-permute-start.20 = (bf16[224,128]{1,0:T(8,128)(2,1)S(1)}, bf16[224,128]{1,0:T(8,128)(2,1)S(1)}, u32[]{:S(2)}, u32[]{:S(2)}) collective-permute-start(bf16[224,128]{1,0:T(8,128)(2,1)S(1)} %coupling_products.7), channel_id=1, source_target_pairs={{0,6},{2,4},{4,2},{6,0},{1,7},{3,5},{5,3},{7,1},{8,14},{10,12},{12... | collective-permute-start | bytes 172040 | tf_op jit(solution)/shard_map/far_sends/ppermute | solution.py:534
  57.8 2.8 %coupling_products.4.keep_ref = f32[224,128]{1,0:T(8,128)S(1)} custom-call(bf16[512,512]{1,0:T(8,128)(2,1)S(1)} %get-tuple-element.62.leaf_table, bf16[64,64]{1,0:T(8,128)(2,1)S(1)} %get-tuple-element.63.parent_table, bf16[16,256,64]{2,1,0:T(8,128)(2,1)S(1)} %get-tuple-element.64.pcouple_ref, ...), custom_call_target="tpu_custom_call" | custom-call | bytes 10560000 | tf_op jit(solution)/shard_map/coupling_products/pallas_call | solution.py:523
  60.6 0.8 %collective-permute-done.20.refs_2_ = bf16[224,128]{1,0:T(8,128)(2,1)S(1)} collective-permute-done((bf16[224,128]{1,0:T(8,128)(2,1)S(1)}, bf16[224,128]{1,0:T(8,128)(2,1)S(1)}, u32[]{:S(2)}, u32[]{:S(2)}) %collective-permute-start.20) | collective-permute-done | bytes 57376 | tf_op jit(solution)/shard_map/far_sends/ppermute | solution.py:534
  61.4 1.5 %collective-permute-start.22 = (bf16[768,128]{1,0:T(8,128)(2,1)S(1)}, bf16[768,128]{1,0:T(8,128)(2,1)S(1)}, u32[]{:S(2)}, u32[]{:S(2)}) collective-permute-start(bf16[768,128]{1,0:T(8,128)(2,1)S(1)} %self_blocks.6), channel_id=1, source_target_pairs={{0,6},{2,4},{4,2},{6,0},{1,7},{3,5},{5,3},{7,1},{8,14},{10,12},{12... | collective-permute-start | bytes 589832 | tf_op jit(solution)/shard_map/self_sends/ppermute | solution.py:534
  63.8 0.8 %collective-permute-start.24 = (bf16[192,128]{1,0:T(8,128)(2,1)S(1)}, bf16[192,128]{1,0:T(8,128)(2,1)S(1)}, u32[]{:S(2)}, u32[]{:S(2)}) collective-permute-start(bf16[192,128]{1,0:T(8,128)(2,1)S(1)} %down_products.1.mine_ref), channel_id=1, source_target_pairs={{0,2},{2,0},{4,6},{6,4},{1,3},{3,1},{5,7},{7,5},{8,10},{10,8},{12,... | collective-permute-start | bytes 147464 | tf_op jit(solution)/shard_map/far_coeff_sends/ppermute | solution.py:534
  64.6 1.3 %collective-permute-start.26 = (bf16[192,128]{1,0:T(8,128)(2,1)S(1)}, bf16[192,128]{1,0:T(8,128)(2,1)S(1)}, u32[]{:S(2)}, u32[]{:S(2)}) collective-permute-start(bf16[192,128]{1,0:T(8,128)(2,1)S(1)} %down_products.1.mine_ref), channel_id=1, source_target_pairs={{0,4},{2,6},{4,0},{6,2},{1,5},{3,7},{5,1},{7,3},{8,12},{10,14},{12... | collective-permute-start | bytes 147464 | tf_op jit(solution)/shard_map/far_coeff_sends/ppermute | solution.py:534
  65.8 1.5 %collective-permute-start.28 = (bf16[192,128]{1,0:T(8,128)(2,1)S(1)}, bf16[192,128]{1,0:T(8,128)(2,1)S(1)}, u32[]{:S(2)}, u32[]{:S(2)}) collective-permute-start(bf16[192,128]{1,0:T(8,128)(2,1)S(1)} %down_products.1.mine_ref), channel_id=1, source_target_pairs={{0,6},{2,4},{4,2},{6,0},{1,7},{3,5},{5,3},{7,1},{8,14},{10,12},{12... | collective-permute-start | bytes 147464 | tf_op jit(solution)/shard_map/far_coeff_sends/ppermute | solution.py:534
  69.5 1.3 %collective-permute-done.28.refs_3_ = bf16[192,128]{1,0:T(8,128)(2,1)S(1)} collective-permute-done((bf16[192,128]{1,0:T(8,128)(2,1)S(1)}, bf16[192,128]{1,0:T(8,128)(2,1)S(1)}, u32[]{:S(2)}, u32[]{:S(2)}) %collective-permute-start.28) | collective-permute-done | bytes 49184 | tf_op jit(solution)/shard_map/far_coeff_sends/ppermute | solution.py:534
  72.1 1.8 %column_products.1 = bf16[32,24,128]{2,1,0:T(8,128)(2,1)} custom-call(s32[3]{0:T(128)S(1)} %pad_add_fusion.2.ids_ref, bf16[64,32,128]{2,1,0:T(8,128)(2,1)S(1)} %copy-done.1, f32[384,128]{1,0:T(8,128)S(1)} %get-tuple-element.69.near_mine, bf16[384,128]{1,0:T(8,128)(2,1)S(1)} %collective-permute-done.23.near_peer, ...), custom_call_target="tpu_custom_call" | custom-call | bytes 6105000 | tf_op jit(solution)/shard_map/column_products/pallas_call | solution.py:523
  (71 shorter events, 11.5 us)
Async XLA Ops:
  0.0 13.0 %collective-permute-start.1 = (bf16[32,64,128]{2,1,0:T(8,128)(2,1)}, bf16[32,64,128]{2,1,0:T(8,128)(2,1)S(1)}, u32[]{:S(2)}, u32[]{:S(2)}) collective-permute-start(bf16[32,64,128]{2,1,0:T(8,128)(2,1)} %basis_ref.1), channel_id=1, source_target_pairs={{0,1},{1,0},{2,3},{3,2},{4,5},{5,4},{6,7},{7,6},{8,9},{9,8},{10,11... | collective-permute-start | bytes 1572872 | tf_op jit(solution)/shard_map/swap_row_basis/ppermute | solution.py:534
  0.5 21.2 %collective-permute-start.9 = (bf16[32,256,128]{2,1,0:T(8,128)(2,1)}, bf16[32,256,128]{2,1,0:T(8,128)(2,1)S(1)}, u32[]{:S(2)}, u32[]{:S(2)}) collective-permute-start(bf16[32,256,128]{2,1,0:T(8,128)(2,1)} %own_ref.7), channel_id=1, source_target_pairs={{0,1},{1,0},{2,3},{3,2},{4,5},{5,4},{6,7},{7,6},{8,9},{9,8},{10,11... | collective-permute-start | bytes 6291464 | tf_op jit(solution)/shard_map/swap_self_blocks/ppermute | solution.py:534
  2.5 5.7 %collective-permute-start = (bf16[192,128]{1,0:T(8,128)(2,1)S(1)}, bf16[192,128]{1,0:T(8,128)(2,1)S(1)}, u32[]{:S(2)}, u32[]{:S(2)}) collective-permute-start(bf16[192,128]{1,0:T(8,128)(2,1)S(1)} %get-tuple-element.74), channel_id=1, source_target_pairs={{0,8},{8,0},{16,24},{24,16},{1,9},{9,1},{17,25},{25,17},{2,10},{10... | collective-permute-start | bytes 147464 | tf_op jit(solution)/shard_map/regroup_sends/ppermute | solution.py:534
  5.6 7.4 %collective-permute-start.3 = (bf16[192,128]{1,0:T(8,128)(2,1)S(1)}, bf16[192,128]{1,0:T(8,128)(2,1)S(1)}, u32[]{:S(2)}, u32[]{:S(2)}) collective-permute-start(bf16[192,128]{1,0:T(8,128)(2,1)S(1)} %get-tuple-element.72), channel_id=1, source_target_pairs={{0,16},{8,24},{16,0},{24,8},{1,17},{9,25},{17,1},{25,9},{2,18},{10... | collective-permute-start | bytes 147464 | tf_op jit(solution)/shard_map/regroup_sends/ppermute | solution.py:534
  8.2 5.9 %collective-permute-start.4 = (bf16[192,128]{1,0:T(8,128)(2,1)S(1)}, bf16[192,128]{1,0:T(8,128)(2,1)S(1)}, u32[]{:S(2)}, u32[]{:S(2)}) collective-permute-start(bf16[192,128]{1,0:T(8,128)(2,1)S(1)} %get-tuple-element.71), channel_id=1, source_target_pairs={{0,24},{8,16},{16,8},{24,0},{1,25},{9,17},{17,9},{25,1},{2,26},{10... | collective-permute-start | bytes 147464 | tf_op jit(solution)/shard_map/regroup_sends/ppermute | solution.py:534
  9.0 4.0 %collective-permute-start.2 = (s32[4,128]{1,0:T(4,128)S(1)}, s32[4,128]{1,0:T(4,128)S(1)}, u32[]{:S(2)}, u32[]{:S(2)}) collective-permute-start(s32[4,128]{1,0:T(4,128)S(1)} %fusion.1.own_codes), channel_id=1, source_target_pairs={{0,1},{1,0},{2,3},{3,2},{4,5},{5,4},{6,7},{7,6},{8,9},{9,8},{10,11... | collective-permute-start | bytes 6152 | tf_op jit(solution)/shard_map/partner_codes/ppermute | solution.py:534
  12.9 8.7 %copy-start = (bf16[32,256,128]{2,1,0:T(8,128)(2,1)S(1)}, bf16[32,256,128]{2,1,0:T(8,128)(2,1)}, u32[]{:S(2)}) copy-start(bf16[32,256,128]{2,1,0:T(8,128)(2,1)} %own_ref.7) | copy-start | bytes 6291460
  14.4 1.6 %collective-permute-start.5 = (bf16[384,128]{1,0:T(8,128)(2,1)S(1)}, bf16[384,128]{1,0:T(8,128)(2,1)S(1)}, u32[]{:S(2)}, u32[]{:S(2)}) collective-permute-start(bf16[384,128]{1,0:T(8,128)(2,1)S(1)} %get-tuple-element.47), channel_id=1, source_target_pairs={{0,1},{1,0},{2,3},{3,2},{4,5},{5,4},{6,7},{7,6},{8,9},{9,8},{10,11... | collective-permute-start | bytes 294920 | tf_op jit(solution)/shard_map/swap_field/ppermute | solution.py:534
  17.6 26.6 %collective-permute-start.14 = (bf16[2,64,64,128]{3,2,1,0:T(8,128)(2,1)S(1)}, bf16[2,64,64,128]{3,2,1,0:T(8,128)(2,1)S(1)}, u32[]{:S(2)}, u32[]{:S(2)}) collective-permute-start(bf16[2,64,64,128]{3,2,1,0:T(8,128)(2,1)S(1)} %bitcast.31), channel_id=1, source_target_pairs={{0,1},{1,0},{2,3},{3,2},{4,5},{5,4},{6,7},{7,6},{8,9},{9,8},{10,11... | collective-permute-start | bytes 6291464 | tf_op jit(solution)/shard_map/swap_coupling/ppermute | solution.py:534
  18.2 6.1 %collective-permute-start.6 = (bf16[192,128]{1,0:T(8,128)(2,1)S(1)}, bf16[192,128]{1,0:T(8,128)(2,1)S(1)}, u32[]{:S(2)}, u32[]{:S(2)}) collective-permute-start(bf16[192,128]{1,0:T(8,128)(2,1)S(1)} %get-tuple-element.49), channel_id=1, source_target_pairs={{0,6},{2,4},{4,2},{6,0},{1,7},{3,5},{5,3},{7,1},{8,14},{10,12},{12... | collective-permute-start | bytes 147464 | tf_op jit(solution)/shard_map/coeff_sends/ppermute | solution.py:534
  20.6 4.1 %collective-permute-start.7 = (bf16[192,128]{1,0:T(8,128)(2,1)S(1)}, bf16[192,128]{1,0:T(8,128)(2,1)S(1)}, u32[]{:S(2)}, u32[]{:S(2)}) collective-permute-start(bf16[192,128]{1,0:T(8,128)(2,1)S(1)} %get-tuple-element.50), channel_id=1, source_target_pairs={{0,4},{2,6},{4,0},{6,2},{1,5},{3,7},{5,1},{7,3},{8,12},{10,14},{12... | collective-permute-start | bytes 147464 | tf_op jit(solution)/shard_map/coeff_sends/ppermute | solution.py:534
  21.1 4.1 %collective-permute-start.8 = (bf16[192,128]{1,0:T(8,128)(2,1)S(1)}, bf16[192,128]{1,0:T(8,128)(2,1)S(1)}, u32[]{:S(2)}, u32[]{:S(2)}) collective-permute-start(bf16[192,128]{1,0:T(8,128)(2,1)S(1)} %get-tuple-element.51), channel_id=1, source_target_pairs={{0,2},{2,0},{4,6},{6,4},{1,3},{3,1},{5,7},{7,5},{8,10},{10,8},{12,... | collective-permute-start | bytes 147464 | tf_op jit(solution)/shard_map/coeff_sends/ppermute | solution.py:534
  21.7 8.8 %copy-start.5 = (bf16[64,64,1,2,16]{1,4,3,2,0:T(8,128)(2,1)S(1)}, bf16[64,64,1,2,16]{1,4,3,2,0:T(8,128)(2,1)}, u32[]{:S(2)}) copy-start(bf16[64,64,1,2,16]{1,4,3,2,0:T(8,128)(2,1)} %param.19) | copy-start | bytes 786436
  26.0 9.6 %collective-permute-start.10 = (bf16[224,128]{1,0:T(8,128)(2,1)S(1)}, bf16[224,128]{1,0:T(8,128)(2,1)S(1)}, u32[]{:S(2)}, u32[]{:S(2)}) collective-permute-start(bf16[224,128]{1,0:T(8,128)(2,1)S(1)} %parent_coeffs.1), channel_id=1, source_target_pairs={{0,8},{8,0},{16,24},{24,16},{1,9},{9,1},{17,25},{25,17},{2,10},{10... | collective-permute-start | bytes 172040 | tf_op jit(solution)/shard_map/owner_sends/ppermute | solution.py:534
  26.5 9.1 %collective-permute-start.11 = (bf16[224,128]{1,0:T(8,128)(2,1)S(1)}, bf16[224,128]{1,0:T(8,128)(2,1)S(1)}, u32[]{:S(2)}, u32[]{:S(2)}) collective-permute-start(bf16[224,128]{1,0:T(8,128)(2,1)S(1)} %parent_coeffs.1), channel_id=1, source_target_pairs={{0,16},{8,24},{16,0},{24,8},{1,17},{9,25},{17,1},{25,9},{2,18},{10... | collective-permute-start | bytes 172040 | tf_op jit(solution)/shard_map/owner_sends/ppermute | solution.py:534
  29.7 6.0 %collective-permute-start.12 = (bf16[224,128]{1,0:T(8,128)(2,1)S(1)}, bf16[224,128]{1,0:T(8,128)(2,1)S(1)}, u32[]{:S(2)}, u32[]{:S(2)}) collective-permute-start(bf16[224,128]{1,0:T(8,128)(2,1)S(1)} %parent_coeffs.1), channel_id=1, source_target_pairs={{0,24},{8,16},{16,8},{24,0},{1,25},{9,17},{17,9},{25,1},{2,26},{10... | collective-permute-start | bytes 172040 | tf_op jit(solution)/shard_map/owner_sends/ppermute | solution.py:534
  30.4 11.4 %collective-permute-start.13 = (bf16[64,32,64]{2,1,0:T(8,128)(2,1)S(1)}, bf16[64,32,64]{2,1,0:T(8,128)(2,1)S(1)}, u32[]{:S(2)}, u32[]{:S(2)}) collective-permute-start(bf16[64,32,64]{2,1,0:T(8,128)(2,1)S(1)} %bitcast.36), channel_id=1, source_target_pairs={{0,1},{1,0},{2,3},{3,2},{4,5},{5,4},{6,7},{7,6},{8,9},{9,8},{10,11... | collective-permute-start | bytes 786440 | tf_op jit(solution)/shard_map/swap_parent_coupling/ppermute | solution.py:534
  35.7 8.5 %collective-permute-start.15 = (bf16[896,128]{1,0:T(8,128)(2,1)S(1)}, bf16[896,128]{1,0:T(8,128)(2,1)S(1)}, u32[]{:S(2)}, u32[]{:S(2)}) collective-permute-start(bf16[896,128]{1,0:T(8,128)(2,1)S(1)} %constant_dynamic-update-slice_fusion.block_ref), channel_id=1, source_target_pairs={{0,2},{2,0},{4,6},{6,4},{1,3},{3,1},{5,7},{7,5},{8,10},{10,8},{12,... | collective-permute-start | bytes 688136 | tf_op jit(solution)/shard_map/level_sends/ppermute | solution.py:534
  36.4 11.7 %collective-permute-start.17 = (bf16[896,128]{1,0:T(8,128)(2,1)S(1)}, bf16[896,128]{1,0:T(8,128)(2,1)S(1)}, u32[]{:S(2)}, u32[]{:S(2)}) collective-permute-start(bf16[896,128]{1,0:T(8,128)(2,1)S(1)} %constant_dynamic-update-slice_fusion.block_ref), channel_id=1, source_target_pairs={{0,4},{2,6},{4,0},{6,2},{1,5},{3,7},{5,1},{7,3},{8,12},{10,14},{12... | collective-permute-start | bytes 688136 | tf_op jit(solution)/shard_map/level_sends/ppermute | solution.py:534
  37.9 15.6 %collective-permute-start.19 = (bf16[896,128]{1,0:T(8,128)(2,1)S(1)}, bf16[896,128]{1,0:T(8,128)(2,1)S(1)}, u32[]{:S(2)}, u32[]{:S(2)}) collective-permute-start(bf16[896,128]{1,0:T(8,128)(2,1)S(1)} %constant_dynamic-update-slice_fusion.block_ref), channel_id=1, source_target_pairs={{0,6},{2,4},{4,2},{6,0},{1,7},{3,5},{5,3},{7,1},{8,14},{10,12},{12... | collective-permute-start | bytes 688136 | tf_op jit(solution)/shard_map/level_sends/ppermute | solution.py:534
  47.0 15.9 %collective-permute-start.16 = (bf16[992,128]{1,0:T(8,128)(2,1)S(1)}, bf16[992,128]{1,0:T(8,128)(2,1)S(1)}, u32[]{:S(2)}, u32[]{:S(2)}) collective-permute-start(bf16[992,128]{1,0:T(8,128)(2,1)S(1)} %coupling_products.5), channel_id=1, source_target_pairs={{0,2},{2,0},{4,6},{6,4},{1,3},{3,1},{5,7},{7,5},{8,10},{10,8},{12,... | collective-permute-start | bytes 761864 | tf_op jit(solution)/shard_map/far_sends/ppermute | solution.py:534
  50.9 12.0 %collective-permute-start.18 = (bf16[992,128]{1,0:T(8,128)(2,1)S(1)}, bf16[992,128]{1,0:T(8,128)(2,1)S(1)}, u32[]{:S(2)}, u32[]{:S(2)}) collective-permute-start(bf16[992,128]{1,0:T(8,128)(2,1)S(1)} %coupling_products.6), channel_id=1, source_target_pairs={{0,4},{2,6},{4,0},{6,2},{1,5},{3,7},{5,1},{7,3},{8,12},{10,14},{12... | collective-permute-start | bytes 761864 | tf_op jit(solution)/shard_map/far_sends/ppermute | solution.py:534
  56.3 5.1 %collective-permute-start.20 = (bf16[224,128]{1,0:T(8,128)(2,1)S(1)}, bf16[224,128]{1,0:T(8,128)(2,1)S(1)}, u32[]{:S(2)}, u32[]{:S(2)}) collective-permute-start(bf16[224,128]{1,0:T(8,128)(2,1)S(1)} %coupling_products.7), channel_id=1, source_target_pairs={{0,6},{2,4},{4,2},{6,0},{1,7},{3,5},{5,3},{7,1},{8,14},{10,12},{12... | collective-permute-start | bytes 172040 | tf_op jit(solution)/shard_map/far_sends/ppermute | solution.py:534
  61.4 6.8 %collective-permute-start.22 = (bf16[768,128]{1,0:T(8,128)(2,1)S(1)}, bf16[768,128]{1,0:T(8,128)(2,1)S(1)}, u32[]{:S(2)}, u32[]{:S(2)}) collective-permute-start(bf16[768,128]{1,0:T(8,128)(2,1)S(1)} %self_blocks.6), channel_id=1, source_target_pairs={{0,6},{2,4},{4,2},{6,0},{1,7},{3,5},{5,3},{7,1},{8,14},{10,12},{12... | collective-permute-start | bytes 589832 | tf_op jit(solution)/shard_map/self_sends/ppermute | solution.py:534
  63.7 3.6 %collective-permute-start.21 = (bf16[192,128]{1,0:T(8,128)(2,1)S(1)}, bf16[192,128]{1,0:T(8,128)(2,1)S(1)}, u32[]{:S(2)}, u32[]{:S(2)}) collective-permute-start(bf16[192,128]{1,0:T(8,128)(2,1)S(1)} %down_products.1.mine_ref), channel_id=1, source_target_pairs={{0,1},{1,0},{2,3},{3,2},{4,5},{5,4},{6,7},{7,6},{8,9},{9,8},{10,11... | collective-permute-start | bytes 147464 | tf_op jit(solution)/shard_map/far_coeff_sends/ppermute | solution.py:534
  63.8 5.1 %collective-permute-start.24 = (bf16[192,128]{1,0:T(8,128)(2,1)S(1)}, bf16[192,128]{1,0:T(8,128)(2,1)S(1)}, u32[]{:S(2)}, u32[]{:S(2)}) collective-permute-start(bf16[192,128]{1,0:T(8,128)(2,1)S(1)} %down_products.1.mine_ref), channel_id=1, source_target_pairs={{0,2},{2,0},{4,6},{6,4},{1,3},{3,1},{5,7},{7,5},{8,10},{10,8},{12,... | collective-permute-start | bytes 147464 | tf_op jit(solution)/shard_map/far_coeff_sends/ppermute | solution.py:534
  64.6 4.8 %collective-permute-start.26 = (bf16[192,128]{1,0:T(8,128)(2,1)S(1)}, bf16[192,128]{1,0:T(8,128)(2,1)S(1)}, u32[]{:S(2)}, u32[]{:S(2)}) collective-permute-start(bf16[192,128]{1,0:T(8,128)(2,1)S(1)} %down_products.1.mine_ref), channel_id=1, source_target_pairs={{0,4},{2,6},{4,0},{6,2},{1,5},{3,7},{5,1},{7,3},{8,12},{10,14},{12... | collective-permute-start | bytes 147464 | tf_op jit(solution)/shard_map/far_coeff_sends/ppermute | solution.py:534
  65.8 5.0 %collective-permute-start.28 = (bf16[192,128]{1,0:T(8,128)(2,1)S(1)}, bf16[192,128]{1,0:T(8,128)(2,1)S(1)}, u32[]{:S(2)}, u32[]{:S(2)}) collective-permute-start(bf16[192,128]{1,0:T(8,128)(2,1)S(1)} %down_products.1.mine_ref), channel_id=1, source_target_pairs={{0,6},{2,4},{4,2},{6,0},{1,7},{3,5},{5,3},{7,1},{8,14},{10,12},{12... | collective-permute-start | bytes 147464 | tf_op jit(solution)/shard_map/far_coeff_sends/ppermute | solution.py:534
  68.8 3.2 %collective-permute-start.23 = (bf16[384,128]{1,0:T(8,128)(2,1)S(1)}, bf16[384,128]{1,0:T(8,128)(2,1)S(1)}, u32[]{:S(2)}, u32[]{:S(2)}) collective-permute-start(bf16[384,128]{1,0:T(8,128)(2,1)S(1)} %get-tuple-element.70), channel_id=1, source_target_pairs={{0,1},{1,0},{2,3},{3,2},{4,5},{5,4},{6,7},{7,6},{8,9},{9,8},{10,11... | collective-permute-start | bytes 294920 | tf_op jit(solution)/shard_map/swap_self_sums/ppermute | solution.py:534
  68.9 1.9 %collective-permute-start.25 = (bf16[192,128]{1,0:T(8,128)(2,1)S(1)}, bf16[192,128]{1,0:T(8,128)(2,1)S(1)}, u32[]{:S(2)}, u32[]{:S(2)}) collective-permute-start(bf16[192,128]{1,0:T(8,128)(2,1)S(1)} %collective-permute-done.24.mine_ref), channel_id=1, source_target_pairs={{0,1},{1,0},{2,3},{3,2},{4,5},{5,4},{6,7},{7,6},{8,9},{9,8},{10,11... | collective-permute-start | bytes 147464 | tf_op jit(solution)/shard_map/far_coeff_sends/ppermute | solution.py:534
  69.4 1.9 %collective-permute-start.27 = (bf16[192,128]{1,0:T(8,128)(2,1)S(1)}, bf16[192,128]{1,0:T(8,128)(2,1)S(1)}, u32[]{:S(2)}, u32[]{:S(2)}) collective-permute-start(bf16[192,128]{1,0:T(8,128)(2,1)S(1)} %collective-permute-done.26.mine_ref), channel_id=1, source_target_pairs={{0,1},{1,0},{2,3},{3,2},{4,5},{5,4},{6,7},{7,6},{8,9},{9,8},{10,11... | collective-permute-start | bytes 147464 | tf_op jit(solution)/shard_map/far_coeff_sends/ppermute | solution.py:534
  70.8 1.2 %collective-permute-start.29 = (bf16[192,128]{1,0:T(8,128)(2,1)S(1)}, bf16[192,128]{1,0:T(8,128)(2,1)S(1)}, u32[]{:S(2)}, u32[]{:S(2)}) collective-permute-start(bf16[192,128]{1,0:T(8,128)(2,1)S(1)} %collective-permute-done.28.refs_3_), channel_id=1, source_target_pairs={{0,1},{1,0},{2,3},{3,2},{4,5},{5,4},{6,7},{7,6},{8,9},{9,8},{10,11... | collective-permute-start | bytes 147464 | tf_op jit(solution)/shard_map/far_coeff_sends/ppermute | solution.py:534
  (4 other events, 20.7 us)

commit v5 on v4

--- a/solution.py
+++ b/solution.py
@@ -78,7 +78,7 @@
     part = (slab // owners) * vh
     for copy in copies:
         copy.wait()
-    rows_scr[...] = own_ref[...].reshape(slab * vectors, leaves).astype(F32)
+    rows_scr[0 : slab * vectors, :] = own_ref[...].reshape(slab * vectors, leaves).astype(F32)
     pieces = []
     for q in range(owners):
         start = q * (slab // owners) * vectors
@@ -259,7 +259,8 @@
             parent_out[start : start + parents, :] = turned[:parents].astype(BF16)
     rank_width, pslots = own_ref.shape[0], own_ref.shape[1] // parents
     for half, ref in enumerate((own_ref, peer_ref)):
-        rows_scr[...] = ref[...].reshape(rank_width * pslots * parents, rank_width).astype(F32)
+        blocks = ref[...].reshape(rank_width * pslots * parents, rank_width)
+        rows_scr[0 : blocks.shape[0], :] = blocks.astype(F32)
         for i in range(pslots):
             place = (half * pslots + i) * rank_width
             for parent in range(parents):
@@ -485,7 +486,8 @@
             inside = jnp.minimum(place, vh - 1)
             near = near_ref[pl.ds(pl.multiple_of(inside * voxels, voxels), voxels), :]
             store(place, n // vs, accs[n] + near.astype(F32))
-    out_ref[...] = out_scr[...].reshape(voxels, vectors, leaves).astype(BF16)
+    whole = out_scr[0 : voxels * vectors, :]
+    out_ref[...] = whole.reshape(voxels, vectors, leaves).astype(BF16)
 
 
 def after(value, *others):
@@ -564,7 +566,7 @@
         ),
         sds((owners, chunk_rows, leaves), BF16),
         [
-            pltpu.VMEM((slab * vectors, leaves), F32),
+            pltpu.VMEM((slab * vectors + 8, leaves), F32),
             pltpu.SMEM(parent_perm.shape, jnp.int32),
             pltpu.VMEM(voxel_field.shape, BF16),
             pltpu.SemaphoreType.DMA((5,)),
@@ -683,7 +685,7 @@
             sds((2 * pslots * parents, owners * parents), BF16),
             sds((parents, 2 * pslots * rank_width, rank_width), BF16),
         ],
-        [pltpu.VMEM((rank_width * pslots * parents, rank_width), F32)],
+        [pltpu.VMEM(((rank_width + 1) * pslots * parents, rank_width), F32)],
         1.5,
     )
     def far_part(t, block):
@@ -753,7 +755,7 @@
         sds((slab, vectors, leaves), BF16),
         [
             pltpu.VMEM((2 * (lvls - early), vs * rank_width, leaves), F32),
-            pltpu.VMEM((slab * vectors, leaves), F32),
+            pltpu.VMEM(((slab + 1) * vectors, leaves), F32),
         ],
         1.85, scalars=1,
     )

time: 74.1 us -> 74.1 us (level)
  no operation moved by 1% of the time
where the time goes in v5:
time: 74.1 us; the launch traced here: 73.9 us
  Pallas kernels  35.9 us (48%)
  starting transfers between devices  28.7 us (39%)
  waiting for transfers between devices  5.74 us (8%)
  local copies, waits for them, and re-layouts  2.26 us (3%)
  other arithmetic  0.89 us (1%)
    pallas_call x21, Pallas kernels, call(): pl.pallas_call(kernel, out_shape=outs, in_specs=specs, out_specs=jax.tree...  35.9 us
    ppermute x30, starting transfers between devices, swap(): return lax.ppermute(value, axis, [(i, i ^ step) for i in range(count)])  28.7 us
    ppermute x30, waiting for transfers between devices, swap(): return lax.ppermute(value, axis, [(i, i ^ step) for i in range(count)])  5.74 us
    optimization_barrier x1, local copies, waits for them, and re-layouts, after(): return lax.optimization_barrier((value,) + others)[0]  2.17 us
  transfers between devices with their start and end apart: 30, of which 9 were waited for; matrix products, arithmetic and copies ran while one was open for 4% of the time, Pallas kernels for 46%

profile of v5, /device:TPU:0, one launch (start us, length us, event | category | flops | bytes accessed | tf_op | source)
XLA Modules:
  0.0 73.9 jit_solution(11075514642013840797)
XLA Ops:
  0.6 1.8 %pack_field.1 = bf16[4,192,128]{2,1,0:T(8,128)(2,1)S(1)} custom-call(s32[3]{0:T(128)S(1)} %pad_add_fusion.2.ids_ref, s32[64]{0:T(128)} %perm_any.3, bf16[32,24,128]{2,1,0:T(8,128)(2,1)} %own_any.1), custom_call_target="tpu_custom_call" | custom-call | bytes 3300000 | tf_op jit(solution)/shard_map/pack_field/pallas_call | solution.py:525
  2.5 3.1 %collective-permute-start = (bf16[192,128]{1,0:T(8,128)(2,1)S(1)}, bf16[192,128]{1,0:T(8,128)(2,1)S(1)}, u32[]{:S(2)}, u32[]{:S(2)}) collective-permute-start(bf16[192,128]{1,0:T(8,128)(2,1)S(1)} %get-tuple-element.74), channel_id=1, source_target_pairs={{0,8},{8,0},{16,24},{24,16},{1,9},{9,1},{17,25},{25,17},{2,10},{10... | collective-permute-start | bytes 147464 | tf_op jit(solution)/shard_map/regroup_sends/ppermute | solution.py:536
  5.6 2.6 %collective-permute-start.3 = (bf16[192,128]{1,0:T(8,128)(2,1)S(1)}, bf16[192,128]{1,0:T(8,128)(2,1)S(1)}, u32[]{:S(2)}, u32[]{:S(2)}) collective-permute-start(bf16[192,128]{1,0:T(8,128)(2,1)S(1)} %get-tuple-element.72), channel_id=1, source_target_pairs={{0,16},{8,24},{16,0},{24,8},{1,17},{9,25},{17,1},{25,9},{2,18},{10... | collective-permute-start | bytes 147464 | tf_op jit(solution)/shard_map/regroup_sends/ppermute | solution.py:536
  8.2 0.8 %fusion.1.own_codes = s32[4,128]{1,0:T(4,128)S(1)} fusion(s32[2,16]{1,0:T(2,128)} %bitcast.38, s32[2,16]{1,0:T(2,128)} %bitcast.39, s32[2,128]{1,0:T(2,128)} %bitcast.40, s32[2,128]{1,0:T(2,128)} %bitcast.41, s32[4]{0:T(128)S(1)} %get-tuple-element.75, s32[]{:T(128)} %axis_index.33, s32[128]{0:T(128)} %param.27, s32[4]{0:T(128)S(1)} %get-tuple-element.76, ...), kind=kLoop, calls=%fused_computation.11 | loop fusion | flops 4096 | bytes 4904 | tf_op jit(solution)/shard_map/partner_codes/jit(_where)/select_n | solution.py:604
  9.0 1.7 %place_codes.1.code_ref = s32[8,128]{1,0:T(8,128)S(1)} custom-call(s32[3]{0:T(128)S(1)} %pad_add_fusion.2.ids_ref, s32[64]{0:T(128)} %perm_any.3), custom_call_target="tpu_custom_call" | custom-call | bytes 990000 | tf_op jit(solution)/shard_map/place_codes/pallas_call | solution.py:525
  10.8 2.2 %copy.17 = bf16[64,64,1,2,128]{4,1,0,3,2:T(8,128)(2,1)S(1)} copy(bf16[64,64,1,2,128]{4,3,2,1,0:T(2,128)(2,1)} %param.18) | data formatting | bytes 4194304 | tf_op jit(solution)/shard_map/coupling_layout/optimization_barrier | solution.py:494
  13.0 1.1 %collective-permute-done.4.refs_3_ = bf16[192,128]{1,0:T(8,128)(2,1)S(1)} collective-permute-done((bf16[192,128]{1,0:T(8,128)(2,1)S(1)}, bf16[192,128]{1,0:T(8,128)(2,1)S(1)}, u32[]{:S(2)}, u32[]{:S(2)}) %collective-permute-start.4) | collective-permute-done | bytes 49184 | tf_op jit(solution)/shard_map/regroup_sends/ppermute | solution.py:536
  14.5 1.5 %coeffs_own_slab.1.own_ref = f32[768,128]{1,0:T(8,128)S(1)} custom-call(s32[3]{0:T(128)S(1)} %pad_add_fusion.2.ids_ref, bf16[32,64,128]{2,1,0:T(8,128)(2,1)S(1)} %copy-done.4, f32[384,128]{1,0:T(8,128)S(1)} %get-tuple-element.60.field_ref.own_field), custom_call_target="tpu_custom_call" | custom-call | bytes 5280000 | tf_op jit(solution)/shard_map/coeffs_own_slab/pallas_call | solution.py:525
  16.0 1.6 %coeffs_other_slab.1 = (f32[384,128]{1,0:T(8,128)S(1)}, f32[192,128]{1,0:T(8,128)S(1)}, bf16[192,128]{1,0:T(8,128)(2,1)S(1)}, bf16[192,128]{1,0:T(8,128)(2,1)S(1)}, bf16[192,128]{1,0:T(8,128)(2,1)S(1)}) custom-call(s32[3]{0:T(128)S(1)} %pad_add_fusion.2.ids_ref, bf16[32,64,128]{2,1,0:T(8,128)(2,1)S(1)} %collective-permute-done.1.basis_ref, ...), custom_call_target="tpu_custom_call" | custom-call | bytes 5280000 | tf_op jit(solution)/shard_map/coeffs_other_slab/pallas_call | solution.py:525
  18.2 2.4 %collective-permute-start.6 = (bf16[192,128]{1,0:T(8,128)(2,1)S(1)}, bf16[192,128]{1,0:T(8,128)(2,1)S(1)}, u32[]{:S(2)}, u32[]{:S(2)}) collective-permute-start(bf16[192,128]{1,0:T(8,128)(2,1)S(1)} %get-tuple-element.49), channel_id=1, source_target_pairs={{0,6},{2,4},{4,2},{6,0},{1,7},{3,5},{5,3},{7,1},{8,14},{10,12},{12... | collective-permute-start | bytes 147464 | tf_op jit(solution)/shard_map/coeff_sends/ppermute | solution.py:536
  21.7 2.6 %self_blocks.4.refs_0_ = bf16[768,128]{1,0:T(8,128)(2,1)S(1)} custom-call(s32[3]{0:T(128)S(1)} %pad_add_fusion.2.ids_ref, f32[384,128]{1,0:T(8,128)S(1)} %get-tuple-element.60.field_ref.own_field, f32[384,128]{1,0:T(8,128)S(1)} %get-tuple-element.53.peer_field, bf16[32,256,128]{2,1,0:T(8,128)(2,1)S(1)} %copy-done, ...), custom_call_target="tpu_custom_call" | custom-call | bytes 7920000 | tf_op jit(solution)/shard_map/self_blocks/pallas_call | solution.py:525
  25.2 0.8 %parent_coeffs.1 = bf16[224,128]{1,0:T(8,128)(2,1)S(1)} custom-call(f32[192,128]{1,0:T(8,128)S(1)} %get-tuple-element.48.keep_ref, bf16[192,128]{1,0:T(8,128)(2,1)S(1)} %collective-permute-done.6.refs_0_, bf16[192,128]{1,0:T(8,128)(2,1)S(1)} %collective-permute-done.7.refs_1_, bf16[192,128]{1,0:T(8,128)(2,1)S(1)} %collective-permute-done.8.refs_2_, ...), custom_call_target="tpu_custom_call" | custom-call | bytes 2640000 | tf_op jit(solution)/shard_map/parent_coeffs/pallas_call | solution.py:525
  26.5 3.1 %collective-permute-start.11 = (bf16[224,128]{1,0:T(8,128)(2,1)S(1)}, bf16[224,128]{1,0:T(8,128)(2,1)S(1)}, u32[]{:S(2)}, u32[]{:S(2)}) collective-permute-start(bf16[224,128]{1,0:T(8,128)(2,1)S(1)} %parent_coeffs.1), channel_id=1, source_target_pairs={{0,16},{8,24},{16,0},{24,8},{1,17},{9,25},{17,1},{25,9},{2,18},{10... | collective-permute-start | bytes 172040 | tf_op jit(solution)/shard_map/owner_sends/ppermute | solution.py:536
  30.4 2.6 %self_blocks.5.refs_0_ = bf16[768,128]{1,0:T(8,128)(2,1)S(1)} custom-call(s32[3]{0:T(128)S(1)} %pad_add_fusion.2.ids_ref, f32[384,128]{1,0:T(8,128)S(1)} %get-tuple-element.60.field_ref.own_field, f32[384,128]{1,0:T(8,128)S(1)} %get-tuple-element.53.peer_field, bf16[32,256,128]{2,1,0:T(8,128)(2,1)S(1)} %copy-done, ...), custom_call_target="tpu_custom_call" | custom-call | bytes 7920000 | tf_op jit(solution)/shard_map/self_blocks/pallas_call | solution.py:525
  33.0 2.6 %self_blocks.6 = bf16[768,128]{1,0:T(8,128)(2,1)S(1)} custom-call(s32[3]{0:T(128)S(1)} %pad_add_fusion.2.ids_ref, f32[384,128]{1,0:T(8,128)S(1)} %get-tuple-element.60.field_ref.own_field, f32[384,128]{1,0:T(8,128)S(1)} %get-tuple-element.53.peer_field, bf16[32,256,128]{2,1,0:T(8,128)(2,1)S(1)} %copy-done, ...), custom_call_target="tpu_custom_call" | custom-call | bytes 7920000 | tf_op jit(solution)/shard_map/self_blocks/pallas_call | solution.py:525
  36.4 1.5 %collective-permute-start.17 = (bf16[896,128]{1,0:T(8,128)(2,1)S(1)}, bf16[896,128]{1,0:T(8,128)(2,1)S(1)}, u32[]{:S(2)}, u32[]{:S(2)}) collective-permute-start(bf16[896,128]{1,0:T(8,128)(2,1)S(1)} %constant_dynamic-update-slice_fusion.block_ref), channel_id=1, source_target_pairs={{0,4},{2,6},{4,0},{6,2},{1,5},{3,7},{5,1},{7,3},{8,12},{10,14},{12... | collective-permute-start | bytes 688136 | tf_op jit(solution)/shard_map/level_sends/ppermute | solution.py:536
  37.9 1.4 %collective-permute-start.19 = (bf16[896,128]{1,0:T(8,128)(2,1)S(1)}, bf16[896,128]{1,0:T(8,128)(2,1)S(1)}, u32[]{:S(2)}, u32[]{:S(2)}) collective-permute-start(bf16[896,128]{1,0:T(8,128)(2,1)S(1)} %constant_dynamic-update-slice_fusion.block_ref), channel_id=1, source_target_pairs={{0,6},{2,4},{4,2},{6,0},{1,7},{3,5},{5,3},{7,1},{8,14},{10,12},{12... | collective-permute-start | bytes 688136 | tf_op jit(solution)/shard_map/level_sends/ppermute | solution.py:536
  39.3 2.6 %self_blocks.7.keep_ref = f32[768,128]{1,0:T(8,128)S(1)} custom-call(s32[3]{0:T(128)S(1)} %pad_add_fusion.2.ids_ref, f32[384,128]{1,0:T(8,128)S(1)} %get-tuple-element.60.field_ref.own_field, f32[384,128]{1,0:T(8,128)S(1)} %get-tuple-element.53.peer_field, bf16[32,256,128]{2,1,0:T(8,128)(2,1)S(1)} %copy-done, ...), custom_call_target="tpu_custom_call" | custom-call | bytes 7920000 | tf_op jit(solution)/shard_map/self_blocks/pallas_call | solution.py:525
  41.8 1.7 %partner_tables.1 = (bf16[512,512]{1,0:T(8,128)(2,1)S(1)}, bf16[64,64]{1,0:T(8,128)(2,1)S(1)}, bf16[16,256,64]{2,1,0:T(8,128)(2,1)S(1)}) custom-call(s32[4,128]{1,0:T(4,128)S(1)} %fusion.1.own_codes, s32[4,128]{1,0:T(4,128)S(1)} %collective-permute-done.2.peer_codes, bf16[64,32,64]{2,1,0:T(8,128)(2,1)S(1)} %bitcast.37, ...), custom_call_target="tpu_custom_call" | custom-call | bytes 4950000 | tf_op jit(solution)/shard_map/partner_tables/pallas_call | solution.py:525
  44.2 2.8 %coupling_products.5 = bf16[992,128]{1,0:T(8,128)(2,1)S(1)} custom-call(bf16[512,512]{1,0:T(8,128)(2,1)S(1)} %get-tuple-element.62.leaf_table, bf16[64,64]{1,0:T(8,128)(2,1)S(1)} %get-tuple-element.63.parent_table, bf16[16,256,64]{2,1,0:T(8,128)(2,1)S(1)} %get-tuple-element.64.pcouple_ref, bf16[896,128]{1,0:T(8,128)(2,1)S(1)} %collective-permute-done.15.block_ref, ...), custom_call_target="tpu_custom_call" | custom-call | bytes 10560000 | tf_op jit(solution)/shard_map/coupling_products/pallas_call | solution.py:525
  48.1 2.8 %coupling_products.6 = bf16[992,128]{1,0:T(8,128)(2,1)S(1)} custom-call(bf16[512,512]{1,0:T(8,128)(2,1)S(1)} %get-tuple-element.62.leaf_table, bf16[64,64]{1,0:T(8,128)(2,1)S(1)} %get-tuple-element.63.parent_table, bf16[16,256,64]{2,1,0:T(8,128)(2,1)S(1)} %get-tuple-element.64.pcouple_ref, bf16[896,128]{1,0:T(8,128)(2,1)S(1)} %collective-permute-done.17.block_ref, ...), custom_call_target="tpu_custom_call" | custom-call | bytes 10560000 | tf_op jit(solution)/shard_map/coupling_products/pallas_call | solution.py:525
  50.9 2.5 %collective-permute-start.18 = (bf16[992,128]{1,0:T(8,128)(2,1)S(1)}, bf16[992,128]{1,0:T(8,128)(2,1)S(1)}, u32[]{:S(2)}, u32[]{:S(2)}) collective-permute-start(bf16[992,128]{1,0:T(8,128)(2,1)S(1)} %coupling_products.6), channel_id=1, source_target_pairs={{0,4},{2,6},{4,0},{6,2},{1,5},{3,7},{5,1},{7,3},{8,12},{10,14},{12... | collective-permute-start | bytes 761864 | tf_op jit(solution)/shard_map/far_sends/ppermute | solution.py:536
  53.4 2.8 %coupling_products.7 = bf16[224,128]{1,0:T(8,128)(2,1)S(1)} custom-call(bf16[512,512]{1,0:T(8,128)(2,1)S(1)} %get-tuple-element.62.leaf_table, bf16[64,64]{1,0:T(8,128)(2,1)S(1)} %get-tuple-element.63.parent_table, bf16[16,256,64]{2,1,0:T(8,128)(2,1)S(1)} %get-tuple-element.64.pcouple_ref, bf16[896,128]{1,0:T(8,128)(2,1)S(1)} %collective-permute-done.19.block_ref, ...), custom_call_target="tpu_custom_call" | custom-call | bytes 10560000 | tf_op jit(solution)/shard_map/coupling_products/pallas_call | solution.py:525
  56.3 1.5 %collective-permute-start.20 = (bf16[224,128]{1,0:T(8,128)(2,1)S(1)}, bf16[224,128]{1,0:T(8,128)(2,1)S(1)}, u32[]{:S(2)}, u32[]{:S(2)}) collective-permute-start(bf16[224,128]{1,0:T(8,128)(2,1)S(1)} %coupling_products.7), channel_id=1, source_target_pairs={{0,6},{2,4},{4,2},{6,0},{1,7},{3,5},{5,3},{7,1},{8,14},{10,12},{12... | collective-permute-start | bytes 172040 | tf_op jit(solution)/shard_map/far_sends/ppermute | solution.py:536
  57.8 2.8 %coupling_products.4.keep_ref = f32[224,128]{1,0:T(8,128)S(1)} custom-call(bf16[512,512]{1,0:T(8,128)(2,1)S(1)} %get-tuple-element.62.leaf_table, bf16[64,64]{1,0:T(8,128)(2,1)S(1)} %get-tuple-element.63.parent_table, bf16[16,256,64]{2,1,0:T(8,128)(2,1)S(1)} %get-tuple-element.64.pcouple_ref, ...), custom_call_target="tpu_custom_call" | custom-call | bytes 10560000 | tf_op jit(solution)/shard_map/coupling_products/pallas_call | solution.py:525
  60.6 0.8 %collective-permute-done.20.refs_2_ = bf16[224,128]{1,0:T(8,128)(2,1)S(1)} collective-permute-done((bf16[224,128]{1,0:T(8,128)(2,1)S(1)}, bf16[224,128]{1,0:T(8,128)(2,1)S(1)}, u32[]{:S(2)}, u32[]{:S(2)}) %collective-permute-start.20) | collective-permute-done | bytes 57376 | tf_op jit(solution)/shard_map/far_sends/ppermute | solution.py:536
  61.4 1.5 %collective-permute-start.22 = (bf16[768,128]{1,0:T(8,128)(2,1)S(1)}, bf16[768,128]{1,0:T(8,128)(2,1)S(1)}, u32[]{:S(2)}, u32[]{:S(2)}) collective-permute-start(bf16[768,128]{1,0:T(8,128)(2,1)S(1)} %self_blocks.6), channel_id=1, source_target_pairs={{0,6},{2,4},{4,2},{6,0},{1,7},{3,5},{5,3},{7,1},{8,14},{10,12},{12... | collective-permute-start | bytes 589832 | tf_op jit(solution)/shard_map/self_sends/ppermute | solution.py:536
  63.8 0.8 %collective-permute-start.24 = (bf16[192,128]{1,0:T(8,128)(2,1)S(1)}, bf16[192,128]{1,0:T(8,128)(2,1)S(1)}, u32[]{:S(2)}, u32[]{:S(2)}) collective-permute-start(bf16[192,128]{1,0:T(8,128)(2,1)S(1)} %down_products.1.mine_ref), channel_id=1, source_target_pairs={{0,2},{2,0},{4,6},{6,4},{1,3},{3,1},{5,7},{7,5},{8,10},{10,8},{12,... | collective-permute-start | bytes 147464 | tf_op jit(solution)/shard_map/far_coeff_sends/ppermute | solution.py:536
  64.6 1.3 %collective-permute-start.26 = (bf16[192,128]{1,0:T(8,128)(2,1)S(1)}, bf16[192,128]{1,0:T(8,128)(2,1)S(1)}, u32[]{:S(2)}, u32[]{:S(2)}) collective-permute-start(bf16[192,128]{1,0:T(8,128)(2,1)S(1)} %down_products.1.mine_ref), channel_id=1, source_target_pairs={{0,4},{2,6},{4,0},{6,2},{1,5},{3,7},{5,1},{7,3},{8,12},{10,14},{12... | collective-permute-start | bytes 147464 | tf_op jit(solution)/shard_map/far_coeff_sends/ppermute | solution.py:536
  65.8 1.5 %collective-permute-start.28 = (bf16[192,128]{1,0:T(8,128)(2,1)S(1)}, bf16[192,128]{1,0:T(8,128)(2,1)S(1)}, u32[]{:S(2)}, u32[]{:S(2)}) collective-permute-start(bf16[192,128]{1,0:T(8,128)(2,1)S(1)} %down_products.1.mine_ref), channel_id=1, source_target_pairs={{0,6},{2,4},{4,2},{6,0},{1,7},{3,5},{5,3},{7,1},{8,14},{10,12},{12... | collective-permute-start | bytes 147464 | tf_op jit(solution)/shard_map/far_coeff_sends/ppermute | solution.py:536
  69.5 1.3 %collective-permute-done.28.refs_3_ = bf16[192,128]{1,0:T(8,128)(2,1)S(1)} collective-permute-done((bf16[192,128]{1,0:T(8,128)(2,1)S(1)}, bf16[192,128]{1,0:T(8,128)(2,1)S(1)}, u32[]{:S(2)}, u32[]{:S(2)}) %collective-permute-start.28) | collective-permute-done | bytes 49184 | tf_op jit(solution)/shard_map/far_coeff_sends/ppermute | solution.py:536
  72.1 1.8 %column_products.1 = bf16[32,24,128]{2,1,0:T(8,128)(2,1)} custom-call(s32[3]{0:T(128)S(1)} %pad_add_fusion.2.ids_ref, bf16[64,32,128]{2,1,0:T(8,128)(2,1)S(1)} %copy-done.1, f32[384,128]{1,0:T(8,128)S(1)} %get-tuple-element.69.near_mine, bf16[384,128]{1,0:T(8,128)(2,1)S(1)} %collective-permute-done.23.near_peer, ...), custom_call_target="tpu_custom_call" | custom-call | bytes 6105000 | tf_op jit(solution)/shard_map/column_products/pallas_call | solution.py:525
  (71 shorter events, 11.5 us)
Async XLA Ops:
  0.0 13.0 %collective-permute-start.1 = (bf16[32,64,128]{2,1,0:T(8,128)(2,1)}, bf16[32,64,128]{2,1,0:T(8,128)(2,1)S(1)}, u32[]{:S(2)}, u32[]{:S(2)}) collective-permute-start(bf16[32,64,128]{2,1,0:T(8,128)(2,1)} %basis_ref.1), channel_id=1, source_target_pairs={{0,1},{1,0},{2,3},{3,2},{4,5},{5,4},{6,7},{7,6},{8,9},{9,8},{10,11... | collective-permute-start | bytes 1572872 | tf_op jit(solution)/shard_map/swap_row_basis/ppermute | solution.py:536
  0.5 21.2 %collective-permute-start.9 = (bf16[32,256,128]{2,1,0:T(8,128)(2,1)}, bf16[32,256,128]{2,1,0:T(8,128)(2,1)S(1)}, u32[]{:S(2)}, u32[]{:S(2)}) collective-permute-start(bf16[32,256,128]{2,1,0:T(8,128)(2,1)} %own_ref.7), channel_id=1, source_target_pairs={{0,1},{1,0},{2,3},{3,2},{4,5},{5,4},{6,7},{7,6},{8,9},{9,8},{10,11... | collective-permute-start | bytes 6291464 | tf_op jit(solution)/shard_map/swap_self_blocks/ppermute | solution.py:536
  2.5 5.7 %collective-permute-start = (bf16[192,128]{1,0:T(8,128)(2,1)S(1)}, bf16[192,128]{1,0:T(8,128)(2,1)S(1)}, u32[]{:S(2)}, u32[]{:S(2)}) collective-permute-start(bf16[192,128]{1,0:T(8,128)(2,1)S(1)} %get-tuple-element.74), channel_id=1, source_target_pairs={{0,8},{8,0},{16,24},{24,16},{1,9},{9,1},{17,25},{25,17},{2,10},{10... | collective-permute-start | bytes 147464 | tf_op jit(solution)/shard_map/regroup_sends/ppermute | solution.py:536
  5.6 7.4 %collective-permute-start.3 = (bf16[192,128]{1,0:T(8,128)(2,1)S(1)}, bf16[192,128]{1,0:T(8,128)(2,1)S(1)}, u32[]{:S(2)}, u32[]{:S(2)}) collective-permute-start(bf16[192,128]{1,0:T(8,128)(2,1)S(1)} %get-tuple-element.72), channel_id=1, source_target_pairs={{0,16},{8,24},{16,0},{24,8},{1,17},{9,25},{17,1},{25,9},{2,18},{10... | collective-permute-start | bytes 147464 | tf_op jit(solution)/shard_map/regroup_sends/ppermute | solution.py:536
  8.2 5.9 %collective-permute-start.4 = (bf16[192,128]{1,0:T(8,128)(2,1)S(1)}, bf16[192,128]{1,0:T(8,128)(2,1)S(1)}, u32[]{:S(2)}, u32[]{:S(2)}) collective-permute-start(bf16[192,128]{1,0:T(8,128)(2,1)S(1)} %get-tuple-element.71), channel_id=1, source_target_pairs={{0,24},{8,16},{16,8},{24,0},{1,25},{9,17},{17,9},{25,1},{2,26},{10... | collective-permute-start | bytes 147464 | tf_op jit(solution)/shard_map/regroup_sends/ppermute | solution.py:536
  9.0 4.0 %collective-permute-start.2 = (s32[4,128]{1,0:T(4,128)S(1)}, s32[4,128]{1,0:T(4,128)S(1)}, u32[]{:S(2)}, u32[]{:S(2)}) collective-permute-start(s32[4,128]{1,0:T(4,128)S(1)} %fusion.1.own_codes), channel_id=1, source_target_pairs={{0,1},{1,0},{2,3},{3,2},{4,5},{5,4},{6,7},{7,6},{8,9},{9,8},{10,11... | collective-permute-start | bytes 6152 | tf_op jit(solution)/shard_map/partner_codes/ppermute | solution.py:536
  12.9 8.7 %copy-start = (bf16[32,256,128]{2,1,0:T(8,128)(2,1)S(1)}, bf16[32,256,128]{2,1,0:T(8,128)(2,1)}, u32[]{:S(2)}) copy-start(bf16[32,256,128]{2,1,0:T(8,128)(2,1)} %own_ref.7) | copy-start | bytes 6291460
  14.4 1.6 %collective-permute-start.5 = (bf16[384,128]{1,0:T(8,128)(2,1)S(1)}, bf16[384,128]{1,0:T(8,128)(2,1)S(1)}, u32[]{:S(2)}, u32[]{:S(2)}) collective-permute-start(bf16[384,128]{1,0:T(8,128)(2,1)S(1)} %get-tuple-element.47), channel_id=1, source_target_pairs={{0,1},{1,0},{2,3},{3,2},{4,5},{5,4},{6,7},{7,6},{8,9},{9,8},{10,11... | collective-permute-start | bytes 294920 | tf_op jit(solution)/shard_map/swap_field/ppermute | solution.py:536
  17.6 26.6 %collective-permute-start.14 = (bf16[2,64,64,128]{3,2,1,0:T(8,128)(2,1)S(1)}, bf16[2,64,64,128]{3,2,1,0:T(8,128)(2,1)S(1)}, u32[]{:S(2)}, u32[]{:S(2)}) collective-permute-start(bf16[2,64,64,128]{3,2,1,0:T(8,128)(2,1)S(1)} %bitcast.31), channel_id=1, source_target_pairs={{0,1},{1,0},{2,3},{3,2},{4,5},{5,4},{6,7},{7,6},{8,9},{9,8},{10,11... | collective-permute-start | bytes 6291464 | tf_op jit(solution)/shard_map/swap_coupling/ppermute | solution.py:536
  18.2 6.1 %collective-permute-start.6 = (bf16[192,128]{1,0:T(8,128)(2,1)S(1)}, bf16[192,128]{1,0:T(8,128)(2,1)S(1)}, u32[]{:S(2)}, u32[]{:S(2)}) collective-permute-start(bf16[192,128]{1,0:T(8,128)(2,1)S(1)} %get-tuple-element.49), channel_id=1, source_target_pairs={{0,6},{2,4},{4,2},{6,0},{1,7},{3,5},{5,3},{7,1},{8,14},{10,12},{12... | collective-permute-start | bytes 147464 | tf_op jit(solution)/shard_map/coeff_sends/ppermute | solution.py:536
  20.6 4.1 %collective-permute-start.7 = (bf16[192,128]{1,0:T(8,128)(2,1)S(1)}, bf16[192,128]{1,0:T(8,128)(2,1)S(1)}, u32[]{:S(2)}, u32[]{:S(2)}) collective-permute-start(bf16[192,128]{1,0:T(8,128)(2,1)S(1)} %get-tuple-element.50), channel_id=1, source_target_pairs={{0,4},{2,6},{4,0},{6,2},{1,5},{3,7},{5,1},{7,3},{8,12},{10,14},{12... | collective-permute-start | bytes 147464 | tf_op jit(solution)/shard_map/coeff_sends/ppermute | solution.py:536
  21.1 4.1 %collective-permute-start.8 = (bf16[192,128]{1,0:T(8,128)(2,1)S(1)}, bf16[192,128]{1,0:T(8,128)(2,1)S(1)}, u32[]{:S(2)}, u32[]{:S(2)}) collective-permute-start(bf16[192,128]{1,0:T(8,128)(2,1)S(1)} %get-tuple-element.51), channel_id=1, source_target_pairs={{0,2},{2,0},{4,6},{6,4},{1,3},{3,1},{5,7},{7,5},{8,10},{10,8},{12,... | collective-permute-start | bytes 147464 | tf_op jit(solution)/shard_map/coeff_sends/ppermute | solution.py:536
  21.7 8.8 %copy-start.5 = (bf16[64,64,1,2,16]{1,4,3,2,0:T(8,128)(2,1)S(1)}, bf16[64,64,1,2,16]{1,4,3,2,0:T(8,128)(2,1)}, u32[]{:S(2)}) copy-start(bf16[64,64,1,2,16]{1,4,3,2,0:T(8,128)(2,1)} %param.19) | copy-start | bytes 786436
  26.0 9.6 %collective-permute-start.10 = (bf16[224,128]{1,0:T(8,128)(2,1)S(1)}, bf16[224,128]{1,0:T(8,128)(2,1)S(1)}, u32[]{:S(2)}, u32[]{:S(2)}) collective-permute-start(bf16[224,128]{1,0:T(8,128)(2,1)S(1)} %parent_coeffs.1), channel_id=1, source_target_pairs={{0,8},{8,0},{16,24},{24,16},{1,9},{9,1},{17,25},{25,17},{2,10},{10... | collective-permute-start | bytes 172040 | tf_op jit(solution)/shard_map/owner_sends/ppermute | solution.py:536
  26.5 9.1 %collective-permute-start.11 = (bf16[224,128]{1,0:T(8,128)(2,1)S(1)}, bf16[224,128]{1,0:T(8,128)(2,1)S(1)}, u32[]{:S(2)}, u32[]{:S(2)}) collective-permute-start(bf16[224,128]{1,0:T(8,128)(2,1)S(1)} %parent_coeffs.1), channel_id=1, source_target_pairs={{0,16},{8,24},{16,0},{24,8},{1,17},{9,25},{17,1},{25,9},{2,18},{10... | collective-permute-start | bytes 172040 | tf_op jit(solution)/shard_map/owner_sends/ppermute | solution.py:536
  29.7 6.0 %collective-permute-start.12 = (bf16[224,128]{1,0:T(8,128)(2,1)S(1)}, bf16[224,128]{1,0:T(8,128)(2,1)S(1)}, u32[]{:S(2)}, u32[]{:S(2)}) collective-permute-start(bf16[224,128]{1,0:T(8,128)(2,1)S(1)} %parent_coeffs.1), channel_id=1, source_target_pairs={{0,24},{8,16},{16,8},{24,0},{1,25},{9,17},{17,9},{25,1},{2,26},{10... | collective-permute-start | bytes 172040 | tf_op jit(solution)/shard_map/owner_sends/ppermute | solution.py:536
  30.4 11.4 %collective-permute-start.13 = (bf16[64,32,64]{2,1,0:T(8,128)(2,1)S(1)}, bf16[64,32,64]{2,1,0:T(8,128)(2,1)S(1)}, u32[]{:S(2)}, u32[]{:S(2)}) collective-permute-start(bf16[64,32,64]{2,1,0:T(8,128)(2,1)S(1)} %bitcast.36), channel_id=1, source_target_pairs={{0,1},{1,0},{2,3},{3,2},{4,5},{5,4},{6,7},{7,6},{8,9},{9,8},{10,11... | collective-permute-start | bytes 786440 | tf_op jit(solution)/shard_map/swap_parent_coupling/ppermute | solution.py:536
  35.7 8.5 %collective-permute-start.15 = (bf16[896,128]{1,0:T(8,128)(2,1)S(1)}, bf16[896,128]{1,0:T(8,128)(2,1)S(1)}, u32[]{:S(2)}, u32[]{:S(2)}) collective-permute-start(bf16[896,128]{1,0:T(8,128)(2,1)S(1)} %constant_dynamic-update-slice_fusion.block_ref), channel_id=1, source_target_pairs={{0,2},{2,0},{4,6},{6,4},{1,3},{3,1},{5,7},{7,5},{8,10},{10,8},{12,... | collective-permute-start | bytes 688136 | tf_op jit(solution)/shard_map/level_sends/ppermute | solution.py:536
  36.4 11.7 %collective-permute-start.17 = (bf16[896,128]{1,0:T(8,128)(2,1)S(1)}, bf16[896,128]{1,0:T(8,128)(2,1)S(1)}, u32[]{:S(2)}, u32[]{:S(2)}) collective-permute-start(bf16[896,128]{1,0:T(8,128)(2,1)S(1)} %constant_dynamic-update-slice_fusion.block_ref), channel_id=1, source_target_pairs={{0,4},{2,6},{4,0},{6,2},{1,5},{3,7},{5,1},{7,3},{8,12},{10,14},{12... | collective-permute-start | bytes 688136 | tf_op jit(solution)/shard_map/level_sends/ppermute | solution.py:536
  37.9 15.6 %collective-permute-start.19 = (bf16[896,128]{1,0:T(8,128)(2,1)S(1)}, bf16[896,128]{1,0:T(8,128)(2,1)S(1)}, u32[]{:S(2)}, u32[]{:S(2)}) collective-permute-start(bf16[896,128]{1,0:T(8,128)(2,1)S(1)} %constant_dynamic-update-slice_fusion.block_ref), channel_id=1, source_target_pairs={{0,6},{2,4},{4,2},{6,0},{1,7},{3,5},{5,3},{7,1},{8,14},{10,12},{12... | collective-permute-start | bytes 688136 | tf_op jit(solution)/shard_map/level_sends/ppermute | solution.py:536
  47.0 15.9 %collective-permute-start.16 = (bf16[992,128]{1,0:T(8,128)(2,1)S(1)}, bf16[992,128]{1,0:T(8,128)(2,1)S(1)}, u32[]{:S(2)}, u32[]{:S(2)}) collective-permute-start(bf16[992,128]{1,0:T(8,128)(2,1)S(1)} %coupling_products.5), channel_id=1, source_target_pairs={{0,2},{2,0},{4,6},{6,4},{1,3},{3,1},{5,7},{7,5},{8,10},{10,8},{12,... | collective-permute-start | bytes 761864 | tf_op jit(solution)/shard_map/far_sends/ppermute | solution.py:536
  50.9 12.0 %collective-permute-start.18 = (bf16[992,128]{1,0:T(8,128)(2,1)S(1)}, bf16[992,128]{1,0:T(8,128)(2,1)S(1)}, u32[]{:S(2)}, u32[]{:S(2)}) collective-permute-start(bf16[992,128]{1,0:T(8,128)(2,1)S(1)} %coupling_products.6), channel_id=1, source_target_pairs={{0,4},{2,6},{4,0},{6,2},{1,5},{3,7},{5,1},{7,3},{8,12},{10,14},{12... | collective-permute-start | bytes 761864 | tf_op jit(solution)/shard_map/far_sends/ppermute | solution.py:536
  56.3 5.1 %collective-permute-start.20 = (bf16[224,128]{1,0:T(8,128)(2,1)S(1)}, bf16[224,128]{1,0:T(8,128)(2,1)S(1)}, u32[]{:S(2)}, u32[]{:S(2)}) collective-permute-start(bf16[224,128]{1,0:T(8,128)(2,1)S(1)} %coupling_products.7), channel_id=1, source_target_pairs={{0,6},{2,4},{4,2},{6,0},{1,7},{3,5},{5,3},{7,1},{8,14},{10,12},{12... | collective-permute-start | bytes 172040 | tf_op jit(solution)/shard_map/far_sends/ppermute | solution.py:536
  61.4 6.8 %collective-permute-start.22 = (bf16[768,128]{1,0:T(8,128)(2,1)S(1)}, bf16[768,128]{1,0:T(8,128)(2,1)S(1)}, u32[]{:S(2)}, u32[]{:S(2)}) collective-permute-start(bf16[768,128]{1,0:T(8,128)(2,1)S(1)} %self_blocks.6), channel_id=1, source_target_pairs={{0,6},{2,4},{4,2},{6,0},{1,7},{3,5},{5,3},{7,1},{8,14},{10,12},{12... | collective-permute-start | bytes 589832 | tf_op jit(solution)/shard_map/self_sends/ppermute | solution.py:536
  63.7 3.6 %collective-permute-start.21 = (bf16[192,128]{1,0:T(8,128)(2,1)S(1)}, bf16[192,128]{1,0:T(8,128)(2,1)S(1)}, u32[]{:S(2)}, u32[]{:S(2)}) collective-permute-start(bf16[192,128]{1,0:T(8,128)(2,1)S(1)} %down_products.1.mine_ref), channel_id=1, source_target_pairs={{0,1},{1,0},{2,3},{3,2},{4,5},{5,4},{6,7},{7,6},{8,9},{9,8},{10,11... | collective-permute-start | bytes 147464 | tf_op jit(solution)/shard_map/far_coeff_sends/ppermute | solution.py:536
  63.8 5.1 %collective-permute-start.24 = (bf16[192,128]{1,0:T(8,128)(2,1)S(1)}, bf16[192,128]{1,0:T(8,128)(2,1)S(1)}, u32[]{:S(2)}, u32[]{:S(2)}) collective-permute-start(bf16[192,128]{1,0:T(8,128)(2,1)S(1)} %down_products.1.mine_ref), channel_id=1, source_target_pairs={{0,2},{2,0},{4,6},{6,4},{1,3},{3,1},{5,7},{7,5},{8,10},{10,8},{12,... | collective-permute-start | bytes 147464 | tf_op jit(solution)/shard_map/far_coeff_sends/ppermute | solution.py:536
  64.6 4.8 %collective-permute-start.26 = (bf16[192,128]{1,0:T(8,128)(2,1)S(1)}, bf16[192,128]{1,0:T(8,128)(2,1)S(1)}, u32[]{:S(2)}, u32[]{:S(2)}) collective-permute-start(bf16[192,128]{1,0:T(8,128)(2,1)S(1)} %down_products.1.mine_ref), channel_id=1, source_target_pairs={{0,4},{2,6},{4,0},{6,2},{1,5},{3,7},{5,1},{7,3},{8,12},{10,14},{12... | collective-permute-start | bytes 147464 | tf_op jit(solution)/shard_map/far_coeff_sends/ppermute | solution.py:536
  65.8 5.0 %collective-permute-start.28 = (bf16[192,128]{1,0:T(8,128)(2,1)S(1)}, bf16[192,128]{1,0:T(8,128)(2,1)S(1)}, u32[]{:S(2)}, u32[]{:S(2)}) collective-permute-start(bf16[192,128]{1,0:T(8,128)(2,1)S(1)} %down_products.1.mine_ref), channel_id=1, source_target_pairs={{0,6},{2,4},{4,2},{6,0},{1,7},{3,5},{5,3},{7,1},{8,14},{10,12},{12... | collective-permute-start | bytes 147464 | tf_op jit(solution)/shard_map/far_coeff_sends/ppermute | solution.py:536
  68.8 3.2 %collective-permute-start.23 = (bf16[384,128]{1,0:T(8,128)(2,1)S(1)}, bf16[384,128]{1,0:T(8,128)(2,1)S(1)}, u32[]{:S(2)}, u32[]{:S(2)}) collective-permute-start(bf16[384,128]{1,0:T(8,128)(2,1)S(1)} %get-tuple-element.70), channel_id=1, source_target_pairs={{0,1},{1,0},{2,3},{3,2},{4,5},{5,4},{6,7},{7,6},{8,9},{9,8},{10,11... | collective-permute-start | bytes 294920 | tf_op jit(solution)/shard_map/swap_self_sums/ppermute | solution.py:536
  68.9 1.9 %collective-permute-start.25 = (bf16[192,128]{1,0:T(8,128)(2,1)S(1)}, bf16[192,128]{1,0:T(8,128)(2,1)S(1)}, u32[]{:S(2)}, u32[]{:S(2)}) collective-permute-start(bf16[192,128]{1,0:T(8,128)(2,1)S(1)} %collective-permute-done.24.mine_ref), channel_id=1, source_target_pairs={{0,1},{1,0},{2,3},{3,2},{4,5},{5,4},{6,7},{7,6},{8,9},{9,8},{10,11... | collective-permute-start | bytes 147464 | tf_op jit(solution)/shard_map/far_coeff_sends/ppermute | solution.py:536
  69.4 1.9 %collective-permute-start.27 = (bf16[192,128]{1,0:T(8,128)(2,1)S(1)}, bf16[192,128]{1,0:T(8,128)(2,1)S(1)}, u32[]{:S(2)}, u32[]{:S(2)}) collective-permute-start(bf16[192,128]{1,0:T(8,128)(2,1)S(1)} %collective-permute-done.26.mine_ref), channel_id=1, source_target_pairs={{0,1},{1,0},{2,3},{3,2},{4,5},{5,4},{6,7},{7,6},{8,9},{9,8},{10,11... | collective-permute-start | bytes 147464 | tf_op jit(solution)/shard_map/far_coeff_sends/ppermute | solution.py:536
  70.8 1.2 %collective-permute-start.29 = (bf16[192,128]{1,0:T(8,128)(2,1)S(1)}, bf16[192,128]{1,0:T(8,128)(2,1)S(1)}, u32[]{:S(2)}, u32[]{:S(2)}) collective-permute-start(bf16[192,128]{1,0:T(8,128)(2,1)S(1)} %collective-permute-done.28.refs_3_), channel_id=1, source_target_pairs={{0,1},{1,0},{2,3},{3,2},{4,5},{5,4},{6,7},{7,6},{8,9},{9,8},{10,11... | collective-permute-start | bytes 147464 | tf_op jit(solution)/shard_map/far_coeff_sends/ppermute | solution.py:536
  (4 other events, 20.7 us)

commit v6 on v5

--- a/solution.py
+++ b/solution.py
@@ -431,30 +431,30 @@
     send_ref[...] = summed((1 - parity) * count).astype(BF16)
 
 
-def column_kernel(vs, column_ref, mine_ref, other_ref, out_ref, rows_scr):
+def column_kernel(vs, column_ref, *refs):
+    blocks, out_ref, rows_scr = refs[:-2], refs[-2], refs[-1]
     rank_width, voxels, leaves = column_ref.shape
-    rows_scr[0] = mine_ref[...].astype(F32)
-    rows_scr[1] = other_ref[...].astype(F32)
+    for b, ref in enumerate(blocks):
+        rows_scr[b] = ref[...].astype(F32)
+    count = len(blocks) * vs
     accs = mac_rows(
         rank_width,
         lambda k: column_ref[k].astype(F32),
         lambda k, n: rows_scr[n // vs, pl.ds((n % vs) * rank_width + k, 1), :],
-        [jnp.zeros((voxels, leaves), F32) for _ in range(2 * vs)],
+        [jnp.zeros((voxels, leaves), F32) for _ in range(count)],
         8,
     )
-    for n in range(2 * vs):
+    for n in range(count):
         out_ref[n * voxels : (n + 1) * voxels, :] = accs[n]
 
 
 def out_kernel(lvls, vh, vs, early, ids_ref, column_ref, near_mine, near_peer, *refs):
-    done, blocks = refs[:early], refs[early : -3]
+    done, last_mine, last_other = refs[:early], refs[early], refs[early + 1]
     out_ref, rows_scr, out_scr = refs[-3:]
     rank_width, voxels, leaves = column_ref.shape
     vectors = out_ref.shape[1]
     lvl, parity = ids_ref[1], ids_ref[2]
-    late = lvls - early
-    for b, ref in enumerate(blocks):
-        rows_scr[b] = ref[...].astype(F32)
+    rows_scr[...] = last_other[...].astype(F32)
 
     def store(place, rep, value):
         def write():
@@ -471,13 +471,12 @@
         if t < early:
             accs = [done[t][n * voxels : (n + 1) * voxels, :] for n in range(2 * vs)]
         else:
-            accs = mac_rows(
+            accs = [last_mine[n * voxels : (n + 1) * voxels, :] for n in range(vs)]
+            accs += mac_rows(
                 rank_width,
                 lambda k: column_ref[k].astype(F32),
-                lambda k, n: rows_scr[
-                    (n // vs) * late + t - early, pl.ds((n % vs) * rank_width + k, 1), :
-                ],
-                [jnp.zeros((voxels, leaves), F32) for _ in range(2 * vs)],
+                lambda k, n: row_of(rows_scr, n * rank_width + k),
+                [jnp.zeros((voxels, leaves), F32) for _ in range(vs)],
                 8,
             )
         for n in range(2 * vs):
@@ -725,17 +724,19 @@
         far_blocks = [far] + swaps([far] * lvls, "lvl", lvls, True)
         far_others = [other(value) for value in far_blocks]
     early = lvls - 1
-    done = [
-        call(
+
+    def column_part(*blocks):
+        return call(
             "column_products_early",
             functools.partial(column_kernel, vs),
-            (column_basis, far_blocks[t], far_others[t]),
-            sds((2 * vs * slab, leaves), F32),
-            [pltpu.VMEM((2, vs * rank_width, leaves), F32)],
-            0.5,
-        )
-        for t in range(early)
-    ]
+            (column_basis, *blocks),
+            sds((len(blocks) * vs * slab, leaves), F32),
+            [pltpu.VMEM((len(blocks), vs * rank_width, leaves), F32)],
+            0.25 * len(blocks),
+        )
+
+    done = [column_part(far_blocks[t], far_others[t]) for t in range(early)]
+    last_mine = column_part(far_blocks[early])
     near_mine, near_send = call(
         "self_sums",
         functools.partial(near_sum_kernel, block_rows),
@@ -750,11 +751,11 @@
         functools.partial(out_kernel, lvls, vh, vs, early),
         (
             ids, column_basis, near_mine, near_peer, *done,
-            *far_blocks[early:], *far_others[early:],
+            last_mine, far_others[early],
         ),
         sds((slab, vectors, leaves), BF16),
         [
-            pltpu.VMEM((2 * (lvls - early), vs * rank_width, leaves), F32),
+            pltpu.VMEM((vs * rank_width, leaves), F32),
             pltpu.VMEM(((slab + 1) * vectors, leaves), F32),
         ],
         1.85, scalars=1,

time: 74.1 us -> 74.1 us (level)
    pallas_call x21 -> x22, Pallas kernels: 35.9 us -> 36 us  [call(): pl.pallas_call(kernel, out_shape=outs, in_specs=specs, out_specs=jax.tree...]
  transfers between devices with their start and end apart: 30 -> 30, of which waited for: 9 -> 8; matrix products, arithmetic and copies ran while one was open for 4% -> 4% of each run, Pallas kernels for 46% -> 47%
where the time goes in v6:
time: 74.1 us; the launch traced here: 73.8 us
  Pallas kernels  36 us (49%)
  starting transfers between devices  28.7 us (39%)
  waiting for transfers between devices  5.55 us (7%)
  local copies, waits for them, and re-layouts  2.26 us (3%)
  other arithmetic  0.89 us (1%)
    pallas_call x22, Pallas kernels, call(): pl.pallas_call(kernel, out_shape=outs, in_specs=specs, out_specs=jax.tree...  36 us
    ppermute x30, starting transfers between devices, swap(): return lax.ppermute(value, axis, [(i, i ^ step) for i in range(count)])  28.7 us
    ppermute x30, waiting for transfers between devices, swap(): return lax.ppermute(value, axis, [(i, i ^ step) for i in range(count)])  5.55 us
    optimization_barrier x1, local copies, waits for them, and re-layouts, after(): return lax.optimization_barrier((value,) + others)[0]  2.17 us
  transfers between devices with their start and end apart: 30, of which 8 were waited for; matrix products, arithmetic and copies ran while one was open for 4% of the time, Pallas kernels for 47%

profile of v6, /device:TPU:0, one launch (start us, length us, event | category | flops | bytes accessed | tf_op | source)
XLA Modules:
  0.0 73.8 jit_solution(9375898633406617559)
XLA Ops:
  0.6 1.8 %pack_field.1 = bf16[4,192,128]{2,1,0:T(8,128)(2,1)S(1)} custom-call(s32[3]{0:T(128)S(1)} %pad_add_fusion.2.ids_ref, s32[64]{0:T(128)} %perm_any.3, bf16[32,24,128]{2,1,0:T(8,128)(2,1)} %own_any.1), custom_call_target="tpu_custom_call" | custom-call | bytes 3300000 | tf_op jit(solution)/shard_map/pack_field/pallas_call | solution.py:524
  2.5 3.1 %collective-permute-start = (bf16[192,128]{1,0:T(8,128)(2,1)S(1)}, bf16[192,128]{1,0:T(8,128)(2,1)S(1)}, u32[]{:S(2)}, u32[]{:S(2)}) collective-permute-start(bf16[192,128]{1,0:T(8,128)(2,1)S(1)} %get-tuple-element.74), channel_id=1, source_target_pairs={{0,8},{8,0},{16,24},{24,16},{1,9},{9,1},{17,25},{25,17},{2,10},{10... | collective-permute-start | bytes 147464 | tf_op jit(solution)/shard_map/regroup_sends/ppermute | solution.py:535
  5.6 2.6 %collective-permute-start.3 = (bf16[192,128]{1,0:T(8,128)(2,1)S(1)}, bf16[192,128]{1,0:T(8,128)(2,1)S(1)}, u32[]{:S(2)}, u32[]{:S(2)}) collective-permute-start(bf16[192,128]{1,0:T(8,128)(2,1)S(1)} %get-tuple-element.72), channel_id=1, source_target_pairs={{0,16},{8,24},{16,0},{24,8},{1,17},{9,25},{17,1},{25,9},{2,18},{10... | collective-permute-start | bytes 147464 | tf_op jit(solution)/shard_map/regroup_sends/ppermute | solution.py:535
  8.2 0.8 %fusion.1.own_codes = s32[4,128]{1,0:T(4,128)S(1)} fusion(s32[2,16]{1,0:T(2,128)} %bitcast.38, s32[2,16]{1,0:T(2,128)} %bitcast.39, s32[2,128]{1,0:T(2,128)} %bitcast.40, s32[2,128]{1,0:T(2,128)} %bitcast.41, s32[4]{0:T(128)S(1)} %get-tuple-element.75, s32[]{:T(128)} %axis_index.33, s32[128]{0:T(128)} %param.27, s32[4]{0:T(128)S(1)} %get-tuple-element.76, ...), kind=kLoop, calls=%fused_computation.11 | loop fusion | flops 4096 | bytes 4904 | tf_op jit(solution)/shard_map/partner_codes/jit(_where)/select_n | solution.py:603
  9.0 1.7 %place_codes.1.code_ref = s32[8,128]{1,0:T(8,128)S(1)} custom-call(s32[3]{0:T(128)S(1)} %pad_add_fusion.2.ids_ref, s32[64]{0:T(128)} %perm_any.3), custom_call_target="tpu_custom_call" | custom-call | bytes 990000 | tf_op jit(solution)/shard_map/place_codes/pallas_call | solution.py:524
  10.8 2.2 %copy.17 = bf16[64,64,1,2,128]{4,1,0,3,2:T(8,128)(2,1)S(1)} copy(bf16[64,64,1,2,128]{4,3,2,1,0:T(2,128)(2,1)} %param.18) | data formatting | bytes 4194304 | tf_op jit(solution)/shard_map/coupling_layout/optimization_barrier | solution.py:493
  13.0 1.1 %collective-permute-done.4.refs_3_ = bf16[192,128]{1,0:T(8,128)(2,1)S(1)} collective-permute-done((bf16[192,128]{1,0:T(8,128)(2,1)S(1)}, bf16[192,128]{1,0:T(8,128)(2,1)S(1)}, u32[]{:S(2)}, u32[]{:S(2)}) %collective-permute-start.4) | collective-permute-done | bytes 49184 | tf_op jit(solution)/shard_map/regroup_sends/ppermute | solution.py:535
  14.5 1.5 %coeffs_own_slab.1.own_ref = f32[768,128]{1,0:T(8,128)S(1)} custom-call(s32[3]{0:T(128)S(1)} %pad_add_fusion.2.ids_ref, bf16[32,64,128]{2,1,0:T(8,128)(2,1)S(1)} %copy-done.4, f32[384,128]{1,0:T(8,128)S(1)} %get-tuple-element.60.field_ref.own_field), custom_call_target="tpu_custom_call" | custom-call | bytes 5280000 | tf_op jit(solution)/shard_map/coeffs_own_slab/pallas_call | solution.py:524
  16.0 1.6 %coeffs_other_slab.1 = (f32[384,128]{1,0:T(8,128)S(1)}, f32[192,128]{1,0:T(8,128)S(1)}, bf16[192,128]{1,0:T(8,128)(2,1)S(1)}, bf16[192,128]{1,0:T(8,128)(2,1)S(1)}, bf16[192,128]{1,0:T(8,128)(2,1)S(1)}) custom-call(s32[3]{0:T(128)S(1)} %pad_add_fusion.2.ids_ref, bf16[32,64,128]{2,1,0:T(8,128)(2,1)S(1)} %collective-permute-done.1.basis_ref, ...), custom_call_target="tpu_custom_call" | custom-call | bytes 5280000 | tf_op jit(solution)/shard_map/coeffs_other_slab/pallas_call | solution.py:524
  18.2 2.4 %collective-permute-start.6 = (bf16[192,128]{1,0:T(8,128)(2,1)S(1)}, bf16[192,128]{1,0:T(8,128)(2,1)S(1)}, u32[]{:S(2)}, u32[]{:S(2)}) collective-permute-start(bf16[192,128]{1,0:T(8,128)(2,1)S(1)} %get-tuple-element.49), channel_id=1, source_target_pairs={{0,6},{2,4},{4,2},{6,0},{1,7},{3,5},{5,3},{7,1},{8,14},{10,12},{12... | collective-permute-start | bytes 147464 | tf_op jit(solution)/shard_map/coeff_sends/ppermute | solution.py:535
  21.7 2.6 %self_blocks.4.refs_0_ = bf16[768,128]{1,0:T(8,128)(2,1)S(1)} custom-call(s32[3]{0:T(128)S(1)} %pad_add_fusion.2.ids_ref, f32[384,128]{1,0:T(8,128)S(1)} %get-tuple-element.60.field_ref.own_field, f32[384,128]{1,0:T(8,128)S(1)} %get-tuple-element.53.peer_field, bf16[32,256,128]{2,1,0:T(8,128)(2,1)S(1)} %copy-done, ...), custom_call_target="tpu_custom_call" | custom-call | bytes 7920000 | tf_op jit(solution)/shard_map/self_blocks/pallas_call | solution.py:524
  25.2 0.8 %parent_coeffs.1 = bf16[224,128]{1,0:T(8,128)(2,1)S(1)} custom-call(f32[192,128]{1,0:T(8,128)S(1)} %get-tuple-element.48.keep_ref, bf16[192,128]{1,0:T(8,128)(2,1)S(1)} %collective-permute-done.6.refs_0_, bf16[192,128]{1,0:T(8,128)(2,1)S(1)} %collective-permute-done.7.refs_1_, bf16[192,128]{1,0:T(8,128)(2,1)S(1)} %collective-permute-done.8.refs_2_, ...), custom_call_target="tpu_custom_call" | custom-call | bytes 2640000 | tf_op jit(solution)/shard_map/parent_coeffs/pallas_call | solution.py:524
  26.5 3.1 %collective-permute-start.11 = (bf16[224,128]{1,0:T(8,128)(2,1)S(1)}, bf16[224,128]{1,0:T(8,128)(2,1)S(1)}, u32[]{:S(2)}, u32[]{:S(2)}) collective-permute-start(bf16[224,128]{1,0:T(8,128)(2,1)S(1)} %parent_coeffs.1), channel_id=1, source_target_pairs={{0,16},{8,24},{16,0},{24,8},{1,17},{9,25},{17,1},{25,9},{2,18},{10... | collective-permute-start | bytes 172040 | tf_op jit(solution)/shard_map/owner_sends/ppermute | solution.py:535
  29.7 0.8 %collective-permute-start.12 = (bf16[224,128]{1,0:T(8,128)(2,1)S(1)}, bf16[224,128]{1,0:T(8,128)(2,1)S(1)}, u32[]{:S(2)}, u32[]{:S(2)}) collective-permute-start(bf16[224,128]{1,0:T(8,128)(2,1)S(1)} %parent_coeffs.1), channel_id=1, source_target_pairs={{0,24},{8,16},{16,8},{24,0},{1,25},{9,17},{17,9},{25,1},{2,26},{10... | collective-permute-start | bytes 172040 | tf_op jit(solution)/shard_map/owner_sends/ppermute | solution.py:535
  30.5 2.6 %self_blocks.5.refs_0_ = bf16[768,128]{1,0:T(8,128)(2,1)S(1)} custom-call(s32[3]{0:T(128)S(1)} %pad_add_fusion.2.ids_ref, f32[384,128]{1,0:T(8,128)S(1)} %get-tuple-element.60.field_ref.own_field, f32[384,128]{1,0:T(8,128)S(1)} %get-tuple-element.53.peer_field, bf16[32,256,128]{2,1,0:T(8,128)(2,1)S(1)} %copy-done, ...), custom_call_target="tpu_custom_call" | custom-call | bytes 7920000 | tf_op jit(solution)/shard_map/self_blocks/pallas_call | solution.py:524
  33.0 2.6 %self_blocks.6 = bf16[768,128]{1,0:T(8,128)(2,1)S(1)} custom-call(s32[3]{0:T(128)S(1)} %pad_add_fusion.2.ids_ref, f32[384,128]{1,0:T(8,128)S(1)} %get-tuple-element.60.field_ref.own_field, f32[384,128]{1,0:T(8,128)S(1)} %get-tuple-element.53.peer_field, bf16[32,256,128]{2,1,0:T(8,128)(2,1)S(1)} %copy-done, ...), custom_call_target="tpu_custom_call" | custom-call | bytes 7920000 | tf_op jit(solution)/shard_map/self_blocks/pallas_call | solution.py:524
  36.4 1.5 %collective-permute-start.17 = (bf16[896,128]{1,0:T(8,128)(2,1)S(1)}, bf16[896,128]{1,0:T(8,128)(2,1)S(1)}, u32[]{:S(2)}, u32[]{:S(2)}) collective-permute-start(bf16[896,128]{1,0:T(8,128)(2,1)S(1)} %constant_dynamic-update-slice_fusion.block_ref), channel_id=1, source_target_pairs={{0,4},{2,6},{4,0},{6,2},{1,5},{3,7},{5,1},{7,3},{8,12},{10,14},{12... | collective-permute-start | bytes 688136 | tf_op jit(solution)/shard_map/level_sends/ppermute | solution.py:535
  37.9 1.4 %collective-permute-start.19 = (bf16[896,128]{1,0:T(8,128)(2,1)S(1)}, bf16[896,128]{1,0:T(8,128)(2,1)S(1)}, u32[]{:S(2)}, u32[]{:S(2)}) collective-permute-start(bf16[896,128]{1,0:T(8,128)(2,1)S(1)} %constant_dynamic-update-slice_fusion.block_ref), channel_id=1, source_target_pairs={{0,6},{2,4},{4,2},{6,0},{1,7},{3,5},{5,3},{7,1},{8,14},{10,12},{12... | collective-permute-start | bytes 688136 | tf_op jit(solution)/shard_map/level_sends/ppermute | solution.py:535
  39.3 2.6 %self_blocks.7.keep_ref = f32[768,128]{1,0:T(8,128)S(1)} custom-call(s32[3]{0:T(128)S(1)} %pad_add_fusion.2.ids_ref, f32[384,128]{1,0:T(8,128)S(1)} %get-tuple-element.60.field_ref.own_field, f32[384,128]{1,0:T(8,128)S(1)} %get-tuple-element.53.peer_field, bf16[32,256,128]{2,1,0:T(8,128)(2,1)S(1)} %copy-done, ...), custom_call_target="tpu_custom_call" | custom-call | bytes 7920000 | tf_op jit(solution)/shard_map/self_blocks/pallas_call | solution.py:524
  41.8 1.7 %partner_tables.1 = (bf16[512,512]{1,0:T(8,128)(2,1)S(1)}, bf16[64,64]{1,0:T(8,128)(2,1)S(1)}, bf16[16,256,64]{2,1,0:T(8,128)(2,1)S(1)}) custom-call(s32[4,128]{1,0:T(4,128)S(1)} %fusion.1.own_codes, s32[4,128]{1,0:T(4,128)S(1)} %collective-permute-done.2.peer_codes, bf16[64,32,64]{2,1,0:T(8,128)(2,1)S(1)} %bitcast.37, ...), custom_call_target="tpu_custom_call" | custom-call | bytes 4950000 | tf_op jit(solution)/shard_map/partner_tables/pallas_call | solution.py:524
  44.2 2.8 %coupling_products.5 = bf16[992,128]{1,0:T(8,128)(2,1)S(1)} custom-call(bf16[512,512]{1,0:T(8,128)(2,1)S(1)} %get-tuple-element.62.leaf_table, bf16[64,64]{1,0:T(8,128)(2,1)S(1)} %get-tuple-element.63.parent_table, bf16[16,256,64]{2,1,0:T(8,128)(2,1)S(1)} %get-tuple-element.64.pcouple_ref, bf16[896,128]{1,0:T(8,128)(2,1)S(1)} %collective-permute-done.15.block_ref, ...), custom_call_target="tpu_custom_call" | custom-call | bytes 10560000 | tf_op jit(solution)/shard_map/coupling_products/pallas_call | solution.py:524
  48.1 2.8 %coupling_products.6 = bf16[992,128]{1,0:T(8,128)(2,1)S(1)} custom-call(bf16[512,512]{1,0:T(8,128)(2,1)S(1)} %get-tuple-element.62.leaf_table, bf16[64,64]{1,0:T(8,128)(2,1)S(1)} %get-tuple-element.63.parent_table, bf16[16,256,64]{2,1,0:T(8,128)(2,1)S(1)} %get-tuple-element.64.pcouple_ref, bf16[896,128]{1,0:T(8,128)(2,1)S(1)} %collective-permute-done.17.block_ref, ...), custom_call_target="tpu_custom_call" | custom-call | bytes 10560000 | tf_op jit(solution)/shard_map/coupling_products/pallas_call | solution.py:524
  50.9 2.5 %collective-permute-start.18 = (bf16[992,128]{1,0:T(8,128)(2,1)S(1)}, bf16[992,128]{1,0:T(8,128)(2,1)S(1)}, u32[]{:S(2)}, u32[]{:S(2)}) collective-permute-start(bf16[992,128]{1,0:T(8,128)(2,1)S(1)} %coupling_products.6), channel_id=1, source_target_pairs={{0,4},{2,6},{4,0},{6,2},{1,5},{3,7},{5,1},{7,3},{8,12},{10,14},{12... | collective-permute-start | bytes 761864 | tf_op jit(solution)/shard_map/far_sends/ppermute | solution.py:535
  53.4 2.8 %coupling_products.7 = bf16[224,128]{1,0:T(8,128)(2,1)S(1)} custom-call(bf16[512,512]{1,0:T(8,128)(2,1)S(1)} %get-tuple-element.62.leaf_table, bf16[64,64]{1,0:T(8,128)(2,1)S(1)} %get-tuple-element.63.parent_table, bf16[16,256,64]{2,1,0:T(8,128)(2,1)S(1)} %get-tuple-element.64.pcouple_ref, bf16[896,128]{1,0:T(8,128)(2,1)S(1)} %collective-permute-done.19.block_ref, ...), custom_call_target="tpu_custom_call" | custom-call | bytes 10560000 | tf_op jit(solution)/shard_map/coupling_products/pallas_call | solution.py:524
  56.3 1.5 %collective-permute-start.20 = (bf16[224,128]{1,0:T(8,128)(2,1)S(1)}, bf16[224,128]{1,0:T(8,128)(2,1)S(1)}, u32[]{:S(2)}, u32[]{:S(2)}) collective-permute-start(bf16[224,128]{1,0:T(8,128)(2,1)S(1)} %coupling_products.7), channel_id=1, source_target_pairs={{0,6},{2,4},{4,2},{6,0},{1,7},{3,5},{5,3},{7,1},{8,14},{10,12},{12... | collective-permute-start | bytes 172040 | tf_op jit(solution)/shard_map/far_sends/ppermute | solution.py:535
  57.8 2.8 %coupling_products.4.keep_ref = f32[224,128]{1,0:T(8,128)S(1)} custom-call(bf16[512,512]{1,0:T(8,128)(2,1)S(1)} %get-tuple-element.62.leaf_table, bf16[64,64]{1,0:T(8,128)(2,1)S(1)} %get-tuple-element.63.parent_table, bf16[16,256,64]{2,1,0:T(8,128)(2,1)S(1)} %get-tuple-element.64.pcouple_ref, ...), custom_call_target="tpu_custom_call" | custom-call | bytes 10560000 | tf_op jit(solution)/shard_map/coupling_products/pallas_call | solution.py:524
  60.6 0.8 %collective-permute-done.20.refs_2_ = bf16[224,128]{1,0:T(8,128)(2,1)S(1)} collective-permute-done((bf16[224,128]{1,0:T(8,128)(2,1)S(1)}, bf16[224,128]{1,0:T(8,128)(2,1)S(1)}, u32[]{:S(2)}, u32[]{:S(2)}) %collective-permute-start.20) | collective-permute-done | bytes 57376 | tf_op jit(solution)/shard_map/far_sends/ppermute | solution.py:535
  61.4 1.5 %collective-permute-start.22 = (bf16[768,128]{1,0:T(8,128)(2,1)S(1)}, bf16[768,128]{1,0:T(8,128)(2,1)S(1)}, u32[]{:S(2)}, u32[]{:S(2)}) collective-permute-start(bf16[768,128]{1,0:T(8,128)(2,1)S(1)} %self_blocks.6), channel_id=1, source_target_pairs={{0,6},{2,4},{4,2},{6,0},{1,7},{3,5},{5,3},{7,1},{8,14},{10,12},{12... | collective-permute-start | bytes 589832 | tf_op jit(solution)/shard_map/self_sends/ppermute | solution.py:535
  64.6 1.3 %collective-permute-start.26 = (bf16[192,128]{1,0:T(8,128)(2,1)S(1)}, bf16[192,128]{1,0:T(8,128)(2,1)S(1)}, u32[]{:S(2)}, u32[]{:S(2)}) collective-permute-start(bf16[192,128]{1,0:T(8,128)(2,1)S(1)} %down_products.1.refs_0_), channel_id=1, source_target_pairs={{0,4},{2,6},{4,0},{6,2},{1,5},{3,7},{5,1},{7,3},{8,12},{10,14},{12... | collective-permute-start | bytes 147464 | tf_op jit(solution)/shard_map/far_coeff_sends/ppermute | solution.py:535
  65.8 1.5 %collective-permute-start.28 = (bf16[192,128]{1,0:T(8,128)(2,1)S(1)}, bf16[192,128]{1,0:T(8,128)(2,1)S(1)}, u32[]{:S(2)}, u32[]{:S(2)}) collective-permute-start(bf16[192,128]{1,0:T(8,128)(2,1)S(1)} %down_products.1.refs_0_), channel_id=1, source_target_pairs={{0,6},{2,4},{4,2},{6,0},{1,7},{3,5},{5,3},{7,1},{8,14},{10,12},{12... | collective-permute-start | bytes 147464 | tf_op jit(solution)/shard_map/far_coeff_sends/ppermute | solution.py:535
  69.5 1.3 %collective-permute-done.28.refs_0_ = bf16[192,128]{1,0:T(8,128)(2,1)S(1)} collective-permute-done((bf16[192,128]{1,0:T(8,128)(2,1)S(1)}, bf16[192,128]{1,0:T(8,128)(2,1)S(1)}, u32[]{:S(2)}, u32[]{:S(2)}) %collective-permute-start.28) | collective-permute-done | bytes 49184 | tf_op jit(solution)/shard_map/far_coeff_sends/ppermute | solution.py:535
  72.2 1.6 %column_products.1 = bf16[32,24,128]{2,1,0:T(8,128)(2,1)} custom-call(s32[3]{0:T(128)S(1)} %pad_add_fusion.2.ids_ref, bf16[64,32,128]{2,1,0:T(8,128)(2,1)S(1)} %copy-done.1, f32[384,128]{1,0:T(8,128)S(1)} %get-tuple-element.69.near_mine, bf16[384,128]{1,0:T(8,128)(2,1)S(1)} %collective-permute-done.23.near_peer, ...), custom_call_target="tpu_custom_call" | custom-call | bytes 6105000 | tf_op jit(solution)/shard_map/column_products/pallas_call | solution.py:524
  (72 shorter events, 11.5 us)
Async XLA Ops:
  0.0 13.0 %collective-permute-start.1 = (bf16[32,64,128]{2,1,0:T(8,128)(2,1)}, bf16[32,64,128]{2,1,0:T(8,128)(2,1)S(1)}, u32[]{:S(2)}, u32[]{:S(2)}) collective-permute-start(bf16[32,64,128]{2,1,0:T(8,128)(2,1)} %basis_ref.1), channel_id=1, source_target_pairs={{0,1},{1,0},{2,3},{3,2},{4,5},{5,4},{6,7},{7,6},{8,9},{9,8},{10,11... | collective-permute-start | bytes 1572872 | tf_op jit(solution)/shard_map/swap_row_basis/ppermute | solution.py:535
  0.5 21.2 %collective-permute-start.9 = (bf16[32,256,128]{2,1,0:T(8,128)(2,1)}, bf16[32,256,128]{2,1,0:T(8,128)(2,1)S(1)}, u32[]{:S(2)}, u32[]{:S(2)}) collective-permute-start(bf16[32,256,128]{2,1,0:T(8,128)(2,1)} %own_ref.7), channel_id=1, source_target_pairs={{0,1},{1,0},{2,3},{3,2},{4,5},{5,4},{6,7},{7,6},{8,9},{9,8},{10,11... | collective-permute-start | bytes 6291464 | tf_op jit(solution)/shard_map/swap_self_blocks/ppermute | solution.py:535
  2.5 5.7 %collective-permute-start = (bf16[192,128]{1,0:T(8,128)(2,1)S(1)}, bf16[192,128]{1,0:T(8,128)(2,1)S(1)}, u32[]{:S(2)}, u32[]{:S(2)}) collective-permute-start(bf16[192,128]{1,0:T(8,128)(2,1)S(1)} %get-tuple-element.74), channel_id=1, source_target_pairs={{0,8},{8,0},{16,24},{24,16},{1,9},{9,1},{17,25},{25,17},{2,10},{10... | collective-permute-start | bytes 147464 | tf_op jit(solution)/shard_map/regroup_sends/ppermute | solution.py:535
  5.6 7.4 %collective-permute-start.3 = (bf16[192,128]{1,0:T(8,128)(2,1)S(1)}, bf16[192,128]{1,0:T(8,128)(2,1)S(1)}, u32[]{:S(2)}, u32[]{:S(2)}) collective-permute-start(bf16[192,128]{1,0:T(8,128)(2,1)S(1)} %get-tuple-element.72), channel_id=1, source_target_pairs={{0,16},{8,24},{16,0},{24,8},{1,17},{9,25},{17,1},{25,9},{2,18},{10... | collective-permute-start | bytes 147464 | tf_op jit(solution)/shard_map/regroup_sends/ppermute | solution.py:535
  8.2 5.9 %collective-permute-start.4 = (bf16[192,128]{1,0:T(8,128)(2,1)S(1)}, bf16[192,128]{1,0:T(8,128)(2,1)S(1)}, u32[]{:S(2)}, u32[]{:S(2)}) collective-permute-start(bf16[192,128]{1,0:T(8,128)(2,1)S(1)} %get-tuple-element.71), channel_id=1, source_target_pairs={{0,24},{8,16},{16,8},{24,0},{1,25},{9,17},{17,9},{25,1},{2,26},{10... | collective-permute-start | bytes 147464 | tf_op jit(solution)/shard_map/regroup_sends/ppermute | solution.py:535
  9.0 4.0 %collective-permute-start.2 = (s32[4,128]{1,0:T(4,128)S(1)}, s32[4,128]{1,0:T(4,128)S(1)}, u32[]{:S(2)}, u32[]{:S(2)}) collective-permute-start(s32[4,128]{1,0:T(4,128)S(1)} %fusion.1.own_codes), channel_id=1, source_target_pairs={{0,1},{1,0},{2,3},{3,2},{4,5},{5,4},{6,7},{7,6},{8,9},{9,8},{10,11... | collective-permute-start | bytes 6152 | tf_op jit(solution)/shard_map/partner_codes/ppermute | solution.py:535
  12.9 8.7 %copy-start = (bf16[32,256,128]{2,1,0:T(8,128)(2,1)S(1)}, bf16[32,256,128]{2,1,0:T(8,128)(2,1)}, u32[]{:S(2)}) copy-start(bf16[32,256,128]{2,1,0:T(8,128)(2,1)} %own_ref.7) | copy-start | bytes 6291460
  14.4 1.6 %collective-permute-start.5 = (bf16[384,128]{1,0:T(8,128)(2,1)S(1)}, bf16[384,128]{1,0:T(8,128)(2,1)S(1)}, u32[]{:S(2)}, u32[]{:S(2)}) collective-permute-start(bf16[384,128]{1,0:T(8,128)(2,1)S(1)} %get-tuple-element.47), channel_id=1, source_target_pairs={{0,1},{1,0},{2,3},{3,2},{4,5},{5,4},{6,7},{7,6},{8,9},{9,8},{10,11... | collective-permute-start | bytes 294920 | tf_op jit(solution)/shard_map/swap_field/ppermute | solution.py:535
  17.6 26.6 %collective-permute-start.14 = (bf16[2,64,64,128]{3,2,1,0:T(8,128)(2,1)S(1)}, bf16[2,64,64,128]{3,2,1,0:T(8,128)(2,1)S(1)}, u32[]{:S(2)}, u32[]{:S(2)}) collective-permute-start(bf16[2,64,64,128]{3,2,1,0:T(8,128)(2,1)S(1)} %bitcast.31), channel_id=1, source_target_pairs={{0,1},{1,0},{2,3},{3,2},{4,5},{5,4},{6,7},{7,6},{8,9},{9,8},{10,11... | collective-permute-start | bytes 6291464 | tf_op jit(solution)/shard_map/swap_coupling/ppermute | solution.py:535
  18.2 6.1 %collective-permute-start.6 = (bf16[192,128]{1,0:T(8,128)(2,1)S(1)}, bf16[192,128]{1,0:T(8,128)(2,1)S(1)}, u32[]{:S(2)}, u32[]{:S(2)}) collective-permute-start(bf16[192,128]{1,0:T(8,128)(2,1)S(1)} %get-tuple-element.49), channel_id=1, source_target_pairs={{0,6},{2,4},{4,2},{6,0},{1,7},{3,5},{5,3},{7,1},{8,14},{10,12},{12... | collective-permute-start | bytes 147464 | tf_op jit(solution)/shard_map/coeff_sends/ppermute | solution.py:535
  20.6 4.1 %collective-permute-start.7 = (bf16[192,128]{1,0:T(8,128)(2,1)S(1)}, bf16[192,128]{1,0:T(8,128)(2,1)S(1)}, u32[]{:S(2)}, u32[]{:S(2)}) collective-permute-start(bf16[192,128]{1,0:T(8,128)(2,1)S(1)} %get-tuple-element.50), channel_id=1, source_target_pairs={{0,4},{2,6},{4,0},{6,2},{1,5},{3,7},{5,1},{7,3},{8,12},{10,14},{12... | collective-permute-start | bytes 147464 | tf_op jit(solution)/shard_map/coeff_sends/ppermute | solution.py:535
  21.1 4.1 %collective-permute-start.8 = (bf16[192,128]{1,0:T(8,128)(2,1)S(1)}, bf16[192,128]{1,0:T(8,128)(2,1)S(1)}, u32[]{:S(2)}, u32[]{:S(2)}) collective-permute-start(bf16[192,128]{1,0:T(8,128)(2,1)S(1)} %get-tuple-element.51), channel_id=1, source_target_pairs={{0,2},{2,0},{4,6},{6,4},{1,3},{3,1},{5,7},{7,5},{8,10},{10,8},{12,... | collective-permute-start | bytes 147464 | tf_op jit(solution)/shard_map/coeff_sends/ppermute | solution.py:535
  21.7 8.8 %copy-start.5 = (bf16[64,64,1,2,16]{1,4,3,2,0:T(8,128)(2,1)S(1)}, bf16[64,64,1,2,16]{1,4,3,2,0:T(8,128)(2,1)}, u32[]{:S(2)}) copy-start(bf16[64,64,1,2,16]{1,4,3,2,0:T(8,128)(2,1)} %param.19) | copy-start | bytes 786436
  26.0 9.6 %collective-permute-start.10 = (bf16[224,128]{1,0:T(8,128)(2,1)S(1)}, bf16[224,128]{1,0:T(8,128)(2,1)S(1)}, u32[]{:S(2)}, u32[]{:S(2)}) collective-permute-start(bf16[224,128]{1,0:T(8,128)(2,1)S(1)} %parent_coeffs.1), channel_id=1, source_target_pairs={{0,8},{8,0},{16,24},{24,16},{1,9},{9,1},{17,25},{25,17},{2,10},{10... | collective-permute-start | bytes 172040 | tf_op jit(solution)/shard_map/owner_sends/ppermute | solution.py:535
  26.5 9.1 %collective-permute-start.11 = (bf16[224,128]{1,0:T(8,128)(2,1)S(1)}, bf16[224,128]{1,0:T(8,128)(2,1)S(1)}, u32[]{:S(2)}, u32[]{:S(2)}) collective-permute-start(bf16[224,128]{1,0:T(8,128)(2,1)S(1)} %parent_coeffs.1), channel_id=1, source_target_pairs={{0,16},{8,24},{16,0},{24,8},{1,17},{9,25},{17,1},{25,9},{2,18},{10... | collective-permute-start | bytes 172040 | tf_op jit(solution)/shard_map/owner_sends/ppermute | solution.py:535
  29.7 6.0 %collective-permute-start.12 = (bf16[224,128]{1,0:T(8,128)(2,1)S(1)}, bf16[224,128]{1,0:T(8,128)(2,1)S(1)}, u32[]{:S(2)}, u32[]{:S(2)}) collective-permute-start(bf16[224,128]{1,0:T(8,128)(2,1)S(1)} %parent_coeffs.1), channel_id=1, source_target_pairs={{0,24},{8,16},{16,8},{24,0},{1,25},{9,17},{17,9},{25,1},{2,26},{10... | collective-permute-start | bytes 172040 | tf_op jit(solution)/shard_map/owner_sends/ppermute | solution.py:535
  30.4 11.4 %collective-permute-start.13 = (bf16[64,32,64]{2,1,0:T(8,128)(2,1)S(1)}, bf16[64,32,64]{2,1,0:T(8,128)(2,1)S(1)}, u32[]{:S(2)}, u32[]{:S(2)}) collective-permute-start(bf16[64,32,64]{2,1,0:T(8,128)(2,1)S(1)} %bitcast.36), channel_id=1, source_target_pairs={{0,1},{1,0},{2,3},{3,2},{4,5},{5,4},{6,7},{7,6},{8,9},{9,8},{10,11... | collective-permute-start | bytes 786440 | tf_op jit(solution)/shard_map/swap_parent_coupling/ppermute | solution.py:535
  35.7 8.5 %collective-permute-start.15 = (bf16[896,128]{1,0:T(8,128)(2,1)S(1)}, bf16[896,128]{1,0:T(8,128)(2,1)S(1)}, u32[]{:S(2)}, u32[]{:S(2)}) collective-permute-start(bf16[896,128]{1,0:T(8,128)(2,1)S(1)} %constant_dynamic-update-slice_fusion.block_ref), channel_id=1, source_target_pairs={{0,2},{2,0},{4,6},{6,4},{1,3},{3,1},{5,7},{7,5},{8,10},{10,8},{12,... | collective-permute-start | bytes 688136 | tf_op jit(solution)/shard_map/level_sends/ppermute | solution.py:535
  36.4 11.7 %collective-permute-start.17 = (bf16[896,128]{1,0:T(8,128)(2,1)S(1)}, bf16[896,128]{1,0:T(8,128)(2,1)S(1)}, u32[]{:S(2)}, u32[]{:S(2)}) collective-permute-start(bf16[896,128]{1,0:T(8,128)(2,1)S(1)} %constant_dynamic-update-slice_fusion.block_ref), channel_id=1, source_target_pairs={{0,4},{2,6},{4,0},{6,2},{1,5},{3,7},{5,1},{7,3},{8,12},{10,14},{12... | collective-permute-start | bytes 688136 | tf_op jit(solution)/shard_map/level_sends/ppermute | solution.py:535
  37.9 15.6 %collective-permute-start.19 = (bf16[896,128]{1,0:T(8,128)(2,1)S(1)}, bf16[896,128]{1,0:T(8,128)(2,1)S(1)}, u32[]{:S(2)}, u32[]{:S(2)}) collective-permute-start(bf16[896,128]{1,0:T(8,128)(2,1)S(1)} %constant_dynamic-update-slice_fusion.block_ref), channel_id=1, source_target_pairs={{0,6},{2,4},{4,2},{6,0},{1,7},{3,5},{5,3},{7,1},{8,14},{10,12},{12... | collective-permute-start | bytes 688136 | tf_op jit(solution)/shard_map/level_sends/ppermute | solution.py:535
  47.0 15.9 %collective-permute-start.16 = (bf16[992,128]{1,0:T(8,128)(2,1)S(1)}, bf16[992,128]{1,0:T(8,128)(2,1)S(1)}, u32[]{:S(2)}, u32[]{:S(2)}) collective-permute-start(bf16[992,128]{1,0:T(8,128)(2,1)S(1)} %coupling_products.5), channel_id=1, source_target_pairs={{0,2},{2,0},{4,6},{6,4},{1,3},{3,1},{5,7},{7,5},{8,10},{10,8},{12,... | collective-permute-start | bytes 761864 | tf_op jit(solution)/shard_map/far_sends/ppermute | solution.py:535
  50.9 12.0 %collective-permute-start.18 = (bf16[992,128]{1,0:T(8,128)(2,1)S(1)}, bf16[992,128]{1,0:T(8,128)(2,1)S(1)}, u32[]{:S(2)}, u32[]{:S(2)}) collective-permute-start(bf16[992,128]{1,0:T(8,128)(2,1)S(1)} %coupling_products.6), channel_id=1, source_target_pairs={{0,4},{2,6},{4,0},{6,2},{1,5},{3,7},{5,1},{7,3},{8,12},{10,14},{12... | collective-permute-start | bytes 761864 | tf_op jit(solution)/shard_map/far_sends/ppermute | solution.py:535
  56.3 5.1 %collective-permute-start.20 = (bf16[224,128]{1,0:T(8,128)(2,1)S(1)}, bf16[224,128]{1,0:T(8,128)(2,1)S(1)}, u32[]{:S(2)}, u32[]{:S(2)}) collective-permute-start(bf16[224,128]{1,0:T(8,128)(2,1)S(1)} %coupling_products.7), channel_id=1, source_target_pairs={{0,6},{2,4},{4,2},{6,0},{1,7},{3,5},{5,3},{7,1},{8,14},{10,12},{12... | collective-permute-start | bytes 172040 | tf_op jit(solution)/shard_map/far_sends/ppermute | solution.py:535
  61.4 6.8 %collective-permute-start.22 = (bf16[768,128]{1,0:T(8,128)(2,1)S(1)}, bf16[768,128]{1,0:T(8,128)(2,1)S(1)}, u32[]{:S(2)}, u32[]{:S(2)}) collective-permute-start(bf16[768,128]{1,0:T(8,128)(2,1)S(1)} %self_blocks.6), channel_id=1, source_target_pairs={{0,6},{2,4},{4,2},{6,0},{1,7},{3,5},{5,3},{7,1},{8,14},{10,12},{12... | collective-permute-start | bytes 589832 | tf_op jit(solution)/shard_map/self_sends/ppermute | solution.py:535
  63.7 3.6 %collective-permute-start.21 = (bf16[192,128]{1,0:T(8,128)(2,1)S(1)}, bf16[192,128]{1,0:T(8,128)(2,1)S(1)}, u32[]{:S(2)}, u32[]{:S(2)}) collective-permute-start(bf16[192,128]{1,0:T(8,128)(2,1)S(1)} %down_products.1.refs_0_), channel_id=1, source_target_pairs={{0,1},{1,0},{2,3},{3,2},{4,5},{5,4},{6,7},{7,6},{8,9},{9,8},{10,11... | collective-permute-start | bytes 147464 | tf_op jit(solution)/shard_map/far_coeff_sends/ppermute | solution.py:535
  63.8 5.1 %collective-permute-start.24 = (bf16[192,128]{1,0:T(8,128)(2,1)S(1)}, bf16[192,128]{1,0:T(8,128)(2,1)S(1)}, u32[]{:S(2)}, u32[]{:S(2)}) collective-permute-start(bf16[192,128]{1,0:T(8,128)(2,1)S(1)} %down_products.1.refs_0_), channel_id=1, source_target_pairs={{0,2},{2,0},{4,6},{6,4},{1,3},{3,1},{5,7},{7,5},{8,10},{10,8},{12,... | collective-permute-start | bytes 147464 | tf_op jit(solution)/shard_map/far_coeff_sends/ppermute | solution.py:535
  64.6 4.8 %collective-permute-start.26 = (bf16[192,128]{1,0:T(8,128)(2,1)S(1)}, bf16[192,128]{1,0:T(8,128)(2,1)S(1)}, u32[]{:S(2)}, u32[]{:S(2)}) collective-permute-start(bf16[192,128]{1,0:T(8,128)(2,1)S(1)} %down_products.1.refs_0_), channel_id=1, source_target_pairs={{0,4},{2,6},{4,0},{6,2},{1,5},{3,7},{5,1},{7,3},{8,12},{10,14},{12... | collective-permute-start | bytes 147464 | tf_op jit(solution)/shard_map/far_coeff_sends/ppermute | solution.py:535
  65.8 5.0 %collective-permute-start.28 = (bf16[192,128]{1,0:T(8,128)(2,1)S(1)}, bf16[192,128]{1,0:T(8,128)(2,1)S(1)}, u32[]{:S(2)}, u32[]{:S(2)}) collective-permute-start(bf16[192,128]{1,0:T(8,128)(2,1)S(1)} %down_products.1.refs_0_), channel_id=1, source_target_pairs={{0,6},{2,4},{4,2},{6,0},{1,7},{3,5},{5,3},{7,1},{8,14},{10,12},{12... | collective-permute-start | bytes 147464 | tf_op jit(solution)/shard_map/far_coeff_sends/ppermute | solution.py:535
  68.8 3.3 %collective-permute-start.23 = (bf16[384,128]{1,0:T(8,128)(2,1)S(1)}, bf16[384,128]{1,0:T(8,128)(2,1)S(1)}, u32[]{:S(2)}, u32[]{:S(2)}) collective-permute-start(bf16[384,128]{1,0:T(8,128)(2,1)S(1)} %get-tuple-element.70), channel_id=1, source_target_pairs={{0,1},{1,0},{2,3},{3,2},{4,5},{5,4},{6,7},{7,6},{8,9},{9,8},{10,11... | collective-permute-start | bytes 294920 | tf_op jit(solution)/shard_map/swap_self_sums/ppermute | solution.py:535
  68.9 2.2 %collective-permute-start.25 = (bf16[192,128]{1,0:T(8,128)(2,1)S(1)}, bf16[192,128]{1,0:T(8,128)(2,1)S(1)}, u32[]{:S(2)}, u32[]{:S(2)}) collective-permute-start(bf16[192,128]{1,0:T(8,128)(2,1)S(1)} %collective-permute-done.24.refs_0_), channel_id=1, source_target_pairs={{0,1},{1,0},{2,3},{3,2},{4,5},{5,4},{6,7},{7,6},{8,9},{9,8},{10,11... | collective-permute-start | bytes 147464 | tf_op jit(solution)/shard_map/far_coeff_sends/ppermute | solution.py:535
  69.4 2.2 %collective-permute-start.27 = (bf16[192,128]{1,0:T(8,128)(2,1)S(1)}, bf16[192,128]{1,0:T(8,128)(2,1)S(1)}, u32[]{:S(2)}, u32[]{:S(2)}) collective-permute-start(bf16[192,128]{1,0:T(8,128)(2,1)S(1)} %collective-permute-done.26.refs_0_), channel_id=1, source_target_pairs={{0,1},{1,0},{2,3},{3,2},{4,5},{5,4},{6,7},{7,6},{8,9},{9,8},{10,11... | collective-permute-start | bytes 147464 | tf_op jit(solution)/shard_map/far_coeff_sends/ppermute | solution.py:535
  70.8 1.3 %collective-permute-start.29 = (bf16[192,128]{1,0:T(8,128)(2,1)S(1)}, bf16[192,128]{1,0:T(8,128)(2,1)S(1)}, u32[]{:S(2)}, u32[]{:S(2)}) collective-permute-start(bf16[192,128]{1,0:T(8,128)(2,1)S(1)} %collective-permute-done.28.refs_0_), channel_id=1, source_target_pairs={{0,1},{1,0},{2,3},{3,2},{4,5},{5,4},{6,7},{7,6},{8,9},{9,8},{10,11... | collective-permute-start | bytes 147464 | tf_op jit(solution)/shard_map/far_coeff_sends/ppermute | solution.py:535
  (4 other events, 20.7 us)

commit v7 on v5

--- a/solution.py
+++ b/solution.py
@@ -574,7 +574,7 @@
         1.0, scalars=1, whole=(1, 2),
     )
     with jax.named_scope("regroup_sends"):
-        chunks = [packed[0]] + swaps([packed[s] for s in range(owners)], "clus", owners, False)
+        chunks = [packed[0]] + swaps([packed[s] for s in range(owners)], "clus", owners, True)
     codes = call(
         "place_codes",
         functools.partial(place_kernel, owners, parents),
@@ -664,7 +664,7 @@
         0.8,
     )
     with jax.named_scope("owner_sends"):
-        blocks = [block] + swaps([block] * owners, "clus", owners, False)
+        blocks = [block] + swaps([block] * owners, "clus", owners, True)
     later = after(field, block)
     for t in range(2, lvls):
         near_parts[t] = near_part(t, later)

time: 74.1 us -> 74.1 us (level)
  no operation moved by 1% of the time
where the time goes in v7:
time: 74.1 us; the launch traced here: 73.9 us
  Pallas kernels  35.9 us (48%)
  starting transfers between devices  28.7 us (39%)
  waiting for transfers between devices  5.74 us (8%)
  local copies, waits for them, and re-layouts  2.26 us (3%)
  other arithmetic  0.89 us (1%)
    pallas_call x21, Pallas kernels, call(): pl.pallas_call(kernel, out_shape=outs, in_specs=specs, out_specs=jax.tree...  35.9 us
    ppermute x30, starting transfers between devices, swap(): return lax.ppermute(value, axis, [(i, i ^ step) for i in range(count)])  28.7 us
    ppermute x30, waiting for transfers between devices, swap(): return lax.ppermute(value, axis, [(i, i ^ step) for i in range(count)])  5.74 us
    optimization_barrier x1, local copies, waits for them, and re-layouts, after(): return lax.optimization_barrier((value,) + others)[0]  2.17 us
  transfers between devices with their start and end apart: 30, of which 9 were waited for; matrix products, arithmetic and copies ran while one was open for 4% of the time, Pallas kernels for 46%

profile of v7, /device:TPU:0, one launch (start us, length us, event | category | flops | bytes accessed | tf_op | source)
XLA Modules:
  0.0 73.9 jit_solution(11075514642013840797)
XLA Ops:
  0.6 1.8 %pack_field.1 = bf16[4,192,128]{2,1,0:T(8,128)(2,1)S(1)} custom-call(s32[3]{0:T(128)S(1)} %pad_add_fusion.2.ids_ref, s32[64]{0:T(128)} %perm_any.3, bf16[32,24,128]{2,1,0:T(8,128)(2,1)} %own_any.1), custom_call_target="tpu_custom_call" | custom-call | bytes 3300000 | tf_op jit(solution)/shard_map/pack_field/pallas_call | solution.py:525
  2.5 3.1 %collective-permute-start = (bf16[192,128]{1,0:T(8,128)(2,1)S(1)}, bf16[192,128]{1,0:T(8,128)(2,1)S(1)}, u32[]{:S(2)}, u32[]{:S(2)}) collective-permute-start(bf16[192,128]{1,0:T(8,128)(2,1)S(1)} %get-tuple-element.74), channel_id=1, source_target_pairs={{0,8},{8,0},{16,24},{24,16},{1,9},{9,1},{17,25},{25,17},{2,10},{10... | collective-permute-start | bytes 147464 | tf_op jit(solution)/shard_map/regroup_sends/ppermute | solution.py:536
  5.6 2.6 %collective-permute-start.3 = (bf16[192,128]{1,0:T(8,128)(2,1)S(1)}, bf16[192,128]{1,0:T(8,128)(2,1)S(1)}, u32[]{:S(2)}, u32[]{:S(2)}) collective-permute-start(bf16[192,128]{1,0:T(8,128)(2,1)S(1)} %get-tuple-element.72), channel_id=1, source_target_pairs={{0,16},{8,24},{16,0},{24,8},{1,17},{9,25},{17,1},{25,9},{2,18},{10... | collective-permute-start | bytes 147464 | tf_op jit(solution)/shard_map/regroup_sends/ppermute | solution.py:536
  8.2 0.8 %fusion.1.own_codes = s32[4,128]{1,0:T(4,128)S(1)} fusion(s32[2,16]{1,0:T(2,128)} %bitcast.38, s32[2,16]{1,0:T(2,128)} %bitcast.39, s32[2,128]{1,0:T(2,128)} %bitcast.40, s32[2,128]{1,0:T(2,128)} %bitcast.41, s32[4]{0:T(128)S(1)} %get-tuple-element.75, s32[]{:T(128)} %axis_index.33, s32[128]{0:T(128)} %param.27, s32[4]{0:T(128)S(1)} %get-tuple-element.76, ...), kind=kLoop, calls=%fused_computation.11 | loop fusion | flops 4096 | bytes 4904 | tf_op jit(solution)/shard_map/partner_codes/jit(_where)/select_n | solution.py:604
  9.0 1.7 %place_codes.1.code_ref = s32[8,128]{1,0:T(8,128)S(1)} custom-call(s32[3]{0:T(128)S(1)} %pad_add_fusion.2.ids_ref, s32[64]{0:T(128)} %perm_any.3), custom_call_target="tpu_custom_call" | custom-call | bytes 990000 | tf_op jit(solution)/shard_map/place_codes/pallas_call | solution.py:525
  10.8 2.2 %copy.17 = bf16[64,64,1,2,128]{4,1,0,3,2:T(8,128)(2,1)S(1)} copy(bf16[64,64,1,2,128]{4,3,2,1,0:T(2,128)(2,1)} %param.18) | data formatting | bytes 4194304 | tf_op jit(solution)/shard_map/coupling_layout/optimization_barrier | solution.py:494
  13.0 1.1 %collective-permute-done.4.refs_3_ = bf16[192,128]{1,0:T(8,128)(2,1)S(1)} collective-permute-done((bf16[192,128]{1,0:T(8,128)(2,1)S(1)}, bf16[192,128]{1,0:T(8,128)(2,1)S(1)}, u32[]{:S(2)}, u32[]{:S(2)}) %collective-permute-start.4) | collective-permute-done | bytes 49184 | tf_op jit(solution)/shard_map/regroup_sends/ppermute | solution.py:536
  14.5 1.5 %coeffs_own_slab.1.own_ref = f32[768,128]{1,0:T(8,128)S(1)} custom-call(s32[3]{0:T(128)S(1)} %pad_add_fusion.2.ids_ref, bf16[32,64,128]{2,1,0:T(8,128)(2,1)S(1)} %copy-done.4, f32[384,128]{1,0:T(8,128)S(1)} %get-tuple-element.60.field_ref.own_field), custom_call_target="tpu_custom_call" | custom-call | bytes 5280000 | tf_op jit(solution)/shard_map/coeffs_own_slab/pallas_call | solution.py:525
  16.0 1.6 %coeffs_other_slab.1 = (f32[384,128]{1,0:T(8,128)S(1)}, f32[192,128]{1,0:T(8,128)S(1)}, bf16[192,128]{1,0:T(8,128)(2,1)S(1)}, bf16[192,128]{1,0:T(8,128)(2,1)S(1)}, bf16[192,128]{1,0:T(8,128)(2,1)S(1)}) custom-call(s32[3]{0:T(128)S(1)} %pad_add_fusion.2.ids_ref, bf16[32,64,128]{2,1,0:T(8,128)(2,1)S(1)} %collective-permute-done.1.basis_ref, ...), custom_call_target="tpu_custom_call" | custom-call | bytes 5280000 | tf_op jit(solution)/shard_map/coeffs_other_slab/pallas_call | solution.py:525
  18.2 2.4 %collective-permute-start.6 = (bf16[192,128]{1,0:T(8,128)(2,1)S(1)}, bf16[192,128]{1,0:T(8,128)(2,1)S(1)}, u32[]{:S(2)}, u32[]{:S(2)}) collective-permute-start(bf16[192,128]{1,0:T(8,128)(2,1)S(1)} %get-tuple-element.49), channel_id=1, source_target_pairs={{0,6},{2,4},{4,2},{6,0},{1,7},{3,5},{5,3},{7,1},{8,14},{10,12},{12... | collective-permute-start | bytes 147464 | tf_op jit(solution)/shard_map/coeff_sends/ppermute | solution.py:536
  21.7 2.6 %self_blocks.4.refs_0_ = bf16[768,128]{1,0:T(8,128)(2,1)S(1)} custom-call(s32[3]{0:T(128)S(1)} %pad_add_fusion.2.ids_ref, f32[384,128]{1,0:T(8,128)S(1)} %get-tuple-element.60.field_ref.own_field, f32[384,128]{1,0:T(8,128)S(1)} %get-tuple-element.53.peer_field, bf16[32,256,128]{2,1,0:T(8,128)(2,1)S(1)} %copy-done, ...), custom_call_target="tpu_custom_call" | custom-call | bytes 7920000 | tf_op jit(solution)/shard_map/self_blocks/pallas_call | solution.py:525
  25.2 0.8 %parent_coeffs.1 = bf16[224,128]{1,0:T(8,128)(2,1)S(1)} custom-call(f32[192,128]{1,0:T(8,128)S(1)} %get-tuple-element.48.keep_ref, bf16[192,128]{1,0:T(8,128)(2,1)S(1)} %collective-permute-done.6.refs_0_, bf16[192,128]{1,0:T(8,128)(2,1)S(1)} %collective-permute-done.7.refs_1_, bf16[192,128]{1,0:T(8,128)(2,1)S(1)} %collective-permute-done.8.refs_2_, ...), custom_call_target="tpu_custom_call" | custom-call | bytes 2640000 | tf_op jit(solution)/shard_map/parent_coeffs/pallas_call | solution.py:525
  26.5 3.1 %collective-permute-start.11 = (bf16[224,128]{1,0:T(8,128)(2,1)S(1)}, bf16[224,128]{1,0:T(8,128)(2,1)S(1)}, u32[]{:S(2)}, u32[]{:S(2)}) collective-permute-start(bf16[224,128]{1,0:T(8,128)(2,1)S(1)} %parent_coeffs.1), channel_id=1, source_target_pairs={{0,16},{8,24},{16,0},{24,8},{1,17},{9,25},{17,1},{25,9},{2,18},{10... | collective-permute-start | bytes 172040 | tf_op jit(solution)/shard_map/owner_sends/ppermute | solution.py:536
  30.4 2.6 %self_blocks.5.refs_0_ = bf16[768,128]{1,0:T(8,128)(2,1)S(1)} custom-call(s32[3]{0:T(128)S(1)} %pad_add_fusion.2.ids_ref, f32[384,128]{1,0:T(8,128)S(1)} %get-tuple-element.60.field_ref.own_field, f32[384,128]{1,0:T(8,128)S(1)} %get-tuple-element.53.peer_field, bf16[32,256,128]{2,1,0:T(8,128)(2,1)S(1)} %copy-done, ...), custom_call_target="tpu_custom_call" | custom-call | bytes 7920000 | tf_op jit(solution)/shard_map/self_blocks/pallas_call | solution.py:525
  33.0 2.6 %self_blocks.6 = bf16[768,128]{1,0:T(8,128)(2,1)S(1)} custom-call(s32[3]{0:T(128)S(1)} %pad_add_fusion.2.ids_ref, f32[384,128]{1,0:T(8,128)S(1)} %get-tuple-element.60.field_ref.own_field, f32[384,128]{1,0:T(8,128)S(1)} %get-tuple-element.53.peer_field, bf16[32,256,128]{2,1,0:T(8,128)(2,1)S(1)} %copy-done, ...), custom_call_target="tpu_custom_call" | custom-call | bytes 7920000 | tf_op jit(solution)/shard_map/self_blocks/pallas_call | solution.py:525
  36.4 1.5 %collective-permute-start.17 = (bf16[896,128]{1,0:T(8,128)(2,1)S(1)}, bf16[896,128]{1,0:T(8,128)(2,1)S(1)}, u32[]{:S(2)}, u32[]{:S(2)}) collective-permute-start(bf16[896,128]{1,0:T(8,128)(2,1)S(1)} %constant_dynamic-update-slice_fusion.block_ref), channel_id=1, source_target_pairs={{0,4},{2,6},{4,0},{6,2},{1,5},{3,7},{5,1},{7,3},{8,12},{10,14},{12... | collective-permute-start | bytes 688136 | tf_op jit(solution)/shard_map/level_sends/ppermute | solution.py:536
  37.9 1.4 %collective-permute-start.19 = (bf16[896,128]{1,0:T(8,128)(2,1)S(1)}, bf16[896,128]{1,0:T(8,128)(2,1)S(1)}, u32[]{:S(2)}, u32[]{:S(2)}) collective-permute-start(bf16[896,128]{1,0:T(8,128)(2,1)S(1)} %constant_dynamic-update-slice_fusion.block_ref), channel_id=1, source_target_pairs={{0,6},{2,4},{4,2},{6,0},{1,7},{3,5},{5,3},{7,1},{8,14},{10,12},{12... | collective-permute-start | bytes 688136 | tf_op jit(solution)/shard_map/level_sends/ppermute | solution.py:536
  39.3 2.6 %self_blocks.7.keep_ref = f32[768,128]{1,0:T(8,128)S(1)} custom-call(s32[3]{0:T(128)S(1)} %pad_add_fusion.2.ids_ref, f32[384,128]{1,0:T(8,128)S(1)} %get-tuple-element.60.field_ref.own_field, f32[384,128]{1,0:T(8,128)S(1)} %get-tuple-element.53.peer_field, bf16[32,256,128]{2,1,0:T(8,128)(2,1)S(1)} %copy-done, ...), custom_call_target="tpu_custom_call" | custom-call | bytes 7920000 | tf_op jit(solution)/shard_map/self_blocks/pallas_call | solution.py:525
  41.8 1.7 %partner_tables.1 = (bf16[512,512]{1,0:T(8,128)(2,1)S(1)}, bf16[64,64]{1,0:T(8,128)(2,1)S(1)}, bf16[16,256,64]{2,1,0:T(8,128)(2,1)S(1)}) custom-call(s32[4,128]{1,0:T(4,128)S(1)} %fusion.1.own_codes, s32[4,128]{1,0:T(4,128)S(1)} %collective-permute-done.2.peer_codes, bf16[64,32,64]{2,1,0:T(8,128)(2,1)S(1)} %bitcast.37, ...), custom_call_target="tpu_custom_call" | custom-call | bytes 4950000 | tf_op jit(solution)/shard_map/partner_tables/pallas_call | solution.py:525
  44.2 2.8 %coupling_products.5 = bf16[992,128]{1,0:T(8,128)(2,1)S(1)} custom-call(bf16[512,512]{1,0:T(8,128)(2,1)S(1)} %get-tuple-element.62.leaf_table, bf16[64,64]{1,0:T(8,128)(2,1)S(1)} %get-tuple-element.63.parent_table, bf16[16,256,64]{2,1,0:T(8,128)(2,1)S(1)} %get-tuple-element.64.pcouple_ref, bf16[896,128]{1,0:T(8,128)(2,1)S(1)} %collective-permute-done.15.block_ref, ...), custom_call_target="tpu_custom_call" | custom-call | bytes 10560000 | tf_op jit(solution)/shard_map/coupling_products/pallas_call | solution.py:525
  48.1 2.8 %coupling_products.6 = bf16[992,128]{1,0:T(8,128)(2,1)S(1)} custom-call(bf16[512,512]{1,0:T(8,128)(2,1)S(1)} %get-tuple-element.62.leaf_table, bf16[64,64]{1,0:T(8,128)(2,1)S(1)} %get-tuple-element.63.parent_table, bf16[16,256,64]{2,1,0:T(8,128)(2,1)S(1)} %get-tuple-element.64.pcouple_ref, bf16[896,128]{1,0:T(8,128)(2,1)S(1)} %collective-permute-done.17.block_ref, ...), custom_call_target="tpu_custom_call" | custom-call | bytes 10560000 | tf_op jit(solution)/shard_map/coupling_products/pallas_call | solution.py:525
  50.9 2.5 %collective-permute-start.18 = (bf16[992,128]{1,0:T(8,128)(2,1)S(1)}, bf16[992,128]{1,0:T(8,128)(2,1)S(1)}, u32[]{:S(2)}, u32[]{:S(2)}) collective-permute-start(bf16[992,128]{1,0:T(8,128)(2,1)S(1)} %coupling_products.6), channel_id=1, source_target_pairs={{0,4},{2,6},{4,0},{6,2},{1,5},{3,7},{5,1},{7,3},{8,12},{10,14},{12... | collective-permute-start | bytes 761864 | tf_op jit(solution)/shard_map/far_sends/ppermute | solution.py:536
  53.4 2.8 %coupling_products.7 = bf16[224,128]{1,0:T(8,128)(2,1)S(1)} custom-call(bf16[512,512]{1,0:T(8,128)(2,1)S(1)} %get-tuple-element.62.leaf_table, bf16[64,64]{1,0:T(8,128)(2,1)S(1)} %get-tuple-element.63.parent_table, bf16[16,256,64]{2,1,0:T(8,128)(2,1)S(1)} %get-tuple-element.64.pcouple_ref, bf16[896,128]{1,0:T(8,128)(2,1)S(1)} %collective-permute-done.19.block_ref, ...), custom_call_target="tpu_custom_call" | custom-call | bytes 10560000 | tf_op jit(solution)/shard_map/coupling_products/pallas_call | solution.py:525
  56.3 1.5 %collective-permute-start.20 = (bf16[224,128]{1,0:T(8,128)(2,1)S(1)}, bf16[224,128]{1,0:T(8,128)(2,1)S(1)}, u32[]{:S(2)}, u32[]{:S(2)}) collective-permute-start(bf16[224,128]{1,0:T(8,128)(2,1)S(1)} %coupling_products.7), channel_id=1, source_target_pairs={{0,6},{2,4},{4,2},{6,0},{1,7},{3,5},{5,3},{7,1},{8,14},{10,12},{12... | collective-permute-start | bytes 172040 | tf_op jit(solution)/shard_map/far_sends/ppermute | solution.py:536
  57.8 2.8 %coupling_products.4.keep_ref = f32[224,128]{1,0:T(8,128)S(1)} custom-call(bf16[512,512]{1,0:T(8,128)(2,1)S(1)} %get-tuple-element.62.leaf_table, bf16[64,64]{1,0:T(8,128)(2,1)S(1)} %get-tuple-element.63.parent_table, bf16[16,256,64]{2,1,0:T(8,128)(2,1)S(1)} %get-tuple-element.64.pcouple_ref, ...), custom_call_target="tpu_custom_call" | custom-call | bytes 10560000 | tf_op jit(solution)/shard_map/coupling_products/pallas_call | solution.py:525
  60.6 0.8 %collective-permute-done.20.refs_2_ = bf16[224,128]{1,0:T(8,128)(2,1)S(1)} collective-permute-done((bf16[224,128]{1,0:T(8,128)(2,1)S(1)}, bf16[224,128]{1,0:T(8,128)(2,1)S(1)}, u32[]{:S(2)}, u32[]{:S(2)}) %collective-permute-start.20) | collective-permute-done | bytes 57376 | tf_op jit(solution)/shard_map/far_sends/ppermute | solution.py:536
  61.4 1.5 %collective-permute-start.22 = (bf16[768,128]{1,0:T(8,128)(2,1)S(1)}, bf16[768,128]{1,0:T(8,128)(2,1)S(1)}, u32[]{:S(2)}, u32[]{:S(2)}) collective-permute-start(bf16[768,128]{1,0:T(8,128)(2,1)S(1)} %self_blocks.6), channel_id=1, source_target_pairs={{0,6},{2,4},{4,2},{6,0},{1,7},{3,5},{5,3},{7,1},{8,14},{10,12},{12... | collective-permute-start | bytes 589832 | tf_op jit(solution)/shard_map/self_sends/ppermute | solution.py:536
  63.8 0.8 %collective-permute-start.24 = (bf16[192,128]{1,0:T(8,128)(2,1)S(1)}, bf16[192,128]{1,0:T(8,128)(2,1)S(1)}, u32[]{:S(2)}, u32[]{:S(2)}) collective-permute-start(bf16[192,128]{1,0:T(8,128)(2,1)S(1)} %down_products.1.mine_ref), channel_id=1, source_target_pairs={{0,2},{2,0},{4,6},{6,4},{1,3},{3,1},{5,7},{7,5},{8,10},{10,8},{12,... | collective-permute-start | bytes 147464 | tf_op jit(solution)/shard_map/far_coeff_sends/ppermute | solution.py:536
  64.6 1.3 %collective-permute-start.26 = (bf16[192,128]{1,0:T(8,128)(2,1)S(1)}, bf16[192,128]{1,0:T(8,128)(2,1)S(1)}, u32[]{:S(2)}, u32[]{:S(2)}) collective-permute-start(bf16[192,128]{1,0:T(8,128)(2,1)S(1)} %down_products.1.mine_ref), channel_id=1, source_target_pairs={{0,4},{2,6},{4,0},{6,2},{1,5},{3,7},{5,1},{7,3},{8,12},{10,14},{12... | collective-permute-start | bytes 147464 | tf_op jit(solution)/shard_map/far_coeff_sends/ppermute | solution.py:536
  65.8 1.5 %collective-permute-start.28 = (bf16[192,128]{1,0:T(8,128)(2,1)S(1)}, bf16[192,128]{1,0:T(8,128)(2,1)S(1)}, u32[]{:S(2)}, u32[]{:S(2)}) collective-permute-start(bf16[192,128]{1,0:T(8,128)(2,1)S(1)} %down_products.1.mine_ref), channel_id=1, source_target_pairs={{0,6},{2,4},{4,2},{6,0},{1,7},{3,5},{5,3},{7,1},{8,14},{10,12},{12... | collective-permute-start | bytes 147464 | tf_op jit(solution)/shard_map/far_coeff_sends/ppermute | solution.py:536
  69.5 1.3 %collective-permute-done.28.refs_3_ = bf16[192,128]{1,0:T(8,128)(2,1)S(1)} collective-permute-done((bf16[192,128]{1,0:T(8,128)(2,1)S(1)}, bf16[192,128]{1,0:T(8,128)(2,1)S(1)}, u32[]{:S(2)}, u32[]{:S(2)}) %collective-permute-start.28) | collective-permute-done | bytes 49184 | tf_op jit(solution)/shard_map/far_coeff_sends/ppermute | solution.py:536
  72.1 1.8 %column_products.1 = bf16[32,24,128]{2,1,0:T(8,128)(2,1)} custom-call(s32[3]{0:T(128)S(1)} %pad_add_fusion.2.ids_ref, bf16[64,32,128]{2,1,0:T(8,128)(2,1)S(1)} %copy-done.1, f32[384,128]{1,0:T(8,128)S(1)} %get-tuple-element.69.near_mine, bf16[384,128]{1,0:T(8,128)(2,1)S(1)} %collective-permute-done.23.near_peer, ...), custom_call_target="tpu_custom_call" | custom-call | bytes 6105000 | tf_op jit(solution)/shard_map/column_products/pallas_call | solution.py:525
  (71 shorter events, 11.5 us)
Async XLA Ops:
  0.0 13.0 %collective-permute-start.1 = (bf16[32,64,128]{2,1,0:T(8,128)(2,1)}, bf16[32,64,128]{2,1,0:T(8,128)(2,1)S(1)}, u32[]{:S(2)}, u32[]{:S(2)}) collective-permute-start(bf16[32,64,128]{2,1,0:T(8,128)(2,1)} %basis_ref.1), channel_id=1, source_target_pairs={{0,1},{1,0},{2,3},{3,2},{4,5},{5,4},{6,7},{7,6},{8,9},{9,8},{10,11... | collective-permute-start | bytes 1572872 | tf_op jit(solution)/shard_map/swap_row_basis/ppermute | solution.py:536
  0.5 21.2 %collective-permute-start.9 = (bf16[32,256,128]{2,1,0:T(8,128)(2,1)}, bf16[32,256,128]{2,1,0:T(8,128)(2,1)S(1)}, u32[]{:S(2)}, u32[]{:S(2)}) collective-permute-start(bf16[32,256,128]{2,1,0:T(8,128)(2,1)} %own_ref.7), channel_id=1, source_target_pairs={{0,1},{1,0},{2,3},{3,2},{4,5},{5,4},{6,7},{7,6},{8,9},{9,8},{10,11... | collective-permute-start | bytes 6291464 | tf_op jit(solution)/shard_map/swap_self_blocks/ppermute | solution.py:536
  2.5 5.7 %collective-permute-start = (bf16[192,128]{1,0:T(8,128)(2,1)S(1)}, bf16[192,128]{1,0:T(8,128)(2,1)S(1)}, u32[]{:S(2)}, u32[]{:S(2)}) collective-permute-start(bf16[192,128]{1,0:T(8,128)(2,1)S(1)} %get-tuple-element.74), channel_id=1, source_target_pairs={{0,8},{8,0},{16,24},{24,16},{1,9},{9,1},{17,25},{25,17},{2,10},{10... | collective-permute-start | bytes 147464 | tf_op jit(solution)/shard_map/regroup_sends/ppermute | solution.py:536
  5.6 7.4 %collective-permute-start.3 = (bf16[192,128]{1,0:T(8,128)(2,1)S(1)}, bf16[192,128]{1,0:T(8,128)(2,1)S(1)}, u32[]{:S(2)}, u32[]{:S(2)}) collective-permute-start(bf16[192,128]{1,0:T(8,128)(2,1)S(1)} %get-tuple-element.72), channel_id=1, source_target_pairs={{0,16},{8,24},{16,0},{24,8},{1,17},{9,25},{17,1},{25,9},{2,18},{10... | collective-permute-start | bytes 147464 | tf_op jit(solution)/shard_map/regroup_sends/ppermute | solution.py:536
  8.2 5.9 %collective-permute-start.4 = (bf16[192,128]{1,0:T(8,128)(2,1)S(1)}, bf16[192,128]{1,0:T(8,128)(2,1)S(1)}, u32[]{:S(2)}, u32[]{:S(2)}) collective-permute-start(bf16[192,128]{1,0:T(8,128)(2,1)S(1)} %get-tuple-element.71), channel_id=1, source_target_pairs={{0,24},{8,16},{16,8},{24,0},{1,25},{9,17},{17,9},{25,1},{2,26},{10... | collective-permute-start | bytes 147464 | tf_op jit(solution)/shard_map/regroup_sends/ppermute | solution.py:536
  9.0 4.0 %collective-permute-start.2 = (s32[4,128]{1,0:T(4,128)S(1)}, s32[4,128]{1,0:T(4,128)S(1)}, u32[]{:S(2)}, u32[]{:S(2)}) collective-permute-start(s32[4,128]{1,0:T(4,128)S(1)} %fusion.1.own_codes), channel_id=1, source_target_pairs={{0,1},{1,0},{2,3},{3,2},{4,5},{5,4},{6,7},{7,6},{8,9},{9,8},{10,11... | collective-permute-start | bytes 6152 | tf_op jit(solution)/shard_map/partner_codes/ppermute | solution.py:536
  12.9 8.7 %copy-start = (bf16[32,256,128]{2,1,0:T(8,128)(2,1)S(1)}, bf16[32,256,128]{2,1,0:T(8,128)(2,1)}, u32[]{:S(2)}) copy-start(bf16[32,256,128]{2,1,0:T(8,128)(2,1)} %own_ref.7) | copy-start | bytes 6291460
  14.4 1.6 %collective-permute-start.5 = (bf16[384,128]{1,0:T(8,128)(2,1)S(1)}, bf16[384,128]{1,0:T(8,128)(2,1)S(1)}, u32[]{:S(2)}, u32[]{:S(2)}) collective-permute-start(bf16[384,128]{1,0:T(8,128)(2,1)S(1)} %get-tuple-element.47), channel_id=1, source_target_pairs={{0,1},{1,0},{2,3},{3,2},{4,5},{5,4},{6,7},{7,6},{8,9},{9,8},{10,11... | collective-permute-start | bytes 294920 | tf_op jit(solution)/shard_map/swap_field/ppermute | solution.py:536
  17.6 26.6 %collective-permute-start.14 = (bf16[2,64,64,128]{3,2,1,0:T(8,128)(2,1)S(1)}, bf16[2,64,64,128]{3,2,1,0:T(8,128)(2,1)S(1)}, u32[]{:S(2)}, u32[]{:S(2)}) collective-permute-start(bf16[2,64,64,128]{3,2,1,0:T(8,128)(2,1)S(1)} %bitcast.31), channel_id=1, source_target_pairs={{0,1},{1,0},{2,3},{3,2},{4,5},{5,4},{6,7},{7,6},{8,9},{9,8},{10,11... | collective-permute-start | bytes 6291464 | tf_op jit(solution)/shard_map/swap_coupling/ppermute | solution.py:536
  18.2 6.1 %collective-permute-start.6 = (bf16[192,128]{1,0:T(8,128)(2,1)S(1)}, bf16[192,128]{1,0:T(8,128)(2,1)S(1)}, u32[]{:S(2)}, u32[]{:S(2)}) collective-permute-start(bf16[192,128]{1,0:T(8,128)(2,1)S(1)} %get-tuple-element.49), channel_id=1, source_target_pairs={{0,6},{2,4},{4,2},{6,0},{1,7},{3,5},{5,3},{7,1},{8,14},{10,12},{12... | collective-permute-start | bytes 147464 | tf_op jit(solution)/shard_map/coeff_sends/ppermute | solution.py:536
  20.6 4.1 %collective-permute-start.7 = (bf16[192,128]{1,0:T(8,128)(2,1)S(1)}, bf16[192,128]{1,0:T(8,128)(2,1)S(1)}, u32[]{:S(2)}, u32[]{:S(2)}) collective-permute-start(bf16[192,128]{1,0:T(8,128)(2,1)S(1)} %get-tuple-element.50), channel_id=1, source_target_pairs={{0,4},{2,6},{4,0},{6,2},{1,5},{3,7},{5,1},{7,3},{8,12},{10,14},{12... | collective-permute-start | bytes 147464 | tf_op jit(solution)/shard_map/coeff_sends/ppermute | solution.py:536
  21.1 4.1 %collective-permute-start.8 = (bf16[192,128]{1,0:T(8,128)(2,1)S(1)}, bf16[192,128]{1,0:T(8,128)(2,1)S(1)}, u32[]{:S(2)}, u32[]{:S(2)}) collective-permute-start(bf16[192,128]{1,0:T(8,128)(2,1)S(1)} %get-tuple-element.51), channel_id=1, source_target_pairs={{0,2},{2,0},{4,6},{6,4},{1,3},{3,1},{5,7},{7,5},{8,10},{10,8},{12,... | collective-permute-start | bytes 147464 | tf_op jit(solution)/shard_map/coeff_sends/ppermute | solution.py:536
  21.7 8.8 %copy-start.5 = (bf16[64,64,1,2,16]{1,4,3,2,0:T(8,128)(2,1)S(1)}, bf16[64,64,1,2,16]{1,4,3,2,0:T(8,128)(2,1)}, u32[]{:S(2)}) copy-start(bf16[64,64,1,2,16]{1,4,3,2,0:T(8,128)(2,1)} %param.19) | copy-start | bytes 786436
  26.0 9.6 %collective-permute-start.10 = (bf16[224,128]{1,0:T(8,128)(2,1)S(1)}, bf16[224,128]{1,0:T(8,128)(2,1)S(1)}, u32[]{:S(2)}, u32[]{:S(2)}) collective-permute-start(bf16[224,128]{1,0:T(8,128)(2,1)S(1)} %parent_coeffs.1), channel_id=1, source_target_pairs={{0,8},{8,0},{16,24},{24,16},{1,9},{9,1},{17,25},{25,17},{2,10},{10... | collective-permute-start | bytes 172040 | tf_op jit(solution)/shard_map/owner_sends/ppermute | solution.py:536
  26.5 9.1 %collective-permute-start.11 = (bf16[224,128]{1,0:T(8,128)(2,1)S(1)}, bf16[224,128]{1,0:T(8,128)(2,1)S(1)}, u32[]{:S(2)}, u32[]{:S(2)}) collective-permute-start(bf16[224,128]{1,0:T(8,128)(2,1)S(1)} %parent_coeffs.1), channel_id=1, source_target_pairs={{0,16},{8,24},{16,0},{24,8},{1,17},{9,25},{17,1},{25,9},{2,18},{10... | collective-permute-start | bytes 172040 | tf_op jit(solution)/shard_map/owner_sends/ppermute | solution.py:536
  29.7 6.0 %collective-permute-start.12 = (bf16[224,128]{1,0:T(8,128)(2,1)S(1)}, bf16[224,128]{1,0:T(8,128)(2,1)S(1)}, u32[]{:S(2)}, u32[]{:S(2)}) collective-permute-start(bf16[224,128]{1,0:T(8,128)(2,1)S(1)} %parent_coeffs.1), channel_id=1, source_target_pairs={{0,24},{8,16},{16,8},{24,0},{1,25},{9,17},{17,9},{25,1},{2,26},{10... | collective-permute-start | bytes 172040 | tf_op jit(solution)/shard_map/owner_sends/ppermute | solution.py:536
  30.4 11.4 %collective-permute-start.13 = (bf16[64,32,64]{2,1,0:T(8,128)(2,1)S(1)}, bf16[64,32,64]{2,1,0:T(8,128)(2,1)S(1)}, u32[]{:S(2)}, u32[]{:S(2)}) collective-permute-start(bf16[64,32,64]{2,1,0:T(8,128)(2,1)S(1)} %bitcast.36), channel_id=1, source_target_pairs={{0,1},{1,0},{2,3},{3,2},{4,5},{5,4},{6,7},{7,6},{8,9},{9,8},{10,11... | collective-permute-start | bytes 786440 | tf_op jit(solution)/shard_map/swap_parent_coupling/ppermute | solution.py:536
  35.7 8.5 %collective-permute-start.15 = (bf16[896,128]{1,0:T(8,128)(2,1)S(1)}, bf16[896,128]{1,0:T(8,128)(2,1)S(1)}, u32[]{:S(2)}, u32[]{:S(2)}) collective-permute-start(bf16[896,128]{1,0:T(8,128)(2,1)S(1)} %constant_dynamic-update-slice_fusion.block_ref), channel_id=1, source_target_pairs={{0,2},{2,0},{4,6},{6,4},{1,3},{3,1},{5,7},{7,5},{8,10},{10,8},{12,... | collective-permute-start | bytes 688136 | tf_op jit(solution)/shard_map/level_sends/ppermute | solution.py:536
  36.4 11.7 %collective-permute-start.17 = (bf16[896,128]{1,0:T(8,128)(2,1)S(1)}, bf16[896,128]{1,0:T(8,128)(2,1)S(1)}, u32[]{:S(2)}, u32[]{:S(2)}) collective-permute-start(bf16[896,128]{1,0:T(8,128)(2,1)S(1)} %constant_dynamic-update-slice_fusion.block_ref), channel_id=1, source_target_pairs={{0,4},{2,6},{4,0},{6,2},{1,5},{3,7},{5,1},{7,3},{8,12},{10,14},{12... | collective-permute-start | bytes 688136 | tf_op jit(solution)/shard_map/level_sends/ppermute | solution.py:536
  37.9 15.6 %collective-permute-start.19 = (bf16[896,128]{1,0:T(8,128)(2,1)S(1)}, bf16[896,128]{1,0:T(8,128)(2,1)S(1)}, u32[]{:S(2)}, u32[]{:S(2)}) collective-permute-start(bf16[896,128]{1,0:T(8,128)(2,1)S(1)} %constant_dynamic-update-slice_fusion.block_ref), channel_id=1, source_target_pairs={{0,6},{2,4},{4,2},{6,0},{1,7},{3,5},{5,3},{7,1},{8,14},{10,12},{12... | collective-permute-start | bytes 688136 | tf_op jit(solution)/shard_map/level_sends/ppermute | solution.py:536
  47.0 15.9 %collective-permute-start.16 = (bf16[992,128]{1,0:T(8,128)(2,1)S(1)}, bf16[992,128]{1,0:T(8,128)(2,1)S(1)}, u32[]{:S(2)}, u32[]{:S(2)}) collective-permute-start(bf16[992,128]{1,0:T(8,128)(2,1)S(1)} %coupling_products.5), channel_id=1, source_target_pairs={{0,2},{2,0},{4,6},{6,4},{1,3},{3,1},{5,7},{7,5},{8,10},{10,8},{12,... | collective-permute-start | bytes 761864 | tf_op jit(solution)/shard_map/far_sends/ppermute | solution.py:536
  50.9 12.0 %collective-permute-start.18 = (bf16[992,128]{1,0:T(8,128)(2,1)S(1)}, bf16[992,128]{1,0:T(8,128)(2,1)S(1)}, u32[]{:S(2)}, u32[]{:S(2)}) collective-permute-start(bf16[992,128]{1,0:T(8,128)(2,1)S(1)} %coupling_products.6), channel_id=1, source_target_pairs={{0,4},{2,6},{4,0},{6,2},{1,5},{3,7},{5,1},{7,3},{8,12},{10,14},{12... | collective-permute-start | bytes 761864 | tf_op jit(solution)/shard_map/far_sends/ppermute | solution.py:536
  56.3 5.1 %collective-permute-start.20 = (bf16[224,128]{1,0:T(8,128)(2,1)S(1)}, bf16[224,128]{1,0:T(8,128)(2,1)S(1)}, u32[]{:S(2)}, u32[]{:S(2)}) collective-permute-start(bf16[224,128]{1,0:T(8,128)(2,1)S(1)} %coupling_products.7), channel_id=1, source_target_pairs={{0,6},{2,4},{4,2},{6,0},{1,7},{3,5},{5,3},{7,1},{8,14},{10,12},{12... | collective-permute-start | bytes 172040 | tf_op jit(solution)/shard_map/far_sends/ppermute | solution.py:536
  61.4 6.8 %collective-permute-start.22 = (bf16[768,128]{1,0:T(8,128)(2,1)S(1)}, bf16[768,128]{1,0:T(8,128)(2,1)S(1)}, u32[]{:S(2)}, u32[]{:S(2)}) collective-permute-start(bf16[768,128]{1,0:T(8,128)(2,1)S(1)} %self_blocks.6), channel_id=1, source_target_pairs={{0,6},{2,4},{4,2},{6,0},{1,7},{3,5},{5,3},{7,1},{8,14},{10,12},{12... | collective-permute-start | bytes 589832 | tf_op jit(solution)/shard_map/self_sends/ppermute | solution.py:536
  63.7 3.6 %collective-permute-start.21 = (bf16[192,128]{1,0:T(8,128)(2,1)S(1)}, bf16[192,128]{1,0:T(8,128)(2,1)S(1)}, u32[]{:S(2)}, u32[]{:S(2)}) collective-permute-start(bf16[192,128]{1,0:T(8,128)(2,1)S(1)} %down_products.1.mine_ref), channel_id=1, source_target_pairs={{0,1},{1,0},{2,3},{3,2},{4,5},{5,4},{6,7},{7,6},{8,9},{9,8},{10,11... | collective-permute-start | bytes 147464 | tf_op jit(solution)/shard_map/far_coeff_sends/ppermute | solution.py:536
  63.8 5.1 %collective-permute-start.24 = (bf16[192,128]{1,0:T(8,128)(2,1)S(1)}, bf16[192,128]{1,0:T(8,128)(2,1)S(1)}, u32[]{:S(2)}, u32[]{:S(2)}) collective-permute-start(bf16[192,128]{1,0:T(8,128)(2,1)S(1)} %down_products.1.mine_ref), channel_id=1, source_target_pairs={{0,2},{2,0},{4,6},{6,4},{1,3},{3,1},{5,7},{7,5},{8,10},{10,8},{12,... | collective-permute-start | bytes 147464 | tf_op jit(solution)/shard_map/far_coeff_sends/ppermute | solution.py:536
  64.6 4.8 %collective-permute-start.26 = (bf16[192,128]{1,0:T(8,128)(2,1)S(1)}, bf16[192,128]{1,0:T(8,128)(2,1)S(1)}, u32[]{:S(2)}, u32[]{:S(2)}) collective-permute-start(bf16[192,128]{1,0:T(8,128)(2,1)S(1)} %down_products.1.mine_ref), channel_id=1, source_target_pairs={{0,4},{2,6},{4,0},{6,2},{1,5},{3,7},{5,1},{7,3},{8,12},{10,14},{12... | collective-permute-start | bytes 147464 | tf_op jit(solution)/shard_map/far_coeff_sends/ppermute | solution.py:536
  65.8 5.0 %collective-permute-start.28 = (bf16[192,128]{1,0:T(8,128)(2,1)S(1)}, bf16[192,128]{1,0:T(8,128)(2,1)S(1)}, u32[]{:S(2)}, u32[]{:S(2)}) collective-permute-start(bf16[192,128]{1,0:T(8,128)(2,1)S(1)} %down_products.1.mine_ref), channel_id=1, source_target_pairs={{0,6},{2,4},{4,2},{6,0},{1,7},{3,5},{5,3},{7,1},{8,14},{10,12},{12... | collective-permute-start | bytes 147464 | tf_op jit(solution)/shard_map/far_coeff_sends/ppermute | solution.py:536
  68.8 3.2 %collective-permute-start.23 = (bf16[384,128]{1,0:T(8,128)(2,1)S(1)}, bf16[384,128]{1,0:T(8,128)(2,1)S(1)}, u32[]{:S(2)}, u32[]{:S(2)}) collective-permute-start(bf16[384,128]{1,0:T(8,128)(2,1)S(1)} %get-tuple-element.70), channel_id=1, source_target_pairs={{0,1},{1,0},{2,3},{3,2},{4,5},{5,4},{6,7},{7,6},{8,9},{9,8},{10,11... | collective-permute-start | bytes 294920 | tf_op jit(solution)/shard_map/swap_self_sums/ppermute | solution.py:536
  68.9 1.9 %collective-permute-start.25 = (bf16[192,128]{1,0:T(8,128)(2,1)S(1)}, bf16[192,128]{1,0:T(8,128)(2,1)S(1)}, u32[]{:S(2)}, u32[]{:S(2)}) collective-permute-start(bf16[192,128]{1,0:T(8,128)(2,1)S(1)} %collective-permute-done.24.mine_ref), channel_id=1, source_target_pairs={{0,1},{1,0},{2,3},{3,2},{4,5},{5,4},{6,7},{7,6},{8,9},{9,8},{10,11... | collective-permute-start | bytes 147464 | tf_op jit(solution)/shard_map/far_coeff_sends/ppermute | solution.py:536
  69.4 1.9 %collective-permute-start.27 = (bf16[192,128]{1,0:T(8,128)(2,1)S(1)}, bf16[192,128]{1,0:T(8,128)(2,1)S(1)}, u32[]{:S(2)}, u32[]{:S(2)}) collective-permute-start(bf16[192,128]{1,0:T(8,128)(2,1)S(1)} %collective-permute-done.26.mine_ref), channel_id=1, source_target_pairs={{0,1},{1,0},{2,3},{3,2},{4,5},{5,4},{6,7},{7,6},{8,9},{9,8},{10,11... | collective-permute-start | bytes 147464 | tf_op jit(solution)/shard_map/far_coeff_sends/ppermute | solution.py:536
  70.8 1.2 %collective-permute-start.29 = (bf16[192,128]{1,0:T(8,128)(2,1)S(1)}, bf16[192,128]{1,0:T(8,128)(2,1)S(1)}, u32[]{:S(2)}, u32[]{:S(2)}) collective-permute-start(bf16[192,128]{1,0:T(8,128)(2,1)S(1)} %collective-permute-done.28.refs_3_), channel_id=1, source_target_pairs={{0,1},{1,0},{2,3},{3,2},{4,5},{5,4},{6,7},{7,6},{8,9},{9,8},{10,11... | collective-permute-start | bytes 147464 | tf_op jit(solution)/shard_map/far_coeff_sends/ppermute | solution.py:536
  (4 other events, 20.7 us)
